TPU v7x, 32 devices: a whole 2x2x4 slice. The times are simulated.
32 devices in a mesh: dp: 8 (over z, core), fsdp: 4 (over y, x).
Axes of the slice: x: 2, y: 2, z: 4, core: 2. Of those that a mesh axis runs over, the one named last changes fastest.
Arguments:
- activations: bfloat16 [1, 8192, 8192], P(None, 'dp', 'fsdp'), may hold values from -6 to 6
- out_grads: bfloat16 [1, 8192, 22016], P(None, 'dp', 'fsdp'), may hold values from -3 to 3
- projector: bfloat16 [1, 8192, 1024], P(None, 'fsdp'), may hold values from -0.046875 to 0.046875
- first_moment: float32 [1, 22016, 1024], P(None, ('fsdp', 'dp')), may hold values from -16 to 16
- second_moment: float32 [1, 22016, 1024], P(None, ('fsdp', 'dp')), may hold values from 0.05 to 2
Outputs:
- weight_update: float32 [1, 4, 5504, 8192], P(None, None, 'dp', 'fsdp')
- first_new: float32 [1, 22016, 1024], P(None, ('fsdp', 'dp'))
- second_new: float32 [1, 22016, 1024], P(None, ('fsdp', 'dp'))
All inputs are finite; a program needn't handle non-finite values.
Results may differ from a plain program's by a relative error of at most 0.018.
Values may be sent and summed in bfloat16 or wider, within the bound.
No kernel may reach another device: no remote copies, remote signals or barrier semaphores. Data moves between devices by JAX's collectives and lax.ppermute only.
A program may use at most 128 MiB of HBM per device.

v0:
```python
import jax
import jax.numpy as jnp
from jax import lax
from jax.sharding import PartitionSpec as P

beta_first = 0.9
beta_second = 0.999
adam_count = 100.0
epsilon = 1e-08


def adam_direction(grad_low, first, second):
    first_next = beta_first * first + (1.0 - beta_first) * grad_low
    second_next = beta_second * second + (1.0 - beta_second) * grad_low * grad_low
    bias_first = 1.0 - beta_first**adam_count
    bias_second = 1.0 - beta_second**adam_count
    direction = first_next / bias_first / (jnp.sqrt(second_next / bias_second) + epsilon)
    return (first_next, second_next, direction.astype(jnp.bfloat16))


def local(activations, out_grads, projector, first_moment, second_moment):
    owned_cols = first_moment.shape[1]
    fsdp_count = lax.axis_size("fsdp")
    features = activations[0]
    grads = out_grads[0]
    basis = projector[0]
    partial_value = jnp.dot(features, basis, preferred_element_type=jnp.float32)
    projected = lax.psum(partial_value.astype(jnp.bfloat16), "fsdp")
    grad_low = lax.psum_scatter(
        lax.dot_general(
            grads, projected, (((0,), (0,)), ((), ())), preferred_element_type=jnp.float32
        ).astype(jnp.bfloat16),
        "dp",
        scatter_dimension=0,
        tiled=True,
    ).astype(jnp.float32)
    first_next, second_next, direction = adam_direction(grad_low, first_moment[0], second_moment[0])
    expanded = lax.dot_general(
        lax.all_gather(direction, "fsdp", axis=0, tiled=True),
        basis,
        (((1,), (1,)), ((), ())),
        preferred_element_type=jnp.float32,
    )
    updates = [expanded.reshape(fsdp_count, owned_cols, basis.shape[0])]
    firsts = [first_next]
    seconds = [second_next]
    return (jnp.stack(updates), jnp.stack(firsts), jnp.stack(seconds))


def solution(mesh):
    in_specs = (
        P(None, "dp", "fsdp"),
        P(None, "dp", "fsdp"),
        P(None, "fsdp", None),
        P(None, ("fsdp", "dp"), None),
        P(None, ("fsdp", "dp"), None),
    )
    out_specs = (
        P(None, None, "dp", "fsdp"),
        P(None, ("fsdp", "dp"), None),
        P(None, ("fsdp", "dp"), None),
    )
    return jax.shard_map(local, mesh=mesh, in_specs=in_specs, out_specs=out_specs, check_vma=False)
```

profile of v0, /device:TPU:0, one launch (start us, length us, event | category | flops | bytes accessed | tf_op | source)
XLA Modules:
  0.0 343.2 jit_solution(16212830976822674939)
XLA Ops:
  7.2 0.0 all-reduce.2.cloned.1.call-start
  7.2 9.3 %fusion.10 = bf16[1024,1024]{1,0:T(8,128)(2,1)} fusion(bf16[1,2048,1024]{2,1,0:T(8,128)(2,1)} %param.7, bf16[1,1024,2048]{2,1,0:T(8,128)(2,1)} %param.5), kind=kOutput, calls=%fused_computation.13 | convolution fusion | flops 4296015872 | bytes 10485760 | tf_op jit(solution)/shard_map/dot_general | solution.py:27
  16.5 0.0 all-reduce.2.cloned.1.call-update
  16.5 0.0 reduce-scatter.4.cloned.1.call-start
  16.6 72.4 %all-reduce.2.cloned.1.call-done = bf16[1024,1024]{1,0:T(8,128)(2,1)} async-done(((bf16[1024,1024]{1,0:T(8,128)(2,1)}), bf16[1024,1024]{1,0:T(8,128)(2,1)}) %all-reduce.2.cloned.1.call-update) | async-done | bytes 2097168 | tf_op jit(solution)/shard_map/psum | solution.py:28
  89.0 19.4 %fusion.1 = bf16[5504,1024]{0,1:T(8,128)(2,1)} fusion(bf16[1024,1024]{1,0:T(8,128)(2,1)} %all-reduce.2.cloned.1.call-done, bf16[1,1024,5504]{2,1,0:T(8,128)(2,1)} %param.6), kind=kOutput, calls=%fused_computation.2 | convolution fusion | flops 11548360704 | bytes 24641536 | tf_op jit(solution)/shard_map/dot_general | solution.py:30
  108.4 15.6 %copy.23 = bf16[5504,1024]{1,0:T(8,128)(2,1)} copy(bf16[5504,1024]{0,1:T(8,128)(2,1)} %fusion.1) | data formatting | bytes 22544384
  124.0 0.0 copy-start
  124.0 0.0 reduce-scatter.4.cloned.1.call-update
  124.1 0.2 all-gather.2.cloned.1.call-start
  124.3 1.5 copy-done
  125.8 2.4 copy.18
  128.3 3.5 %copy.19 = f32[1,688,1024]{1,2,0:T(8,128)} copy(f32[1,688,1024]{2,1,0:T(8,128)} %param.9) | data formatting | bytes 5636096 | tf_op args[4]
  131.7 109.3 %reduce-scatter.4.cloned.1.call-done = bf16[688,1024]{1,0:T(8,128)(2,1)} async-done(((bf16[5504,1024]{1,0:T(8,128)(2,1)}), bf16[688,1024]{1,0:T(8,128)(2,1)}) %reduce-scatter.4.cloned.1.call-update) | async-done | bytes 1409040
  241.1 2.5 copy.24
  243.6 7.8 %fusion.16 = (f32[1,688,1024]{1,2,0:T(8,128)}, bf16[688,1024]{0,1:T(8,128)(2,1)}, f32[1,688,1024]{1,2,0:T(8,128)S(1)}) fusion(bf16[688,1024]{0,1:T(8,128)(2,1)} %copy.24, f32[1,688,1024]{1,2,0:T(8,128)} %copy.19, f32[1,688,1024]{1,2,0:T(8,128)} %copy.18), kind=kLoop, calls=%fused_computation.15 | loop fusion | flops 9158656 | bytes 14090240 | tf_op jit(solution)/shard_map/stack | solution.py:47
  251.4 2.6 copy.20
  253.9 0.0 all-gather.2.cloned.1.call-update
  254.0 3.4 copy.22
  257.4 2.2 copy.21
  259.6 57.6 %all-gather.2.cloned.1.call-done = bf16[2752,1024]{1,0:T(8,128)(2,1)} async-done(((bf16[688,1024]{1,0:T(8,128)(2,1)}), bf16[2752,1024]{1,0:T(8,128)(2,1)}) %all-gather.2.cloned.1.call-update) | async-done | bytes 5636112 | tf_op jit(solution)/shard_map/all_gather | solution.py:39
  317.2 19.5 %convolution_bitcast_fusion = f32[1,4,688,2048]{3,2,1,0:T(8,128)} fusion(bf16[4,688,1024]{2,1,0:T(8,128)(2,1)} %bitcast.42, bf16[1,2048,1024]{2,1,0:T(8,128)(2,1)} %param.7), kind=kOutput, calls=%fused_computation.3 | convolution fusion | flops 11542724608 | bytes 32374784 | tf_op jit(solution)/shard_map/dot_general | solution.py:38
Async XLA Ops:
  7.2 81.8 %all-reduce.2.cloned.1.call-start = ((), (), s32[]{:S(2)}) async-start(), calls=%async_computation.1 | async-start | bytes 4194304 | tf_op jit(solution)/shard_map/psum | solution.py:28
  16.5 224.5 %reduce-scatter.4.cloned.1.call-start = ((), (), s32[]{:S(2)}) async-start(), calls=%async_computation.3 | async-start | bytes 12681216
  124.0 1.8 copy-start
  124.1 193.1 %all-gather.2.cloned.1.call-start = ((), (), s32[]{:S(2)}) async-start(), calls=%async_computation.2 | async-start | bytes 7045120 | tf_op jit(solution)/shard_map/all_gather | solution.py:39
Sparse Core Ops, SparseCore 0:
  16.6 72.3 all-reduce.1
  124.2 116.8 reduce-scatter.3
  254.1 63.0 all-gather.1
where the time goes:
time: 344 us; the launch traced here: 343 us
  waiting for transfers between devices  239 us (69%)
  matrix products  48.2 us (14%)
  local copies, waits for them, and re-layouts  33.8 us (10%)
  between operations  13.7 us (4%)
  other arithmetic  7.76 us (2%)
    unnamed x4, waiting for transfers between devices  109 us
    psum x1, waiting for transfers between devices, local(): projected = lax.psum(partial_value.astype(jnp.bfloat16), 'fsdp')  72.4 us
    all_gather x1, waiting for transfers between devices, local(): lax.all_gather(direction, 'fsdp', axis=0, tiled=True)  57.6 us
    unnamed x8, local copies, waits for them, and re-layouts  31.2 us
    dot_general x1, matrix products, local(): lax.dot_general(lax.all_gather(direction, 'fsdp', axis=0, tiled=True), ba...  19.5 us
    dot_general x1, matrix products, local(): lax.dot_general(grads, projected, (((0,), (0,)), ((), ())), preferred_ele...  19.4 us
    dot_general x1, matrix products, local(): partial_value = jnp.dot(features, basis, preferred_element_type=jnp.float32)  9.27 us
    another operation x1, other arithmetic, local(): return (jnp.stack(updates), jnp.stack(firsts), jnp.stack(seconds))  7.76 us
  transfers between devices with their start and end apart: 3, of which 3 were waited for; matrix products, arithmetic and copies ran while one was open for 3% of the time, Pallas kernels for 0%

commit v1 on v0

v1 whole, which is shorter than its diff:
```python
import functools

import jax
import jax.numpy as jnp
from jax import lax
from jax.experimental import pallas as pl
from jax.experimental.pallas import tpu as pltpu
from jax.sharding import PartitionSpec as P

beta_first = 0.9
beta_second = 0.999
adam_count = 100.0
epsilon = 1e-08

F32 = jnp.float32
BF16 = jnp.bfloat16
VMEM_LIMIT = 56 * 1024 * 1024
PARTS = 4


def project(features, basis, order, part, width):
    tokens, depth = features.shape
    count = order.shape[0]
    rows = tokens // count

    def kernel(order_ref, features_ref, basis_ref, *out_refs):
        value = jnp.dot(features_ref[...], basis_ref[...], preferred_element_type=F32).astype(BF16)
        for index, out_ref in enumerate(out_refs):

            @pl.when(pl.program_id(0) == index)
            def _(out_ref=out_ref):
                out_ref[...] = value

    return pl.pallas_call(
        kernel,
        out_shape=[jax.ShapeDtypeStruct((rows, width), BF16)] * count,
        grid_spec=pltpu.PrefetchScalarGridSpec(
            num_scalar_prefetch=1,
            grid=(count,),
            in_specs=[
                pl.BlockSpec((rows, depth), lambda i, order_ref: (order_ref[i], 0)),
                pl.BlockSpec((depth, width), lambda i, order_ref: (0, part)),
            ],
            out_specs=[pl.BlockSpec((rows, width), lambda i, order_ref: (0, 0))] * count,
        ),
        compiler_params=pltpu.CompilerParams(vmem_limit_bytes=VMEM_LIMIT),
        cost_estimate=pl.CostEstimate(
            flops=2 * tokens * depth * width,
            bytes_accessed=2 * (tokens * depth + depth * width + tokens * width),
            transcendentals=0,
        ),
        name="project",
    )(order, features, basis)


def gradient(grads_t, pieces, order, owners):
    _, owned, tokens = grads_t.shape
    rows, width = pieces[0].shape
    count = owners.shape[0]

    def kernel(order_ref, owners_ref, grads_ref, *refs):
        piece_refs, (out_ref, whole_ref) = refs[:-2], refs[-2:]

        @pl.when(pl.program_id(0) == 0)
        def _():
            for index, piece_ref in enumerate(piece_refs):
                start = pl.multiple_of(order_ref[index] * rows, rows)
                whole_ref[pl.ds(start, rows), :] = piece_ref[...]

        out_ref[0] = jnp.dot(grads_ref[0], whole_ref[...], preferred_element_type=F32).astype(BF16)

    return pl.pallas_call(
        kernel,
        out_shape=jax.ShapeDtypeStruct((count, owned, width), BF16),
        grid_spec=pltpu.PrefetchScalarGridSpec(
            num_scalar_prefetch=2,
            grid=(count,),
            in_specs=[pl.BlockSpec((1, owned, tokens), lambda i, order_ref, owners_ref: (owners_ref[i], 0, 0))]
            + [pl.BlockSpec((rows, width), lambda i, order_ref, owners_ref: (0, 0))] * len(pieces),
            out_specs=pl.BlockSpec((1, owned, width), lambda i, order_ref, owners_ref: (i, 0, 0)),
            scratch_shapes=[pltpu.VMEM((tokens, width), BF16)],
        ),
        compiler_params=pltpu.CompilerParams(vmem_limit_bytes=VMEM_LIMIT),
        cost_estimate=pl.CostEstimate(
            flops=2 * count * owned * tokens * width,
            bytes_accessed=2 * (count * owned * tokens + tokens * width + count * owned * width),
            transcendentals=0,
        ),
        name="gradient",
    )(order, owners, grads_t, *pieces)


def adam(arrived, own, other, first, second, held, part):
    owned, rank = first.shape
    width = arrived.shape[1]
    last = own.shape[0] - 1

    def kernel(arrived_ref, own_ref, other_ref, first_ref, second_ref, *refs):
        first_out, second_out, direction_out = refs[-3:]
        grad_low = arrived_ref[...].astype(F32) + own_ref[0].astype(F32) + other_ref[0].astype(F32)
        first_next = beta_first * first_ref[...] + (1.0 - beta_first) * grad_low
        second_next = beta_second * second_ref[...] + (1.0 - beta_second) * grad_low * grad_low
        first_out[...] = first_next
        second_out[...] = second_next
        bias_first = 1.0 - beta_first**adam_count
        bias_second = 1.0 - beta_second**adam_count
        direction = first_next / bias_first / (jnp.sqrt(second_next / bias_second) + epsilon)
        direction_out[...] = direction.astype(BF16)

    column = pl.BlockSpec((owned, width), lambda i: (0, part))
    return pl.pallas_call(
        kernel,
        grid=(1,),
        out_shape=[
            jax.ShapeDtypeStruct((owned, rank), F32),
            jax.ShapeDtypeStruct((owned, rank), F32),
            jax.ShapeDtypeStruct((owned, width), BF16),
        ],
        in_specs=[
            pl.BlockSpec((owned, width), lambda i: (0, 0)),
            pl.BlockSpec((1, owned, width), lambda i: (last, 0, 0)),
            pl.BlockSpec((1, owned, width), lambda i: (last, 0, 0)),
            column,
            column,
        ]
        + [pl.BlockSpec(memory_space=pl.ANY)] * len(held),
        out_specs=[column, column, pl.BlockSpec((owned, width), lambda i: (0, 0))],
        input_output_aliases={5 + index: index for index in range(len(held))},
        compiler_params=pltpu.CompilerParams(vmem_limit_bytes=VMEM_LIMIT),
        cost_estimate=pl.CostEstimate(
            flops=12 * owned * width, bytes_accessed=24 * owned * width, transcendentals=owned * width
        ),
        name="adam",
    )(arrived, own, other, first, second, *held)


def expand(directions, basis, target, held, count):
    owned, width = directions[0].shape
    features, rank = basis.shape
    block = min(512, features)

    def kernel(target_ref, basis_ref, *refs):
        direction_refs, out_ref = refs[: len(directions)], refs[-1]
        total = None
        for index, direction_ref in enumerate(direction_refs):
            term = lax.dot_general(
                direction_ref[...],
                basis_ref[:, index * width : (index + 1) * width],
                (((1,), (1,)), ((), ())),
                preferred_element_type=F32,
            )
            total = term if total is None else total + term
        out_ref[0] = total

    return pl.pallas_call(
        kernel,
        out_shape=jax.ShapeDtypeStruct((count, owned, features), F32),
        grid_spec=pltpu.PrefetchScalarGridSpec(
            num_scalar_prefetch=1,
            grid=(features // block,),
            in_specs=[pl.BlockSpec((block, rank), lambda i, target_ref: (i, 0))]
            + [pl.BlockSpec((owned, width), lambda i, target_ref: (0, 0))] * len(directions)
            + [pl.BlockSpec(memory_space=pl.ANY)] * len(held),
            out_specs=pl.BlockSpec((1, owned, block), lambda i, target_ref: (target_ref[0], 0, i)),
        ),
        input_output_aliases={2 + len(directions): 0} if held else {},
        compiler_params=pltpu.CompilerParams(vmem_limit_bytes=VMEM_LIMIT),
        cost_estimate=pl.CostEstimate(
            flops=2 * owned * rank * features,
            bytes_accessed=2 * (owned * rank + rank * features) + 4 * owned * features,
            transcendentals=0,
        ),
        name="expand",
    )(target, basis, *directions, *held)


def total_of(terms):
    total = terms[0].astype(F32)
    for term in terms[1:]:
        total = total + term.astype(F32)
    return total.astype(BF16)


def local(activations, out_grads, projector, first_moment, second_moment):
    owned = first_moment.shape[1]
    features = activations[0]
    basis = projector[0]
    rank = basis.shape[1]
    tokens = features.shape[0]
    dp_count, fsdp_count = lax.axis_size("dp"), lax.axis_size("fsdp")
    dp, fsdp = lax.axis_index("dp"), lax.axis_index("fsdp")
    chips = dp_count // 2
    chip, core = dp // 2, dp % 2
    width = rank // PARTS

    partner = functools.partial(lax.bitwise_xor, fsdp)
    order = jnp.stack([partner(jnp.int32(offset)) for offset in range(fsdp_count)]).astype(jnp.int32)
    hops = jnp.arange(chips, dtype=jnp.int32)
    ring_order = (chip - 1 - hops + chips) % chips
    own_owners = (ring_order * 2 + core).astype(jnp.int32)
    other_owners = (ring_order * 2 + 1 - core).astype(jnp.int32)

    def across(value, offset):
        return lax.ppermute(value, "fsdp", [(index, index ^ offset) for index in range(fsdp_count)])

    def sibling(value):
        return lax.ppermute(value, "dp", [(index, index ^ 1) for index in range(dp_count)])

    def onward(value):
        return lax.ppermute(value, "dp", [(index, (index + 2) % dp_count) for index in range(dp_count)])

    partials = [project(features, basis, order, part, width) for part in range(PARTS)]
    grads_t = out_grads[0].reshape(tokens, dp_count, owned).transpose(1, 2, 0)

    held = ()
    directions = []
    for part in range(PARTS):
        pieces = partials[part]
        mine = total_of([pieces[0]] + [across(pieces[offset], offset) for offset in range(1, fsdp_count)])
        projected = [mine] + [across(mine, offset) for offset in range(1, fsdp_count)]
        other = sibling(gradient(grads_t, projected, order, other_owners))
        own = gradient(grads_t, projected, order, own_owners)
        travelling = onward(total_of([own[0], other[0]]))
        for hop in range(1, chips - 1):
            travelling = onward(total_of([travelling, own[hop], other[hop]]))
        first_next, second_next, direction = adam(
            travelling, own, other, first_moment[0], second_moment[0], held, part
        )
        held = (first_next, second_next)
        directions.append([direction] + [across(direction, offset) for offset in range(1, fsdp_count)])

    update = ()
    for offset in range(fsdp_count):
        update = (
            expand(
                [gathered[offset] for gathered in directions],
                basis,
                order[offset : offset + 1],
                update,
                fsdp_count,
            ),
        )
    return (update[0][None], held[0][None], held[1][None])


def solution(mesh):
    in_specs = (
        P(None, "dp", "fsdp"),
        P(None, "dp", "fsdp"),
        P(None, "fsdp", None),
        P(None, ("fsdp", "dp"), None),
        P(None, ("fsdp", "dp"), None),
    )
    out_specs = (
        P(None, None, "dp", "fsdp"),
        P(None, ("fsdp", "dp"), None),
        P(None, ("fsdp", "dp"), None),
    )
    return jax.shard_map(local, mesh=mesh, in_specs=in_specs, out_specs=out_specs, check_vma=False)
```

time: 344 us -> 327 us (0.951)
  Pallas kernels: 0 us -> 116 us
  waiting for transfers between devices: 239 us -> 127 us
  matrix products: 48.2 us -> 0 us
  starting transfers between devices: 0.3 us -> 44.8 us
  between operations: 13.7 us -> 1.17 us
  local copies, waits for them, and re-layouts: 33.8 us -> 23.5 us
  other arithmetic: 7.76 us -> 12.5 us
    ppermute x0 -> x52, waiting for transfers between devices: none -> 127 us  [the longest x12 71.9 us: onward(): lax.ppermute(value, 'dp', [(index, (index + 2) % dp_count) for index in r...]
    pallas_call x0 -> x20, Pallas kernels: none -> 116 us  [the longest x8 50.1 us: gradient(): pl.pallas_call(kernel, out_shape=jax.ShapeDtypeStruct((count, owned, widt...]
    unnamed x4 -> x0, waiting for transfers between devices: 109 us -> none
    psum x1 -> x0, waiting for transfers between devices: 72.4 us -> none  [local(): projected = lax.psum(partial_value.astype(jnp.bfloat16), 'fsdp')]
    all_gather x1 -> x0, waiting for transfers between devices: 57.6 us -> none  [local(): lax.all_gather(direction, 'fsdp', axis=0, tiled=True)]
    dot_general x3 -> x0, matrix products: 48.2 us -> none  [the longest x1 19.5 us: local(): lax.dot_general(lax.all_gather(direction, 'fsdp', axis=0, tiled=True), ba...]
    ppermute x0 -> x52, starting transfers between devices: none -> 44.8 us  [the longest x36 37 us: across(): lax.ppermute(value, 'fsdp', [(index, index ^ offset) for index in range(f...]
    convert_element_type x0 -> x16, other arithmetic: none -> 10.7 us  [total_of(): return total.astype(BF16)]
  transfers between devices with their start and end apart: 3 -> 52, of which waited for: 3 -> 19; matrix products, arithmetic and copies ran while one was open for 3% -> 8% of each run, Pallas kernels for 0% -> 31%
where the time goes in v1:
time: 327 us; the launch traced here: 325 us
  waiting for transfers between devices  127 us (39%)
  Pallas kernels  116 us (35%)
  starting transfers between devices  44.8 us (14%)
  local copies, waits for them, and re-layouts  23.5 us (7%)
  other arithmetic  12.5 us (4%)
    ppermute x12, waiting for transfers between devices, onward(): lax.ppermute(value, 'dp', [(index, (index + 2) % dp_count) for index in r...  71.9 us
    ppermute x36, waiting for transfers between devices, across(): lax.ppermute(value, 'fsdp', [(index, index ^ offset) for index in range(f...  55.3 us
    pallas_call x8, Pallas kernels, gradient(): pl.pallas_call(kernel, out_shape=jax.ShapeDtypeStruct((count, owned, widt...  50.1 us
    ppermute x36, starting transfers between devices, across(): lax.ppermute(value, 'fsdp', [(index, index ^ offset) for index in range(f...  37 us
    pallas_call x4, Pallas kernels, expand(): pl.pallas_call(kernel, out_shape=jax.ShapeDtypeStruct((count, owned, feat...  29.4 us
    unnamed x111, local copies, waits for them, and re-layouts  23.5 us
    pallas_call x4, Pallas kernels, project(): pl.pallas_call(kernel, out_shape=[jax.ShapeDtypeStruct((rows, width), BF1...  23 us
    pallas_call x4, Pallas kernels, adam(): pl.pallas_call(kernel, grid=(1,), out_shape=[jax.ShapeDtypeStruct((owned,...  13.1 us
  transfers between devices with their start and end apart: 52, of which 19 were waited for; matrix products, arithmetic and copies ran while one was open for 8% of the time, Pallas kernels for 31%

profile of v1, /device:TPU:0, one launch (start us, length us, event | category | flops | bytes accessed | tf_op | source)
XLA Modules:
  0.0 324.8 jit_solution(14792226056607765020)
XLA Ops:
  1.3 5.8 %project.7 = (bf16[256,256]{1,0:T(8,128)(2,1)}, bf16[256,256]{1,0:T(8,128)(2,1)}, bf16[256,256]{1,0:T(8,128)(2,1)}, bf16[256,256]{1,0:T(8,128)(2,1)}) custom-call(s32[4]{0:T(128)} %pad_add_fusion.order_ref, bf16[1024,2048]{1,0:T(8,128)(2,1)} %bitcast.119, bf16[2048,1024]{1,0:T(8,128)(2,1)} %bitcast.111), custom_call_target="tpu_custom_call" | custom-call | flops 1073741824 | bytes 5767168 | tf_op jit(solution)/shard_map/project/pallas_call | solution.py:34
  7.1 2.9 collective-permute-start.33
  10.0 1.5 collective-permute-start.34
  11.5 5.8 %project.6 = (bf16[256,256]{1,0:T(8,128)(2,1)}, bf16[256,256]{1,0:T(8,128)(2,1)}, bf16[256,256]{1,0:T(8,128)(2,1)}, bf16[256,256]{1,0:T(8,128)(2,1)}) custom-call(s32[4]{0:T(128)} %pad_add_fusion.order_ref, bf16[1024,2048]{1,0:T(8,128)(2,1)} %bitcast.120, bf16[2048,1024]{1,0:T(8,128)(2,1)} %bitcast.112), custom_call_target="tpu_custom_call" | custom-call | flops 1073741824 | bytes 5767168 | tf_op jit(solution)/shard_map/project/pallas_call | solution.py:34
  17.3 2.0 collective-permute-start.22
  19.2 1.5 collective-permute-start.23
  20.7 5.8 %project.5 = (bf16[256,256]{1,0:T(8,128)(2,1)}, bf16[256,256]{1,0:T(8,128)(2,1)}, bf16[256,256]{1,0:T(8,128)(2,1)}, bf16[256,256]{1,0:T(8,128)(2,1)}) custom-call(s32[4]{0:T(128)} %pad_add_fusion.order_ref, bf16[1024,2048]{1,0:T(8,128)(2,1)} %bitcast.121, bf16[2048,1024]{1,0:T(8,128)(2,1)} %bitcast.113), custom_call_target="tpu_custom_call" | custom-call | flops 1073741824 | bytes 5767168 | tf_op jit(solution)/shard_map/project/pallas_call | solution.py:34
  26.5 5.7 %project.4 = (bf16[256,256]{1,0:T(8,128)(2,1)}, bf16[256,256]{1,0:T(8,128)(2,1)}, bf16[256,256]{1,0:T(8,128)(2,1)}, bf16[256,256]{1,0:T(8,128)(2,1)}) custom-call(s32[4]{0:T(128)} %pad_add_fusion.order_ref, bf16[1024,2048]{1,0:T(8,128)(2,1)} %bitcast.122, bf16[2048,1024]{1,0:T(8,128)(2,1)} %bitcast.114), custom_call_target="tpu_custom_call" | custom-call | flops 1073741824 | bytes 5767168 | tf_op jit(solution)/shard_map/project/pallas_call | solution.py:34
  32.3 15.7 %copy.17 = bf16[1,1024,5504]{1,2,0:T(8,128)(2,1)} copy(bf16[1,1024,5504]{2,1,0:T(8,128)(2,1)} %param.6) | data formatting | bytes 22544384 | tf_op args[1]
  48.6 1.9 collective-permute-start.11
  50.5 1.5 collective-permute-start.12
  52.3 1.9 collective-permute-start
  54.2 1.8 collective-permute-done.24
  56.5 1.2 collective-permute-done.11
  57.8 1.2 collective-permute-done.12
  59.9 1.7 collective-permute-done.13
  61.6 4.6 %collective-permute-done.36.refs_1_ = bf16[256,256]{1,0:T(8,128)(2,1)S(1)} collective-permute-done((bf16[256,256]{1,0:T(8,128)(2,1)S(1)}, bf16[256,256]{1,0:T(8,128)(2,1)S(1)}, u32[]{:S(2)}, u32[]{:S(2)}) %collective-permute-start.36) | collective-permute-done | bytes 131104 | tf_op jit(solution)/shard_map/ppermute | solution.py:204
  66.3 2.0 collective-permute-start.26
  68.2 1.2 collective-permute-done.38.refs_3_
  70.1 6.3 %gradient.15 = bf16[4,688,256]{2,1,0:T(8,128)(2,1)} custom-call(s32[4]{0:T(128)} %pad_add_fusion.order_ref, s32[4]{0:T(128)} %add_subtract_fusion.owners_ref, bf16[8,688,1024]{2,1,0:T(8,128)(2,1)} %bitcast.102, bf16[256,256]{1,0:T(8,128)(2,1)} %copy-done.5, bf16[256,256]{1,0:T(8,128)(2,1)} %copy-done.9, bf16[256,256]{1,0:T(8,128)(2,1)} %copy-done.10, ...), custom_call_target="tpu_custom_call" | custom-call | flops 1442840576 | bytes 7569408 | tf_op jit(solution)/shard_map/gradient/pallas_call | solution.py:72
  76.5 2.4 collective-permute-start.2
  79.8 6.2 %gradient.13 = bf16[4,688,256]{2,1,0:T(8,128)(2,1)} custom-call(s32[4]{0:T(128)} %pad_add_fusion.order_ref, s32[4]{0:T(128)} %add_subtract_fusion.owners_ref, bf16[8,688,1024]{2,1,0:T(8,128)(2,1)} %bitcast.103, bf16[256,256]{1,0:T(8,128)(2,1)} %copy-done.6, bf16[256,256]{1,0:T(8,128)(2,1)} %copy-done.12, bf16[256,256]{1,0:T(8,128)(2,1)} %copy-done.13, ...), custom_call_target="tpu_custom_call" | custom-call | flops 1442840576 | bytes 7569408 | tf_op jit(solution)/shard_map/gradient/pallas_call | solution.py:72
  86.9 2.3 collective-permute-start.16
  89.7 4.4 %collective-permute-done.15.refs_2_ = bf16[256,256]{1,0:T(8,128)(2,1)S(1)} collective-permute-done((bf16[256,256]{1,0:T(8,128)(2,1)S(1)}, bf16[256,256]{1,0:T(8,128)(2,1)S(1)}, u32[]{:S(2)}, u32[]{:S(2)}) %collective-permute-start.15) | collective-permute-done | bytes 131104 | tf_op jit(solution)/shard_map/ppermute | solution.py:204
  95.0 2.3 collective-permute-start.5
  97.3 6.2 %gradient.11 = bf16[4,688,256]{2,1,0:T(8,128)(2,1)} custom-call(s32[4]{0:T(128)} %pad_add_fusion.order_ref, s32[4]{0:T(128)} %add_subtract_fusion.owners_ref, bf16[8,688,1024]{2,1,0:T(8,128)(2,1)} %bitcast.104, bf16[256,256]{1,0:T(8,128)(2,1)} %copy-done.7, bf16[256,256]{1,0:T(8,128)(2,1)} %copy-done.15, bf16[256,256]{1,0:T(8,128)(2,1)} %copy-done.16, ...), custom_call_target="tpu_custom_call" | custom-call | flops 1442840576 | bytes 7569408 | tf_op jit(solution)/shard_map/gradient/pallas_call | solution.py:72
  104.9 6.2 %gradient.9 = bf16[4,688,256]{2,1,0:T(8,128)(2,1)} custom-call(s32[4]{0:T(128)} %pad_add_fusion.order_ref, s32[4]{0:T(128)} %add_subtract_fusion.owners_ref, bf16[8,688,1024]{2,1,0:T(8,128)(2,1)} %bitcast.105, bf16[256,256]{1,0:T(8,128)(2,1)} %copy-done.8, bf16[256,256]{1,0:T(8,128)(2,1)} %copy-done.18, bf16[256,256]{1,0:T(8,128)(2,1)} %copy-done.19, ...), custom_call_target="tpu_custom_call" | custom-call | flops 1442840576 | bytes 7569408 | tf_op jit(solution)/shard_map/gradient/pallas_call | solution.py:72
  112.1 6.2 %gradient.14.own_ref = bf16[4,688,256]{2,1,0:T(8,128)(2,1)} custom-call(s32[4]{0:T(128)} %pad_add_fusion.order_ref, s32[4]{0:T(128)} %broadcast_add_fusion.owners_ref, bf16[8,688,1024]{2,1,0:T(8,128)(2,1)} %bitcast.106, bf16[256,256]{1,0:T(8,128)(2,1)} %copy-done.5, bf16[256,256]{1,0:T(8,128)(2,1)} %copy-done.9, bf16[256,256]{1,0:T(8,128)(2,1)} %copy-done.10, ...), custom_call_target="tpu_custom_call" | custom-call | flops 1442840576 | bytes 7569408 | tf_op jit(solution)/shard_map/gradient/pallas_call | solution.py:72
  118.3 6.2 %gradient.12.own_ref = bf16[4,688,256]{2,1,0:T(8,128)(2,1)} custom-call(s32[4]{0:T(128)} %pad_add_fusion.order_ref, s32[4]{0:T(128)} %broadcast_add_fusion.owners_ref, bf16[8,688,1024]{2,1,0:T(8,128)(2,1)} %bitcast.107, bf16[256,256]{1,0:T(8,128)(2,1)} %copy-done.6, bf16[256,256]{1,0:T(8,128)(2,1)} %copy-done.12, bf16[256,256]{1,0:T(8,128)(2,1)} %copy-done.13, ...), custom_call_target="tpu_custom_call" | custom-call | flops 1442840576 | bytes 7569408 | tf_op jit(solution)/shard_map/gradient/pallas_call | solution.py:72
  124.5 6.2 %gradient.10.own_ref = bf16[4,688,256]{2,1,0:T(8,128)(2,1)} custom-call(s32[4]{0:T(128)} %pad_add_fusion.order_ref, s32[4]{0:T(128)} %broadcast_add_fusion.owners_ref, bf16[8,688,1024]{2,1,0:T(8,128)(2,1)} %bitcast.108, bf16[256,256]{1,0:T(8,128)(2,1)} %copy-done.7, bf16[256,256]{1,0:T(8,128)(2,1)} %copy-done.15, bf16[256,256]{1,0:T(8,128)(2,1)} %copy-done.16, ...), custom_call_target="tpu_custom_call" | custom-call | flops 1442840576 | bytes 7569408 | tf_op jit(solution)/shard_map/gradient/pallas_call | solution.py:72
  130.7 6.8 %gradient.8.own_ref = bf16[4,688,256]{2,1,0:T(8,128)(2,1)} custom-call(s32[4]{0:T(128)} %pad_add_fusion.order_ref, s32[4]{0:T(128)} %broadcast_add_fusion.owners_ref, bf16[8,688,1024]{2,1,0:T(8,128)(2,1)} %bitcast.109, bf16[256,256]{1,0:T(8,128)(2,1)} %copy-done.8, bf16[256,256]{1,0:T(8,128)(2,1)} %copy-done.18, bf16[256,256]{1,0:T(8,128)(2,1)} %copy-done.19, ...), custom_call_target="tpu_custom_call" | custom-call | flops 1442840576 | bytes 7569408 | tf_op jit(solution)/shard_map/gradient/pallas_call | solution.py:72
  137.5 1.2 fusion.11
  138.6 1.6 collective-permute-start.40
  141.3 1.6 collective-permute-start.29
  144.1 1.6 collective-permute-start.18
  146.1 5.5 %collective-permute-done.40 = bf16[688,256]{1,0:T(8,128)(2,1)S(1)} collective-permute-done((bf16[688,256]{1,0:T(8,128)(2,1)S(1)}, bf16[688,256]{1,0:T(8,128)(2,1)S(1)}, u32[]{:S(2)}, u32[]{:S(2)}) %collective-permute-start.40) | collective-permute-done | bytes 352288 | tf_op jit(solution)/shard_map/ppermute | solution.py:210
  152.8 6.4 %collective-permute-done.29 = bf16[688,256]{1,0:T(8,128)(2,1)S(1)} collective-permute-done((bf16[688,256]{1,0:T(8,128)(2,1)S(1)}, bf16[688,256]{1,0:T(8,128)(2,1)S(1)}, u32[]{:S(2)}, u32[]{:S(2)}) %collective-permute-start.29) | collective-permute-done | bytes 352288 | tf_op jit(solution)/shard_map/ppermute | solution.py:210
  159.1 1.1 fusion.3
  160.3 6.3 %collective-permute-done.18 = bf16[688,256]{1,0:T(8,128)(2,1)S(1)} collective-permute-done((bf16[688,256]{1,0:T(8,128)(2,1)S(1)}, bf16[688,256]{1,0:T(8,128)(2,1)S(1)}, u32[]{:S(2)}, u32[]{:S(2)}) %collective-permute-start.18) | collective-permute-done | bytes 352288 | tf_op jit(solution)/shard_map/ppermute | solution.py:210
  167.9 6.4 %collective-permute-done.7 = bf16[688,256]{1,0:T(8,128)(2,1)S(1)} collective-permute-done((bf16[688,256]{1,0:T(8,128)(2,1)S(1)}, bf16[688,256]{1,0:T(8,128)(2,1)S(1)}, u32[]{:S(2)}, u32[]{:S(2)}) %collective-permute-start.7) | collective-permute-done | bytes 352288 | tf_op jit(solution)/shard_map/ppermute | solution.py:210
  174.5 14.9 %collective-permute-done.30 = bf16[688,256]{1,0:T(8,128)(2,1)S(1)} collective-permute-done((bf16[688,256]{1,0:T(8,128)(2,1)S(1)}, bf16[688,256]{1,0:T(8,128)(2,1)S(1)}, u32[]{:S(2)}, u32[]{:S(2)}) %collective-permute-start.30) | collective-permute-done | bytes 352288 | tf_op jit(solution)/shard_map/ppermute | solution.py:210
  189.3 1.1 fusion.2
  190.5 6.4 %collective-permute-done.19 = bf16[688,256]{1,0:T(8,128)(2,1)S(1)} collective-permute-done((bf16[688,256]{1,0:T(8,128)(2,1)S(1)}, bf16[688,256]{1,0:T(8,128)(2,1)S(1)}, u32[]{:S(2)}, u32[]{:S(2)}) %collective-permute-start.19) | collective-permute-done | bytes 352288 | tf_op jit(solution)/shard_map/ppermute | solution.py:210
  198.1 6.4 %collective-permute-done.8 = bf16[688,256]{1,0:T(8,128)(2,1)S(1)} collective-permute-done((bf16[688,256]{1,0:T(8,128)(2,1)S(1)}, bf16[688,256]{1,0:T(8,128)(2,1)S(1)}, u32[]{:S(2)}, u32[]{:S(2)}) %collective-permute-start.8) | collective-permute-done | bytes 352288 | tf_op jit(solution)/shard_map/ppermute | solution.py:210
  205.8 1.6 collective-permute-start.42
  207.3 19.7 %collective-permute-done.9.arrived_ref = bf16[688,256]{1,0:T(8,128)(2,1)S(1)} collective-permute-done((bf16[688,256]{1,0:T(8,128)(2,1)S(1)}, bf16[688,256]{1,0:T(8,128)(2,1)S(1)}, u32[]{:S(2)}, u32[]{:S(2)}) %collective-permute-start.9) | collective-permute-done | bytes 352288 | tf_op jit(solution)/shard_map/ppermute | solution.py:210
  227.8 3.3 %adam.4 = (f32[688,1024]{1,0:T(8,128)}, f32[688,1024]{1,0:T(8,128)}, bf16[688,256]{1,0:T(8,128)(2,1)}) custom-call(bf16[688,256]{1,0:T(8,128)(2,1)} %copy-done.40, bf16[4,688,256]{2,1,0:T(8,128)(2,1)} %gradient.8.own_ref, bf16[4,688,256]{2,1,0:T(8,128)(2,1)} %copy-done.4, f32[688,1024]{1,0:T(8,128)} %bitcast.123, f32[688,1024]{1,0:T(8,128)} %bitcast.127), custom_call_target="tpu_custom_call" | custom-call | flops 2113536 | bytes 4227072 | tf_op jit(solution)/shard_map/adam/pallas_call | solution.py:111
  231.8 3.2 adam.5
  235.8 3.3 %adam.6 = (f32[688,1024]{1,0:T(8,128)}, f32[688,1024]{1,0:T(8,128)}, bf16[688,256]{1,0:T(8,128)(2,1)}) custom-call(bf16[688,256]{1,0:T(8,128)(2,1)} %copy-done.41, bf16[4,688,256]{2,1,0:T(8,128)(2,1)} %gradient.12.own_ref, bf16[4,688,256]{2,1,0:T(8,128)(2,1)} %collective-permute-done.28.other_ref, ...), custom_call_target="tpu_custom_call", output_to_operand_aliasing={{0}: (5, {}), {1}: (6, {})} | custom-call | flops 2113536 | bytes 4227072 | tf_op jit(solution)/shard_map/adam/pallas_call | solution.py:111
  239.8 3.3 %adam.7 = (f32[688,1024]{1,0:T(8,128)}, f32[688,1024]{1,0:T(8,128)}, bf16[688,256]{1,0:T(8,128)(2,1)}) custom-call(bf16[688,256]{1,0:T(8,128)(2,1)} %copy-done.42, bf16[4,688,256]{2,1,0:T(8,128)(2,1)} %gradient.14.own_ref, bf16[4,688,256]{2,1,0:T(8,128)(2,1)} %collective-permute-done.39.other_ref, ...), custom_call_target="tpu_custom_call", output_to_operand_aliasing={{0}: (5, {}), {1}: (6, {})} | custom-call | flops 2113536 | bytes 4227072 | tf_op jit(solution)/shard_map/adam/pallas_call | solution.py:111
  243.4 1.7 collective-permute-start.50
  245.5 1.8 collective-permute-start.48
  247.4 7.2 %collective-permute-done.51.refs_3_ = bf16[688,256]{1,0:T(8,128)(2,1)S(1)} collective-permute-done((bf16[688,256]{1,0:T(8,128)(2,1)}, bf16[688,256]{1,0:T(8,128)(2,1)S(1)}, u32[]{:S(2)}, u32[]{:S(2)}) %collective-permute-start.51) | collective-permute-done | bytes 352288 | tf_op jit(solution)/shard_map/ppermute | solution.py:204
  254.6 7.5 %collective-permute-done.50.refs_2_ = bf16[688,256]{1,0:T(8,128)(2,1)S(1)} collective-permute-done((bf16[688,256]{1,0:T(8,128)(2,1)S(1)}, bf16[688,256]{1,0:T(8,128)(2,1)S(1)}, u32[]{:S(2)}, u32[]{:S(2)}) %collective-permute-start.50) | collective-permute-done | bytes 352288 | tf_op jit(solution)/shard_map/ppermute | solution.py:204
  262.1 7.5 %collective-permute-done.49.refs_1_ = bf16[688,256]{1,0:T(8,128)(2,1)S(1)} collective-permute-done((bf16[688,256]{1,0:T(8,128)(2,1)S(1)}, bf16[688,256]{1,0:T(8,128)(2,1)S(1)}, u32[]{:S(2)}, u32[]{:S(2)}) %collective-permute-start.49) | collective-permute-done | bytes 352288 | tf_op jit(solution)/shard_map/ppermute | solution.py:204
  269.7 7.4 %expand.4.refs_4_ = f32[4,688,2048]{2,1,0:T(8,128)} custom-call(s32[1]{0:T(128)} %bitcast.2.target_ref, bf16[2048,1024]{1,0:T(8,128)(2,1)} %bitcast.115, bf16[688,256]{1,0:T(8,128)(2,1)} %get-tuple-element.35.refs_0_, bf16[688,256]{1,0:T(8,128)(2,1)} %get-tuple-element.42.refs_1_, bf16[688,256]{1,0:T(8,128)(2,1)} %get-tuple-element.49.refs_2_, ...), custom_call_target="tpu_custom_call" | custom-call | flops 2885681152 | bytes 11239424 | tf_op jit(solution)/shard_map/expand/pallas_call | solution.py:155
  277.1 1.7 collective-permute-start.43
  278.8 1.4 collective-permute-start.32
  280.2 1.7 collective-permute-start.21
  281.9 1.4 collective-permute-start.10
  283.3 7.3 %expand.5.refs_4_ = f32[4,688,2048]{2,1,0:T(8,128)} custom-call(s32[1]{0:T(128)} %bitcast.3.target_ref, bf16[2048,1024]{1,0:T(8,128)(2,1)} %bitcast.116, bf16[688,256]{1,0:T(8,128)(2,1)} %copy-done.32, bf16[688,256]{1,0:T(8,128)(2,1)} %copy-done.30, bf16[688,256]{1,0:T(8,128)(2,1)} %copy-done.29, ...), custom_call_target="tpu_custom_call", output_to_operand_aliasing={{}: (6, {})} | custom-call | flops 2885681152 | bytes 11239424 | tf_op jit(solution)/shard_map/expand/pallas_call | solution.py:155
  290.6 17.1 %collective-permute-done.44.refs_0_ = bf16[688,256]{1,0:T(8,128)(2,1)S(1)} collective-permute-done((bf16[688,256]{1,0:T(8,128)(2,1)S(1)}, bf16[688,256]{1,0:T(8,128)(2,1)S(1)}, u32[]{:S(2)}, u32[]{:S(2)}) %collective-permute-start.44) | collective-permute-done | bytes 352288 | tf_op jit(solution)/shard_map/ppermute | solution.py:204
  308.5 7.3 %expand.6.refs_4_ = f32[4,688,2048]{2,1,0:T(8,128)} custom-call(s32[1]{0:T(128)} %bitcast.4.target_ref, bf16[2048,1024]{1,0:T(8,128)(2,1)} %bitcast.117, bf16[688,256]{1,0:T(8,128)(2,1)} %copy-done.37, bf16[688,256]{1,0:T(8,128)(2,1)} %copy-done.35, bf16[688,256]{1,0:T(8,128)(2,1)} %copy-done.33, ...), custom_call_target="tpu_custom_call", output_to_operand_aliasing={{}: (6, {})} | custom-call | flops 2885681152 | bytes 11239424 | tf_op jit(solution)/shard_map/expand/pallas_call | solution.py:155
  317.5 7.3 %expand.7 = f32[4,688,2048]{2,1,0:T(8,128)} custom-call(s32[1]{0:T(128)} %bitcast.target_ref, bf16[2048,1024]{1,0:T(8,128)(2,1)} %bitcast.118, bf16[688,256]{1,0:T(8,128)(2,1)} %copy-done.39, bf16[688,256]{1,0:T(8,128)(2,1)} %copy-done.38, bf16[688,256]{1,0:T(8,128)(2,1)} %copy-done.36, bf16[688,256]{1,0:T(8,128)(2,1)} %copy-done.34, ...), custom_call_target="tpu_custom_call", output_to_operand_aliasing={{}: (6, {})} | custom-call | flops 2885681152 | bytes 11239424 | tf_op jit(solution)/shard_map/expand/pallas_call | solution.py:155
  (190 shorter events, 23.4 us)
Async XLA Ops:
  7.1 41.4 %collective-permute-start.33 = (bf16[256,256]{1,0:T(8,128)(2,1)}, bf16[256,256]{1,0:T(8,128)(2,1)S(1)}, u32[]{:S(2)}, u32[]{:S(2)}) collective-permute-start(bf16[256,256]{1,0:T(8,128)(2,1)} %get-tuple-element.51), channel_id=1, source_target_pairs={{0,1},{1,0},{2,3},{3,2},{4,5},{5,4},{6,7},{7,6},{8,9},{9,8},{10,11... | collective-permute-start | bytes 393224 | tf_op jit(solution)/shard_map/ppermute | solution.py:204
  10.0 38.6 %collective-permute-start.34 = (bf16[256,256]{1,0:T(8,128)(2,1)}, bf16[256,256]{1,0:T(8,128)(2,1)S(1)}, u32[]{:S(2)}, u32[]{:S(2)}) collective-permute-start(bf16[256,256]{1,0:T(8,128)(2,1)} %get-tuple-element.52), channel_id=1, source_target_pairs={{0,2},{1,3},{2,0},{3,1},{4,6},{5,7},{6,4},{7,5},{8,10},{9,11},{10,... | collective-permute-start | bytes 393224 | tf_op jit(solution)/shard_map/ppermute | solution.py:204
  11.5 39.0 %collective-permute-start.35 = (bf16[256,256]{1,0:T(8,128)(2,1)}, bf16[256,256]{1,0:T(8,128)(2,1)S(1)}, u32[]{:S(2)}, u32[]{:S(2)}) collective-permute-start(bf16[256,256]{1,0:T(8,128)(2,1)} %get-tuple-element.53), channel_id=1, source_target_pairs={{0,3},{1,2},{2,1},{3,0},{4,7},{5,6},{6,5},{7,4},{8,11},{9,10},{10,... | collective-permute-start | bytes 393224 | tf_op jit(solution)/shard_map/ppermute | solution.py:204
  17.3 34.9 %collective-permute-start.22 = (bf16[256,256]{1,0:T(8,128)(2,1)}, bf16[256,256]{1,0:T(8,128)(2,1)S(1)}, u32[]{:S(2)}, u32[]{:S(2)}) collective-permute-start(bf16[256,256]{1,0:T(8,128)(2,1)} %get-tuple-element.44), channel_id=1, source_target_pairs={{0,1},{1,0},{2,3},{3,2},{4,5},{5,4},{6,7},{7,6},{8,9},{9,8},{10,11... | collective-permute-start | bytes 393224 | tf_op jit(solution)/shard_map/ppermute | solution.py:204
  19.2 33.1 %collective-permute-start.23 = (bf16[256,256]{1,0:T(8,128)(2,1)}, bf16[256,256]{1,0:T(8,128)(2,1)S(1)}, u32[]{:S(2)}, u32[]{:S(2)}) collective-permute-start(bf16[256,256]{1,0:T(8,128)(2,1)} %get-tuple-element.45), channel_id=1, source_target_pairs={{0,2},{1,3},{2,0},{3,1},{4,6},{5,7},{6,4},{7,5},{8,10},{9,11},{10,... | collective-permute-start | bytes 393224 | tf_op jit(solution)/shard_map/ppermute | solution.py:204
  32.3 19.9 %copy-start.51 = (bf16[256,256]{1,0:T(8,128)(2,1)S(1)}, bf16[256,256]{1,0:T(8,128)(2,1)}, u32[]{:S(2)}) copy-start(bf16[256,256]{1,0:T(8,128)(2,1)} %get-tuple-element.39) | copy-start | bytes 393220
  32.3 20.0 %copy-start.50 = (bf16[256,256]{1,0:T(8,128)(2,1)S(1)}, bf16[256,256]{1,0:T(8,128)(2,1)}, u32[]{:S(2)}) copy-start(bf16[256,256]{1,0:T(8,128)(2,1)} %get-tuple-element.32) | copy-start | bytes 393220
  32.3 23.7 %copy-start.49 = (bf16[256,256]{1,0:T(8,128)(2,1)S(1)}, bf16[256,256]{1,0:T(8,128)(2,1)}, u32[]{:S(2)}) copy-start(bf16[256,256]{1,0:T(8,128)(2,1)} %get-tuple-element.33) | copy-start | bytes 393220
  32.3 24.2 %copy-start.46 = (bf16[256,256]{1,0:T(8,128)(2,1)S(1)}, bf16[256,256]{1,0:T(8,128)(2,1)}, u32[]{:S(2)}) copy-start(bf16[256,256]{1,0:T(8,128)(2,1)} %get-tuple-element.43) | copy-start | bytes 393220
  48.5 7.4 %collective-permute-start.24 = (bf16[256,256]{1,0:T(8,128)(2,1)S(1)}, bf16[256,256]{1,0:T(8,128)(2,1)S(1)}, u32[]{:S(2)}, u32[]{:S(2)}) collective-permute-start(bf16[256,256]{1,0:T(8,128)(2,1)S(1)} %copy-done.54), channel_id=1, source_target_pairs={{0,3},{1,2},{2,1},{3,0},{4,7},{5,6},{6,5},{7,4},{8,11},{9,10},{10,... | collective-permute-start | bytes 393224 | tf_op jit(solution)/shard_map/ppermute | solution.py:204
  48.6 9.2 %collective-permute-start.11 = (bf16[256,256]{1,0:T(8,128)(2,1)S(1)}, bf16[256,256]{1,0:T(8,128)(2,1)S(1)}, u32[]{:S(2)}, u32[]{:S(2)}) collective-permute-start(bf16[256,256]{1,0:T(8,128)(2,1)S(1)} %copy-done.53), channel_id=1, source_target_pairs={{0,1},{1,0},{2,3},{3,2},{4,5},{5,4},{6,7},{7,6},{8,9},{9,8},{10,11... | collective-permute-start | bytes 393224 | tf_op jit(solution)/shard_map/ppermute | solution.py:204
  50.5 8.5 %collective-permute-start.12 = (bf16[256,256]{1,0:T(8,128)(2,1)S(1)}, bf16[256,256]{1,0:T(8,128)(2,1)S(1)}, u32[]{:S(2)}, u32[]{:S(2)}) collective-permute-start(bf16[256,256]{1,0:T(8,128)(2,1)S(1)} %copy-done.52), channel_id=1, source_target_pairs={{0,2},{1,3},{2,0},{3,1},{4,6},{5,7},{6,4},{7,5},{8,10},{9,11},{10,... | collective-permute-start | bytes 393224 | tf_op jit(solution)/shard_map/ppermute | solution.py:204
  52.1 9.4 %collective-permute-start.13 = (bf16[256,256]{1,0:T(8,128)(2,1)S(1)}, bf16[256,256]{1,0:T(8,128)(2,1)S(1)}, u32[]{:S(2)}, u32[]{:S(2)}) collective-permute-start(bf16[256,256]{1,0:T(8,128)(2,1)S(1)} %copy-done.51), channel_id=1, source_target_pairs={{0,3},{1,2},{2,1},{3,0},{4,7},{5,6},{6,5},{7,4},{8,11},{9,10},{10,... | collective-permute-start | bytes 393224 | tf_op jit(solution)/shard_map/ppermute | solution.py:204
  52.3 33.7 %collective-permute-start = (bf16[256,256]{1,0:T(8,128)(2,1)S(1)}, bf16[256,256]{1,0:T(8,128)(2,1)S(1)}, u32[]{:S(2)}, u32[]{:S(2)}) collective-permute-start(bf16[256,256]{1,0:T(8,128)(2,1)S(1)} %copy-done.50), channel_id=1, source_target_pairs={{0,1},{1,0},{2,3},{3,2},{4,5},{5,4},{6,7},{7,6},{8,9},{9,8},{10,11... | collective-permute-start | bytes 393224 | tf_op jit(solution)/shard_map/ppermute | solution.py:204
  56.0 30.9 %collective-permute-start.1 = (bf16[256,256]{1,0:T(8,128)(2,1)S(1)}, bf16[256,256]{1,0:T(8,128)(2,1)S(1)}, u32[]{:S(2)}, u32[]{:S(2)}) collective-permute-start(bf16[256,256]{1,0:T(8,128)(2,1)S(1)} %copy-done.49), channel_id=1, source_target_pairs={{0,2},{1,3},{2,0},{3,1},{4,6},{5,7},{6,4},{7,5},{8,10},{9,11},{10,... | collective-permute-start | bytes 393224 | tf_op jit(solution)/shard_map/ppermute | solution.py:204
  56.5 19.9 %copy-start.6 = (bf16[256,256]{1,0:T(8,128)(2,1)}, bf16[256,256]{1,0:T(8,128)(2,1)S(1)}, u32[]{:S(2)}) copy-start(bf16[256,256]{1,0:T(8,128)(2,1)S(1)} %add_convert_fusion.5.refs_0_) | copy-start | bytes 393220
  57.8 8.4 %collective-permute-start.36 = (bf16[256,256]{1,0:T(8,128)(2,1)S(1)}, bf16[256,256]{1,0:T(8,128)(2,1)S(1)}, u32[]{:S(2)}, u32[]{:S(2)}) collective-permute-start(bf16[256,256]{1,0:T(8,128)(2,1)S(1)} %add_convert_fusion.4.refs_0_), channel_id=1, source_target_pairs={{0,1},{1,0},{2,3},{3,2},{4,5},{5,4},{6,7},{7,6},{8,9},{9,8},{10,11... | collective-permute-start | bytes 393224 | tf_op jit(solution)/shard_map/ppermute | solution.py:204
  59.0 7.2 %collective-permute-start.37 = (bf16[256,256]{1,0:T(8,128)(2,1)S(1)}, bf16[256,256]{1,0:T(8,128)(2,1)S(1)}, u32[]{:S(2)}, u32[]{:S(2)}) collective-permute-start(bf16[256,256]{1,0:T(8,128)(2,1)S(1)} %add_convert_fusion.4.refs_0_), channel_id=1, source_target_pairs={{0,2},{1,3},{2,0},{3,1},{4,6},{5,7},{6,4},{7,5},{8,10},{9,11},{10,... | collective-permute-start | bytes 393224 | tf_op jit(solution)/shard_map/ppermute | solution.py:204
  61.5 8.0 %collective-permute-start.38 = (bf16[256,256]{1,0:T(8,128)(2,1)S(1)}, bf16[256,256]{1,0:T(8,128)(2,1)S(1)}, u32[]{:S(2)}, u32[]{:S(2)}) collective-permute-start(bf16[256,256]{1,0:T(8,128)(2,1)S(1)} %add_convert_fusion.4.refs_0_), channel_id=1, source_target_pairs={{0,3},{1,2},{2,1},{3,0},{4,7},{5,6},{6,5},{7,4},{8,11},{9,10},{10,... | collective-permute-start | bytes 393224 | tf_op jit(solution)/shard_map/ppermute | solution.py:204
  61.6 25.3 %copy-start.7 = (bf16[256,256]{1,0:T(8,128)(2,1)}, bf16[256,256]{1,0:T(8,128)(2,1)S(1)}, u32[]{:S(2)}) copy-start(bf16[256,256]{1,0:T(8,128)(2,1)S(1)} %add_convert_fusion.6.refs_0_) | copy-start | bytes 393220
  66.2 10.3 %collective-permute-start.25 = (bf16[256,256]{1,0:T(8,128)(2,1)S(1)}, bf16[256,256]{1,0:T(8,128)(2,1)S(1)}, u32[]{:S(2)}, u32[]{:S(2)}) collective-permute-start(bf16[256,256]{1,0:T(8,128)(2,1)S(1)} %add_convert_fusion.5.refs_0_), channel_id=1, source_target_pairs={{0,1},{1,0},{2,3},{3,2},{4,5},{5,4},{6,7},{7,6},{8,9},{9,8},{10,11... | collective-permute-start | bytes 393224 | tf_op jit(solution)/shard_map/ppermute | solution.py:204
  66.3 12.6 %collective-permute-start.26 = (bf16[256,256]{1,0:T(8,128)(2,1)S(1)}, bf16[256,256]{1,0:T(8,128)(2,1)S(1)}, u32[]{:S(2)}, u32[]{:S(2)}) collective-permute-start(bf16[256,256]{1,0:T(8,128)(2,1)S(1)} %add_convert_fusion.5.refs_0_), channel_id=1, source_target_pairs={{0,2},{1,3},{2,0},{3,1},{4,6},{5,7},{6,4},{7,5},{8,10},{9,11},{10,... | collective-permute-start | bytes 393224 | tf_op jit(solution)/shard_map/ppermute | solution.py:204
  69.5 9.7 %collective-permute-start.27 = (bf16[256,256]{1,0:T(8,128)(2,1)S(1)}, bf16[256,256]{1,0:T(8,128)(2,1)S(1)}, u32[]{:S(2)}, u32[]{:S(2)}) collective-permute-start(bf16[256,256]{1,0:T(8,128)(2,1)S(1)} %add_convert_fusion.5.refs_0_), channel_id=1, source_target_pairs={{0,3},{1,2},{2,1},{3,0},{4,7},{5,6},{6,5},{7,4},{8,11},{9,10},{10,... | collective-permute-start | bytes 393224 | tf_op jit(solution)/shard_map/ppermute | solution.py:204
  76.5 12.7 %collective-permute-start.2 = (bf16[256,256]{1,0:T(8,128)(2,1)S(1)}, bf16[256,256]{1,0:T(8,128)(2,1)S(1)}, u32[]{:S(2)}, u32[]{:S(2)}) collective-permute-start(bf16[256,256]{1,0:T(8,128)(2,1)S(1)} %copy-done.48), channel_id=1, source_target_pairs={{0,3},{1,2},{2,1},{3,0},{4,7},{5,6},{6,5},{7,4},{8,11},{9,10},{10,... | collective-permute-start | bytes 393224 | tf_op jit(solution)/shard_map/ppermute | solution.py:204
  78.9 10.4 %collective-permute-start.14 = (bf16[256,256]{1,0:T(8,128)(2,1)S(1)}, bf16[256,256]{1,0:T(8,128)(2,1)S(1)}, u32[]{:S(2)}, u32[]{:S(2)}) collective-permute-start(bf16[256,256]{1,0:T(8,128)(2,1)S(1)} %add_convert_fusion.6.refs_0_), channel_id=1, source_target_pairs={{0,1},{1,0},{2,3},{3,2},{4,5},{5,4},{6,7},{7,6},{8,9},{9,8},{10,11... | collective-permute-start | bytes 393224 | tf_op jit(solution)/shard_map/ppermute | solution.py:204
  79.1 58.3 %collective-permute-start.39 = (bf16[4,688,256]{2,1,0:T(8,128)(2,1)}, bf16[4,688,256]{2,1,0:T(8,128)(2,1)}, u32[]{:S(2)}, u32[]{:S(2)}) collective-permute-start(bf16[4,688,256]{2,1,0:T(8,128)(2,1)} %gradient.15), channel_id=1, source_target_pairs={{0,4},{4,0},{8,12},{12,8},{16,20},{20,16},{24,28},{28,24},{1,5},{5... | collective-permute-start | bytes 4227080 | tf_op jit(solution)/shard_map/ppermute | solution.py:207
  86.0 8.1 %collective-permute-start.15 = (bf16[256,256]{1,0:T(8,128)(2,1)S(1)}, bf16[256,256]{1,0:T(8,128)(2,1)S(1)}, u32[]{:S(2)}, u32[]{:S(2)}) collective-permute-start(bf16[256,256]{1,0:T(8,128)(2,1)S(1)} %add_convert_fusion.6.refs_0_), channel_id=1, source_target_pairs={{0,2},{1,3},{2,0},{3,1},{4,6},{5,7},{6,4},{7,5},{8,10},{9,11},{10,... | collective-permute-start | bytes 393224 | tf_op jit(solution)/shard_map/ppermute | solution.py:204
  86.9 8.1 %collective-permute-start.16 = (bf16[256,256]{1,0:T(8,128)(2,1)S(1)}, bf16[256,256]{1,0:T(8,128)(2,1)S(1)}, u32[]{:S(2)}, u32[]{:S(2)}) collective-permute-start(bf16[256,256]{1,0:T(8,128)(2,1)S(1)} %add_convert_fusion.6.refs_0_), channel_id=1, source_target_pairs={{0,3},{1,2},{2,1},{3,0},{4,7},{5,6},{6,5},{7,4},{8,11},{9,10},{10,... | collective-permute-start | bytes 393224 | tf_op jit(solution)/shard_map/ppermute | solution.py:204
  89.2 51.1 %collective-permute-start.28 = (bf16[4,688,256]{2,1,0:T(8,128)(2,1)}, bf16[4,688,256]{2,1,0:T(8,128)(2,1)}, u32[]{:S(2)}, u32[]{:S(2)}) collective-permute-start(bf16[4,688,256]{2,1,0:T(8,128)(2,1)} %gradient.13), channel_id=1, source_target_pairs={{0,4},{4,0},{8,12},{12,8},{16,20},{20,16},{24,28},{28,24},{1,5},{5... | collective-permute-start | bytes 4227080 | tf_op jit(solution)/shard_map/ppermute | solution.py:207
  89.3 14.1 %collective-permute-start.3 = (bf16[256,256]{1,0:T(8,128)(2,1)S(1)}, bf16[256,256]{1,0:T(8,128)(2,1)S(1)}, u32[]{:S(2)}, u32[]{:S(2)}) collective-permute-start(bf16[256,256]{1,0:T(8,128)(2,1)S(1)} %add_convert_fusion.7.refs_0_), channel_id=1, source_target_pairs={{0,1},{1,0},{2,3},{3,2},{4,5},{5,4},{6,7},{7,6},{8,9},{9,8},{10,11... | collective-permute-start | bytes 393224 | tf_op jit(solution)/shard_map/ppermute | solution.py:204
  94.1 9.5 %collective-permute-start.4 = (bf16[256,256]{1,0:T(8,128)(2,1)S(1)}, bf16[256,256]{1,0:T(8,128)(2,1)S(1)}, u32[]{:S(2)}, u32[]{:S(2)}) collective-permute-start(bf16[256,256]{1,0:T(8,128)(2,1)S(1)} %add_convert_fusion.7.refs_0_), channel_id=1, source_target_pairs={{0,2},{1,3},{2,0},{3,1},{4,6},{5,7},{6,4},{7,5},{8,10},{9,11},{10,... | collective-permute-start | bytes 393224 | tf_op jit(solution)/shard_map/ppermute | solution.py:204
  95.0 8.6 %collective-permute-start.5 = (bf16[256,256]{1,0:T(8,128)(2,1)S(1)}, bf16[256,256]{1,0:T(8,128)(2,1)S(1)}, u32[]{:S(2)}, u32[]{:S(2)}) collective-permute-start(bf16[256,256]{1,0:T(8,128)(2,1)S(1)} %add_convert_fusion.7.refs_0_), channel_id=1, source_target_pairs={{0,3},{1,2},{2,1},{3,0},{4,7},{5,6},{6,5},{7,4},{8,11},{9,10},{10,... | collective-permute-start | bytes 393224 | tf_op jit(solution)/shard_map/ppermute | solution.py:204
  103.5 39.5 %collective-permute-start.17 = (bf16[4,688,256]{2,1,0:T(8,128)(2,1)}, bf16[4,688,256]{2,1,0:T(8,128)(2,1)}, u32[]{:S(2)}, u32[]{:S(2)}) collective-permute-start(bf16[4,688,256]{2,1,0:T(8,128)(2,1)} %gradient.11), channel_id=1, source_target_pairs={{0,4},{4,0},{8,12},{12,8},{16,20},{20,16},{24,28},{28,24},{1,5},{5... | collective-permute-start | bytes 4227080 | tf_op jit(solution)/shard_map/ppermute | solution.py:207
  111.1 34.6 %collective-permute-start.6 = (bf16[4,688,256]{2,1,0:T(8,128)(2,1)}, bf16[4,688,256]{2,1,0:T(8,128)(2,1)S(1)}, u32[]{:S(2)}, u32[]{:S(2)}) collective-permute-start(bf16[4,688,256]{2,1,0:T(8,128)(2,1)} %gradient.9), channel_id=1, source_target_pairs={{0,4},{4,0},{8,12},{12,8},{16,20},{20,16},{24,28},{28,24},{1,5},{5... | collective-permute-start | bytes 4227080 | tf_op jit(solution)/shard_map/ppermute | solution.py:207
  138.6 12.9 %collective-permute-start.40 = (bf16[688,256]{1,0:T(8,128)(2,1)S(1)}, bf16[688,256]{1,0:T(8,128)(2,1)S(1)}, u32[]{:S(2)}, u32[]{:S(2)}) collective-permute-start(bf16[688,256]{1,0:T(8,128)(2,1)S(1)} %fusion.11), channel_id=1, source_target_pairs={{0,8},{4,12},{8,16},{12,20},{16,24},{20,28},{24,0},{28,4},{1,9},{5... | collective-permute-start | bytes 1056776 | tf_op jit(solution)/shard_map/ppermute | solution.py:210
  141.3 17.8 %collective-permute-start.29 = (bf16[688,256]{1,0:T(8,128)(2,1)S(1)}, bf16[688,256]{1,0:T(8,128)(2,1)S(1)}, u32[]{:S(2)}, u32[]{:S(2)}) collective-permute-start(bf16[688,256]{1,0:T(8,128)(2,1)S(1)} %fusion.10), channel_id=1, source_target_pairs={{0,8},{4,12},{8,16},{12,20},{16,24},{20,28},{24,0},{28,4},{1,9},{5... | collective-permute-start | bytes 1056776 | tf_op jit(solution)/shard_map/ppermute | solution.py:210
  144.1 22.6 %collective-permute-start.18 = (bf16[688,256]{1,0:T(8,128)(2,1)S(1)}, bf16[688,256]{1,0:T(8,128)(2,1)S(1)}, u32[]{:S(2)}, u32[]{:S(2)}) collective-permute-start(bf16[688,256]{1,0:T(8,128)(2,1)S(1)} %fusion.9), channel_id=1, source_target_pairs={{0,8},{4,12},{8,16},{12,20},{16,24},{20,28},{24,0},{28,4},{1,9},{5... | collective-permute-start | bytes 1056776 | tf_op jit(solution)/shard_map/ppermute | solution.py:210
  145.7 58.7 %copy-start.4 = (bf16[4,688,256]{2,1,0:T(8,128)(2,1)}, bf16[4,688,256]{2,1,0:T(8,128)(2,1)S(1)}, u32[]{:S(2)}) copy-start(bf16[4,688,256]{2,1,0:T(8,128)(2,1)S(1)} %collective-permute-done.6.other_ref) | copy-start | bytes 4227076
  145.8 28.5 %collective-permute-start.7 = (bf16[688,256]{1,0:T(8,128)(2,1)S(1)}, bf16[688,256]{1,0:T(8,128)(2,1)S(1)}, u32[]{:S(2)}, u32[]{:S(2)}) collective-permute-start(bf16[688,256]{1,0:T(8,128)(2,1)S(1)} %fusion.8), channel_id=1, source_target_pairs={{0,8},{4,12},{8,16},{12,20},{16,24},{20,28},{24,0},{28,4},{1,9},{5... | collective-permute-start | bytes 1056776 | tf_op jit(solution)/shard_map/ppermute | solution.py:210
  152.7 51.9 %collective-permute-start.41 = (bf16[688,256]{1,0:T(8,128)(2,1)S(1)}, bf16[688,256]{1,0:T(8,128)(2,1)S(1)}, u32[]{:S(2)}, u32[]{:S(2)}) collective-permute-start(bf16[688,256]{1,0:T(8,128)(2,1)S(1)} %fusion.1), channel_id=1, source_target_pairs={{0,8},{4,12},{8,16},{12,20},{16,24},{20,28},{24,0},{28,4},{1,9},{5... | collective-permute-start | bytes 1056776 | tf_op jit(solution)/shard_map/ppermute | solution.py:210
  160.3 29.1 %collective-permute-start.30 = (bf16[688,256]{1,0:T(8,128)(2,1)S(1)}, bf16[688,256]{1,0:T(8,128)(2,1)S(1)}, u32[]{:S(2)}, u32[]{:S(2)}) collective-permute-start(bf16[688,256]{1,0:T(8,128)(2,1)S(1)} %fusion.3), channel_id=1, source_target_pairs={{0,8},{4,12},{8,16},{12,20},{16,24},{20,28},{24,0},{28,4},{1,9},{5... | collective-permute-start | bytes 1056776 | tf_op jit(solution)/shard_map/ppermute | solution.py:210
  167.8 29.1 %collective-permute-start.19 = (bf16[688,256]{1,0:T(8,128)(2,1)S(1)}, bf16[688,256]{1,0:T(8,128)(2,1)S(1)}, u32[]{:S(2)}, u32[]{:S(2)}) collective-permute-start(bf16[688,256]{1,0:T(8,128)(2,1)S(1)} %fusion.5), channel_id=1, source_target_pairs={{0,8},{4,12},{8,16},{12,20},{16,24},{20,28},{24,0},{28,4},{1,9},{5... | collective-permute-start | bytes 1056776 | tf_op jit(solution)/shard_map/ppermute | solution.py:210
  174.4 30.0 %collective-permute-start.8 = (bf16[688,256]{1,0:T(8,128)(2,1)S(1)}, bf16[688,256]{1,0:T(8,128)(2,1)S(1)}, u32[]{:S(2)}, u32[]{:S(2)}) collective-permute-start(bf16[688,256]{1,0:T(8,128)(2,1)S(1)} %fusion.7), channel_id=1, source_target_pairs={{0,8},{4,12},{8,16},{12,20},{16,24},{20,28},{24,0},{28,4},{1,9},{5... | collective-permute-start | bytes 1056776 | tf_op jit(solution)/shard_map/ppermute | solution.py:210
  190.5 44.6 %collective-permute-start.31 = (bf16[688,256]{1,0:T(8,128)(2,1)S(1)}, bf16[688,256]{1,0:T(8,128)(2,1)S(1)}, u32[]{:S(2)}, u32[]{:S(2)}) collective-permute-start(bf16[688,256]{1,0:T(8,128)(2,1)S(1)} %fusion.2), channel_id=1, source_target_pairs={{0,8},{4,12},{8,16},{12,20},{16,24},{20,28},{24,0},{28,4},{1,9},{5... | collective-permute-start | bytes 1056776 | tf_op jit(solution)/shard_map/ppermute | solution.py:210
  198.0 33.1 %collective-permute-start.20 = (bf16[688,256]{1,0:T(8,128)(2,1)S(1)}, bf16[688,256]{1,0:T(8,128)(2,1)S(1)}, u32[]{:S(2)}, u32[]{:S(2)}) collective-permute-start(bf16[688,256]{1,0:T(8,128)(2,1)S(1)} %fusion.4), channel_id=1, source_target_pairs={{0,8},{4,12},{8,16},{12,20},{16,24},{20,28},{24,0},{28,4},{1,9},{5... | collective-permute-start | bytes 1056776 | tf_op jit(solution)/shard_map/ppermute | solution.py:210
  204.6 22.5 %collective-permute-start.9 = (bf16[688,256]{1,0:T(8,128)(2,1)S(1)}, bf16[688,256]{1,0:T(8,128)(2,1)S(1)}, u32[]{:S(2)}, u32[]{:S(2)}) collective-permute-start(bf16[688,256]{1,0:T(8,128)(2,1)S(1)} %fusion.6), channel_id=1, source_target_pairs={{0,8},{4,12},{8,16},{12,20},{16,24},{20,28},{24,0},{28,4},{1,9},{5... | collective-permute-start | bytes 1056776 | tf_op jit(solution)/shard_map/ppermute | solution.py:210
  205.8 33.3 %collective-permute-start.42 = (bf16[688,256]{1,0:T(8,128)(2,1)S(1)}, bf16[688,256]{1,0:T(8,128)(2,1)S(1)}, u32[]{:S(2)}, u32[]{:S(2)}) collective-permute-start(bf16[688,256]{1,0:T(8,128)(2,1)S(1)} %fusion), channel_id=1, source_target_pairs={{0,8},{4,12},{8,16},{12,20},{16,24},{20,28},{24,0},{28,4},{1,9},{5... | collective-permute-start | bytes 1056776 | tf_op jit(solution)/shard_map/ppermute | solution.py:210
  243.1 11.4 %collective-permute-start.51 = (bf16[688,256]{1,0:T(8,128)(2,1)}, bf16[688,256]{1,0:T(8,128)(2,1)S(1)}, u32[]{:S(2)}, u32[]{:S(2)}) collective-permute-start(bf16[688,256]{1,0:T(8,128)(2,1)} %get-tuple-element.56.refs_3_), channel_id=1, source_target_pairs={{0,1},{1,0},{2,3},{3,2},{4,5},{5,4},{6,7},{7,6},{8,9},{9,8},{10,11... | collective-permute-start | bytes 1056776 | tf_op jit(solution)/shard_map/ppermute | solution.py:204
  243.4 18.6 %collective-permute-start.50 = (bf16[688,256]{1,0:T(8,128)(2,1)S(1)}, bf16[688,256]{1,0:T(8,128)(2,1)S(1)}, u32[]{:S(2)}, u32[]{:S(2)}) collective-permute-start(bf16[688,256]{1,0:T(8,128)(2,1)S(1)} %copy-done.25), channel_id=1, source_target_pairs={{0,1},{1,0},{2,3},{3,2},{4,5},{5,4},{6,7},{7,6},{8,9},{9,8},{10,11... | collective-permute-start | bytes 1056776 | tf_op jit(solution)/shard_map/ppermute | solution.py:204
  245.2 24.4 %collective-permute-start.49 = (bf16[688,256]{1,0:T(8,128)(2,1)S(1)}, bf16[688,256]{1,0:T(8,128)(2,1)S(1)}, u32[]{:S(2)}, u32[]{:S(2)}) collective-permute-start(bf16[688,256]{1,0:T(8,128)(2,1)S(1)} %copy-done.23), channel_id=1, source_target_pairs={{0,1},{1,0},{2,3},{3,2},{4,5},{5,4},{6,7},{7,6},{8,9},{9,8},{10,11... | collective-permute-start | bytes 1056776 | tf_op jit(solution)/shard_map/ppermute | solution.py:204
  245.4 31.7 %copy-start.27 = (bf16[688,256]{1,0:T(8,128)(2,1)S(1)}, bf16[688,256]{1,0:T(8,128)(2,1)}, u32[]{:S(2)}) copy-start(bf16[688,256]{1,0:T(8,128)(2,1)} %get-tuple-element.56.refs_3_) | copy-start | bytes 1056772
  245.5 33.4 %copy-start.26 = (bf16[688,256]{1,0:T(8,128)(2,1)S(1)}, bf16[688,256]{1,0:T(8,128)(2,1)}, u32[]{:S(2)}) copy-start(bf16[688,256]{1,0:T(8,128)(2,1)} %get-tuple-element.49.refs_2_) | copy-start | bytes 1056772
  245.5 34.7 %copy-start.24 = (bf16[688,256]{1,0:T(8,128)(2,1)S(1)}, bf16[688,256]{1,0:T(8,128)(2,1)}, u32[]{:S(2)}) copy-start(bf16[688,256]{1,0:T(8,128)(2,1)} %get-tuple-element.42.refs_1_) | copy-start | bytes 1056772
  245.5 36.4 %copy-start.22 = (bf16[688,256]{1,0:T(8,128)(2,1)S(1)}, bf16[688,256]{1,0:T(8,128)(2,1)}, u32[]{:S(2)}) copy-start(bf16[688,256]{1,0:T(8,128)(2,1)} %get-tuple-element.35.refs_0_) | copy-start | bytes 1056772
  245.5 31.6 %collective-permute-start.48 = (bf16[688,256]{1,0:T(8,128)(2,1)S(1)}, bf16[688,256]{1,0:T(8,128)(2,1)S(1)}, u32[]{:S(2)}, u32[]{:S(2)}) collective-permute-start(bf16[688,256]{1,0:T(8,128)(2,1)S(1)} %copy-done.21), channel_id=1, source_target_pairs={{0,1},{1,0},{2,3},{3,2},{4,5},{5,4},{6,7},{7,6},{8,9},{9,8},{10,11... | collective-permute-start | bytes 1056776 | tf_op jit(solution)/shard_map/ppermute | solution.py:204
  247.3 31.5 %collective-permute-start.47 = (bf16[688,256]{1,0:T(8,128)(2,1)}, bf16[688,256]{1,0:T(8,128)(2,1)S(1)}, u32[]{:S(2)}, u32[]{:S(2)}) collective-permute-start(bf16[688,256]{1,0:T(8,128)(2,1)} %get-tuple-element.56.refs_3_), channel_id=1, source_target_pairs={{0,2},{1,3},{2,0},{3,1},{4,6},{5,7},{6,4},{7,5},{8,10},{9,11},{10,... | collective-permute-start | bytes 1056776 | tf_op jit(solution)/shard_map/ppermute | solution.py:204
  254.5 22.6 %copy-start.28 = (bf16[688,256]{1,0:T(8,128)(2,1)}, bf16[688,256]{1,0:T(8,128)(2,1)S(1)}, u32[]{:S(2)}) copy-start(bf16[688,256]{1,0:T(8,128)(2,1)S(1)} %collective-permute-done.51.refs_3_) | copy-start | bytes 1056772
  254.5 25.7 %collective-permute-start.46 = (bf16[688,256]{1,0:T(8,128)(2,1)S(1)}, bf16[688,256]{1,0:T(8,128)(2,1)S(1)}, u32[]{:S(2)}, u32[]{:S(2)}) collective-permute-start(bf16[688,256]{1,0:T(8,128)(2,1)S(1)} %copy-done.25), channel_id=1, source_target_pairs={{0,2},{1,3},{2,0},{3,1},{4,6},{5,7},{6,4},{7,5},{8,10},{9,11},{10,... | collective-permute-start | bytes 1056776 | tf_op jit(solution)/shard_map/ppermute | solution.py:204
  262.1 19.8 %collective-permute-start.45 = (bf16[688,256]{1,0:T(8,128)(2,1)S(1)}, bf16[688,256]{1,0:T(8,128)(2,1)S(1)}, u32[]{:S(2)}, u32[]{:S(2)}) collective-permute-start(bf16[688,256]{1,0:T(8,128)(2,1)S(1)} %copy-done.23), channel_id=1, source_target_pairs={{0,2},{1,3},{2,0},{3,1},{4,6},{5,7},{6,4},{7,5},{8,10},{9,11},{10,... | collective-permute-start | bytes 1056776 | tf_op jit(solution)/shard_map/ppermute | solution.py:204
  269.6 38.1 %collective-permute-start.44 = (bf16[688,256]{1,0:T(8,128)(2,1)S(1)}, bf16[688,256]{1,0:T(8,128)(2,1)S(1)}, u32[]{:S(2)}, u32[]{:S(2)}) collective-permute-start(bf16[688,256]{1,0:T(8,128)(2,1)S(1)} %copy-done.21), channel_id=1, source_target_pairs={{0,2},{1,3},{2,0},{3,1},{4,6},{5,7},{6,4},{7,5},{8,10},{9,11},{10,... | collective-permute-start | bytes 1056776 | tf_op jit(solution)/shard_map/ppermute | solution.py:204
  277.1 38.6 %collective-permute-start.43 = (bf16[688,256]{1,0:T(8,128)(2,1)S(1)}, bf16[688,256]{1,0:T(8,128)(2,1)S(1)}, u32[]{:S(2)}, u32[]{:S(2)}) collective-permute-start(bf16[688,256]{1,0:T(8,128)(2,1)S(1)} %copy-done.27), channel_id=1, source_target_pairs={{0,3},{1,2},{2,1},{3,0},{4,7},{5,6},{6,5},{7,4},{8,11},{9,10},{10,... | collective-permute-start | bytes 1056776 | tf_op jit(solution)/shard_map/ppermute | solution.py:204
  278.8 37.0 %collective-permute-start.32 = (bf16[688,256]{1,0:T(8,128)(2,1)S(1)}, bf16[688,256]{1,0:T(8,128)(2,1)S(1)}, u32[]{:S(2)}, u32[]{:S(2)}) collective-permute-start(bf16[688,256]{1,0:T(8,128)(2,1)S(1)} %copy-done.26), channel_id=1, source_target_pairs={{0,3},{1,2},{2,1},{3,0},{4,7},{5,6},{6,5},{7,4},{8,11},{9,10},{10,... | collective-permute-start | bytes 1056776 | tf_op jit(solution)/shard_map/ppermute | solution.py:204
  280.2 35.6 %collective-permute-start.21 = (bf16[688,256]{1,0:T(8,128)(2,1)S(1)}, bf16[688,256]{1,0:T(8,128)(2,1)S(1)}, u32[]{:S(2)}, u32[]{:S(2)}) collective-permute-start(bf16[688,256]{1,0:T(8,128)(2,1)S(1)} %copy-done.24), channel_id=1, source_target_pairs={{0,3},{1,2},{2,1},{3,0},{4,7},{5,6},{6,5},{7,4},{8,11},{9,10},{10,... | collective-permute-start | bytes 1056776 | tf_op jit(solution)/shard_map/ppermute | solution.py:204
  281.9 34.0 %collective-permute-start.10 = (bf16[688,256]{1,0:T(8,128)(2,1)S(1)}, bf16[688,256]{1,0:T(8,128)(2,1)S(1)}, u32[]{:S(2)}, u32[]{:S(2)}) collective-permute-start(bf16[688,256]{1,0:T(8,128)(2,1)S(1)} %copy-done.22), channel_id=1, source_target_pairs={{0,3},{1,2},{2,1},{3,0},{4,7},{5,6},{6,5},{7,4},{8,11},{9,10},{10,... | collective-permute-start | bytes 1056776 | tf_op jit(solution)/shard_map/ppermute | solution.py:204
  (43 other events, 280.1 us)

commit v2 on v0

v2 whole, which is shorter than its diff:
```python
import functools

import jax
import jax.numpy as jnp
from jax import lax
from jax.experimental import pallas as pl
from jax.experimental.pallas import tpu as pltpu
from jax.sharding import PartitionSpec as P

beta_first = 0.9
beta_second = 0.999
adam_count = 100.0
epsilon = 1e-08

F32 = jnp.float32
BF16 = jnp.bfloat16
VMEM_LIMIT = 56 * 1024 * 1024
PARTS = 4


def adam(place, arrived, own, other, first, second, held, part):
    owned, rank = first.shape
    width = arrived.shape[1]
    block = min(128, width)
    steps = width // block

    def kernel(place_ref, arrived_ref, own_ref, other_ref, first_ref, second_ref, *refs):
        first_out, second_out, direction_out = refs[-3:]
        grad_low = arrived_ref[...].astype(F32) + own_ref[0].astype(F32) + other_ref[0].astype(F32)
        first_next = beta_first * first_ref[...] + (1.0 - beta_first) * grad_low
        second_next = beta_second * second_ref[...] + (1.0 - beta_second) * grad_low * grad_low
        first_out[...] = first_next
        second_out[...] = second_next
        bias_first = 1.0 - beta_first**adam_count
        bias_second = 1.0 - beta_second**adam_count
        direction = first_next / bias_first / (jnp.sqrt(second_next / bias_second) + epsilon)
        direction_out[...] = direction.astype(BF16)

    column = pl.BlockSpec((owned, block), lambda i, place_ref: (0, part * steps + i))
    narrow = pl.BlockSpec((owned, block), lambda i, place_ref: (0, i))
    return pl.pallas_call(
        kernel,
        out_shape=[
            jax.ShapeDtypeStruct((owned, rank), F32),
            jax.ShapeDtypeStruct((owned, rank), F32),
            jax.ShapeDtypeStruct((owned, width), BF16),
        ],
        grid_spec=pltpu.PrefetchScalarGridSpec(
            num_scalar_prefetch=1,
            grid=(steps,),
            in_specs=[
                narrow,
                pl.BlockSpec((1, owned, block), lambda i, place_ref: (place_ref[0], 0, i)),
                pl.BlockSpec((1, owned, block), lambda i, place_ref: (place_ref[0], 0, i)),
                column,
                column,
            ]
            + [pl.BlockSpec(memory_space=pl.ANY)] * len(held),
            out_specs=[column, column, narrow],
        ),
        input_output_aliases={6 + index: index for index in range(len(held))},
        compiler_params=pltpu.CompilerParams(vmem_limit_bytes=VMEM_LIMIT),
        cost_estimate=pl.CostEstimate(
            flops=12 * owned * width, bytes_accessed=24 * owned * width, transcendentals=owned * width
        ),
        name="adam",
    )(place, arrived, own, other, first, second, *held)


def expand(target, gathered, last, basis_t, held):
    owned, width = last.shape
    rank, features = basis_t.shape
    count = gathered[0].shape[0]
    block = min(512, features)

    def kernel(target_ref, basis_ref, last_ref, *refs):
        gathered_refs, out_ref, whole_ref = refs[: len(gathered)], refs[-2], refs[-1]

        @pl.when(pl.program_id(0) == 0)
        def _():
            for index, gathered_ref in enumerate(gathered_refs):
                whole_ref[:, index * width : (index + 1) * width] = gathered_ref[0]
            whole_ref[:, rank - width :] = last_ref[...]

        out_ref[0] = jnp.dot(whole_ref[...], basis_ref[...], preferred_element_type=F32)

    return pl.pallas_call(
        kernel,
        out_shape=jax.ShapeDtypeStruct((count, owned, features), F32),
        grid_spec=pltpu.PrefetchScalarGridSpec(
            num_scalar_prefetch=1,
            grid=(features // block,),
            in_specs=[
                pl.BlockSpec((rank, block), lambda i, target_ref: (0, i)),
                pl.BlockSpec((owned, width), lambda i, target_ref: (0, 0)),
            ]
            + [pl.BlockSpec((1, owned, width), lambda i, target_ref: (target_ref[0], 0, 0))] * len(gathered)
            + [pl.BlockSpec(memory_space=pl.ANY)] * len(held),
            out_specs=pl.BlockSpec((1, owned, block), lambda i, target_ref: (target_ref[0], 0, i)),
            scratch_shapes=[pltpu.VMEM((owned, rank), BF16)],
        ),
        input_output_aliases={3 + len(gathered): 0} if held else {},
        compiler_params=pltpu.CompilerParams(vmem_limit_bytes=VMEM_LIMIT),
        cost_estimate=pl.CostEstimate(
            flops=2 * owned * rank * features,
            bytes_accessed=2 * (owned * rank + rank * features) + 4 * owned * features,
            transcendentals=0,
        ),
        name="expand",
    )(target, basis_t, last, *gathered, *held)


def transpose(value):
    rows, columns = value.shape
    block = min(512, rows)

    def kernel(value_ref, out_ref):
        out_ref[...] = value_ref[...].T

    return pl.pallas_call(
        kernel,
        out_shape=jax.ShapeDtypeStruct((columns, rows), value.dtype),
        grid=(rows // block,),
        in_specs=[pl.BlockSpec((block, columns), lambda i: (i, 0))],
        out_specs=pl.BlockSpec((columns, block), lambda i: (0, i)),
        compiler_params=pltpu.CompilerParams(vmem_limit_bytes=VMEM_LIMIT),
        cost_estimate=pl.CostEstimate(flops=0, bytes_accessed=4 * rows * columns, transcendentals=0),
        name="transpose",
    )(value)


def total_of(*terms):
    total = terms[0].astype(F32)
    for term in terms[1:]:
        total = total + term.astype(F32)
    return total.astype(BF16)


def after(value, *earlier):
    return lax.optimization_barrier((value, *earlier))[0]


def local(activations, out_grads, projector, first_moment, second_moment):
    owned = first_moment.shape[1]
    features = activations[0]
    basis = projector[0]
    rank = basis.shape[1]
    tokens = features.shape[0]
    dp_count, fsdp_count = lax.axis_size("dp"), lax.axis_size("fsdp")
    dp, fsdp = lax.axis_index("dp"), lax.axis_index("fsdp")
    chips = dp_count // 2
    chip, core = dp // 2, dp % 2
    width = rank // PARTS

    offsets = [1 << bit for bit in range(fsdp_count.bit_length() - 1)]
    order = jnp.stack([fsdp ^ offset for offset in range(fsdp_count)]).astype(jnp.int32)
    place = jnp.stack([chip, core]).astype(jnp.int32)

    def across(value, offset):
        return lax.ppermute(value, "fsdp", [(index, index ^ offset) for index in range(fsdp_count)])

    def sibling(value):
        return lax.ppermute(value, "dp", [(index, index ^ 1) for index in range(dp_count)])

    def onward(value):
        return lax.ppermute(value, "dp", [(index, (index + 2) % dp_count) for index in range(dp_count)])

    def sum_step(halves, step):
        return [
            total_of(half, across(half, steps[step])) for half, steps in zip(halves, (offsets, offsets[::-1]))
        ]

    def halves_of(value):
        return [value[: tokens // 2], value[tokens // 2 :]]

    def gradient(projected):
        product = lax.dot_general(
            out_grads[0], projected, (((0,), (0,)), ((), ())), preferred_element_type=F32
        ).astype(BF16)
        return product.reshape(chips, 2, owned, projected.shape[1])

    def parity(product, which):
        return lax.dynamic_slice_in_dim(product, which, 1, axis=1)[:, 0]

    def block_at(hop, blocks):
        return lax.dynamic_index_in_dim(blocks, (chip - 1 - hop + chips) % chips, axis=0, keepdims=False)

    early = jnp.dot(features, basis[:, :width], preferred_element_type=F32).astype(BF16)
    late = jnp.dot(after(features, early), basis[:, width:], preferred_element_type=F32).astype(BF16)
    rest = lax.psum(late[:, width:], "fsdp")
    sums_0 = sum_step(halves_of(early), 0)
    basis_t = transpose(after(basis, *sums_0))
    sums_1 = sum_step([after(half, *sums_0) for half in halves_of(late[:, :width])], 0)
    for step in range(1, len(offsets)):
        sums_0 = sum_step(sums_0, step)

    def send_out(product, token):
        outgoing = parity(after(product, token), 1 - core)
        return (parity(product, core), sibling(outgoing)), outgoing

    blocks = [None] * PARTS
    product = gradient(jnp.concatenate(sums_0))
    blocks[0], token = send_out(product, product)
    travelling = [None] * PARTS

    held = ()
    gathered = []
    hops = chips - 1
    for slot in range(hops + PARTS):
        if slot == 1:
            for step in range(1, len(offsets)):
                sums_1 = sum_step(sums_1, step)
            product = gradient(after(jnp.concatenate(sums_1), token))
            blocks[1], token = send_out(product, product)
        if slot == 2:
            product = gradient(after(rest, token))
            for part in range(2, PARTS):
                begin = (part - 2) * width
                blocks[part], token = send_out(product[..., begin : begin + width], token if part > 2 else product)
        for part in range(PARTS):
            hop = slot - part
            if not 0 <= hop <= hops:
                continue
            own, other = blocks[part]
            if hop < hops:
                terms = (block_at(hop, own), block_at(hop, other))
                if hop == 0:
                    leaving = total_of(after(terms[0], token), terms[1])
                else:
                    leaving = total_of(after(travelling[part], token), *terms)
                travelling[part] = onward(leaving)
                token = leaving
            else:
                first_next, second_next, direction = adam(
                    place, after(travelling[part], token), own, other, first_moment[0], second_moment[0], held, part
                )
                held = (first_next, second_next)
                token = direction
                if part < PARTS - 1:
                    if gathered:
                        direction = after(direction, gathered[-1])
                    gathered.append(lax.all_gather(direction, "fsdp"))

    last = [direction] + [across(direction, offset) for offset in range(1, fsdp_count)]
    update = ()
    for offset in range(fsdp_count):
        update = (expand(order[offset : offset + 1], gathered, last[offset], basis_t, update),)
    return (update[0][None], held[0][None], held[1][None])


def solution(mesh):
    in_specs = (
        P(None, "dp", "fsdp"),
        P(None, "dp", "fsdp"),
        P(None, "fsdp", None),
        P(None, ("fsdp", "dp"), None),
        P(None, ("fsdp", "dp"), None),
    )
    out_specs = (
        P(None, None, "dp", "fsdp"),
        P(None, ("fsdp", "dp"), None),
        P(None, ("fsdp", "dp"), None),
    )
    return jax.shard_map(local, mesh=mesh, in_specs=in_specs, out_specs=out_specs, check_vma=False)
```

time: 344 us -> 335 us (0.974)
  waiting for transfers between devices: 239 us -> 149 us
  Pallas kernels: 0 us -> 49.2 us
  starting transfers between devices: 0.3 us -> 21.9 us
  local copies, waits for them, and re-layouts: 33.8 us -> 46.4 us
  matrix products: 48.2 us -> 37.2 us
  other arithmetic: 7.76 us -> 15.9 us
    ppermute x0 -> x27, waiting for transfers between devices: none -> 110 us  [the longest x12 87.8 us: onward(): lax.ppermute(value, 'dp', [(index, (index + 2) % dp_count) for index in r...]
    unnamed x4, waiting for transfers between devices: 109 us -> 0.07 us
    all_gather x1 -> x3, waiting for transfers between devices: 57.6 us -> 0.01 us  [local(): gathered.append(lax.all_gather(direction, 'fsdp'))]
    pallas_call x0 -> x9, Pallas kernels: none -> 49.2 us  [the longest x4 29.8 us: expand(): pl.pallas_call(kernel, out_shape=jax.ShapeDtypeStruct((count, owned, feat...]
    psum x1, waiting for transfers between devices: 72.4 us -> 38.8 us  [local(): rest = lax.psum(late[:, width:], 'fsdp')]
    unnamed x8 -> x32, local copies, waits for them, and re-layouts: 31.2 us -> 7.79 us
    ppermute x0 -> x27, starting transfers between devices: none -> 21.7 us  [the longest x11 15.3 us: across(): lax.ppermute(value, 'fsdp', [(index, index ^ offset) for index in range(f...]
    squeeze x0 -> x12, local copies, waits for them, and re-layouts: none -> 16.1 us  [the longest x8 14 us: parity(): return lax.dynamic_slice_in_dim(product, which, 1, axis=1)[:, 0]]
  transfers between devices with their start and end apart: 3 -> 31, of which waited for: 3 -> 19; matrix products, arithmetic and copies ran while one was open for 3% -> 13% of each run, Pallas kernels for 0% -> 11%
where the time goes in v2:
time: 335 us; the launch traced here: 333 us
  waiting for transfers between devices  149 us (44%)
  Pallas kernels  49.2 us (15%)
  local copies, waits for them, and re-layouts  46.4 us (14%)
  matrix products  37.2 us (11%)
  starting transfers between devices  21.9 us (7%)
  other arithmetic  15.9 us (5%)
  between operations  14.1 us (4%)
    ppermute x12, waiting for transfers between devices, onward(): lax.ppermute(value, 'dp', [(index, (index + 2) % dp_count) for index in r...  87.8 us
    psum x1, waiting for transfers between devices, local(): rest = lax.psum(late[:, width:], 'fsdp')  38.8 us
    dot_general x3, matrix products, gradient(): lax.dot_general(out_grads[0], projected, (((0,), (0,)), ((), ())), prefer...  30 us
    pallas_call x4, Pallas kernels, expand(): pl.pallas_call(kernel, out_shape=jax.ShapeDtypeStruct((count, owned, feat...  29.8 us
    ppermute x11, waiting for transfers between devices, across(): lax.ppermute(value, 'fsdp', [(index, index ^ offset) for index in range(f...  22 us
    convert_element_type x3, local copies, waits for them, and re-layouts, gradient(): product = lax.dot_general(out_grads[0], projected, (((0,), (0,)), ((), ()...  16.8 us
    convert_element_type x19, other arithmetic, total_of(): return total.astype(BF16)  15.3 us
    ppermute x11, starting transfers between devices, across(): lax.ppermute(value, 'fsdp', [(index, index ^ offset) for index in range(f...  15.3 us
  transfers between devices with their start and end apart: 31, of which 19 were waited for; matrix products, arithmetic and copies ran while one was open for 13% of the time, Pallas kernels for 11%

profile of v2, /device:TPU:0, one launch (start us, length us, event | category | flops | bytes accessed | tf_op | source)
XLA Modules:
  0.0 333.4 jit_solution(13611395494197178022)
XLA Ops:
  7.2 3.9 %convolution_convert_fusion = bf16[1024,256]{1,0:T(8,128)(2,1)S(1)} fusion(bf16[2048,1024]{1,0:T(8,128)(2,1)} %bitcast.167, bf16[1,1024,2048]{2,1,0:T(8,128)(2,1)} %param.5), kind=kOutput, calls=%fused_computation.23 | convolution fusion | flops 1074003968 | bytes 5767168 | tf_op jit(solution)/shard_map/dot_general | solution.py:188
  11.2 3.0 collective-permute-start
  14.2 1.5 collective-permute-start.1
  15.7 4.8 %collective-permute-done = bf16[512,256]{1,0:T(8,128)(2,1)S(1)} collective-permute-done((bf16[512,256]{1,0:T(8,128)(2,1)S(1)}, bf16[512,256]{1,0:T(8,128)(2,1)S(1)}, u32[]{:S(2)}, u32[]{:S(2)}) %collective-permute-start) | collective-permute-done | bytes 262176 | tf_op jit(solution)/shard_map/ppermute | solution.py:160
  20.5 1.5 collective-permute-done.1
  22.5 3.4 %fusion.26 = bf16[1024,768]{1,0:T(8,128)(2,1)S(1)} fusion(bf16[1024,2048]{1,0:T(8,128)(2,1)S(1)} %bitcast.170, bf16[2048,1024]{1,0:T(8,128)(2,1)S(1)} %bitcast.169), kind=kOutput, calls=%fused_computation.14 | convolution fusion | flops 3222011904 | bytes 8912896 | tf_op jit(solution)/shard_map/dot_general | solution.py:189
  25.9 1.8 collective-permute-start.6
  27.8 1.6 collective-permute-start.2
  29.4 3.5 %collective-permute-done.6 = bf16[512,256]{1,0:T(8,128)(2,1)S(1)} collective-permute-done((bf16[512,256]{1,0:T(8,128)(2,1)S(1)}, bf16[512,256]{1,0:T(8,128)(2,1)S(1)}, u32[]{:S(2)}, u32[]{:S(2)}) %collective-permute-start.6) | collective-permute-done | bytes 262176 | tf_op jit(solution)/shard_map/ppermute | solution.py:160
  33.0 8.8 %fusion.21 = bf16[5504,256]{0,1:T(8,128)(2,1)} fusion(bf16[1,1024,5504]{2,1,0:T(8,128)(2,1)} %param.6, bf16[512,256]{1,0:T(8,128)(2,1)S(1)} %add_convert_fusion, bf16[512,256]{1,0:T(8,128)(2,1)S(1)} %add_convert_fusion.1), kind=kOutput, calls=%fused_computation.11 | convolution fusion | flops 2888138752 | bytes 14614528 | tf_op jit(solution)/shard_map/dot_general | solution.py:177
  41.8 3.9 %copy.17 = bf16[5504,256]{1,0:T(8,128)(2,1)S(1)} copy(bf16[5504,256]{0,1:T(8,128)(2,1)} %fusion.21) | data formatting | bytes 5636096 | tf_op jit(solution)/shard_map/convert_element_type | solution.py:179
  45.7 1.2 dynamic-slice_bitcast_fusion.7
  46.9 1.4 collective-permute-start.4
  50.0 6.1 %collective-permute-done.4 = bf16[512,256]{1,0:T(8,128)(2,1)} collective-permute-done((bf16[512,256]{1,0:T(8,128)(2,1)S(1)}, bf16[512,256]{1,0:T(8,128)(2,1)}, u32[]{:S(2)}, u32[]{:S(2)}) %collective-permute-start.4) | collective-permute-done | bytes 262176 | tf_op jit(solution)/shard_map/ppermute | solution.py:160
  57.1 1.4 collective-permute-start.5
  58.5 2.7 collective-permute-done.3
  61.3 3.4 %collective-permute-done.5 = bf16[512,256]{1,0:T(8,128)(2,1)S(1)} collective-permute-done((bf16[512,256]{1,0:T(8,128)(2,1)S(1)}, bf16[512,256]{1,0:T(8,128)(2,1)S(1)}, u32[]{:S(2)}, u32[]{:S(2)}) %collective-permute-start.5) | collective-permute-done | bytes 262176 | tf_op jit(solution)/shard_map/ppermute | solution.py:160
  65.9 8.8 %fusion.18 = bf16[5504,256]{0,1:T(8,128)(2,1)} fusion(bf16[1024,256]{1,0:T(8,128)(2,1)S(1)} %pad_maximum_fusion, bf16[1,1024,5504]{2,1,0:T(8,128)(2,1)} %param.6), kind=kOutput, calls=%fused_computation.10 | convolution fusion | flops 2887090176 | bytes 14614528 | tf_op jit(solution)/shard_map/dot_general | solution.py:177
  74.7 4.6 %copy.18 = bf16[5504,256]{1,0:T(8,128)(2,1)} copy(bf16[5504,256]{0,1:T(8,128)(2,1)} %fusion.18) | data formatting | bytes 5636096 | tf_op jit(solution)/shard_map/convert_element_type | solution.py:179
  79.3 2.6 dynamic-slice_bitcast_fusion.6
  83.1 1.7 collective-permute-start.9
  85.8 10.0 %collective-permute-done.9 = bf16[688,256]{1,0:T(8,128)(2,1)} collective-permute-done((bf16[688,256]{1,0:T(8,128)(2,1)S(1)}, bf16[688,256]{1,0:T(8,128)(2,1)}, u32[]{:S(2)}, u32[]{:S(2)}) %collective-permute-start.9) | collective-permute-done | bytes 352288 | tf_op jit(solution)/shard_map/ppermute | solution.py:166
  95.9 1.2 fusion.40
  98.2 38.8 %all-reduce.2.cloned.1.call-done = bf16[1024,512]{1,0:T(8,128)(2,1)} async-done(((bf16[1024,512]{1,0:T(8,128)(2,1)}), bf16[1024,512]{1,0:T(8,128)(2,1)}) %all-reduce.2.cloned.1.call-update) | async-done | bytes 1048592 | tf_op jit(solution)/shard_map/psum | solution.py:190
  137.0 12.3 %fusion.9 = bf16[5504,512]{0,1:T(8,128)(2,1)} fusion(bf16[1024,512]{1,0:T(8,128)(2,1)} %all-reduce.2.cloned.1.call-done, bf16[1,1024,5504]{2,1,0:T(8,128)(2,1)} %param.6), kind=kOutput, calls=%fused_computation.7 | convolution fusion | flops 5774180352 | bytes 17956864 | tf_op jit(solution)/shard_map/dot_general | solution.py:177
  149.4 8.3 %copy.19 = bf16[5504,512]{1,0:T(8,128)(2,1)} copy(bf16[5504,512]{0,1:T(8,128)(2,1)} %fusion.9) | data formatting | bytes 11272192 | tf_op jit(solution)/shard_map/convert_element_type | solution.py:179
  157.7 4.6 %fusion.47 = (bf16[4,2,688,256]{3,2,1,0:T(8,128)(2,1)S(1)}, bf16[4,2,688,256]{3,2,1,0:T(8,128)(2,1)}) fusion(bf16[4,2,688,512]{3,2,1,0:T(8,128)(2,1)} %bitcast.156), kind=kLoop, calls=%fused_computation.76 | loop fusion | bytes 11272192 | tf_op jit(solution)/shard_map/slice | solution.py:219
  162.3 1.5 copy-done.2
  163.8 1.2 dynamic-slice_bitcast_fusion.5
  165.0 1.5 collective-permute-start.12
  167.1 1.2 dynamic-slice_bitcast_fusion.3.own_ref
  168.3 1.5 collective-permute-start.11
  169.8 1.2 dynamic-slice_bitcast_fusion.4
  170.9 6.9 %collective-permute-done.12 = bf16[688,256]{1,0:T(8,128)(2,1)S(1)} collective-permute-done((bf16[688,256]{1,0:T(8,128)(2,1)S(1)}, bf16[688,256]{1,0:T(8,128)(2,1)S(1)}, u32[]{:S(2)}, u32[]{:S(2)}) %collective-permute-start.12) | collective-permute-done | bytes 352288 | tf_op jit(solution)/shard_map/ppermute | solution.py:166
  177.8 1.1 fusion.38
  180.0 5.3 %collective-permute-done.11 = bf16[688,256]{1,0:T(8,128)(2,1)S(1)} collective-permute-done((bf16[688,256]{1,0:T(8,128)(2,1)S(1)}, bf16[688,256]{1,0:T(8,128)(2,1)S(1)}, u32[]{:S(2)}, u32[]{:S(2)}) %collective-permute-start.11) | collective-permute-done | bytes 352288 | tf_op jit(solution)/shard_map/ppermute | solution.py:166
  185.4 1.2 fusion.37
  187.7 4.8 %collective-permute-done.16.arrived_ref = bf16[688,256]{1,0:T(8,128)(2,1)S(1)} collective-permute-done((bf16[688,256]{1,0:T(8,128)(2,1)S(1)}, bf16[688,256]{1,0:T(8,128)(2,1)S(1)}, u32[]{:S(2)}, u32[]{:S(2)}) %collective-permute-start.16) | collective-permute-done | bytes 352288 | tf_op jit(solution)/shard_map/ppermute | solution.py:166
  193.3 3.5 %adam.4 = (f32[688,1024]{1,0:T(8,128)}, f32[688,1024]{1,0:T(8,128)}, bf16[688,256]{1,0:T(8,128)(2,1)}) custom-call(s32[2]{0:T(128)} %pad_add_fusion.place_ref, bf16[688,256]{1,0:T(8,128)(2,1)} %copy-done.14, bf16[4,688,256]{2,1,0:T(8,128)(2,1)} %dynamic-slice_bitcast_fusion.3.own_ref, bf16[4,688,256]{2,1,0:T(8,128)(2,1)} %collective-permute-done.8.other_ref, ...), custom_call_target="tpu_custom_call" | custom-call | flops 2113536 | bytes 4227072 | tf_op jit(solution)/shard_map/adam/pallas_call | solution.py:41
  197.0 2.8 dynamic-slice_bitcast_fusion.2.own_ref
  200.8 9.0 %collective-permute-done.15 = bf16[688,256]{1,0:T(8,128)(2,1)S(1)} collective-permute-done((bf16[688,256]{1,0:T(8,128)(2,1)S(1)}, bf16[688,256]{1,0:T(8,128)(2,1)S(1)}, u32[]{:S(2)}, u32[]{:S(2)}) %collective-permute-start.15) | collective-permute-done | bytes 352288 | tf_op jit(solution)/shard_map/ppermute | solution.py:166
  209.8 1.2 fusion.35
  211.1 6.2 %collective-permute-done.14 = bf16[688,256]{1,0:T(8,128)(2,1)S(1)} collective-permute-done((bf16[688,256]{1,0:T(8,128)(2,1)S(1)}, bf16[688,256]{1,0:T(8,128)(2,1)S(1)}, u32[]{:S(2)}, u32[]{:S(2)}) %collective-permute-start.14) | collective-permute-done | bytes 352288 | tf_op jit(solution)/shard_map/ppermute | solution.py:166
  217.4 1.2 fusion.34
  219.8 4.7 %collective-permute-done.20.arrived_ref = bf16[688,256]{1,0:T(8,128)(2,1)S(1)} collective-permute-done((bf16[688,256]{1,0:T(8,128)(2,1)S(1)}, bf16[688,256]{1,0:T(8,128)(2,1)S(1)}, u32[]{:S(2)}, u32[]{:S(2)}) %collective-permute-start.20) | collective-permute-done | bytes 352288 | tf_op jit(solution)/shard_map/ppermute | solution.py:166
  225.2 3.5 %adam.5 = (f32[688,1024]{1,0:T(8,128)}, f32[688,1024]{1,0:T(8,128)}, bf16[688,256]{1,0:T(8,128)(2,1)}) custom-call(s32[2]{0:T(128)} %pad_add_fusion.place_ref, bf16[688,256]{1,0:T(8,128)(2,1)} %copy-done.10, bf16[4,688,256]{2,1,0:T(8,128)(2,1)} %dynamic-slice_bitcast_fusion.2.own_ref, ...), custom_call_target="tpu_custom_call", output_to_operand_aliasing={{0}: (6, {}), {1}: (7, {})} | custom-call | flops 2113536 | bytes 4227072 | tf_op jit(solution)/shard_map/adam/pallas_call | solution.py:41
  228.9 12.9 %collective-permute-done.19 = bf16[688,256]{1,0:T(8,128)(2,1)S(1)} collective-permute-done((bf16[688,256]{1,0:T(8,128)(2,1)S(1)}, bf16[688,256]{1,0:T(8,128)(2,1)S(1)}, u32[]{:S(2)}, u32[]{:S(2)}) %collective-permute-start.19) | collective-permute-done | bytes 352288 | tf_op jit(solution)/shard_map/ppermute | solution.py:166
  241.8 1.2 fusion.32
  243.1 2.6 dynamic-slice_bitcast_fusion.1.own_ref
  245.8 3.6 %collective-permute-done.18 = bf16[688,256]{1,0:T(8,128)(2,1)S(1)} collective-permute-done((bf16[688,256]{1,0:T(8,128)(2,1)S(1)}, bf16[688,256]{1,0:T(8,128)(2,1)S(1)}, u32[]{:S(2)}, u32[]{:S(2)}) %collective-permute-start.18) | collective-permute-done | bytes 352288 | tf_op jit(solution)/shard_map/ppermute | solution.py:166
  249.4 1.1 fusion.31
  250.5 5.1 %collective-permute-done.22.arrived_ref = bf16[688,256]{1,0:T(8,128)(2,1)S(1)} collective-permute-done((bf16[688,256]{1,0:T(8,128)(2,1)S(1)}, bf16[688,256]{1,0:T(8,128)(2,1)S(1)}, u32[]{:S(2)}, u32[]{:S(2)}) %collective-permute-start.22) | collective-permute-done | bytes 352288 | tf_op jit(solution)/shard_map/ppermute | solution.py:166
  256.3 3.5 %adam.6 = (f32[688,1024]{1,0:T(8,128)}, f32[688,1024]{1,0:T(8,128)}, bf16[688,256]{1,0:T(8,128)(2,1)}) custom-call(s32[2]{0:T(128)} %pad_add_fusion.place_ref, bf16[688,256]{1,0:T(8,128)(2,1)} %copy-done.11, bf16[4,688,256]{2,1,0:T(8,128)(2,1)} %dynamic-slice_bitcast_fusion.1.own_ref, ...), custom_call_target="tpu_custom_call", output_to_operand_aliasing={{0}: (6, {}), {1}: (7, {})} | custom-call | flops 2113536 | bytes 4227072 | tf_op jit(solution)/shard_map/adam/pallas_call | solution.py:41
  259.9 10.7 %collective-permute-done.21 = bf16[688,256]{1,0:T(8,128)(2,1)S(1)} collective-permute-done((bf16[688,256]{1,0:T(8,128)(2,1)S(1)}, bf16[688,256]{1,0:T(8,128)(2,1)S(1)}, u32[]{:S(2)}, u32[]{:S(2)}) %collective-permute-start.21) | collective-permute-done | bytes 352288 | tf_op jit(solution)/shard_map/ppermute | solution.py:166
  272.0 1.2 dynamic-slice_bitcast_fusion.own_ref
  273.2 8.6 %collective-permute-done.23.arrived_ref = bf16[688,256]{1,0:T(8,128)(2,1)S(1)} collective-permute-done((bf16[688,256]{1,0:T(8,128)(2,1)S(1)}, bf16[688,256]{1,0:T(8,128)(2,1)S(1)}, u32[]{:S(2)}, u32[]{:S(2)}) %collective-permute-start.23) | collective-permute-done | bytes 352288 | tf_op jit(solution)/shard_map/ppermute | solution.py:166
  282.5 3.5 %adam.7 = (f32[688,1024]{1,0:T(8,128)}, f32[688,1024]{1,0:T(8,128)}, bf16[688,256]{1,0:T(8,128)(2,1)}) custom-call(s32[2]{0:T(128)} %pad_add_fusion.place_ref, bf16[688,256]{1,0:T(8,128)(2,1)} %copy-done.13, bf16[4,688,256]{2,1,0:T(8,128)(2,1)} %dynamic-slice_bitcast_fusion.own_ref, ...), custom_call_target="tpu_custom_call", output_to_operand_aliasing={{0}: (6, {}), {1}: (7, {})} | custom-call | flops 2113536 | bytes 4227072 | tf_op jit(solution)/shard_map/adam/pallas_call | solution.py:41
  286.1 1.5 collective-permute-start.26
  287.5 5.3 %transpose.18.basis_ref = bf16[1024,2048]{1,0:T(8,128)(2,1)} custom-call(bf16[2048,1024]{1,0:T(8,128)(2,1)} %bitcast.168), custom_call_target="tpu_custom_call" | custom-call | bytes 8388608 | tf_op jit(solution)/shard_map/transpose/pallas_call | solution.py:120
  293.4 1.5 collective-permute-start.24
  294.9 7.5 %expand.4.refs_3_ = f32[4,688,2048]{2,1,0:T(8,128)} custom-call(s32[1]{0:T(128)} %bitcast.51.target_ref, bf16[1024,2048]{1,0:T(8,128)(2,1)} %transpose.18.basis_ref, bf16[688,256]{1,0:T(8,128)(2,1)} %get-tuple-element.78.last_ref, bf16[4,688,256]{2,1,0:T(8,128)(2,1)} %bitcast.144, bf16[4,688,256]{2,1,0:T(8,128)(2,1)} %bitcast.148, bf16[4,688,256]{2,1,0:T(8,128)(2,1)} %bitcast.152), custom_call_target="tpu_custom_call" | custom-call | flops 2885681152 | bytes 11239424 | tf_op jit(solution)/shard_map/expand/pallas_call | solution.py:87
  303.1 7.4 %expand.5.refs_3_ = f32[4,688,2048]{2,1,0:T(8,128)} custom-call(s32[1]{0:T(128)} %bitcast.50.target_ref, bf16[1024,2048]{1,0:T(8,128)(2,1)} %transpose.18.basis_ref, bf16[688,256]{1,0:T(8,128)(2,1)} %copy-done.8, bf16[4,688,256]{2,1,0:T(8,128)(2,1)} %bitcast.145, bf16[4,688,256]{2,1,0:T(8,128)(2,1)} %bitcast.149, ...), custom_call_target="tpu_custom_call", output_to_operand_aliasing={{}: (6, {})} | custom-call | flops 2885681152 | bytes 11239424 | tf_op jit(solution)/shard_map/expand/pallas_call | solution.py:87
  311.3 7.4 %expand.6.refs_3_ = f32[4,688,2048]{2,1,0:T(8,128)} custom-call(s32[1]{0:T(128)} %bitcast.49.target_ref, bf16[1024,2048]{1,0:T(8,128)(2,1)} %transpose.18.basis_ref, bf16[688,256]{1,0:T(8,128)(2,1)} %copy-done.12, bf16[4,688,256]{2,1,0:T(8,128)(2,1)} %bitcast.146, bf16[4,688,256]{2,1,0:T(8,128)(2,1)} %bitcast.150, ...), custom_call_target="tpu_custom_call", output_to_operand_aliasing={{}: (6, {})} | custom-call | flops 2885681152 | bytes 11239424 | tf_op jit(solution)/shard_map/expand/pallas_call | solution.py:87
  319.5 7.4 %expand.7 = f32[4,688,2048]{2,1,0:T(8,128)} custom-call(s32[1]{0:T(128)} %bitcast.target_ref, bf16[1024,2048]{1,0:T(8,128)(2,1)} %transpose.18.basis_ref, bf16[688,256]{1,0:T(8,128)(2,1)} %copy-done.9, bf16[4,688,256]{2,1,0:T(8,128)(2,1)} %bitcast.147, bf16[4,688,256]{2,1,0:T(8,128)(2,1)} %bitcast.151, ...), custom_call_target="tpu_custom_call", output_to_operand_aliasing={{}: (6, {})} | custom-call | flops 2885681152 | bytes 11239424 | tf_op jit(solution)/shard_map/expand/pallas_call | solution.py:87
  (88 shorter events, 20.7 us)
Async XLA Ops:
  7.2 129.8 %all-reduce.2.cloned.1.call-start = ((), (), s32[]{:S(2)}) async-start(), calls=%async_computation | async-start | bytes 2097152 | tf_op jit(solution)/shard_map/psum | solution.py:190
  7.2 15.3 %copy-start.4 = (bf16[1,2048,1024]{2,1,0:T(8,128)(2,1)S(1)}, bf16[1,2048,1024]{2,1,0:T(8,128)(2,1)}, u32[]{:S(2)}) copy-start(bf16[1,2048,1024]{2,1,0:T(8,128)(2,1)} %param.7) | copy-start | bytes 12582916
  7.2 15.3 %copy-start.15 = (bf16[1,1024,2048]{2,1,0:T(8,128)(2,1)S(1)}, bf16[1,1024,2048]{2,1,0:T(8,128)(2,1)}, u32[]{:S(2)}) copy-start(bf16[1,1024,2048]{2,1,0:T(8,128)(2,1)} %param.5) | copy-start | bytes 12582916
  11.2 9.3 %collective-permute-start = (bf16[512,256]{1,0:T(8,128)(2,1)S(1)}, bf16[512,256]{1,0:T(8,128)(2,1)S(1)}, u32[]{:S(2)}, u32[]{:S(2)}) collective-permute-start(bf16[512,256]{1,0:T(8,128)(2,1)S(1)} %get-tuple-element.90), channel_id=1, source_target_pairs={{0,1},{1,0},{2,3},{3,2},{4,5},{5,4},{6,7},{7,6},{8,9},{9,8},{10,11... | collective-permute-start | bytes 786440 | tf_op jit(solution)/shard_map/ppermute | solution.py:160
  14.2 7.8 %collective-permute-start.1 = (bf16[512,256]{1,0:T(8,128)(2,1)S(1)}, bf16[512,256]{1,0:T(8,128)(2,1)S(1)}, u32[]{:S(2)}, u32[]{:S(2)}) collective-permute-start(bf16[512,256]{1,0:T(8,128)(2,1)S(1)} %get-tuple-element.89), channel_id=1, source_target_pairs={{0,2},{1,3},{2,0},{3,1},{4,6},{5,7},{6,4},{7,5},{8,10},{9,11},{10,... | collective-permute-start | bytes 786440 | tf_op jit(solution)/shard_map/ppermute | solution.py:160
  22.1 7.3 %collective-permute-start.7 = (bf16[512,256]{1,0:T(8,128)(2,1)S(1)}, bf16[512,256]{1,0:T(8,128)(2,1)S(1)}, u32[]{:S(2)}, u32[]{:S(2)}) collective-permute-start(bf16[512,256]{1,0:T(8,128)(2,1)S(1)} %get-tuple-element.87), channel_id=1, source_target_pairs={{0,1},{1,0},{2,3},{3,2},{4,5},{5,4},{6,7},{7,6},{8,9},{9,8},{10,11... | collective-permute-start | bytes 786440 | tf_op jit(solution)/shard_map/ppermute | solution.py:160
  25.9 1.8 copy-start.5
  25.9 7.0 %collective-permute-start.6 = (bf16[512,256]{1,0:T(8,128)(2,1)S(1)}, bf16[512,256]{1,0:T(8,128)(2,1)S(1)}, u32[]{:S(2)}, u32[]{:S(2)}) collective-permute-start(bf16[512,256]{1,0:T(8,128)(2,1)S(1)} %get-tuple-element.88), channel_id=1, source_target_pairs={{0,2},{1,3},{2,0},{3,1},{4,6},{5,7},{6,4},{7,5},{8,10},{9,11},{10,... | collective-permute-start | bytes 786440 | tf_op jit(solution)/shard_map/ppermute | solution.py:160
  27.8 20.6 %collective-permute-start.2 = (bf16[512,256]{1,0:T(8,128)(2,1)S(1)}, bf16[512,256]{1,0:T(8,128)(2,1)}, u32[]{:S(2)}, u32[]{:S(2)}) collective-permute-start(bf16[512,256]{1,0:T(8,128)(2,1)S(1)} %get-tuple-element.45), channel_id=1, source_target_pairs={{0,1},{1,0},{2,3},{3,2},{4,5},{5,4},{6,7},{7,6},{8,9},{9,8},{10,11... | collective-permute-start | bytes 786440 | tf_op jit(solution)/shard_map/ppermute | solution.py:160
  46.9 18.0 %collective-permute-start.8 = (bf16[4,688,256]{2,1,0:T(8,128)(2,1)}, bf16[4,688,256]{2,1,0:T(8,128)(2,1)}, u32[]{:S(2)}, u32[]{:S(2)}) collective-permute-start(bf16[4,688,256]{2,1,0:T(8,128)(2,1)} %dynamic-slice_bitcast_fusion.7), channel_id=1, source_target_pairs={{0,4},{4,0},{8,12},{12,8},{16,20},{20,16},{24,28},{28,24},{1,5},{5... | collective-permute-start | bytes 4227080 | tf_op jit(solution)/shard_map/ppermute | solution.py:163
  46.9 9.2 %collective-permute-start.4 = (bf16[512,256]{1,0:T(8,128)(2,1)S(1)}, bf16[512,256]{1,0:T(8,128)(2,1)}, u32[]{:S(2)}, u32[]{:S(2)}) collective-permute-start(bf16[512,256]{1,0:T(8,128)(2,1)S(1)} %get-tuple-element.46), channel_id=1, source_target_pairs={{0,2},{1,3},{2,0},{3,1},{4,6},{5,7},{6,4},{7,5},{8,10},{9,11},{10,... | collective-permute-start | bytes 786440 | tf_op jit(solution)/shard_map/ppermute | solution.py:160
  49.3 11.9 %collective-permute-start.3 = (bf16[512,256]{1,0:T(8,128)(2,1)S(1)}, bf16[512,256]{1,0:T(8,128)(2,1)S(1)}, u32[]{:S(2)}, u32[]{:S(2)}) collective-permute-start(bf16[512,256]{1,0:T(8,128)(2,1)S(1)} %add_convert_fusion.5), channel_id=1, source_target_pairs={{0,2},{1,3},{2,0},{3,1},{4,6},{5,7},{6,4},{7,5},{8,10},{9,11},{10,... | collective-permute-start | bytes 786440 | tf_op jit(solution)/shard_map/ppermute | solution.py:160
  57.1 7.6 %collective-permute-start.5 = (bf16[512,256]{1,0:T(8,128)(2,1)S(1)}, bf16[512,256]{1,0:T(8,128)(2,1)S(1)}, u32[]{:S(2)}, u32[]{:S(2)}) collective-permute-start(bf16[512,256]{1,0:T(8,128)(2,1)S(1)} %add_convert_fusion.3), channel_id=1, source_target_pairs={{0,1},{1,0},{2,3},{3,2},{4,5},{5,4},{6,7},{7,6},{8,9},{9,8},{10,11... | collective-permute-start | bytes 786440 | tf_op jit(solution)/shard_map/ppermute | solution.py:160
  79.3 2.7 copy-start.6
  82.0 15.1 %collective-permute-start.10 = (bf16[4,688,256]{2,1,0:T(8,128)(2,1)}, bf16[4,688,256]{2,1,0:T(8,128)(2,1)}, u32[]{:S(2)}, u32[]{:S(2)}) collective-permute-start(bf16[4,688,256]{2,1,0:T(8,128)(2,1)} %dynamic-slice_bitcast_fusion.6), channel_id=1, source_target_pairs={{0,4},{4,0},{8,12},{12,8},{16,20},{20,16},{24,28},{28,24},{1,5},{5... | collective-permute-start | bytes 4227080 | tf_op jit(solution)/shard_map/ppermute | solution.py:163
  83.0 145.7 %all-gather.7.cloned.1.call-start = ((), (), s32[]{:S(2)}) async-start(), calls=%async_computation.1 | async-start | bytes 1761280 | tf_op jit(solution)/shard_map/all_gather | solution.py:242
  83.1 12.8 %collective-permute-start.9 = (bf16[688,256]{1,0:T(8,128)(2,1)S(1)}, bf16[688,256]{1,0:T(8,128)(2,1)}, u32[]{:S(2)}, u32[]{:S(2)}) collective-permute-start(bf16[688,256]{1,0:T(8,128)(2,1)S(1)} %fusion.41), channel_id=1, source_target_pairs={{0,8},{4,12},{8,16},{12,20},{16,24},{20,28},{24,0},{28,4},{1,9},{5... | collective-permute-start | bytes 1056776 | tf_op jit(solution)/shard_map/ppermute | solution.py:166
  162.3 1.5 copy-start.2
  165.0 21.6 %collective-permute-start.13 = (bf16[4,688,256]{2,1,0:T(8,128)(2,1)}, bf16[4,688,256]{2,1,0:T(8,128)(2,1)}, u32[]{:S(2)}, u32[]{:S(2)}) collective-permute-start(bf16[4,688,256]{2,1,0:T(8,128)(2,1)} %dynamic-slice_bitcast_fusion.5), channel_id=1, source_target_pairs={{0,4},{4,0},{8,12},{12,8},{16,20},{20,16},{24,28},{28,24},{1,5},{5... | collective-permute-start | bytes 4227080 | tf_op jit(solution)/shard_map/ppermute | solution.py:163
  165.0 4.8 %copy-start = (bf16[4,2,688,256]{3,2,1,0:T(8,128)(2,1)S(1)}, bf16[4,2,688,256]{3,2,1,0:T(8,128)(2,1)}, u32[]{:S(2)}) copy-start(bf16[4,2,688,256]{3,2,1,0:T(8,128)(2,1)} %get-tuple-element.55) | copy-start | bytes 8454148
  165.0 12.8 %collective-permute-start.12 = (bf16[688,256]{1,0:T(8,128)(2,1)S(1)}, bf16[688,256]{1,0:T(8,128)(2,1)S(1)}, u32[]{:S(2)}, u32[]{:S(2)}) collective-permute-start(bf16[688,256]{1,0:T(8,128)(2,1)S(1)} %fusion.40), channel_id=1, source_target_pairs={{0,8},{4,12},{8,16},{12,20},{16,24},{20,28},{24,0},{28,4},{1,9},{5... | collective-permute-start | bytes 1056776 | tf_op jit(solution)/shard_map/ppermute | solution.py:166
  168.3 17.1 %collective-permute-start.11 = (bf16[688,256]{1,0:T(8,128)(2,1)S(1)}, bf16[688,256]{1,0:T(8,128)(2,1)S(1)}, u32[]{:S(2)}, u32[]{:S(2)}) collective-permute-start(bf16[688,256]{1,0:T(8,128)(2,1)S(1)} %fusion.39), channel_id=1, source_target_pairs={{0,8},{4,12},{8,16},{12,20},{16,24},{20,28},{24,0},{28,4},{1,9},{5... | collective-permute-start | bytes 1056776 | tf_op jit(solution)/shard_map/ppermute | solution.py:166
  178.9 13.6 %collective-permute-start.16 = (bf16[688,256]{1,0:T(8,128)(2,1)S(1)}, bf16[688,256]{1,0:T(8,128)(2,1)S(1)}, u32[]{:S(2)}, u32[]{:S(2)}) collective-permute-start(bf16[688,256]{1,0:T(8,128)(2,1)S(1)} %fusion.38), channel_id=1, source_target_pairs={{0,8},{4,12},{8,16},{12,20},{16,24},{20,28},{24,0},{28,4},{1,9},{5... | collective-permute-start | bytes 1056776 | tf_op jit(solution)/shard_map/ppermute | solution.py:166
  192.5 0.7 copy-start.14
  196.8 4.0 %copy-start.1 = (bf16[4,2,688,256]{3,2,1,0:T(8,128)(2,1)S(1)}, bf16[4,2,688,256]{3,2,1,0:T(8,128)(2,1)}, u32[]{:S(2)}) copy-start(bf16[4,2,688,256]{3,2,1,0:T(8,128)(2,1)} %get-tuple-element.55) | copy-start | bytes 8454148
  196.8 63.0 %all-gather.9.cloned.1.call-start = ((), (), s32[]{:S(2)}) async-start(), calls=%async_computation.2 | async-start | bytes 1761280 | tf_op jit(solution)/shard_map/all_gather | solution.py:242
  196.9 21.7 %collective-permute-start.17 = (bf16[4,688,256]{2,1,0:T(8,128)(2,1)}, bf16[4,688,256]{2,1,0:T(8,128)(2,1)S(1)}, u32[]{:S(2)}, u32[]{:S(2)}) collective-permute-start(bf16[4,688,256]{2,1,0:T(8,128)(2,1)} %dynamic-slice_bitcast_fusion.4), channel_id=1, source_target_pairs={{0,4},{4,0},{8,12},{12,8},{16,20},{20,16},{24,28},{28,24},{1,5},{5... | collective-permute-start | bytes 4227080 | tf_op jit(solution)/shard_map/ppermute | solution.py:163
  196.9 12.9 %collective-permute-start.15 = (bf16[688,256]{1,0:T(8,128)(2,1)S(1)}, bf16[688,256]{1,0:T(8,128)(2,1)S(1)}, u32[]{:S(2)}, u32[]{:S(2)}) collective-permute-start(bf16[688,256]{1,0:T(8,128)(2,1)S(1)} %fusion.37), channel_id=1, source_target_pairs={{0,8},{4,12},{8,16},{12,20},{16,24},{20,28},{24,0},{28,4},{1,9},{5... | collective-permute-start | bytes 1056776 | tf_op jit(solution)/shard_map/ppermute | solution.py:166
  199.8 17.6 %collective-permute-start.14 = (bf16[688,256]{1,0:T(8,128)(2,1)S(1)}, bf16[688,256]{1,0:T(8,128)(2,1)S(1)}, u32[]{:S(2)}, u32[]{:S(2)}) collective-permute-start(bf16[688,256]{1,0:T(8,128)(2,1)S(1)} %fusion.36), channel_id=1, source_target_pairs={{0,8},{4,12},{8,16},{12,20},{16,24},{20,28},{24,0},{28,4},{1,9},{5... | collective-permute-start | bytes 1056776 | tf_op jit(solution)/shard_map/ppermute | solution.py:166
  211.1 13.4 %collective-permute-start.20 = (bf16[688,256]{1,0:T(8,128)(2,1)S(1)}, bf16[688,256]{1,0:T(8,128)(2,1)S(1)}, u32[]{:S(2)}, u32[]{:S(2)}) collective-permute-start(bf16[688,256]{1,0:T(8,128)(2,1)S(1)} %fusion.35), channel_id=1, source_target_pairs={{0,8},{4,12},{8,16},{12,20},{16,24},{20,28},{24,0},{28,4},{1,9},{5... | collective-permute-start | bytes 1056776 | tf_op jit(solution)/shard_map/ppermute | solution.py:166
  218.6 1.1 copy-start.3
  224.5 0.7 copy-start.10
  228.8 66.1 %all-gather.11.cloned.1.call-start = ((), (), s32[]{:S(2)}) async-start(), calls=%async_computation.3 | async-start | bytes 1761280 | tf_op jit(solution)/shard_map/all_gather | solution.py:242
  228.8 13.0 %collective-permute-start.19 = (bf16[688,256]{1,0:T(8,128)(2,1)S(1)}, bf16[688,256]{1,0:T(8,128)(2,1)S(1)}, u32[]{:S(2)}, u32[]{:S(2)}) collective-permute-start(bf16[688,256]{1,0:T(8,128)(2,1)S(1)} %fusion.34), channel_id=1, source_target_pairs={{0,8},{4,12},{8,16},{12,20},{16,24},{20,28},{24,0},{28,4},{1,9},{5... | collective-permute-start | bytes 1056776 | tf_op jit(solution)/shard_map/ppermute | solution.py:166
  228.9 20.5 %collective-permute-start.18 = (bf16[688,256]{1,0:T(8,128)(2,1)S(1)}, bf16[688,256]{1,0:T(8,128)(2,1)S(1)}, u32[]{:S(2)}, u32[]{:S(2)}) collective-permute-start(bf16[688,256]{1,0:T(8,128)(2,1)S(1)} %fusion.33), channel_id=1, source_target_pairs={{0,8},{4,12},{8,16},{12,20},{16,24},{20,28},{24,0},{28,4},{1,9},{5... | collective-permute-start | bytes 1056776 | tf_op jit(solution)/shard_map/ppermute | solution.py:166
  243.1 12.5 %collective-permute-start.22 = (bf16[688,256]{1,0:T(8,128)(2,1)S(1)}, bf16[688,256]{1,0:T(8,128)(2,1)S(1)}, u32[]{:S(2)}, u32[]{:S(2)}) collective-permute-start(bf16[688,256]{1,0:T(8,128)(2,1)S(1)} %fusion.32), channel_id=1, source_target_pairs={{0,8},{4,12},{8,16},{12,20},{16,24},{20,28},{24,0},{28,4},{1,9},{5... | collective-permute-start | bytes 1056776 | tf_op jit(solution)/shard_map/ppermute | solution.py:166
  255.6 0.7 copy-start.11
  259.8 10.8 %collective-permute-start.21 = (bf16[688,256]{1,0:T(8,128)(2,1)S(1)}, bf16[688,256]{1,0:T(8,128)(2,1)S(1)}, u32[]{:S(2)}, u32[]{:S(2)}) collective-permute-start(bf16[688,256]{1,0:T(8,128)(2,1)S(1)} %fusion.31), channel_id=1, source_target_pairs={{0,8},{4,12},{8,16},{12,20},{16,24},{20,28},{24,0},{28,4},{1,9},{5... | collective-permute-start | bytes 1056776 | tf_op jit(solution)/shard_map/ppermute | solution.py:166
  271.7 10.1 %collective-permute-start.23 = (bf16[688,256]{1,0:T(8,128)(2,1)S(1)}, bf16[688,256]{1,0:T(8,128)(2,1)S(1)}, u32[]{:S(2)}, u32[]{:S(2)}) collective-permute-start(bf16[688,256]{1,0:T(8,128)(2,1)S(1)} %fusion.30), channel_id=1, source_target_pairs={{0,8},{4,12},{8,16},{12,20},{16,24},{20,28},{24,0},{28,4},{1,9},{5... | collective-permute-start | bytes 1056776 | tf_op jit(solution)/shard_map/ppermute | solution.py:166
  281.8 0.7 copy-start.13
  286.1 16.3 %collective-permute-start.26 = (bf16[688,256]{1,0:T(8,128)(2,1)}, bf16[688,256]{1,0:T(8,128)(2,1)S(1)}, u32[]{:S(2)}, u32[]{:S(2)}) collective-permute-start(bf16[688,256]{1,0:T(8,128)(2,1)} %get-tuple-element.78.last_ref), channel_id=1, source_target_pairs={{0,1},{1,0},{2,3},{3,2},{4,5},{5,4},{6,7},{7,6},{8,9},{9,8},{10,11... | collective-permute-start | bytes 1056776 | tf_op jit(solution)/shard_map/ppermute | solution.py:160
  287.5 5.4 %copy-start.7 = (bf16[688,256]{1,0:T(8,128)(2,1)S(1)}, bf16[688,256]{1,0:T(8,128)(2,1)}, u32[]{:S(2)}) copy-start(bf16[688,256]{1,0:T(8,128)(2,1)} %get-tuple-element.78.last_ref) | copy-start | bytes 1056772
  292.9 17.7 %collective-permute-start.25 = (bf16[688,256]{1,0:T(8,128)(2,1)S(1)}, bf16[688,256]{1,0:T(8,128)(2,1)S(1)}, u32[]{:S(2)}, u32[]{:S(2)}) collective-permute-start(bf16[688,256]{1,0:T(8,128)(2,1)S(1)} %copy-done.7), channel_id=1, source_target_pairs={{0,2},{1,3},{2,0},{3,1},{4,6},{5,7},{6,4},{7,5},{8,10},{9,11},{10,... | collective-permute-start | bytes 1056776 | tf_op jit(solution)/shard_map/ppermute | solution.py:160
  293.4 25.3 %collective-permute-start.24 = (bf16[688,256]{1,0:T(8,128)(2,1)S(1)}, bf16[688,256]{1,0:T(8,128)(2,1)S(1)}, u32[]{:S(2)}, u32[]{:S(2)}) collective-permute-start(bf16[688,256]{1,0:T(8,128)(2,1)S(1)} %copy-done.7), channel_id=1, source_target_pairs={{0,3},{1,2},{2,1},{3,0},{4,7},{5,6},{6,5},{7,4},{8,11},{9,10},{10,... | collective-permute-start | bytes 1056776 | tf_op jit(solution)/shard_map/ppermute | solution.py:160
  302.4 0.7 copy-start.8
  310.5 0.7 copy-start.12
  318.7 0.7 copy-start.9
Sparse Core Ops, SparseCore 0:
  83.2 53.7 all-reduce.1
  196.9 27.8 all-gather.6
  228.9 27.3 all-gather.8
  260.0 28.4 all-gather.10

commit v3 on v0

v3 whole, which is shorter than its diff:
```python
import functools

import jax
import jax.numpy as jnp
from jax import lax
from jax.experimental import pallas as pl
from jax.experimental.pallas import tpu as pltpu
from jax.sharding import PartitionSpec as P

beta_first = 0.9
beta_second = 0.999
adam_count = 100.0
epsilon = 1e-08

F32 = jnp.float32
BF16 = jnp.bfloat16
VMEM_LIMIT = 56 * 1024 * 1024
COST = pl.CostEstimate(flops=1024, bytes_accessed=1024, transcendentals=0)
PARAMS = pltpu.CompilerParams(vmem_limit_bytes=VMEM_LIMIT)


def transpose(value, block):
    rows, columns = value.shape

    def kernel(value_ref, out_ref):
        out_ref[...] = value_ref[...].T

    return pl.pallas_call(
        kernel,
        out_shape=jax.ShapeDtypeStruct((columns, rows), value.dtype),
        grid=(rows // block,),
        in_specs=[pl.BlockSpec((block, columns), lambda i: (i, 0))],
        out_specs=pl.BlockSpec((columns, block), lambda i: (0, i)),
        compiler_params=PARAMS,
        cost_estimate=COST,
        name="transpose",
    )(value)


def project(features, basis, begin, width):
    tokens, depth = features.shape
    rows = tokens // 4
    blocks = basis.shape[1] // begin

    def kernel(features_ref, *refs):
        basis_refs, (low_ref, high_ref) = refs[:-2], refs[-2:]
        for index, basis_ref in enumerate(basis_refs):
            value = jnp.dot(features_ref[...], basis_ref[...], preferred_element_type=F32).astype(BF16)
            columns = slice(index * begin, (index + 1) * begin)

            @pl.when(pl.program_id(0) < 2)
            def _():
                low_ref[:, columns] = value

            @pl.when(pl.program_id(0) >= 2)
            def _():
                high_ref[:, columns] = value

    return pl.pallas_call(
        kernel,
        out_shape=[jax.ShapeDtypeStruct((tokens // 2, width), BF16)] * 2,
        grid=(4,),
        in_specs=[pl.BlockSpec((rows, depth), lambda i: (i, 0))]
        + [pl.BlockSpec((depth, begin), functools.partial(lambda at, i: (0, at), at)) for at in range(1, blocks)],
        out_specs=[
            pl.BlockSpec((rows, width), lambda i: (jnp.minimum(i, 1), 0)),
            pl.BlockSpec((rows, width), lambda i: (jnp.maximum(i - 2, 0), 0)),
        ],
        compiler_params=PARAMS,
        cost_estimate=COST,
        name="project",
    )(features, *[basis] * (blocks - 1))


def gradient(grads_t, halves, owners, widths):
    _, owned, tokens = grads_t.shape
    rows, width = halves[0].shape
    count = owners.shape[0]

    def kernel(owners_ref, grads_ref, low_ref, high_ref, *refs):
        out_refs, whole_ref = refs[:-1], refs[-1]

        @pl.when(pl.program_id(0) == 0)
        def _():
            whole_ref[:rows, :] = low_ref[...]
            whole_ref[rows:, :] = high_ref[...]

        value = jnp.dot(grads_ref[0], whole_ref[...], preferred_element_type=F32).astype(BF16)
        begin = 0
        for out_ref, size in zip(out_refs, widths):
            out_ref[0] = value[:, begin : begin + size]
            begin += size

    return pl.pallas_call(
        kernel,
        out_shape=[jax.ShapeDtypeStruct((count, owned, size), BF16) for size in widths],
        grid_spec=pltpu.PrefetchScalarGridSpec(
            num_scalar_prefetch=1,
            grid=(count,),
            in_specs=[pl.BlockSpec((1, owned, tokens), lambda i, owners_ref: (owners_ref[i], 0, 0))]
            + [pl.BlockSpec((rows, width), lambda i, owners_ref: (0, 0))] * 2,
            out_specs=[pl.BlockSpec((1, owned, size), lambda i, owners_ref: (i, 0, 0)) for size in widths],
            scratch_shapes=[pltpu.VMEM((tokens, width), BF16)],
        ),
        compiler_params=PARAMS,
        cost_estimate=COST,
        name="gradient",
    )(owners, grads_t, *halves)


def accumulate(arrived, own, coming, hop):
    _, owned, width = own.shape

    def kernel(*refs):
        out_ref = refs[-1]
        total = refs[0][0].astype(F32) + refs[1][0].astype(F32)
        if arrived:
            total = total + refs[2][...].astype(F32)
        out_ref[...] = total.astype(BF16)

    block = pl.BlockSpec((1, owned, width), lambda i: (hop, 0, 0))
    return pl.pallas_call(
        kernel,
        grid=(1,),
        out_shape=jax.ShapeDtypeStruct((owned, width), BF16),
        in_specs=[block, block] + [pl.BlockSpec(memory_space=pltpu.VMEM)] * len(arrived),
        out_specs=pl.BlockSpec(memory_space=pltpu.VMEM),
        compiler_params=PARAMS,
        cost_estimate=COST,
        name="accumulate",
    )(own, coming, *arrived)


def adam(pieces, first, second, held, begin):
    owned, rank = first.shape
    widths = [piece[0].shape[1] for piece in pieces]
    width = sum(widths)
    last = pieces[0][1].shape[0] - 1

    def kernel(*refs):
        first_ref, second_ref = refs[3 * len(pieces) : 3 * len(pieces) + 2]
        first_out, second_out, direction_out = refs[-3:]
        at = 0
        for index, size in enumerate(widths):
            arrived_ref, own_ref, other_ref = refs[3 * index : 3 * index + 3]
            columns = slice(at, at + size)
            at += size
            grad_low = arrived_ref[...].astype(F32) + own_ref[0].astype(F32) + other_ref[0].astype(F32)
            first_next = beta_first * first_ref[:, columns] + (1.0 - beta_first) * grad_low
            second_next = beta_second * second_ref[:, columns] + (1.0 - beta_second) * grad_low * grad_low
            first_out[:, columns] = first_next
            second_out[:, columns] = second_next
            bias_first = 1.0 - beta_first**adam_count
            bias_second = 1.0 - beta_second**adam_count
            direction = first_next / bias_first / (jnp.sqrt(second_next / bias_second) + epsilon)
            direction_out[:, columns] = direction.astype(BF16)

    column = pl.BlockSpec((owned, width), lambda i: (0, begin // width))
    piece_specs = []
    for size in widths:
        piece_specs += [pl.BlockSpec(memory_space=pltpu.VMEM)]
        piece_specs += [pl.BlockSpec((1, owned, size), lambda i: (last, 0, 0))] * 2
    inputs = len(piece_specs) + 2
    return pl.pallas_call(
        kernel,
        grid=(1,),
        out_shape=[
            jax.ShapeDtypeStruct((owned, rank), F32),
            jax.ShapeDtypeStruct((owned, rank), F32),
            jax.ShapeDtypeStruct((owned, width), BF16),
        ],
        in_specs=piece_specs + [column, column] + [pl.BlockSpec(memory_space=pl.ANY)] * len(held),
        out_specs=[column, column, pl.BlockSpec((owned, width), lambda i: (0, 0))],
        input_output_aliases={inputs + index: index for index in range(len(held))},
        compiler_params=PARAMS,
        cost_estimate=COST,
        name="adam",
    )(*[array for piece in pieces for array in piece], first, second, *held)


def expand(target, directions, basis_t, held, count):
    owned, width = directions[0].shape
    rank, features = basis_t.shape
    block = min(1024, features)

    def kernel(target_ref, basis_ref, *refs):
        direction_refs, out_ref, whole_ref = refs[: len(directions)], refs[-2], refs[-1]

        @pl.when(pl.program_id(0) == 0)
        def _():
            for index, direction_ref in enumerate(direction_refs):
                whole_ref[:, index * width : (index + 1) * width] = direction_ref[...]

        out_ref[0] = jnp.dot(whole_ref[...], basis_ref[...], preferred_element_type=F32)

    return pl.pallas_call(
        kernel,
        out_shape=jax.ShapeDtypeStruct((count, owned, features), F32),
        grid_spec=pltpu.PrefetchScalarGridSpec(
            num_scalar_prefetch=1,
            grid=(features // block,),
            in_specs=[pl.BlockSpec((rank, block), lambda i, target_ref: (0, i))]
            + [pl.BlockSpec((owned, width), lambda i, target_ref: (0, 0))] * len(directions)
            + [pl.BlockSpec(memory_space=pl.ANY)] * len(held),
            out_specs=pl.BlockSpec((1, owned, block), lambda i, target_ref: (target_ref[0], 0, i)),
            scratch_shapes=[pltpu.VMEM((owned, rank), BF16)],
        ),
        input_output_aliases={2 + len(directions): 0} if held else {},
        compiler_params=PARAMS,
        cost_estimate=COST,
        name="expand",
    )(target, basis_t, *directions, *held)


def total_of(*terms):
    total = terms[0].astype(F32)
    for term in terms[1:]:
        total = total + term.astype(F32)
    return total.astype(BF16)


def after(value, *earlier):
    return lax.optimization_barrier((value, *earlier))[0]


def local(activations, out_grads, projector, first_moment, second_moment):
    owned = first_moment.shape[1]
    features = activations[0]
    basis = projector[0]
    rank = basis.shape[1]
    tokens = features.shape[0]
    dp_count, fsdp_count = lax.axis_size("dp"), lax.axis_size("fsdp")
    dp, fsdp = lax.axis_index("dp"), lax.axis_index("fsdp")
    chips = dp_count // 2
    chip, core = dp // 2, dp % 2
    width = rank // 4

    offsets = [1 << bit for bit in range(fsdp_count.bit_length() - 1)]
    order = jnp.stack([fsdp ^ offset for offset in range(fsdp_count)]).astype(jnp.int32)
    hops = chips - 1
    ring_order = (chip - 1 - jnp.arange(chips, dtype=jnp.int32) + chips) % chips
    own_owners = (ring_order * 2 + core).astype(jnp.int32)
    other_owners = (ring_order * 2 + 1 - core).astype(jnp.int32)

    def across(value, offset):
        return lax.ppermute(value, "fsdp", [(index, index ^ offset) for index in range(fsdp_count)])

    def sibling(value):
        return lax.ppermute(value, "dp", [(index, index ^ 1) for index in range(dp_count)])

    def onward(value):
        return lax.ppermute(value, "dp", [(index, (index + 2) % dp_count) for index in range(dp_count)])

    def exchange(halves, step):
        return [across(half, steps[step]) for half, steps in zip(halves, (offsets, offsets[::-1]))]

    def add(halves, arrived):
        return [total_of(half, term) for half, term in zip(halves, arrived)]

    early = jnp.dot(features, basis[:, :width], preferred_element_type=F32).astype(BF16)
    sums_0 = [early[: tokens // 2], early[tokens // 2 :]]
    coming_0 = exchange(sums_0, 0)
    sums_1 = project(after(features, early), basis, width, rank - width)
    sums_0 = add(sums_0, [after(term, *sums_1) for term in coming_0])
    for step in range(1, len(offsets) - 1):
        sums_0 = add(sums_0, exchange(sums_0, step))
    coming_0 = exchange(sums_0, len(offsets) - 1)
    sums_1 = [after(half, *sums_0) for half in sums_1]
    coming_1 = exchange(sums_1, 0)
    grads_t = transpose(after(out_grads[0], *sums_0), min(256, tokens)).reshape(dp_count, owned, tokens)
    sums_0 = add(sums_0, [after(term, grads_t) for term in coming_0])

    def blocks_of(grads_t, sums, widths, between=lambda token: []):
        other = gradient(grads_t, sums, other_owners, widths)
        coming = [sibling(value) for value in other]
        own = gradient(after(grads_t, *other, *between(other[0])), sums, own_owners, widths)
        return own, coming

    def ring(parts, stride, token, between, finish):
        events = sorted(
            (2 * hop + stride * part, part, hop) for part in range(len(parts)) for hop in range(hops + 1)
        )
        arrived = [None] * len(parts)
        for number, (_, part, hop) in enumerate(events):
            own, coming = parts[part]
            if hop < hops:
                before = () if arrived[part] is None else (arrived[part],)
                token = accumulate(before, after(own, token), coming, hop)
                arrived[part] = onward(token)
            else:
                token = finish(part, after(arrived[part], token), token)
            if number in between:
                token = between[number](token, arrived)
        return token

    held = ()
    directions = []

    def step_of(pieces, begin):
        nonlocal held
        first_next, second_next, direction = adam(pieces, first_moment[0], second_moment[0], held, begin)
        held = (first_next, second_next)
        directions.append([direction] + [across(direction, offset) for offset in range(1, fsdp_count)])
        return direction

    rest = {}
    waiting = []

    def middle(token):
        sums = add(sums_1, [after(term, token) for term in coming_1])
        for step in range(1, len(offsets)):
            coming = exchange(sums, step)
            if step == len(offsets) - 1:
                rest["sums"], rest["coming"] = sums, coming
            else:
                sums = add(sums, coming)
        return sums

    own, coming = blocks_of(grads_t, sums_0, [width // 2] * 2, middle)
    parts_0 = list(zip(own, coming))

    def finish_0(part, arrived, token):
        waiting.append((arrived, *parts_0[part]))
        return step_of(waiting, 0) if len(waiting) == len(parts_0) else token

    def last(token, arrived):
        basis_t = transpose(after(basis, token), min(512, basis.shape[0]))
        sums = add(rest["sums"], [after(term, basis_t, *arrived) for term in rest["coming"]])
        rest["basis_t"] = basis_t
        own, coming = blocks_of(grads_t, sums, [width] * 3)
        rest["parts"] = list(zip(own, coming))
        return own[0]

    final_send = 2 * hops - 1
    token = ring(parts_0, 1, own[0], {final_send: last}, finish_0)
    parts_1 = rest["parts"]

    def finish_1(part, arrived, token):
        if part in (0, 2):
            arrived = after(arrived, *directions[part // 2])
        return step_of([(arrived, *parts_1[part])], (part + 1) * width)

    ring(parts_1, 1.5, token, {}, finish_1)

    directions[-1][0] = after(directions[-1][0], *directions[-2])
    update = ()
    for offset in range(fsdp_count):
        update = (
            expand(
                order[offset : offset + 1],
                [gathered[offset] for gathered in directions],
                rest["basis_t"],
                update,
                fsdp_count,
            ),
        )
    return (update[0][None], held[0][None], held[1][None])


def solution(mesh):
    in_specs = (
        P(None, "dp", "fsdp"),
        P(None, "dp", "fsdp"),
        P(None, "fsdp", None),
        P(None, ("fsdp", "dp"), None),
        P(None, ("fsdp", "dp"), None),
    )
    out_specs = (
        P(None, None, "dp", "fsdp"),
        P(None, ("fsdp", "dp"), None),
        P(None, ("fsdp", "dp"), None),
    )
    return jax.shard_map(local, mesh=mesh, in_specs=in_specs, out_specs=out_specs, check_vma=False)
```

time: 344 us -> 244 us (0.71)
  waiting for transfers between devices: 239 us -> 64.5 us
  Pallas kernels: 0 us -> 126 us
  matrix products: 48.2 us -> 3.73 us
  starting transfers between devices: 0.3 us -> 27.7 us
  local copies, waits for them, and re-layouts: 33.8 us -> 15.4 us
  between operations: 13.7 us -> 0.85 us
    pallas_call x0 -> x30, Pallas kernels: none -> 126 us  [the longest x4 30.5 us: gradient(): pl.pallas_call(kernel, out_shape=[jax.ShapeDtypeStruct((count, owned, siz...]
    unnamed x4 -> x0, waiting for transfers between devices: 109 us -> none
    psum x1 -> x0, waiting for transfers between devices: 72.4 us -> none  [local(): projected = lax.psum(partial_value.astype(jnp.bfloat16), 'fsdp')]
    ppermute x0 -> x40, waiting for transfers between devices: none -> 64.5 us  [the longest x15 46.6 us: onward(): lax.ppermute(value, 'dp', [(index, (index + 2) % dp_count) for index in r...]
    all_gather x1 -> x0, waiting for transfers between devices: 57.6 us -> none  [local(): lax.all_gather(direction, 'fsdp', axis=0, tiled=True)]
    dot_general x3 -> x1, matrix products: 48.2 us -> 3.73 us  [local(): jnp.dot(features, basis[:, :width], preferred_element_type=F32).astype(BF16)]
    ppermute x0 -> x40, starting transfers between devices: none -> 27.7 us  [the longest x20 21.2 us: across(): lax.ppermute(value, 'fsdp', [(index, index ^ offset) for index in range(f...]
    unnamed x8 -> x72, local copies, waits for them, and re-layouts: 31.2 us -> 15.4 us
  transfers between devices with their start and end apart: 3 -> 40, of which waited for: 3 -> 22; matrix products, arithmetic and copies ran while one was open for 3% -> 1% of each run, Pallas kernels for 0% -> 45%
where the time goes in v3:
time: 244 us; the launch traced here: 243 us
  Pallas kernels  126 us (52%)
  waiting for transfers between devices  64.5 us (26%)
  starting transfers between devices  27.7 us (11%)
  local copies, waits for them, and re-layouts  15.4 us (6%)
  other arithmetic  4.78 us (2%)
  matrix products  3.73 us (2%)
    ppermute x15, waiting for transfers between devices, onward(): lax.ppermute(value, 'dp', [(index, (index + 2) % dp_count) for index in r...  46.6 us
    pallas_call x4, Pallas kernels, gradient(): pl.pallas_call(kernel, out_shape=[jax.ShapeDtypeStruct((count, owned, siz...  30.5 us
    pallas_call x15, Pallas kernels, accumulate(): pl.pallas_call(kernel, grid=(1,), out_shape=jax.ShapeDtypeStruct((owned,...  28.9 us
    pallas_call x4, Pallas kernels, expand(): pl.pallas_call(kernel, out_shape=jax.ShapeDtypeStruct((count, owned, feat...  28 us
    ppermute x20, starting transfers between devices, across(): lax.ppermute(value, 'fsdp', [(index, index ^ offset) for index in range(f...  21.2 us
    ppermute x20, waiting for transfers between devices, across(): lax.ppermute(value, 'fsdp', [(index, index ^ offset) for index in range(f...  17.8 us
    unnamed x72, local copies, waits for them, and re-layouts  15.4 us
    pallas_call x2, Pallas kernels, transpose(): pl.pallas_call(kernel, out_shape=jax.ShapeDtypeStruct((columns, rows), va...  14.9 us
  transfers between devices with their start and end apart: 40, of which 22 were waited for; matrix products, arithmetic and copies ran while one was open for 1% of the time, Pallas kernels for 45%

profile of v3, /device:TPU:0, one launch (start us, length us, event | category | flops | bytes accessed | tf_op | source)
XLA Modules:
  0.0 243.2 jit_solution(486523725541544090)
XLA Ops:
  0.6 3.7 %convolution_convert_fusion = bf16[1024,256]{1,0:T(8,128)(2,1)S(1)} fusion(bf16[2048,1024]{1,0:T(8,128)(2,1)} %bitcast.20, bf16[1,1024,2048]{2,1,0:T(8,128)(2,1)} %param.5), kind=kOutput, calls=%fused_computation.4 | convolution fusion | flops 1074003968 | bytes 5767168 | tf_op jit(solution)/shard_map/dot_general | solution.py:260
  4.4 3.0 %collective-permute-start = (bf16[512,256]{1,0:T(8,128)(2,1)S(1)}, bf16[512,256]{1,0:T(8,128)(2,1)S(1)}, u32[]{:S(2)}, u32[]{:S(2)}) collective-permute-start(bf16[512,256]{1,0:T(8,128)(2,1)S(1)} %get-tuple-element.130), channel_id=1, source_target_pairs={{0,1},{1,0},{2,3},{3,2},{4,5},{5,4},{6,7},{7,6},{8,9},{9,8},{10,11... | collective-permute-start | bytes 786440 | tf_op jit(solution)/shard_map/ppermute | solution.py:246
  7.4 1.5 collective-permute-start.1
  8.9 10.7 %project.1 = (bf16[512,768]{1,0:T(8,128)(2,1)}, bf16[512,768]{1,0:T(8,128)(2,1)}) custom-call(bf16[1024,2048]{1,0:T(8,128)(2,1)} %bitcast.36, bf16[2048,1024]{1,0:T(8,128)(2,1)} %bitcast.21, bf16[2048,1024]{1,0:T(8,128)(2,1)} %bitcast.22, bf16[2048,1024]{1,0:T(8,128)(2,1)} %bitcast.23), custom_call_target="tpu_custom_call" | custom-call | flops 1024 | bytes 1024 | tf_op jit(solution)/shard_map/project/pallas_call | solution.py:59
  20.4 2.0 collective-permute-start.5
  22.4 1.5 collective-permute-start.4
  24.5 9.7 %transpose.4 = bf16[5504,1024]{1,0:T(8,128)(2,1)} custom-call(bf16[1024,5504]{1,0:T(8,128)(2,1)} %bitcast.35), custom_call_target="tpu_custom_call" | custom-call | flops 1024 | bytes 1024 | tf_op jit(solution)/shard_map/transpose/pallas_call | solution.py:28
  35.7 6.3 %gradient.4 = (bf16[4,688,128]{2,1,0:T(8,128)(2,1)}, bf16[4,688,128]{2,1,0:T(8,128)(2,1)}) custom-call(s32[4]{0:T(128)} %get-tuple-element.131.owners_ref, bf16[8,688,1024]{2,1,0:T(8,128)(2,1)} %bitcast.16, bf16[512,256]{1,0:T(8,128)(2,1)} %add_convert_fusion.5.low_ref, bf16[512,256]{1,0:T(8,128)(2,1)} %add_convert_fusion.4.high_ref), custom_call_target="tpu_custom_call" | custom-call | flops 1024 | bytes 1024 | tf_op jit(solution)/shard_map/gradient/pallas_call | solution.py:94
  42.5 1.8 collective-permute-done.5
  44.6 1.6 collective-permute-start.15
  46.3 6.2 %gradient.5 = (bf16[4,688,128]{2,1,0:T(8,128)(2,1)}, bf16[4,688,128]{2,1,0:T(8,128)(2,1)}) custom-call(s32[4]{0:T(128)} %get-tuple-element.132.owners_ref, bf16[8,688,1024]{2,1,0:T(8,128)(2,1)} %bitcast.17, bf16[512,256]{1,0:T(8,128)(2,1)} %add_convert_fusion.5.low_ref, bf16[512,256]{1,0:T(8,128)(2,1)} %add_convert_fusion.4.high_ref), custom_call_target="tpu_custom_call" | custom-call | flops 1024 | bytes 1024 | tf_op jit(solution)/shard_map/gradient/pallas_call | solution.py:94
  53.4 1.7 accumulate.15
  55.1 1.6 collective-permute-start.8
  57.5 1.7 accumulate.16
  59.2 1.6 collective-permute-start.9
  61.3 2.4 collective-permute-done.8.refs_2_
  64.4 1.8 accumulate.17
  67.7 1.8 accumulate.18
  70.3 4.8 %collective-permute-done.10.refs_2_ = bf16[688,128]{1,0:T(8,128)(2,1)S(1)} collective-permute-done((bf16[688,128]{1,0:T(8,128)(2,1)}, bf16[688,128]{1,0:T(8,128)(2,1)S(1)}, u32[]{:S(2)}, u32[]{:S(2)}) %collective-permute-start.10) | collective-permute-done | bytes 176160 | tf_op jit(solution)/shard_map/ppermute | solution.py:252
  75.8 1.8 accumulate.19
  78.3 1.8 accumulate.20
  80.6 5.3 %transpose.5.basis_ref = bf16[1024,2048]{1,0:T(8,128)(2,1)} custom-call(bf16[2048,1024]{1,0:T(8,128)(2,1)} %bitcast.24), custom_call_target="tpu_custom_call" | custom-call | flops 1024 | bytes 1024 | tf_op jit(solution)/shard_map/transpose/pallas_call | solution.py:28
  85.8 1.8 collective-permute-done.14.refs_3_
  87.6 1.9 collective-permute-done.12.refs_0_
  89.5 1.1 add_convert_fusion.high_ref
  91.6 9.0 %gradient.6 = (bf16[4,688,256]{2,1,0:T(8,128)(2,1)}, bf16[4,688,256]{2,1,0:T(8,128)(2,1)}, bf16[4,688,256]{2,1,0:T(8,128)(2,1)}) custom-call(s32[4]{0:T(128)} %get-tuple-element.131.owners_ref, bf16[8,688,1024]{2,1,0:T(8,128)(2,1)} %bitcast.18, bf16[512,768]{1,0:T(8,128)(2,1)} %add_convert_fusion.1.low_ref, bf16[512,768]{1,0:T(8,128)(2,1)} %add_convert_fusion.high_ref), custom_call_target="tpu_custom_call" | custom-call | flops 1024 | bytes 1024 | tf_op jit(solution)/shard_map/gradient/pallas_call | solution.py:94
  101.3 9.0 %gradient.7 = (bf16[4,688,256]{2,1,0:T(8,128)(2,1)}, bf16[4,688,256]{2,1,0:T(8,128)(2,1)}, bf16[4,688,256]{2,1,0:T(8,128)(2,1)}) custom-call(s32[4]{0:T(128)} %get-tuple-element.132.owners_ref, bf16[8,688,1024]{2,1,0:T(8,128)(2,1)} %bitcast.19, bf16[512,768]{1,0:T(8,128)(2,1)} %add_convert_fusion.1.low_ref, bf16[512,768]{1,0:T(8,128)(2,1)} %add_convert_fusion.high_ref), custom_call_target="tpu_custom_call" | custom-call | flops 1024 | bytes 1024 | tf_op jit(solution)/shard_map/gradient/pallas_call | solution.py:94
  110.3 3.3 %adam.4 = (f32[688,1024]{1,0:T(8,128)}, f32[688,1024]{1,0:T(8,128)}, bf16[688,256]{1,0:T(8,128)(2,1)}) custom-call(bf16[688,128]{1,0:T(8,128)(2,1)} %copy-done.31, bf16[4,688,128]{2,1,0:T(8,128)(2,1)} %get-tuple-element.86.refs_0_.refs_1_, bf16[4,688,128]{2,1,0:T(8,128)(2,1)} %copy-done.3, bf16[688,128]{1,0:T(8,128)(2,1)} %copy-done.30, ...), custom_call_target="tpu_custom_call" | custom-call | flops 1024 | bytes 1024 | tf_op jit(solution)/shard_map/adam/pallas_call | solution.py:164
  113.6 1.1 copy-done.2
  114.7 1.9 accumulate.21
  116.6 1.1 copy-done.1
  117.7 1.9 accumulate.22
  120.5 9.2 %collective-permute-done.19.refs_2_ = bf16[688,256]{1,0:T(8,128)(2,1)S(1)} collective-permute-done((bf16[688,256]{1,0:T(8,128)(2,1)}, bf16[688,256]{1,0:T(8,128)(2,1)S(1)}, u32[]{:S(2)}, u32[]{:S(2)}) %collective-permute-start.19) | collective-permute-done | bytes 352288 | tf_op jit(solution)/shard_map/ppermute | solution.py:252
  130.4 2.1 accumulate.23
  132.5 1.1 copy-done
  133.6 1.9 accumulate.24
  135.6 1.6 collective-permute-done.21.refs_2_
  137.8 2.1 accumulate.25
  139.9 5.8 %collective-permute-done.22.refs_2_ = bf16[688,256]{1,0:T(8,128)(2,1)S(1)} collective-permute-done((bf16[688,256]{1,0:T(8,128)(2,1)}, bf16[688,256]{1,0:T(8,128)(2,1)S(1)}, u32[]{:S(2)}, u32[]{:S(2)}) %collective-permute-start.22) | collective-permute-done | bytes 352288 | tf_op jit(solution)/shard_map/ppermute | solution.py:252
  146.5 2.1 accumulate.26
  149.1 1.4 collective-permute-start.26
  150.5 2.8 %collective-permute-done.24.refs_2_ = bf16[688,256]{1,0:T(8,128)(2,1)S(1)} collective-permute-done((bf16[688,256]{1,0:T(8,128)(2,1)}, bf16[688,256]{1,0:T(8,128)(2,1)S(1)}, u32[]{:S(2)}, u32[]{:S(2)}) %collective-permute-start.24) | collective-permute-done | bytes 352288 | tf_op jit(solution)/shard_map/ppermute | solution.py:252
  154.0 2.1 accumulate.27
  156.1 4.7 %collective-permute-done.25.refs_2_ = bf16[688,256]{1,0:T(8,128)(2,1)S(1)} collective-permute-done((bf16[688,256]{1,0:T(8,128)(2,1)}, bf16[688,256]{1,0:T(8,128)(2,1)S(1)}, u32[]{:S(2)}, u32[]{:S(2)}) %collective-permute-start.25) | collective-permute-done | bytes 352288 | tf_op jit(solution)/shard_map/ppermute | solution.py:252
  161.5 2.1 accumulate.28
  163.6 4.8 %collective-permute-done.23.refs_0_ = bf16[688,256]{1,0:T(8,128)(2,1)S(1)} collective-permute-done((bf16[688,256]{1,0:T(8,128)(2,1)}, bf16[688,256]{1,0:T(8,128)(2,1)S(1)}, u32[]{:S(2)}, u32[]{:S(2)}) %collective-permute-start.23) | collective-permute-done | bytes 352288 | tf_op jit(solution)/shard_map/ppermute | solution.py:252
  169.1 3.3 %adam.5 = (f32[688,1024]{1,0:T(8,128)}, f32[688,1024]{1,0:T(8,128)}, bf16[688,256]{1,0:T(8,128)(2,1)}) custom-call(bf16[688,256]{1,0:T(8,128)(2,1)} %copy-done.28, bf16[4,688,256]{2,1,0:T(8,128)(2,1)} %get-tuple-element.106.refs_0_.refs_1_, bf16[4,688,256]{2,1,0:T(8,128)(2,1)} %copy-done.2, ...), custom_call_target="tpu_custom_call", output_to_operand_aliasing={{0}: (5, {}), {1}: (6, {})} | custom-call | flops 1024 | bytes 1024 | tf_op jit(solution)/shard_map/adam/pallas_call | solution.py:164
  172.3 3.5 %collective-permute-done.30.refs_2_ = bf16[688,256]{1,0:T(8,128)(2,1)S(1)} collective-permute-done((bf16[688,256]{1,0:T(8,128)(2,1)}, bf16[688,256]{1,0:T(8,128)(2,1)S(1)}, u32[]{:S(2)}, u32[]{:S(2)}) %collective-permute-start.30) | collective-permute-done | bytes 352288 | tf_op jit(solution)/shard_map/ppermute | solution.py:252
  176.6 2.1 accumulate.29
  179.3 1.4 collective-permute-start.33
  180.7 1.5 collective-permute-start.34
  182.2 1.2 collective-permute-done.29.refs_0_
  184.2 3.3 %adam.6 = (f32[688,1024]{1,0:T(8,128)}, f32[688,1024]{1,0:T(8,128)}, bf16[688,256]{1,0:T(8,128)(2,1)}) custom-call(bf16[688,256]{1,0:T(8,128)(2,1)} %copy-done.29, bf16[4,688,256]{2,1,0:T(8,128)(2,1)} %get-tuple-element.108.refs_0_.refs_1_, bf16[4,688,256]{2,1,0:T(8,128)(2,1)} %copy-done.1, ...), custom_call_target="tpu_custom_call", output_to_operand_aliasing={{0}: (5, {}), {1}: (6, {})} | custom-call | flops 1024 | bytes 1024 | tf_op jit(solution)/shard_map/adam/pallas_call | solution.py:164
  188.0 1.6 collective-permute-done.32.refs_0_
  191.4 6.0 %collective-permute-done.33.refs_1_ = bf16[688,256]{1,0:T(8,128)(2,1)S(1)} collective-permute-done((bf16[688,256]{1,0:T(8,128)(2,1)S(1)}, bf16[688,256]{1,0:T(8,128)(2,1)S(1)}, u32[]{:S(2)}, u32[]{:S(2)}) %collective-permute-start.33) | collective-permute-done | bytes 352288 | tf_op jit(solution)/shard_map/ppermute | solution.py:246
  197.4 2.1 collective-permute-done.34.refs_1_
  199.5 3.4 %adam.7 = (f32[688,1024]{1,0:T(8,128)}, f32[688,1024]{1,0:T(8,128)}, bf16[688,256]{1,0:T(8,128)(2,1)}) custom-call(bf16[688,256]{1,0:T(8,128)(2,1)} %copy-done.27, bf16[4,688,256]{2,1,0:T(8,128)(2,1)} %get-tuple-element.114.refs_0_.refs_1_, bf16[4,688,256]{2,1,0:T(8,128)(2,1)} %copy-done, ...), custom_call_target="tpu_custom_call", output_to_operand_aliasing={{0}: (5, {}), {1}: (6, {})} | custom-call | flops 1024 | bytes 1024 | tf_op jit(solution)/shard_map/adam/pallas_call | solution.py:164
  203.6 1.5 collective-permute-start.37
  206.5 3.7 %collective-permute-done.36.refs_2_ = bf16[688,256]{1,0:T(8,128)(2,1)S(1)} collective-permute-done((bf16[688,256]{1,0:T(8,128)(2,1)}, bf16[688,256]{1,0:T(8,128)(2,1)S(1)}, u32[]{:S(2)}, u32[]{:S(2)}) %collective-permute-start.36) | collective-permute-done | bytes 352288 | tf_op jit(solution)/shard_map/ppermute | solution.py:246
  210.2 2.2 collective-permute-done.38.refs_2_
  212.5 7.1 %expand.4.refs_4_ = f32[4,688,2048]{2,1,0:T(8,128)} custom-call(s32[1]{0:T(128)} %bitcast.9.target_ref, bf16[1024,2048]{1,0:T(8,128)(2,1)} %transpose.5.basis_ref, bf16[688,256]{1,0:T(8,128)(2,1)} %get-tuple-element.98.refs_0_, bf16[688,256]{1,0:T(8,128)(2,1)} %get-tuple-element.113.refs_1_, bf16[688,256]{1,0:T(8,128)(2,1)} %get-tuple-element.118.refs_2_, ...), custom_call_target="tpu_custom_call" | custom-call | flops 1024 | bytes 1024 | tf_op jit(solution)/shard_map/expand/pallas_call | solution.py:196
  220.8 7.0 %expand.5.refs_4_ = f32[4,688,2048]{2,1,0:T(8,128)} custom-call(s32[1]{0:T(128)} %bitcast.8.target_ref, bf16[1024,2048]{1,0:T(8,128)(2,1)} %transpose.5.basis_ref, bf16[688,256]{1,0:T(8,128)(2,1)} %copy-done.10, bf16[688,256]{1,0:T(8,128)(2,1)} %copy-done.15, bf16[688,256]{1,0:T(8,128)(2,1)} %copy-done.17, ...), custom_call_target="tpu_custom_call", output_to_operand_aliasing={{}: (6, {})} | custom-call | flops 1024 | bytes 1024 | tf_op jit(solution)/shard_map/expand/pallas_call | solution.py:196
  228.5 7.0 %expand.6.refs_4_ = f32[4,688,2048]{2,1,0:T(8,128)} custom-call(s32[1]{0:T(128)} %bitcast.7.target_ref, bf16[1024,2048]{1,0:T(8,128)(2,1)} %transpose.5.basis_ref, bf16[688,256]{1,0:T(8,128)(2,1)} %copy-done.9, bf16[688,256]{1,0:T(8,128)(2,1)} %copy-done.13, bf16[688,256]{1,0:T(8,128)(2,1)} %copy-done.16, ...), custom_call_target="tpu_custom_call", output_to_operand_aliasing={{}: (6, {})} | custom-call | flops 1024 | bytes 1024 | tf_op jit(solution)/shard_map/expand/pallas_call | solution.py:196
  236.2 7.0 %expand.7 = f32[4,688,2048]{2,1,0:T(8,128)} custom-call(s32[1]{0:T(128)} %bitcast.target_ref, bf16[1024,2048]{1,0:T(8,128)(2,1)} %transpose.5.basis_ref, bf16[688,256]{1,0:T(8,128)(2,1)} %copy-done.8, bf16[688,256]{1,0:T(8,128)(2,1)} %copy-done.11, bf16[688,256]{1,0:T(8,128)(2,1)} %copy-done.14, ...), custom_call_target="tpu_custom_call", output_to_operand_aliasing={{}: (6, {})} | custom-call | flops 1024 | bytes 1024 | tf_op jit(solution)/shard_map/expand/pallas_call | solution.py:196
  (128 shorter events, 27.9 us)
Async XLA Ops:
  4.4 15.2 %collective-permute-start = (bf16[512,256]{1,0:T(8,128)(2,1)S(1)}, bf16[512,256]{1,0:T(8,128)(2,1)S(1)}, u32[]{:S(2)}, u32[]{:S(2)}) collective-permute-start(bf16[512,256]{1,0:T(8,128)(2,1)S(1)} %get-tuple-element.130), channel_id=1, source_target_pairs={{0,1},{1,0},{2,3},{3,2},{4,5},{5,4},{6,7},{7,6},{8,9},{9,8},{10,11... | collective-permute-start | bytes 786440 | tf_op jit(solution)/shard_map/ppermute | solution.py:246
  7.4 12.2 %collective-permute-start.1 = (bf16[512,256]{1,0:T(8,128)(2,1)S(1)}, bf16[512,256]{1,0:T(8,128)(2,1)S(1)}, u32[]{:S(2)}, u32[]{:S(2)}) collective-permute-start(bf16[512,256]{1,0:T(8,128)(2,1)S(1)} %get-tuple-element.129), channel_id=1, source_target_pairs={{0,2},{1,3},{2,0},{3,1},{4,6},{5,7},{6,4},{7,5},{8,10},{9,11},{10,... | collective-permute-start | bytes 786440 | tf_op jit(solution)/shard_map/ppermute | solution.py:246
  19.7 14.4 %collective-permute-start.3 = (bf16[512,256]{1,0:T(8,128)(2,1)S(1)}, bf16[512,256]{1,0:T(8,128)(2,1)S(1)}, u32[]{:S(2)}, u32[]{:S(2)}) collective-permute-start(bf16[512,256]{1,0:T(8,128)(2,1)S(1)} %get-tuple-element.127), channel_id=1, source_target_pairs={{0,1},{1,0},{2,3},{3,2},{4,5},{5,4},{6,7},{7,6},{8,9},{9,8},{10,11... | collective-permute-start | bytes 786440 | tf_op jit(solution)/shard_map/ppermute | solution.py:246
  20.3 13.8 %collective-permute-start.2 = (bf16[512,256]{1,0:T(8,128)(2,1)S(1)}, bf16[512,256]{1,0:T(8,128)(2,1)S(1)}, u32[]{:S(2)}, u32[]{:S(2)}) collective-permute-start(bf16[512,256]{1,0:T(8,128)(2,1)S(1)} %get-tuple-element.128), channel_id=1, source_target_pairs={{0,2},{1,3},{2,0},{3,1},{4,6},{5,7},{6,4},{7,5},{8,10},{9,11},{10,... | collective-permute-start | bytes 786440 | tf_op jit(solution)/shard_map/ppermute | solution.py:246
  20.4 24.0 %collective-permute-start.5 = (bf16[512,768]{1,0:T(8,128)(2,1)}, bf16[512,768]{1,0:T(8,128)(2,1)S(1)}, u32[]{:S(2)}, u32[]{:S(2)}) collective-permute-start(bf16[512,768]{1,0:T(8,128)(2,1)} %get-tuple-element.77), channel_id=1, source_target_pairs={{0,2},{1,3},{2,0},{3,1},{4,6},{5,7},{6,4},{7,5},{8,10},{9,11},{10,... | collective-permute-start | bytes 2359304 | tf_op jit(solution)/shard_map/ppermute | solution.py:246
  22.4 22.0 %collective-permute-start.4 = (bf16[512,768]{1,0:T(8,128)(2,1)}, bf16[512,768]{1,0:T(8,128)(2,1)S(1)}, u32[]{:S(2)}, u32[]{:S(2)}) collective-permute-start(bf16[512,768]{1,0:T(8,128)(2,1)} %get-tuple-element.75), channel_id=1, source_target_pairs={{0,1},{1,0},{2,3},{3,2},{4,5},{5,4},{6,7},{7,6},{8,9},{9,8},{10,11... | collective-permute-start | bytes 2359304 | tf_op jit(solution)/shard_map/ppermute | solution.py:246
  35.7 8.7 %copy-start.6 = (bf16[512,768]{1,0:T(8,128)(2,1)S(1)}, bf16[512,768]{1,0:T(8,128)(2,1)}, u32[]{:S(2)}) copy-start(bf16[512,768]{1,0:T(8,128)(2,1)} %get-tuple-element.77) | copy-start | bytes 2359300
  42.0 4.1 %copy-start.5 = (bf16[512,768]{1,0:T(8,128)(2,1)S(1)}, bf16[512,768]{1,0:T(8,128)(2,1)}, u32[]{:S(2)}) copy-start(bf16[512,768]{1,0:T(8,128)(2,1)} %get-tuple-element.75) | copy-start | bytes 2359300
  42.0 10.5 %collective-permute-start.6 = (bf16[4,688,128]{2,1,0:T(8,128)(2,1)}, bf16[4,688,128]{2,1,0:T(8,128)(2,1)S(1)}, u32[]{:S(2)}, u32[]{:S(2)}) collective-permute-start(bf16[4,688,128]{2,1,0:T(8,128)(2,1)} %get-tuple-element.73), channel_id=1, source_target_pairs={{0,4},{4,0},{8,12},{12,8},{16,20},{20,16},{24,28},{28,24},{1,5},{5... | collective-permute-start | bytes 2113544 | tf_op jit(solution)/shard_map/ppermute | solution.py:249
  42.0 14.6 %collective-permute-start.7 = (bf16[4,688,128]{2,1,0:T(8,128)(2,1)}, bf16[4,688,128]{2,1,0:T(8,128)(2,1)S(1)}, u32[]{:S(2)}, u32[]{:S(2)}) collective-permute-start(bf16[4,688,128]{2,1,0:T(8,128)(2,1)} %get-tuple-element.74), channel_id=1, source_target_pairs={{0,4},{4,0},{8,12},{12,8},{16,20},{20,16},{24,28},{28,24},{1,5},{5... | collective-permute-start | bytes 2113544 | tf_op jit(solution)/shard_map/ppermute | solution.py:249
  44.6 44.9 %collective-permute-start.15 = (bf16[512,768]{1,0:T(8,128)(2,1)S(1)}, bf16[512,768]{1,0:T(8,128)(2,1)S(1)}, u32[]{:S(2)}, u32[]{:S(2)}) collective-permute-start(bf16[512,768]{1,0:T(8,128)(2,1)S(1)} %add_convert_fusion.2), channel_id=1, source_target_pairs={{0,1},{1,0},{2,3},{3,2},{4,5},{5,4},{6,7},{7,6},{8,9},{9,8},{10,11... | collective-permute-start | bytes 2359304 | tf_op jit(solution)/shard_map/ppermute | solution.py:246
  52.5 0.9 copy-start.3
  55.1 8.7 %collective-permute-start.8 = (bf16[688,128]{1,0:T(8,128)(2,1)}, bf16[688,128]{1,0:T(8,128)(2,1)S(1)}, u32[]{:S(2)}, u32[]{:S(2)}) collective-permute-start(bf16[688,128]{1,0:T(8,128)(2,1)} %accumulate.15), channel_id=1, source_target_pairs={{0,8},{4,12},{8,16},{12,20},{16,24},{20,28},{24,0},{28,4},{1,9},{5... | collective-permute-start | bytes 528392 | tf_op jit(solution)/shard_map/ppermute | solution.py:252
  56.7 0.9 copy-start.4
  59.2 7.8 %collective-permute-start.9 = (bf16[688,128]{1,0:T(8,128)(2,1)}, bf16[688,128]{1,0:T(8,128)(2,1)S(1)}, u32[]{:S(2)}, u32[]{:S(2)}) collective-permute-start(bf16[688,128]{1,0:T(8,128)(2,1)} %accumulate.16), channel_id=1, source_target_pairs={{0,8},{4,12},{8,16},{12,20},{16,24},{20,28},{24,0},{28,4},{1,9},{5... | collective-permute-start | bytes 528392 | tf_op jit(solution)/shard_map/ppermute | solution.py:252
  60.8 29.7 %collective-permute-start.13 = (bf16[512,768]{1,0:T(8,128)(2,1)S(1)}, bf16[512,768]{1,0:T(8,128)(2,1)S(1)}, u32[]{:S(2)}, u32[]{:S(2)}) collective-permute-start(bf16[512,768]{1,0:T(8,128)(2,1)S(1)} %add_convert_fusion.3), channel_id=1, source_target_pairs={{0,2},{1,3},{2,0},{3,1},{4,6},{5,7},{6,4},{7,5},{8,10},{9,11},{10,... | collective-permute-start | bytes 2359304 | tf_op jit(solution)/shard_map/ppermute | solution.py:246
  66.2 8.9 %collective-permute-start.10 = (bf16[688,128]{1,0:T(8,128)(2,1)}, bf16[688,128]{1,0:T(8,128)(2,1)S(1)}, u32[]{:S(2)}, u32[]{:S(2)}) collective-permute-start(bf16[688,128]{1,0:T(8,128)(2,1)} %accumulate.17), channel_id=1, source_target_pairs={{0,8},{4,12},{8,16},{12,20},{16,24},{20,28},{24,0},{28,4},{1,9},{5... | collective-permute-start | bytes 528392 | tf_op jit(solution)/shard_map/ppermute | solution.py:252
  69.5 8.1 %collective-permute-start.11 = (bf16[688,128]{1,0:T(8,128)(2,1)}, bf16[688,128]{1,0:T(8,128)(2,1)S(1)}, u32[]{:S(2)}, u32[]{:S(2)}) collective-permute-start(bf16[688,128]{1,0:T(8,128)(2,1)} %accumulate.18), channel_id=1, source_target_pairs={{0,8},{4,12},{8,16},{12,20},{16,24},{20,28},{24,0},{28,4},{1,9},{5... | collective-permute-start | bytes 528392 | tf_op jit(solution)/shard_map/ppermute | solution.py:252
  80.1 7.5 %collective-permute-start.14 = (bf16[688,128]{1,0:T(8,128)(2,1)}, bf16[688,128]{1,0:T(8,128)(2,1)S(1)}, u32[]{:S(2)}, u32[]{:S(2)}) collective-permute-start(bf16[688,128]{1,0:T(8,128)(2,1)} %accumulate.20), channel_id=1, source_target_pairs={{0,8},{4,12},{8,16},{12,20},{16,24},{20,28},{24,0},{28,4},{1,9},{5... | collective-permute-start | bytes 528392 | tf_op jit(solution)/shard_map/ppermute | solution.py:252
  80.1 9.4 %collective-permute-start.12 = (bf16[688,128]{1,0:T(8,128)(2,1)}, bf16[688,128]{1,0:T(8,128)(2,1)S(1)}, u32[]{:S(2)}, u32[]{:S(2)}) collective-permute-start(bf16[688,128]{1,0:T(8,128)(2,1)} %accumulate.19), channel_id=1, source_target_pairs={{0,8},{4,12},{8,16},{12,20},{16,24},{20,28},{24,0},{28,4},{1,9},{5... | collective-permute-start | bytes 528392 | tf_op jit(solution)/shard_map/ppermute | solution.py:252
  87.6 13.0 %copy-start.30 = (bf16[688,128]{1,0:T(8,128)(2,1)}, bf16[688,128]{1,0:T(8,128)(2,1)S(1)}, u32[]{:S(2)}) copy-start(bf16[688,128]{1,0:T(8,128)(2,1)S(1)} %collective-permute-done.14.refs_3_) | copy-start | bytes 528388
  89.5 11.1 %copy-start.31 = (bf16[688,128]{1,0:T(8,128)(2,1)}, bf16[688,128]{1,0:T(8,128)(2,1)S(1)}, u32[]{:S(2)}) copy-start(bf16[688,128]{1,0:T(8,128)(2,1)S(1)} %collective-permute-done.12.refs_0_) | copy-start | bytes 528388
  100.6 13.0 %collective-permute-start.17 = (bf16[4,688,256]{2,1,0:T(8,128)(2,1)}, bf16[4,688,256]{2,1,0:T(8,128)(2,1)S(1)}, u32[]{:S(2)}, u32[]{:S(2)}) collective-permute-start(bf16[4,688,256]{2,1,0:T(8,128)(2,1)} %get-tuple-element.91), channel_id=1, source_target_pairs={{0,4},{4,0},{8,12},{12,8},{16,20},{20,16},{24,28},{28,24},{1,5},{5... | collective-permute-start | bytes 4227080 | tf_op jit(solution)/shard_map/ppermute | solution.py:249
  100.7 15.9 %collective-permute-start.18 = (bf16[4,688,256]{2,1,0:T(8,128)(2,1)}, bf16[4,688,256]{2,1,0:T(8,128)(2,1)S(1)}, u32[]{:S(2)}, u32[]{:S(2)}) collective-permute-start(bf16[4,688,256]{2,1,0:T(8,128)(2,1)} %get-tuple-element.92), channel_id=1, source_target_pairs={{0,4},{4,0},{8,12},{12,8},{16,20},{20,16},{24,28},{28,24},{1,5},{5... | collective-permute-start | bytes 4227080 | tf_op jit(solution)/shard_map/ppermute | solution.py:249
  101.2 31.3 %collective-permute-start.20 = (bf16[4,688,256]{2,1,0:T(8,128)(2,1)}, bf16[4,688,256]{2,1,0:T(8,128)(2,1)S(1)}, u32[]{:S(2)}, u32[]{:S(2)}) collective-permute-start(bf16[4,688,256]{2,1,0:T(8,128)(2,1)} %get-tuple-element.93), channel_id=1, source_target_pairs={{0,4},{4,0},{8,12},{12,8},{16,20},{20,16},{24,28},{28,24},{1,5},{5... | collective-permute-start | bytes 4227080 | tf_op jit(solution)/shard_map/ppermute | solution.py:249
  113.6 1.1 copy-start.2
  116.6 13.0 %collective-permute-start.19 = (bf16[688,256]{1,0:T(8,128)(2,1)}, bf16[688,256]{1,0:T(8,128)(2,1)S(1)}, u32[]{:S(2)}, u32[]{:S(2)}) collective-permute-start(bf16[688,256]{1,0:T(8,128)(2,1)} %accumulate.21), channel_id=1, source_target_pairs={{0,8},{4,12},{8,16},{12,20},{16,24},{20,28},{24,0},{28,4},{1,9},{5... | collective-permute-start | bytes 1056776 | tf_op jit(solution)/shard_map/ppermute | solution.py:252
  116.6 1.1 copy-start.1
  119.6 17.5 %collective-permute-start.21 = (bf16[688,256]{1,0:T(8,128)(2,1)}, bf16[688,256]{1,0:T(8,128)(2,1)S(1)}, u32[]{:S(2)}, u32[]{:S(2)}) collective-permute-start(bf16[688,256]{1,0:T(8,128)(2,1)} %accumulate.22), channel_id=1, source_target_pairs={{0,8},{4,12},{8,16},{12,20},{16,24},{20,28},{24,0},{28,4},{1,9},{5... | collective-permute-start | bytes 1056776 | tf_op jit(solution)/shard_map/ppermute | solution.py:252
  132.5 13.2 %collective-permute-start.22 = (bf16[688,256]{1,0:T(8,128)(2,1)}, bf16[688,256]{1,0:T(8,128)(2,1)S(1)}, u32[]{:S(2)}, u32[]{:S(2)}) collective-permute-start(bf16[688,256]{1,0:T(8,128)(2,1)} %accumulate.23), channel_id=1, source_target_pairs={{0,8},{4,12},{8,16},{12,20},{16,24},{20,28},{24,0},{28,4},{1,9},{5... | collective-permute-start | bytes 1056776 | tf_op jit(solution)/shard_map/ppermute | solution.py:252
  132.5 1.1 copy-start
  135.5 13.0 %copy-start.7 = (bf16[688,256]{1,0:T(8,128)(2,1)S(1)}, bf16[688,256]{1,0:T(8,128)(2,1)}, u32[]{:S(2)}) copy-start(bf16[688,256]{1,0:T(8,128)(2,1)} %get-tuple-element.98.refs_0_) | copy-start | bytes 1056772
  135.6 17.7 %collective-permute-start.24 = (bf16[688,256]{1,0:T(8,128)(2,1)}, bf16[688,256]{1,0:T(8,128)(2,1)S(1)}, u32[]{:S(2)}, u32[]{:S(2)}) collective-permute-start(bf16[688,256]{1,0:T(8,128)(2,1)} %accumulate.24), channel_id=1, source_target_pairs={{0,8},{4,12},{8,16},{12,20},{16,24},{20,28},{24,0},{28,4},{1,9},{5... | collective-permute-start | bytes 1056776 | tf_op jit(solution)/shard_map/ppermute | solution.py:252
  139.9 20.9 %collective-permute-start.25 = (bf16[688,256]{1,0:T(8,128)(2,1)}, bf16[688,256]{1,0:T(8,128)(2,1)S(1)}, u32[]{:S(2)}, u32[]{:S(2)}) collective-permute-start(bf16[688,256]{1,0:T(8,128)(2,1)} %accumulate.25), channel_id=1, source_target_pairs={{0,8},{4,12},{8,16},{12,20},{16,24},{20,28},{24,0},{28,4},{1,9},{5... | collective-permute-start | bytes 1056776 | tf_op jit(solution)/shard_map/ppermute | solution.py:252
  145.7 0.8 copy-start.25
  148.5 19.8 %collective-permute-start.23 = (bf16[688,256]{1,0:T(8,128)(2,1)}, bf16[688,256]{1,0:T(8,128)(2,1)S(1)}, u32[]{:S(2)}, u32[]{:S(2)}) collective-permute-start(bf16[688,256]{1,0:T(8,128)(2,1)} %accumulate.26), channel_id=1, source_target_pairs={{0,8},{4,12},{8,16},{12,20},{16,24},{20,28},{24,0},{28,4},{1,9},{5... | collective-permute-start | bytes 1056776 | tf_op jit(solution)/shard_map/ppermute | solution.py:252
  148.5 19.8 %collective-permute-start.16 = (bf16[688,256]{1,0:T(8,128)(2,1)S(1)}, bf16[688,256]{1,0:T(8,128)(2,1)S(1)}, u32[]{:S(2)}, u32[]{:S(2)}) collective-permute-start(bf16[688,256]{1,0:T(8,128)(2,1)S(1)} %copy-done.7), channel_id=1, source_target_pairs={{0,3},{1,2},{2,1},{3,0},{4,7},{5,6},{6,5},{7,4},{8,11},{9,10},{10,... | collective-permute-start | bytes 1056776 | tf_op jit(solution)/shard_map/ppermute | solution.py:246
  149.1 19.2 %collective-permute-start.26 = (bf16[688,256]{1,0:T(8,128)(2,1)S(1)}, bf16[688,256]{1,0:T(8,128)(2,1)S(1)}, u32[]{:S(2)}, u32[]{:S(2)}) collective-permute-start(bf16[688,256]{1,0:T(8,128)(2,1)S(1)} %copy-done.7), channel_id=1, source_target_pairs={{0,1},{1,0},{2,3},{3,2},{4,5},{5,4},{6,7},{7,6},{8,9},{9,8},{10,11... | collective-permute-start | bytes 1056776 | tf_op jit(solution)/shard_map/ppermute | solution.py:246
  153.2 0.8 copy-start.21
  153.2 15.1 %collective-permute-start.27 = (bf16[688,256]{1,0:T(8,128)(2,1)S(1)}, bf16[688,256]{1,0:T(8,128)(2,1)S(1)}, u32[]{:S(2)}, u32[]{:S(2)}) collective-permute-start(bf16[688,256]{1,0:T(8,128)(2,1)S(1)} %copy-done.7), channel_id=1, source_target_pairs={{0,2},{1,3},{2,0},{3,1},{4,6},{5,7},{6,4},{7,5},{8,10},{9,11},{10,... | collective-permute-start | bytes 1056776 | tf_op jit(solution)/shard_map/ppermute | solution.py:246
  160.8 15.1 %collective-permute-start.30 = (bf16[688,256]{1,0:T(8,128)(2,1)}, bf16[688,256]{1,0:T(8,128)(2,1)S(1)}, u32[]{:S(2)}, u32[]{:S(2)}) collective-permute-start(bf16[688,256]{1,0:T(8,128)(2,1)} %accumulate.27), channel_id=1, source_target_pairs={{0,8},{4,12},{8,16},{12,20},{16,24},{20,28},{24,0},{28,4},{1,9},{5... | collective-permute-start | bytes 1056776 | tf_op jit(solution)/shard_map/ppermute | solution.py:252
  168.3 15.1 %collective-permute-start.29 = (bf16[688,256]{1,0:T(8,128)(2,1)}, bf16[688,256]{1,0:T(8,128)(2,1)S(1)}, u32[]{:S(2)}, u32[]{:S(2)}) collective-permute-start(bf16[688,256]{1,0:T(8,128)(2,1)} %accumulate.28), channel_id=1, source_target_pairs={{0,8},{4,12},{8,16},{12,20},{16,24},{20,28},{24,0},{28,4},{1,9},{5... | collective-permute-start | bytes 1056776 | tf_op jit(solution)/shard_map/ppermute | solution.py:252
  168.3 4.0 %copy-start.8 = (bf16[688,256]{1,0:T(8,128)(2,1)}, bf16[688,256]{1,0:T(8,128)(2,1)S(1)}, u32[]{:S(2)}) copy-start(bf16[688,256]{1,0:T(8,128)(2,1)S(1)} %collective-permute-done.16.refs_0_) | copy-start | bytes 1056772
  168.4 4.0 %copy-start.10 = (bf16[688,256]{1,0:T(8,128)(2,1)}, bf16[688,256]{1,0:T(8,128)(2,1)S(1)}, u32[]{:S(2)}) copy-start(bf16[688,256]{1,0:T(8,128)(2,1)S(1)} %collective-permute-done.26.refs_0_) | copy-start | bytes 1056772
  168.4 3.9 %copy-start.9 = (bf16[688,256]{1,0:T(8,128)(2,1)}, bf16[688,256]{1,0:T(8,128)(2,1)S(1)}, u32[]{:S(2)}) copy-start(bf16[688,256]{1,0:T(8,128)(2,1)S(1)} %collective-permute-done.27.refs_0_) | copy-start | bytes 1056772
  172.3 6.4 %copy-start.12 = (bf16[688,256]{1,0:T(8,128)(2,1)S(1)}, bf16[688,256]{1,0:T(8,128)(2,1)}, u32[]{:S(2)}) copy-start(bf16[688,256]{1,0:T(8,128)(2,1)} %get-tuple-element.113.refs_1_) | copy-start | bytes 1056772
  178.7 10.9 %collective-permute-start.32 = (bf16[688,256]{1,0:T(8,128)(2,1)}, bf16[688,256]{1,0:T(8,128)(2,1)S(1)}, u32[]{:S(2)}, u32[]{:S(2)}) collective-permute-start(bf16[688,256]{1,0:T(8,128)(2,1)} %accumulate.29), channel_id=1, source_target_pairs={{0,8},{4,12},{8,16},{12,20},{16,24},{20,28},{24,0},{28,4},{1,9},{5... | collective-permute-start | bytes 1056776 | tf_op jit(solution)/shard_map/ppermute | solution.py:252
  178.7 12.1 %collective-permute-start.28 = (bf16[688,256]{1,0:T(8,128)(2,1)S(1)}, bf16[688,256]{1,0:T(8,128)(2,1)S(1)}, u32[]{:S(2)}, u32[]{:S(2)}) collective-permute-start(bf16[688,256]{1,0:T(8,128)(2,1)S(1)} %copy-done.12), channel_id=1, source_target_pairs={{0,3},{1,2},{2,1},{3,0},{4,7},{5,6},{6,5},{7,4},{8,11},{9,10},{10,... | collective-permute-start | bytes 1056776 | tf_op jit(solution)/shard_map/ppermute | solution.py:246
  179.3 18.1 %collective-permute-start.33 = (bf16[688,256]{1,0:T(8,128)(2,1)S(1)}, bf16[688,256]{1,0:T(8,128)(2,1)S(1)}, u32[]{:S(2)}, u32[]{:S(2)}) collective-permute-start(bf16[688,256]{1,0:T(8,128)(2,1)S(1)} %copy-done.12), channel_id=1, source_target_pairs={{0,1},{1,0},{2,3},{3,2},{4,5},{5,4},{6,7},{7,6},{8,9},{9,8},{10,11... | collective-permute-start | bytes 1056776 | tf_op jit(solution)/shard_map/ppermute | solution.py:246
  180.7 18.8 %collective-permute-start.34 = (bf16[688,256]{1,0:T(8,128)(2,1)S(1)}, bf16[688,256]{1,0:T(8,128)(2,1)S(1)}, u32[]{:S(2)}, u32[]{:S(2)}) collective-permute-start(bf16[688,256]{1,0:T(8,128)(2,1)S(1)} %copy-done.12), channel_id=1, source_target_pairs={{0,2},{1,3},{2,0},{3,1},{4,6},{5,7},{6,4},{7,5},{8,10},{9,11},{10,... | collective-permute-start | bytes 1056776 | tf_op jit(solution)/shard_map/ppermute | solution.py:246
  187.4 18.4 %collective-permute-start.31 = (bf16[688,256]{1,0:T(8,128)(2,1)}, bf16[688,256]{1,0:T(8,128)(2,1)S(1)}, u32[]{:S(2)}, u32[]{:S(2)}) collective-permute-start(bf16[688,256]{1,0:T(8,128)(2,1)} %get-tuple-element.118.refs_2_), channel_id=1, source_target_pairs={{0,3},{1,2},{2,1},{3,0},{4,7},{5,6},{6,5},{7,4},{8,11},{9,10},{10,... | collective-permute-start | bytes 1056776 | tf_op jit(solution)/shard_map/ppermute | solution.py:246
  189.6 9.9 %copy-start.27 = (bf16[688,256]{1,0:T(8,128)(2,1)}, bf16[688,256]{1,0:T(8,128)(2,1)S(1)}, u32[]{:S(2)}) copy-start(bf16[688,256]{1,0:T(8,128)(2,1)S(1)} %collective-permute-done.32.refs_0_) | copy-start | bytes 1056772
  189.6 20.6 %collective-permute-start.36 = (bf16[688,256]{1,0:T(8,128)(2,1)}, bf16[688,256]{1,0:T(8,128)(2,1)S(1)}, u32[]{:S(2)}, u32[]{:S(2)}) collective-permute-start(bf16[688,256]{1,0:T(8,128)(2,1)} %get-tuple-element.118.refs_2_), channel_id=1, source_target_pairs={{0,2},{1,3},{2,0},{3,1},{4,6},{5,7},{6,4},{7,5},{8,10},{9,11},{10,... | collective-permute-start | bytes 1056776 | tf_op jit(solution)/shard_map/ppermute | solution.py:246
  190.8 12.0 %copy-start.11 = (bf16[688,256]{1,0:T(8,128)(2,1)}, bf16[688,256]{1,0:T(8,128)(2,1)S(1)}, u32[]{:S(2)}) copy-start(bf16[688,256]{1,0:T(8,128)(2,1)S(1)} %collective-permute-done.28.refs_1_) | copy-start | bytes 1056772
  190.8 21.7 %collective-permute-start.38 = (bf16[688,256]{1,0:T(8,128)(2,1)}, bf16[688,256]{1,0:T(8,128)(2,1)S(1)}, u32[]{:S(2)}, u32[]{:S(2)}) collective-permute-start(bf16[688,256]{1,0:T(8,128)(2,1)} %get-tuple-element.118.refs_2_), channel_id=1, source_target_pairs={{0,1},{1,0},{2,3},{3,2},{4,5},{5,4},{6,7},{7,6},{8,9},{9,8},{10,11... | collective-permute-start | bytes 1056776 | tf_op jit(solution)/shard_map/ppermute | solution.py:246
  197.4 5.5 %copy-start.15 = (bf16[688,256]{1,0:T(8,128)(2,1)}, bf16[688,256]{1,0:T(8,128)(2,1)S(1)}, u32[]{:S(2)}) copy-start(bf16[688,256]{1,0:T(8,128)(2,1)S(1)} %collective-permute-done.33.refs_1_) | copy-start | bytes 1056772
  199.4 3.4 %copy-start.13 = (bf16[688,256]{1,0:T(8,128)(2,1)}, bf16[688,256]{1,0:T(8,128)(2,1)S(1)}, u32[]{:S(2)}) copy-start(bf16[688,256]{1,0:T(8,128)(2,1)S(1)} %collective-permute-done.34.refs_1_) | copy-start | bytes 1056772
  202.8 17.2 %collective-permute-start.39 = (bf16[688,256]{1,0:T(8,128)(2,1)}, bf16[688,256]{1,0:T(8,128)(2,1)S(1)}, u32[]{:S(2)}, u32[]{:S(2)}) collective-permute-start(bf16[688,256]{1,0:T(8,128)(2,1)} %get-tuple-element.124.refs_3_), channel_id=1, source_target_pairs={{0,1},{1,0},{2,3},{3,2},{4,5},{5,4},{6,7},{7,6},{8,9},{9,8},{10,11... | collective-permute-start | bytes 1056776 | tf_op jit(solution)/shard_map/ppermute | solution.py:246
  203.6 24.2 %collective-permute-start.37 = (bf16[688,256]{1,0:T(8,128)(2,1)}, bf16[688,256]{1,0:T(8,128)(2,1)S(1)}, u32[]{:S(2)}, u32[]{:S(2)}) collective-permute-start(bf16[688,256]{1,0:T(8,128)(2,1)} %get-tuple-element.124.refs_3_), channel_id=1, source_target_pairs={{0,2},{1,3},{2,0},{3,1},{4,6},{5,7},{6,4},{7,5},{8,10},{9,11},{10,... | collective-permute-start | bytes 1056776 | tf_op jit(solution)/shard_map/ppermute | solution.py:246
  205.9 13.7 %copy-start.14 = (bf16[688,256]{1,0:T(8,128)(2,1)}, bf16[688,256]{1,0:T(8,128)(2,1)S(1)}, u32[]{:S(2)}) copy-start(bf16[688,256]{1,0:T(8,128)(2,1)S(1)} %collective-permute-done.31.refs_2_) | copy-start | bytes 1056772
  205.9 29.6 %collective-permute-start.35 = (bf16[688,256]{1,0:T(8,128)(2,1)}, bf16[688,256]{1,0:T(8,128)(2,1)S(1)}, u32[]{:S(2)}, u32[]{:S(2)}) collective-permute-start(bf16[688,256]{1,0:T(8,128)(2,1)} %get-tuple-element.124.refs_3_), channel_id=1, source_target_pairs={{0,3},{1,2},{2,1},{3,0},{4,7},{5,6},{6,5},{7,4},{8,11},{9,10},{10,... | collective-permute-start | bytes 1056776 | tf_op jit(solution)/shard_map/ppermute | solution.py:246
  210.2 9.3 %copy-start.16 = (bf16[688,256]{1,0:T(8,128)(2,1)}, bf16[688,256]{1,0:T(8,128)(2,1)S(1)}, u32[]{:S(2)}) copy-start(bf16[688,256]{1,0:T(8,128)(2,1)S(1)} %collective-permute-done.36.refs_2_) | copy-start | bytes 1056772
  212.5 7.1 %copy-start.17 = (bf16[688,256]{1,0:T(8,128)(2,1)}, bf16[688,256]{1,0:T(8,128)(2,1)S(1)}, u32[]{:S(2)}) copy-start(bf16[688,256]{1,0:T(8,128)(2,1)S(1)} %collective-permute-done.38.refs_2_) | copy-start | bytes 1056772
  235.4 0.8 copy-start.18
  (12 other events, 8.6 us)

commit v4 on v3

v4 whole, which is shorter than its diff:
```python
import functools

import jax
import jax.numpy as jnp
from jax import lax
from jax.experimental import pallas as pl
from jax.experimental.pallas import tpu as pltpu
from jax.sharding import PartitionSpec as P

beta_first = 0.9
beta_second = 0.999
adam_count = 100.0
epsilon = 1e-08

F32 = jnp.float32
BF16 = jnp.bfloat16
VMEM_LIMIT = 64 * 1024 * 1024
COST = pl.CostEstimate(flops=1024, bytes_accessed=1024, transcendentals=0)
PARAMS = pltpu.CompilerParams(vmem_limit_bytes=VMEM_LIMIT)


def transpose(value, block, begin=0, count=None, held=()):
    rows, columns = value.shape
    count = rows // block if count is None else count

    def kernel(value_ref, *refs):
        refs[-1][...] = value_ref[...].T

    return pl.pallas_call(
        kernel,
        out_shape=jax.ShapeDtypeStruct((columns, rows), value.dtype),
        grid=(count,),
        in_specs=[pl.BlockSpec((block, columns), lambda i: (begin + i, 0))]
        + [pl.BlockSpec(memory_space=pl.ANY)] * len(held),
        out_specs=pl.BlockSpec((columns, block), lambda i: (0, begin + i)),
        input_output_aliases={1: 0} if held else {},
        compiler_params=PARAMS,
        cost_estimate=COST,
        name="transpose",
    )(value, *held)


def gradient(grads_t, halves, owners, widths, arrived=()):
    _, owned, tokens = grads_t.shape
    rows, width = halves[0].shape
    count = owners.shape[0]
    top = (owned // 2 + 15) // 16 * 16

    def kernel(owners_ref, grads_ref, low_ref, high_ref, *refs):
        arrived_refs, out_refs, whole_ref = refs[: len(arrived)], refs[len(arrived) : -1], refs[-1]

        @pl.when(pl.program_id(0) == 0)
        def _():
            whole_ref[:rows, :] = low_ref[...]
            whole_ref[rows:, :] = high_ref[...]

        for part in (slice(0, top), slice(top, owned)):
            value = jnp.dot(grads_ref[0, part, :], whole_ref[...], preferred_element_type=F32)
            begin = 0
            for run, size in enumerate(widths):
                columns = value[:, begin : begin + size]
                begin += size
                if not arrived:
                    out_refs[run][0, part, :] = columns.astype(BF16)
                    continue
                columns = (columns + arrived_refs[run][0, part, :].astype(F32)).astype(BF16)
                for block in range(count):

                    @pl.when(pl.program_id(0) == block)
                    def _(out_ref=out_refs[run * count + block], columns=columns):
                        out_ref[part, :] = columns

    if arrived:
        out_shape = [jax.ShapeDtypeStruct((owned, size), BF16) for size in widths for _ in range(count)]
        out_specs = [pl.BlockSpec(out.shape, lambda i, owners_ref: (0, 0)) for out in out_shape]
    else:
        out_shape = [jax.ShapeDtypeStruct((count, owned, size), BF16) for size in widths]
        out_specs = [pl.BlockSpec((1, owned, size), lambda i, owners_ref: (i, 0, 0)) for size in widths]
    results = pl.pallas_call(
        kernel,
        out_shape=out_shape,
        grid_spec=pltpu.PrefetchScalarGridSpec(
            num_scalar_prefetch=1,
            grid=(count,),
            in_specs=[pl.BlockSpec((1, owned, tokens), lambda i, owners_ref: (owners_ref[i], 0, 0))]
            + [pl.BlockSpec((rows, width), lambda i, owners_ref: (0, 0))] * 2
            + [pl.BlockSpec((1, owned, term.shape[2]), lambda i, owners_ref: (i, 0, 0)) for term in arrived],
            out_specs=out_specs,
            scratch_shapes=[pltpu.VMEM((tokens, width), BF16)],
        ),
        compiler_params=PARAMS,
        cost_estimate=COST,
        name="gradient",
    )(owners, grads_t, *halves, *arrived)
    return [results[run * count : (run + 1) * count] for run in range(len(widths))] if arrived else results


def accumulate(arrived, own):
    def kernel(arrived_ref, own_ref, out_ref):
        out_ref[...] = (arrived_ref[...].astype(F32) + own_ref[...].astype(F32)).astype(BF16)

    return pl.pallas_call(
        kernel,
        out_shape=jax.ShapeDtypeStruct(own.shape, BF16),
        in_specs=[pl.BlockSpec(memory_space=pltpu.VMEM)] * 2,
        out_specs=pl.BlockSpec(memory_space=pltpu.VMEM),
        compiler_params=PARAMS,
        cost_estimate=COST,
        name="accumulate",
    )(arrived, own)


def adam(pieces, first, second, held, begin):
    owned, rank = first.shape
    widths = [piece[0].shape[1] for piece in pieces]
    width = sum(widths)

    def kernel(*refs):
        first_ref, second_ref = refs[2 * len(pieces) : 2 * len(pieces) + 2]
        first_out, second_out, direction_out = refs[-3:]
        at = 0
        for index, size in enumerate(widths):
            arrived_ref, own_ref = refs[2 * index : 2 * index + 2]
            columns = slice(at, at + size)
            at += size
            grad_low = arrived_ref[...].astype(F32) + own_ref[...].astype(F32)
            first_next = beta_first * first_ref[:, columns] + (1.0 - beta_first) * grad_low
            second_next = beta_second * second_ref[:, columns] + (1.0 - beta_second) * grad_low * grad_low
            first_out[:, columns] = first_next
            second_out[:, columns] = second_next
            bias_first = 1.0 - beta_first**adam_count
            bias_second = 1.0 - beta_second**adam_count
            direction = first_next / bias_first / (jnp.sqrt(second_next / bias_second) + epsilon)
            direction_out[:, columns] = direction.astype(BF16)

    column = pl.BlockSpec((owned, width), lambda i: (0, begin // width))
    piece_specs = [pl.BlockSpec(memory_space=pltpu.VMEM)] * (2 * len(pieces))
    inputs = len(piece_specs) + 2
    return pl.pallas_call(
        kernel,
        grid=(1,),
        out_shape=[
            jax.ShapeDtypeStruct((owned, rank), F32),
            jax.ShapeDtypeStruct((owned, rank), F32),
            jax.ShapeDtypeStruct((owned, width), BF16),
        ],
        in_specs=piece_specs + [column, column] + [pl.BlockSpec(memory_space=pl.ANY)] * len(held),
        out_specs=[column, column, pl.BlockSpec((owned, width), lambda i: (0, 0))],
        input_output_aliases={inputs + index: index for index in range(len(held))},
        compiler_params=PARAMS,
        cost_estimate=COST,
        name="adam",
    )(*[array for piece in pieces for array in piece], first, second, *held)


def expand(target, directions, basis_t, held, count):
    owned, width = directions[0].shape
    rank, features = basis_t.shape
    block = min(1024, features)

    def kernel(target_ref, basis_ref, *refs):
        direction_refs, out_ref, whole_ref = refs[: len(directions)], refs[-2], refs[-1]

        @pl.when(pl.program_id(0) == 0)
        def _():
            for index, direction_ref in enumerate(direction_refs):
                whole_ref[:, index * width : (index + 1) * width] = direction_ref[...]

        out_ref[0] = jnp.dot(whole_ref[...], basis_ref[...], preferred_element_type=F32)

    return pl.pallas_call(
        kernel,
        out_shape=jax.ShapeDtypeStruct((count, owned, features), F32),
        grid_spec=pltpu.PrefetchScalarGridSpec(
            num_scalar_prefetch=1,
            grid=(features // block,),
            in_specs=[pl.BlockSpec((rank, block), lambda i, target_ref: (0, i))]
            + [pl.BlockSpec((owned, width), lambda i, target_ref: (0, 0))] * len(directions)
            + [pl.BlockSpec(memory_space=pl.ANY)] * len(held),
            out_specs=pl.BlockSpec((1, owned, block), lambda i, target_ref: (target_ref[0], 0, i)),
            scratch_shapes=[pltpu.VMEM((owned, rank), BF16)],
        ),
        input_output_aliases={2 + len(directions): 0} if held else {},
        compiler_params=PARAMS,
        cost_estimate=COST,
        name="expand",
    )(target, basis_t, *directions, *held)


def total_of(*terms):
    total = terms[0].astype(F32)
    for term in terms[1:]:
        total = total + term.astype(F32)
    return total.astype(BF16)


def after(value, *earlier):
    return lax.optimization_barrier((value, *earlier))[0]


def local(activations, out_grads, projector, first_moment, second_moment):
    owned = first_moment.shape[1]
    features = activations[0]
    basis = projector[0]
    rank = basis.shape[1]
    tokens = features.shape[0]
    dp_count, fsdp_count = lax.axis_size("dp"), lax.axis_size("fsdp")
    dp, fsdp = lax.axis_index("dp"), lax.axis_index("fsdp")
    chips = dp_count // 2
    chip, core = dp // 2, dp % 2
    width = rank // 4

    offsets = [1 << bit for bit in range(fsdp_count.bit_length() - 1)]
    order = jnp.stack([fsdp ^ offset for offset in range(fsdp_count)]).astype(jnp.int32)
    hops = chips - 1
    ring_order = (chip - 1 - jnp.arange(chips, dtype=jnp.int32) + chips) % chips
    own_owners = (ring_order * 2 + core).astype(jnp.int32)
    other_owners = (ring_order * 2 + 1 - core).astype(jnp.int32)

    def across(value, offset):
        return lax.ppermute(value, "fsdp", [(index, index ^ offset) for index in range(fsdp_count)])

    def sibling(value):
        return lax.ppermute(value, "dp", [(index, index ^ 1) for index in range(dp_count)])

    def onward(value):
        return lax.ppermute(value, "dp", [(index, (index + 2) % dp_count) for index in range(dp_count)])

    def exchange(halves, step):
        return [across(half, steps[step]) for half, steps in zip(halves, (offsets, offsets[::-1]))]

    def add(halves, arrived):
        return [total_of(half, term) for half, term in zip(halves, arrived)]

    partial = jnp.dot(features, basis, preferred_element_type=F32).astype(BF16)
    low, high = partial[: tokens // 2], partial[tokens // 2 :]
    sums_0 = [low[:, :width], high[:, :width]]
    sums_1 = [low[:, width:], high[:, width:]]
    coming_0 = exchange(sums_0, 0)
    block = tokens // 4
    grads_t = transpose(after(out_grads[0], *sums_0), block, 0, 2)
    sums_0 = add(sums_0, [after(term, grads_t) for term in coming_0])
    for step in range(1, len(offsets) - 1):
        sums_0 = add(sums_0, exchange(sums_0, step))
    coming_0 = exchange(sums_0, len(offsets) - 1)
    grads_t = transpose(after(out_grads[0], *sums_0), block, 2, 2, (grads_t,)).reshape(dp_count, owned, tokens)
    coming_1 = exchange([after(half, grads_t) for half in sums_1], 0)
    sums_0 = add(sums_0, [after(term, grads_t) for term in coming_0])
    other = gradient(grads_t, sums_0, other_owners, [width // 2] * 2)
    coming = [sibling(value) for value in other]
    sums_1 = add(sums_1, [after(term, *other) for term in coming_1])
    for step in range(1, len(offsets) - 1):
        sums_1 = add(sums_1, exchange(sums_1, step))
    coming_1 = exchange(sums_1, len(offsets) - 1)
    parts_0 = gradient(after(grads_t, *sums_1), sums_0, own_owners, [width // 2] * 2, coming)

    def ring(parts, stride, token, between, finish):
        events = sorted(
            (2 * hop + stride * part, part, hop)
            for part in range(len(parts))
            for hop in range(hops + (finish is not None))
        )
        arrived = [None] * len(parts)
        for number, (_, part, hop) in enumerate(events):
            if hop == hops:
                token = finish(part, after(arrived[part], token))
            else:
                leaving = parts[part][hop] if hop == 0 else accumulate(arrived[part], after(parts[part][hop], token))
                arrived[part] = onward(leaving)
                token = leaving
            if number in between:
                token = between[number](token, arrived)
        return token, arrived

    held = ()
    directions = []
    rest = {}

    def step_of(pieces, begin, *earlier):
        nonlocal held
        first_next, second_next, direction = adam(pieces, first_moment[0], second_moment[0], held, begin)
        held = (first_next, second_next)
        sent = after(direction, *earlier) if earlier else direction
        directions.append([direction] + [across(sent, offset) for offset in range(1, fsdp_count)])
        return direction

    def send_other(token, arrived):
        rest["sums"] = add(sums_1, [after(term, token) for term in coming_1])
        rest["other"] = gradient(grads_t, rest["sums"], other_owners, [width] * 3)
        return rest["other"][0]

    def start_rest(token, arrived):
        coming = [sibling(after(value, token)) for value in rest["other"]]
        rest["basis_t"] = transpose(after(basis, token), min(512, basis.shape[0]))
        tied = after(grads_t, rest["basis_t"], *arrived)
        rest["parts"] = gradient(tied, rest["sums"], own_owners, [width] * 3, coming)
        return rest["parts"][0][0]

    token, last_0 = ring(
        parts_0, 1, parts_0[0][0], {3: send_other, 2 * hops - 1: start_rest}, None
    )

    def finish_0(token, arrived):
        pieces = [(after(value, token), part[hops]) for value, part in zip(last_0, parts_0)]
        return step_of(pieces, 0)

    def finish_1(part, arrived):
        earlier = directions[part - 1] if part > 0 else ()
        return step_of([(arrived, rest["parts"][part][hops])], (part + 1) * width, *earlier)

    ring(rest["parts"], 1.5, token, {1: finish_0}, finish_1)

    update = ()
    for offset in range(fsdp_count):
        pieces = [gathered[offset] for gathered in directions]
        if offset == 1:
            pieces[-1] = after(pieces[-1], *directions[-2])
        update = (expand(order[offset : offset + 1], pieces, rest["basis_t"], update, fsdp_count),)
    return (update[0][None], held[0][None], held[1][None])


def solution(mesh):
    in_specs = (
        P(None, "dp", "fsdp"),
        P(None, "dp", "fsdp"),
        P(None, "fsdp", None),
        P(None, ("fsdp", "dp"), None),
        P(None, ("fsdp", "dp"), None),
    )
    out_specs = (
        P(None, None, "dp", "fsdp"),
        P(None, ("fsdp", "dp"), None),
        P(None, ("fsdp", "dp"), None),
    )
    return jax.shard_map(local, mesh=mesh, in_specs=in_specs, out_specs=out_specs, check_vma=False)
```

time: 244 us -> 263 us (1.078)
  waiting for transfers between devices: 64.5 us -> 86.5 us
  Pallas kernels: 126 us -> 111 us
  local copies, waits for them, and re-layouts: 15.4 us -> 4.8 us
  other arithmetic: 4.78 us -> 14.9 us
  starting transfers between devices: 27.7 us -> 36 us
  matrix products: 3.73 us -> 7.95 us
    ppermute x20, waiting for transfers between devices: 17.8 us -> 35.4 us  [across(): lax.ppermute(value, 'fsdp', [(index, index ^ offset) for index in range(f...]
    pallas_call x20 -> x14, Pallas kernels: 70.1 us -> 55.3 us  [the longest x4 37 us: gradient(): pl.pallas_call(kernel, out_shape=out_shape, grid_spec=pltpu.PrefetchScala...]
    unnamed x72 -> x2, local copies, waits for them, and re-layouts: 15.4 us -> 1.31 us
    convert_element_type x7 -> x6, other arithmetic: 4.18 us -> 13.8 us  [total_of(): return total.astype(BF16)]
    ppermute x15, waiting for transfers between devices: 46.6 us -> 51.1 us  [onward(): lax.ppermute(value, 'dp', [(index, (index + 2) % dp_count) for index in r...]
    ppermute x20, starting transfers between devices: 21.2 us -> 25.6 us  [across(): lax.ppermute(value, 'fsdp', [(index, index ^ offset) for index in range(f...]
    dot_general x1, matrix products: 3.73 us -> 7.95 us  [local(): partial = jnp.dot(features, basis, preferred_element_type=F32).astype(BF16)]
    ppermute x15, starting transfers between devices: 5.37 us -> 9.4 us  [onward(): lax.ppermute(value, 'dp', [(index, (index + 2) % dp_count) for index in r...]
  transfers between devices with their start and end apart: 40 -> 40, of which waited for: 22 -> 19; matrix products, arithmetic and copies ran while one was open for 1% -> 6% of each run, Pallas kernels for 45% -> 32%
where the time goes in v4:
time: 263 us; the launch traced here: 262 us
  Pallas kernels  111 us (42%)
  waiting for transfers between devices  86.5 us (33%)
  starting transfers between devices  36 us (14%)
  other arithmetic  14.9 us (6%)
  matrix products  7.95 us (3%)
  local copies, waits for them, and re-layouts  4.8 us (2%)
    ppermute x15, waiting for transfers between devices, onward(): lax.ppermute(value, 'dp', [(index, (index + 2) % dp_count) for index in r...  51.1 us
    pallas_call x4, Pallas kernels, gradient(): pl.pallas_call(kernel, out_shape=out_shape, grid_spec=pltpu.PrefetchScala...  37 us
    ppermute x20, waiting for transfers between devices, across(): lax.ppermute(value, 'fsdp', [(index, index ^ offset) for index in range(f...  35.4 us
    pallas_call x4, Pallas kernels, expand(): pl.pallas_call(kernel, out_shape=jax.ShapeDtypeStruct((count, owned, feat...  27.9 us
    ppermute x20, starting transfers between devices, across(): lax.ppermute(value, 'fsdp', [(index, index ^ offset) for index in range(f...  25.6 us
    pallas_call x10, Pallas kernels, accumulate(): pl.pallas_call(kernel, out_shape=jax.ShapeDtypeStruct(own.shape, BF16), i...  18.3 us
    pallas_call x3, Pallas kernels, transpose(): pl.pallas_call(kernel, out_shape=jax.ShapeDtypeStruct((columns, rows), va...  15.4 us
    convert_element_type x6, other arithmetic, total_of(): return total.astype(BF16)  13.8 us
  transfers between devices with their start and end apart: 40, of which 19 were waited for; matrix products, arithmetic and copies ran while one was open for 6% of the time, Pallas kernels for 32%

profile of v4, /device:TPU:0, one launch (start us, length us, event | category | flops | bytes accessed | tf_op | source)
XLA Modules:
  0.0 261.9 jit_solution(3083617313976562286)
XLA Ops:
  0.6 8.0 %fusion.2 = bf16[1024,1024]{1,0:T(8,128)(2,1)S(1)} fusion(bf16[1,1024,2048]{2,1,0:T(8,128)(2,1)} %param.5, bf16[1,2048,1024]{2,1,0:T(8,128)(2,1)} %param.7), kind=kOutput, calls=%fused_computation.2 | convolution fusion | flops 4296015872 | bytes 10485760 | tf_op jit(solution)/shard_map/dot_general | solution.py:235
  10.8 2.9 %collective-permute-start = (bf16[512,256]{1,0:T(8,128)(2,1)}, bf16[512,256]{1,0:T(8,128)(2,1)}, u32[]{:S(2)}, u32[]{:S(2)}) collective-permute-start(bf16[512,256]{1,0:T(8,128)(2,1)} %get-tuple-element.156), channel_id=1, source_target_pairs={{0,1},{1,0},{2,3},{3,2},{4,5},{5,4},{6,7},{7,6},{8,9},{9,8},{10,11... | collective-permute-start | bytes 786440 | tf_op jit(solution)/shard_map/ppermute | solution.py:221
  13.7 1.5 collective-permute-start.1
  15.2 5.1 %transpose.5.refs_0_ = bf16[5504,1024]{1,0:T(8,128)(2,1)} custom-call(bf16[1024,5504]{1,0:T(8,128)(2,1)} %bitcast.32), custom_call_target="tpu_custom_call" | custom-call | flops 1024 | bytes 1024 | tf_op jit(solution)/shard_map/transpose/pallas_call | solution.py:29
  20.3 2.6 %fusion.8 = (bf16[512,768]{1,0:T(8,128)(2,1)}, bf16[512,768]{1,0:T(8,128)(2,1)}) fusion(bf16[1024,1024]{1,0:T(8,128)(2,1)} %copy-done), kind=kLoop, calls=%fused_computation.19 | loop fusion | bytes 3145728 | tf_op jit(solution)/shard_map/slice | solution.py:238
  22.9 2.1 add_convert_fusion.6
  25.0 5.1 %transpose.6 = bf16[5504,1024]{1,0:T(8,128)(2,1)} custom-call(bf16[1024,5504]{1,0:T(8,128)(2,1)} %bitcast.33, bf16[5504,1024]{1,0:T(8,128)(2,1)} %transpose.5.refs_0_), custom_call_target="tpu_custom_call", output_to_operand_aliasing={{}: (1, {})} | custom-call | flops 1024 | bytes 1024 | tf_op jit(solution)/shard_map/transpose/pallas_call | solution.py:29
  31.0 1.6 collective-permute-start.4
  32.6 1.5 collective-permute-start.3
  34.7 20.0 %collective-permute-done.4 = bf16[512,256]{1,0:T(8,128)(2,1)S(1)} collective-permute-done((bf16[512,256]{1,0:T(8,128)(2,1)}, bf16[512,256]{1,0:T(8,128)(2,1)S(1)}, u32[]{:S(2)}, u32[]{:S(2)}) %collective-permute-start.4) | collective-permute-done | bytes 262176 | tf_op jit(solution)/shard_map/ppermute | solution.py:221
  54.9 1.7 add_convert_fusion.4.high_ref
  56.6 1.7 add_convert_fusion.5.low_ref
  58.4 6.2 %gradient.4 = (bf16[4,688,128]{2,1,0:T(8,128)(2,1)}, bf16[4,688,128]{2,1,0:T(8,128)(2,1)}) custom-call(s32[4]{0:T(128)} %add_subtract_fusion.owners_ref, bf16[8,688,1024]{2,1,0:T(8,128)(2,1)} %bitcast.19, bf16[512,256]{1,0:T(8,128)(2,1)} %add_convert_fusion.5.low_ref, bf16[512,256]{1,0:T(8,128)(2,1)} %add_convert_fusion.4.high_ref), custom_call_target="tpu_custom_call" | custom-call | flops 1024 | bytes 1024 | tf_op jit(solution)/shard_map/gradient/pallas_call | solution.py:79
  65.1 3.4 %add_convert_fusion.2 = (bf16[512,768]{1,0:T(8,128)(2,1)}, bf16[512,768]{1,0:T(8,128)(2,1)}) fusion(bf16[512,768]{1,0:T(8,128)(2,1)} %collective-permute-done.5, bf16[1024,1024]{1,0:T(8,128)(2,1)} %copy-done, bf16[512,768]{1,0:T(8,128)(2,1)} %collective-permute-done.2), kind=kLoop, calls=%fused_computation.5 | loop fusion | flops 3145728 | bytes 4718592 | tf_op jit(solution)/shard_map/convert_element_type | solution.py:194
  68.5 1.5 collective-permute-start.13
  71.0 8.4 %gradient.5 = (bf16[688,128]{1,0:T(8,128)(2,1)}, bf16[688,128]{1,0:T(8,128)(2,1)}, bf16[688,128]{1,0:T(8,128)(2,1)}, bf16[688,128]{1,0:T(8,128)(2,1)}, bf16[688,...) custom-call(s32[4]{0:T(128)} %broadcast_add_fusion.owners_ref, ...), custom_call_target="tpu_custom_call" | custom-call | flops 1024 | bytes 1024 | tf_op jit(solution)/shard_map/gradient/pallas_call | solution.py:79
  79.4 1.6 collective-permute-start.9
  81.0 1.6 collective-permute-start.8
  82.6 6.4 %collective-permute-done.9.arrived_ref = bf16[688,128]{1,0:T(8,128)(2,1)} collective-permute-done((bf16[688,128]{1,0:T(8,128)(2,1)}, bf16[688,128]{1,0:T(8,128)(2,1)}, u32[]{:S(2)}, u32[]{:S(2)}) %collective-permute-start.9) | collective-permute-done | bytes 176160 | tf_op jit(solution)/shard_map/ppermute | solution.py:227
  89.0 1.7 accumulate.10
  91.2 1.7 accumulate.11
  93.8 2.4 add_convert_fusion.high_ref
  96.2 2.4 add_convert_fusion.1.low_ref
  98.6 9.0 %gradient.6 = (bf16[4,688,256]{2,1,0:T(8,128)(2,1)}, bf16[4,688,256]{2,1,0:T(8,128)(2,1)}, bf16[4,688,256]{2,1,0:T(8,128)(2,1)}) custom-call(s32[4]{0:T(128)} %add_subtract_fusion.owners_ref, bf16[8,688,1024]{2,1,0:T(8,128)(2,1)} %bitcast.21, bf16[512,768]{1,0:T(8,128)(2,1)} %add_convert_fusion.1.low_ref, bf16[512,768]{1,0:T(8,128)(2,1)} %add_convert_fusion.high_ref), custom_call_target="tpu_custom_call" | custom-call | flops 1024 | bytes 1024 | tf_op jit(solution)/shard_map/gradient/pallas_call | solution.py:79
  107.6 1.7 accumulate.12
  109.3 1.7 accumulate.13
  111.5 1.6 collective-permute-start.15
  113.1 2.0 collective-permute-start.14
  115.1 5.3 %transpose.7.basis_ref = bf16[1024,2048]{1,0:T(8,128)(2,1)} custom-call(bf16[2048,1024]{1,0:T(8,128)(2,1)} %bitcast.36), custom_call_target="tpu_custom_call" | custom-call | flops 1024 | bytes 1024 | tf_op jit(solution)/shard_map/transpose/pallas_call | solution.py:29
  120.9 3.4 %collective-permute-done.14.refs_0_ = bf16[688,128]{1,0:T(8,128)(2,1)} collective-permute-done((bf16[688,128]{1,0:T(8,128)(2,1)}, bf16[688,128]{1,0:T(8,128)(2,1)}, u32[]{:S(2)}, u32[]{:S(2)}) %collective-permute-start.14) | collective-permute-done | bytes 176160 | tf_op jit(solution)/shard_map/ppermute | solution.py:227
  124.3 13.5 %gradient.7 = (bf16[688,256]{1,0:T(8,128)(2,1)}, bf16[688,256]{1,0:T(8,128)(2,1)}, bf16[688,256]{1,0:T(8,128)(2,1)}, bf16[688,256]{1,0:T(8,128)(2,1)}, bf16[688,...) custom-call(s32[4]{0:T(128)} %broadcast_add_fusion.owners_ref, ...), custom_call_target="tpu_custom_call" | custom-call | flops 1024 | bytes 1024 | tf_op jit(solution)/shard_map/gradient/pallas_call | solution.py:79
  137.8 1.8 collective-permute-start.22
  139.6 3.1 %adam.4 = (f32[688,1024]{1,0:T(8,128)}, f32[688,1024]{1,0:T(8,128)}, bf16[688,256]{1,0:T(8,128)(2,1)}) custom-call(bf16[688,128]{1,0:T(8,128)(2,1)} %collective-permute-done.14.refs_0_, bf16[688,128]{1,0:T(8,128)(2,1)} %get-tuple-element.111.refs_1_, bf16[688,128]{1,0:T(8,128)(2,1)} %collective-permute-done.15.refs_2_, ...), custom_call_target="tpu_custom_call" | custom-call | flops 1024 | bytes 1024 | tf_op jit(solution)/shard_map/adam/pallas_call | solution.py:139
  142.7 8.4 %collective-permute-done.20.arrived_ref = bf16[688,256]{1,0:T(8,128)(2,1)} collective-permute-done((bf16[688,256]{1,0:T(8,128)(2,1)}, bf16[688,256]{1,0:T(8,128)(2,1)}, u32[]{:S(2)}, u32[]{:S(2)}) %collective-permute-start.20) | collective-permute-done | bytes 352288 | tf_op jit(solution)/shard_map/ppermute | solution.py:227
  151.0 1.9 accumulate.14
  153.0 5.6 %collective-permute-done.22.arrived_ref = bf16[688,256]{1,0:T(8,128)(2,1)} collective-permute-done((bf16[688,256]{1,0:T(8,128)(2,1)}, bf16[688,256]{1,0:T(8,128)(2,1)}, u32[]{:S(2)}, u32[]{:S(2)}) %collective-permute-start.22) | collective-permute-done | bytes 352288 | tf_op jit(solution)/shard_map/ppermute | solution.py:227
  158.6 1.9 accumulate.15
  160.5 5.7 %collective-permute-done.21.arrived_ref = bf16[688,256]{1,0:T(8,128)(2,1)} collective-permute-done((bf16[688,256]{1,0:T(8,128)(2,1)}, bf16[688,256]{1,0:T(8,128)(2,1)}, u32[]{:S(2)}, u32[]{:S(2)}) %collective-permute-start.21) | collective-permute-done | bytes 352288 | tf_op jit(solution)/shard_map/ppermute | solution.py:227
  166.2 1.9 accumulate.16
  168.1 5.6 %collective-permute-done.25.arrived_ref = bf16[688,256]{1,0:T(8,128)(2,1)} collective-permute-done((bf16[688,256]{1,0:T(8,128)(2,1)}, bf16[688,256]{1,0:T(8,128)(2,1)}, u32[]{:S(2)}, u32[]{:S(2)}) %collective-permute-start.25) | collective-permute-done | bytes 352288 | tf_op jit(solution)/shard_map/ppermute | solution.py:227
  173.8 1.9 accumulate.17
  175.7 1.5 collective-permute-start.19
  178.7 2.7 %collective-permute-done.24.arrived_ref = bf16[688,256]{1,0:T(8,128)(2,1)} collective-permute-done((bf16[688,256]{1,0:T(8,128)(2,1)}, bf16[688,256]{1,0:T(8,128)(2,1)}, u32[]{:S(2)}, u32[]{:S(2)}) %collective-permute-start.24) | collective-permute-done | bytes 352288 | tf_op jit(solution)/shard_map/ppermute | solution.py:227
  181.3 1.9 accumulate.18
  183.2 5.6 %collective-permute-done.23.refs_0_ = bf16[688,256]{1,0:T(8,128)(2,1)} collective-permute-done((bf16[688,256]{1,0:T(8,128)(2,1)}, bf16[688,256]{1,0:T(8,128)(2,1)}, u32[]{:S(2)}, u32[]{:S(2)}) %collective-permute-start.23) | collective-permute-done | bytes 352288 | tf_op jit(solution)/shard_map/ppermute | solution.py:227
  188.9 1.5 collective-permute-start.30
  190.4 3.1 %adam.5 = (f32[688,1024]{1,0:T(8,128)}, f32[688,1024]{1,0:T(8,128)}, bf16[688,256]{1,0:T(8,128)(2,1)}) custom-call(bf16[688,256]{1,0:T(8,128)(2,1)} %collective-permute-done.23.refs_0_, bf16[688,256]{1,0:T(8,128)(2,1)} %get-tuple-element.128.refs_1_, f32[688,1024]{1,0:T(8,128)} %bitcast.25, ...), custom_call_target="tpu_custom_call", output_to_operand_aliasing={{0}: (4, {}), {1}: (5, {})} | custom-call | flops 1024 | bytes 1024 | tf_op jit(solution)/shard_map/adam/pallas_call | solution.py:139
  193.5 2.9 %collective-permute-done.28.arrived_ref = bf16[688,256]{1,0:T(8,128)(2,1)} collective-permute-done((bf16[688,256]{1,0:T(8,128)(2,1)}, bf16[688,256]{1,0:T(8,128)(2,1)}, u32[]{:S(2)}, u32[]{:S(2)}) %collective-permute-start.28) | collective-permute-done | bytes 352288 | tf_op jit(solution)/shard_map/ppermute | solution.py:227
  196.4 1.9 accumulate.19
  198.3 1.5 collective-permute-start.26
  199.8 1.5 collective-permute-start.33
  201.3 2.7 %collective-permute-done.27.refs_0_ = bf16[688,256]{1,0:T(8,128)(2,1)} collective-permute-done((bf16[688,256]{1,0:T(8,128)(2,1)}, bf16[688,256]{1,0:T(8,128)(2,1)}, u32[]{:S(2)}, u32[]{:S(2)}) %collective-permute-start.27) | collective-permute-done | bytes 352288 | tf_op jit(solution)/shard_map/ppermute | solution.py:227
  204.0 1.5 collective-permute-start.34
  205.5 3.1 %adam.6 = (f32[688,1024]{1,0:T(8,128)}, f32[688,1024]{1,0:T(8,128)}, bf16[688,256]{1,0:T(8,128)(2,1)}) custom-call(bf16[688,256]{1,0:T(8,128)(2,1)} %collective-permute-done.27.refs_0_, bf16[688,256]{1,0:T(8,128)(2,1)} %get-tuple-element.135.refs_1_, f32[688,1024]{1,0:T(8,128)} %bitcast.26, ...), custom_call_target="tpu_custom_call", output_to_operand_aliasing={{0}: (4, {}), {1}: (5, {})} | custom-call | flops 1024 | bytes 1024 | tf_op jit(solution)/shard_map/adam/pallas_call | solution.py:139
  210.2 1.5 collective-permute-start.36
  211.7 3.1 %adam.7 = (f32[688,1024]{1,0:T(8,128)}, f32[688,1024]{1,0:T(8,128)}, bf16[688,256]{1,0:T(8,128)(2,1)}) custom-call(bf16[688,256]{1,0:T(8,128)(2,1)} %collective-permute-done.32.refs_0_, bf16[688,256]{1,0:T(8,128)(2,1)} %get-tuple-element.141.refs_1_, f32[688,1024]{1,0:T(8,128)} %bitcast.27, ...), custom_call_target="tpu_custom_call", output_to_operand_aliasing={{0}: (4, {}), {1}: (5, {})} | custom-call | flops 1024 | bytes 1024 | tf_op jit(solution)/shard_map/adam/pallas_call | solution.py:139
  215.3 3.0 %collective-permute-done.33.refs_1_ = bf16[688,256]{1,0:T(8,128)(2,1)} collective-permute-done((bf16[688,256]{1,0:T(8,128)(2,1)}, bf16[688,256]{1,0:T(8,128)(2,1)}, u32[]{:S(2)}, u32[]{:S(2)}) %collective-permute-start.33) | collective-permute-done | bytes 352288 | tf_op jit(solution)/shard_map/ppermute | solution.py:221
  218.3 4.7 %collective-permute-done.34.refs_1_ = bf16[688,256]{1,0:T(8,128)(2,1)} collective-permute-done((bf16[688,256]{1,0:T(8,128)(2,1)}, bf16[688,256]{1,0:T(8,128)(2,1)}, u32[]{:S(2)}, u32[]{:S(2)}) %collective-permute-start.34) | collective-permute-done | bytes 352288 | tf_op jit(solution)/shard_map/ppermute | solution.py:221
  223.6 1.5 collective-permute-start.37
  227.3 7.0 %expand.4.refs_4_ = f32[4,688,2048]{2,1,0:T(8,128)} custom-call(s32[1]{0:T(128)} %bitcast.9.target_ref, bf16[1024,2048]{1,0:T(8,128)(2,1)} %transpose.7.basis_ref, bf16[688,256]{1,0:T(8,128)(2,1)} %get-tuple-element.114.refs_0_, bf16[688,256]{1,0:T(8,128)(2,1)} %get-tuple-element.131.refs_1_, bf16[688,256]{1,0:T(8,128)(2,1)} %get-tuple-element.139.refs_2_, ...), custom_call_target="tpu_custom_call" | custom-call | flops 1024 | bytes 1024 | tf_op jit(solution)/shard_map/expand/pallas_call | solution.py:171
  234.3 6.7 %collective-permute-done.39.refs_3_ = bf16[688,256]{1,0:T(8,128)(2,1)} collective-permute-done((bf16[688,256]{1,0:T(8,128)(2,1)}, bf16[688,256]{1,0:T(8,128)(2,1)}, u32[]{:S(2)}, u32[]{:S(2)}) %collective-permute-start.39) | collective-permute-done | bytes 352288 | tf_op jit(solution)/shard_map/ppermute | solution.py:221
  241.0 7.0 %expand.5.refs_4_ = f32[4,688,2048]{2,1,0:T(8,128)} custom-call(s32[1]{0:T(128)} %bitcast.8.target_ref, bf16[1024,2048]{1,0:T(8,128)(2,1)} %transpose.7.basis_ref, bf16[688,256]{1,0:T(8,128)(2,1)} %collective-permute-done.29.refs_0_, bf16[688,256]{1,0:T(8,128)(2,1)} %collective-permute-done.33.refs_1_, ...), custom_call_target="tpu_custom_call", output_to_operand_aliasing={{}: (6, {})} | custom-call | flops 1024 | bytes 1024 | tf_op jit(solution)/shard_map/expand/pallas_call | solution.py:171
  247.9 7.0 %expand.6.refs_4_ = f32[4,688,2048]{2,1,0:T(8,128)} custom-call(s32[1]{0:T(128)} %bitcast.7.target_ref, bf16[1024,2048]{1,0:T(8,128)(2,1)} %transpose.7.basis_ref, bf16[688,256]{1,0:T(8,128)(2,1)} %collective-permute-done.30.refs_0_, bf16[688,256]{1,0:T(8,128)(2,1)} %collective-permute-done.34.refs_1_, ...), custom_call_target="tpu_custom_call", output_to_operand_aliasing={{}: (6, {})} | custom-call | flops 1024 | bytes 1024 | tf_op jit(solution)/shard_map/expand/pallas_call | solution.py:171
  254.9 7.0 %expand.7 = f32[4,688,2048]{2,1,0:T(8,128)} custom-call(s32[1]{0:T(128)} %bitcast.target_ref, bf16[1024,2048]{1,0:T(8,128)(2,1)} %transpose.7.basis_ref, bf16[688,256]{1,0:T(8,128)(2,1)} %collective-permute-done.19.refs_0_, bf16[688,256]{1,0:T(8,128)(2,1)} %collective-permute-done.26.refs_1_, ...), custom_call_target="tpu_custom_call", output_to_operand_aliasing={{}: (6, {})} | custom-call | flops 1024 | bytes 1024 | tf_op jit(solution)/shard_map/expand/pallas_call | solution.py:171
  (54 shorter events, 14.2 us)
Async XLA Ops:
  8.6 1.3 copy-start
  10.8 12.1 %collective-permute-start = (bf16[512,256]{1,0:T(8,128)(2,1)}, bf16[512,256]{1,0:T(8,128)(2,1)}, u32[]{:S(2)}, u32[]{:S(2)}) collective-permute-start(bf16[512,256]{1,0:T(8,128)(2,1)} %get-tuple-element.156), channel_id=1, source_target_pairs={{0,1},{1,0},{2,3},{3,2},{4,5},{5,4},{6,7},{7,6},{8,9},{9,8},{10,11... | collective-permute-start | bytes 786440 | tf_op jit(solution)/shard_map/ppermute | solution.py:221
  13.7 9.2 %collective-permute-start.1 = (bf16[512,256]{1,0:T(8,128)(2,1)}, bf16[512,256]{1,0:T(8,128)(2,1)}, u32[]{:S(2)}, u32[]{:S(2)}) collective-permute-start(bf16[512,256]{1,0:T(8,128)(2,1)} %get-tuple-element.155), channel_id=1, source_target_pairs={{0,2},{1,3},{2,0},{3,1},{4,6},{5,7},{6,4},{7,5},{8,10},{9,11},{10,... | collective-permute-start | bytes 786440 | tf_op jit(solution)/shard_map/ppermute | solution.py:221
  30.1 35.0 %collective-permute-start.2 = (bf16[512,768]{1,0:T(8,128)(2,1)}, bf16[512,768]{1,0:T(8,128)(2,1)}, u32[]{:S(2)}, u32[]{:S(2)}) collective-permute-start(bf16[512,768]{1,0:T(8,128)(2,1)} %get-tuple-element.80), channel_id=1, source_target_pairs={{0,1},{1,0},{2,3},{3,2},{4,5},{5,4},{6,7},{7,6},{8,9},{9,8},{10,11... | collective-permute-start | bytes 2359304 | tf_op jit(solution)/shard_map/ppermute | solution.py:221
  30.6 34.5 %collective-permute-start.5 = (bf16[512,768]{1,0:T(8,128)(2,1)}, bf16[512,768]{1,0:T(8,128)(2,1)}, u32[]{:S(2)}, u32[]{:S(2)}) collective-permute-start(bf16[512,768]{1,0:T(8,128)(2,1)} %get-tuple-element.86), channel_id=1, source_target_pairs={{0,2},{1,3},{2,0},{3,1},{4,6},{5,7},{6,4},{7,5},{8,10},{9,11},{10,... | collective-permute-start | bytes 2359304 | tf_op jit(solution)/shard_map/ppermute | solution.py:221
  31.0 23.6 %collective-permute-start.4 = (bf16[512,256]{1,0:T(8,128)(2,1)}, bf16[512,256]{1,0:T(8,128)(2,1)S(1)}, u32[]{:S(2)}, u32[]{:S(2)}) collective-permute-start(bf16[512,256]{1,0:T(8,128)(2,1)} %get-tuple-element.153), channel_id=1, source_target_pairs={{0,1},{1,0},{2,3},{3,2},{4,5},{5,4},{6,7},{7,6},{8,9},{9,8},{10,11... | collective-permute-start | bytes 786440 | tf_op jit(solution)/shard_map/ppermute | solution.py:221
  32.6 22.3 %collective-permute-start.3 = (bf16[512,256]{1,0:T(8,128)(2,1)}, bf16[512,256]{1,0:T(8,128)(2,1)S(1)}, u32[]{:S(2)}, u32[]{:S(2)}) collective-permute-start(bf16[512,256]{1,0:T(8,128)(2,1)} %get-tuple-element.154), channel_id=1, source_target_pairs={{0,2},{1,3},{2,0},{3,1},{4,6},{5,7},{6,4},{7,5},{8,10},{9,11},{10,... | collective-permute-start | bytes 786440 | tf_op jit(solution)/shard_map/ppermute | solution.py:221
  64.6 6.4 %collective-permute-start.6 = (bf16[4,688,128]{2,1,0:T(8,128)(2,1)}, bf16[4,688,128]{2,1,0:T(8,128)(2,1)}, u32[]{:S(2)}, u32[]{:S(2)}) collective-permute-start(bf16[4,688,128]{2,1,0:T(8,128)(2,1)} %get-tuple-element.83), channel_id=1, source_target_pairs={{0,4},{4,0},{8,12},{12,8},{16,20},{20,16},{24,28},{28,24},{1,5},{5... | collective-permute-start | bytes 2113544 | tf_op jit(solution)/shard_map/ppermute | solution.py:224
  64.6 6.4 %collective-permute-start.7 = (bf16[4,688,128]{2,1,0:T(8,128)(2,1)}, bf16[4,688,128]{2,1,0:T(8,128)(2,1)}, u32[]{:S(2)}, u32[]{:S(2)}) collective-permute-start(bf16[4,688,128]{2,1,0:T(8,128)(2,1)} %get-tuple-element.84), channel_id=1, source_target_pairs={{0,4},{4,0},{8,12},{12,8},{16,20},{20,16},{24,28},{28,24},{1,5},{5... | collective-permute-start | bytes 2113544 | tf_op jit(solution)/shard_map/ppermute | solution.py:224
  68.5 25.3 %collective-permute-start.13 = (bf16[512,768]{1,0:T(8,128)(2,1)}, bf16[512,768]{1,0:T(8,128)(2,1)}, u32[]{:S(2)}, u32[]{:S(2)}) collective-permute-start(bf16[512,768]{1,0:T(8,128)(2,1)} %get-tuple-element.149), channel_id=1, source_target_pairs={{0,1},{1,0},{2,3},{3,2},{4,5},{5,4},{6,7},{7,6},{8,9},{9,8},{10,11... | collective-permute-start | bytes 2359304 | tf_op jit(solution)/shard_map/ppermute | solution.py:221
  70.0 26.2 %collective-permute-start.12 = (bf16[512,768]{1,0:T(8,128)(2,1)}, bf16[512,768]{1,0:T(8,128)(2,1)}, u32[]{:S(2)}, u32[]{:S(2)}) collective-permute-start(bf16[512,768]{1,0:T(8,128)(2,1)} %get-tuple-element.150), channel_id=1, source_target_pairs={{0,2},{1,3},{2,0},{3,1},{4,6},{5,7},{6,4},{7,5},{8,10},{9,11},{10,... | collective-permute-start | bytes 2359304 | tf_op jit(solution)/shard_map/ppermute | solution.py:221
  79.4 9.5 %collective-permute-start.9 = (bf16[688,128]{1,0:T(8,128)(2,1)}, bf16[688,128]{1,0:T(8,128)(2,1)}, u32[]{:S(2)}, u32[]{:S(2)}) collective-permute-start(bf16[688,128]{1,0:T(8,128)(2,1)} %get-tuple-element.91), channel_id=1, source_target_pairs={{0,8},{4,12},{8,16},{12,20},{16,24},{20,28},{24,0},{28,4},{1,9},{5... | collective-permute-start | bytes 528392 | tf_op jit(solution)/shard_map/ppermute | solution.py:227
  81.0 10.2 %collective-permute-start.8 = (bf16[688,128]{1,0:T(8,128)(2,1)}, bf16[688,128]{1,0:T(8,128)(2,1)}, u32[]{:S(2)}, u32[]{:S(2)}) collective-permute-start(bf16[688,128]{1,0:T(8,128)(2,1)} %get-tuple-element.89), channel_id=1, source_target_pairs={{0,8},{4,12},{8,16},{12,20},{16,24},{20,28},{24,0},{28,4},{1,9},{5... | collective-permute-start | bytes 528392 | tf_op jit(solution)/shard_map/ppermute | solution.py:227
  90.7 16.9 %collective-permute-start.11 = (bf16[688,128]{1,0:T(8,128)(2,1)}, bf16[688,128]{1,0:T(8,128)(2,1)}, u32[]{:S(2)}, u32[]{:S(2)}) collective-permute-start(bf16[688,128]{1,0:T(8,128)(2,1)} %accumulate.10), channel_id=1, source_target_pairs={{0,8},{4,12},{8,16},{12,20},{16,24},{20,28},{24,0},{28,4},{1,9},{5... | collective-permute-start | bytes 528392 | tf_op jit(solution)/shard_map/ppermute | solution.py:227
  92.9 16.4 %collective-permute-start.10 = (bf16[688,128]{1,0:T(8,128)(2,1)}, bf16[688,128]{1,0:T(8,128)(2,1)}, u32[]{:S(2)}, u32[]{:S(2)}) collective-permute-start(bf16[688,128]{1,0:T(8,128)(2,1)} %accumulate.11), channel_id=1, source_target_pairs={{0,8},{4,12},{8,16},{12,20},{16,24},{20,28},{24,0},{28,4},{1,9},{5... | collective-permute-start | bytes 528392 | tf_op jit(solution)/shard_map/ppermute | solution.py:227
  111.0 13.3 %collective-permute-start.18 = (bf16[4,688,256]{2,1,0:T(8,128)(2,1)}, bf16[4,688,256]{2,1,0:T(8,128)(2,1)}, u32[]{:S(2)}, u32[]{:S(2)}) collective-permute-start(bf16[4,688,256]{2,1,0:T(8,128)(2,1)} %get-tuple-element.108), channel_id=1, source_target_pairs={{0,4},{4,0},{8,12},{12,8},{16,20},{20,16},{24,28},{28,24},{1,5},{5... | collective-permute-start | bytes 4227080 | tf_op jit(solution)/shard_map/ppermute | solution.py:224
  111.0 13.3 %collective-permute-start.17 = (bf16[4,688,256]{2,1,0:T(8,128)(2,1)}, bf16[4,688,256]{2,1,0:T(8,128)(2,1)}, u32[]{:S(2)}, u32[]{:S(2)}) collective-permute-start(bf16[4,688,256]{2,1,0:T(8,128)(2,1)} %get-tuple-element.106), channel_id=1, source_target_pairs={{0,4},{4,0},{8,12},{12,8},{16,20},{20,16},{24,28},{28,24},{1,5},{5... | collective-permute-start | bytes 4227080 | tf_op jit(solution)/shard_map/ppermute | solution.py:224
  111.5 12.8 %collective-permute-start.16 = (bf16[4,688,256]{2,1,0:T(8,128)(2,1)}, bf16[4,688,256]{2,1,0:T(8,128)(2,1)}, u32[]{:S(2)}, u32[]{:S(2)}) collective-permute-start(bf16[4,688,256]{2,1,0:T(8,128)(2,1)} %get-tuple-element.104), channel_id=1, source_target_pairs={{0,4},{4,0},{8,12},{12,8},{16,20},{20,16},{24,28},{28,24},{1,5},{5... | collective-permute-start | bytes 4227080 | tf_op jit(solution)/shard_map/ppermute | solution.py:224
  111.5 9.4 %collective-permute-start.15 = (bf16[688,128]{1,0:T(8,128)(2,1)}, bf16[688,128]{1,0:T(8,128)(2,1)}, u32[]{:S(2)}, u32[]{:S(2)}) collective-permute-start(bf16[688,128]{1,0:T(8,128)(2,1)} %accumulate.13), channel_id=1, source_target_pairs={{0,8},{4,12},{8,16},{12,20},{16,24},{20,28},{24,0},{28,4},{1,9},{5... | collective-permute-start | bytes 528392 | tf_op jit(solution)/shard_map/ppermute | solution.py:227
  113.1 11.2 %collective-permute-start.14 = (bf16[688,128]{1,0:T(8,128)(2,1)}, bf16[688,128]{1,0:T(8,128)(2,1)}, u32[]{:S(2)}, u32[]{:S(2)}) collective-permute-start(bf16[688,128]{1,0:T(8,128)(2,1)} %accumulate.12), channel_id=1, source_target_pairs={{0,8},{4,12},{8,16},{12,20},{16,24},{20,28},{24,0},{28,4},{1,9},{5... | collective-permute-start | bytes 528392 | tf_op jit(solution)/shard_map/ppermute | solution.py:227
  137.8 13.3 %collective-permute-start.20 = (bf16[688,256]{1,0:T(8,128)(2,1)}, bf16[688,256]{1,0:T(8,128)(2,1)}, u32[]{:S(2)}, u32[]{:S(2)}) collective-permute-start(bf16[688,256]{1,0:T(8,128)(2,1)} %get-tuple-element.115), channel_id=1, source_target_pairs={{0,8},{4,12},{8,16},{12,20},{16,24},{20,28},{24,0},{28,4},{1,9},{5... | collective-permute-start | bytes 1056776 | tf_op jit(solution)/shard_map/ppermute | solution.py:227
  137.8 20.8 %collective-permute-start.22 = (bf16[688,256]{1,0:T(8,128)(2,1)}, bf16[688,256]{1,0:T(8,128)(2,1)}, u32[]{:S(2)}, u32[]{:S(2)}) collective-permute-start(bf16[688,256]{1,0:T(8,128)(2,1)} %get-tuple-element.109), channel_id=1, source_target_pairs={{0,8},{4,12},{8,16},{12,20},{16,24},{20,28},{24,0},{28,4},{1,9},{5... | collective-permute-start | bytes 1056776 | tf_op jit(solution)/shard_map/ppermute | solution.py:227
  152.9 13.3 %collective-permute-start.21 = (bf16[688,256]{1,0:T(8,128)(2,1)}, bf16[688,256]{1,0:T(8,128)(2,1)}, u32[]{:S(2)}, u32[]{:S(2)}) collective-permute-start(bf16[688,256]{1,0:T(8,128)(2,1)} %accumulate.14), channel_id=1, source_target_pairs={{0,8},{4,12},{8,16},{12,20},{16,24},{20,28},{24,0},{28,4},{1,9},{5... | collective-permute-start | bytes 1056776 | tf_op jit(solution)/shard_map/ppermute | solution.py:227
  153.0 20.8 %collective-permute-start.25 = (bf16[688,256]{1,0:T(8,128)(2,1)}, bf16[688,256]{1,0:T(8,128)(2,1)}, u32[]{:S(2)}, u32[]{:S(2)}) collective-permute-start(bf16[688,256]{1,0:T(8,128)(2,1)} %get-tuple-element.120), channel_id=1, source_target_pairs={{0,8},{4,12},{8,16},{12,20},{16,24},{20,28},{24,0},{28,4},{1,9},{5... | collective-permute-start | bytes 1056776 | tf_op jit(solution)/shard_map/ppermute | solution.py:227
  160.5 20.8 %collective-permute-start.24 = (bf16[688,256]{1,0:T(8,128)(2,1)}, bf16[688,256]{1,0:T(8,128)(2,1)}, u32[]{:S(2)}, u32[]{:S(2)}) collective-permute-start(bf16[688,256]{1,0:T(8,128)(2,1)} %accumulate.15), channel_id=1, source_target_pairs={{0,8},{4,12},{8,16},{12,20},{16,24},{20,28},{24,0},{28,4},{1,9},{5... | collective-permute-start | bytes 1056776 | tf_op jit(solution)/shard_map/ppermute | solution.py:227
  168.1 20.7 %collective-permute-start.23 = (bf16[688,256]{1,0:T(8,128)(2,1)}, bf16[688,256]{1,0:T(8,128)(2,1)}, u32[]{:S(2)}, u32[]{:S(2)}) collective-permute-start(bf16[688,256]{1,0:T(8,128)(2,1)} %accumulate.16), channel_id=1, source_target_pairs={{0,8},{4,12},{8,16},{12,20},{16,24},{20,28},{24,0},{28,4},{1,9},{5... | collective-permute-start | bytes 1056776 | tf_op jit(solution)/shard_map/ppermute | solution.py:227
  175.7 20.8 %collective-permute-start.28 = (bf16[688,256]{1,0:T(8,128)(2,1)}, bf16[688,256]{1,0:T(8,128)(2,1)}, u32[]{:S(2)}, u32[]{:S(2)}) collective-permute-start(bf16[688,256]{1,0:T(8,128)(2,1)} %accumulate.17), channel_id=1, source_target_pairs={{0,8},{4,12},{8,16},{12,20},{16,24},{20,28},{24,0},{28,4},{1,9},{5... | collective-permute-start | bytes 1056776 | tf_op jit(solution)/shard_map/ppermute | solution.py:227
  175.7 22.7 %collective-permute-start.19 = (bf16[688,256]{1,0:T(8,128)(2,1)}, bf16[688,256]{1,0:T(8,128)(2,1)}, u32[]{:S(2)}, u32[]{:S(2)}) collective-permute-start(bf16[688,256]{1,0:T(8,128)(2,1)} %get-tuple-element.114.refs_0_), channel_id=1, source_target_pairs={{0,3},{1,2},{2,1},{3,0},{4,7},{5,6},{6,5},{7,4},{8,11},{9,10},{10,... | collective-permute-start | bytes 1056776 | tf_op jit(solution)/shard_map/ppermute | solution.py:221
  177.2 22.7 %collective-permute-start.29 = (bf16[688,256]{1,0:T(8,128)(2,1)}, bf16[688,256]{1,0:T(8,128)(2,1)}, u32[]{:S(2)}, u32[]{:S(2)}) collective-permute-start(bf16[688,256]{1,0:T(8,128)(2,1)} %get-tuple-element.114.refs_0_), channel_id=1, source_target_pairs={{0,1},{1,0},{2,3},{3,2},{4,5},{5,4},{6,7},{7,6},{8,9},{9,8},{10,11... | collective-permute-start | bytes 1056776 | tf_op jit(solution)/shard_map/ppermute | solution.py:221
  183.2 20.7 %collective-permute-start.27 = (bf16[688,256]{1,0:T(8,128)(2,1)}, bf16[688,256]{1,0:T(8,128)(2,1)}, u32[]{:S(2)}, u32[]{:S(2)}) collective-permute-start(bf16[688,256]{1,0:T(8,128)(2,1)} %accumulate.18), channel_id=1, source_target_pairs={{0,8},{4,12},{8,16},{12,20},{16,24},{20,28},{24,0},{28,4},{1,9},{5... | collective-permute-start | bytes 1056776 | tf_op jit(solution)/shard_map/ppermute | solution.py:227
  188.9 19.7 %collective-permute-start.30 = (bf16[688,256]{1,0:T(8,128)(2,1)}, bf16[688,256]{1,0:T(8,128)(2,1)}, u32[]{:S(2)}, u32[]{:S(2)}) collective-permute-start(bf16[688,256]{1,0:T(8,128)(2,1)} %get-tuple-element.114.refs_0_), channel_id=1, source_target_pairs={{0,2},{1,3},{2,0},{3,1},{4,6},{5,7},{6,4},{7,5},{8,10},{9,11},{10,... | collective-permute-start | bytes 1056776 | tf_op jit(solution)/shard_map/ppermute | solution.py:221
  198.3 11.8 %collective-permute-start.32 = (bf16[688,256]{1,0:T(8,128)(2,1)}, bf16[688,256]{1,0:T(8,128)(2,1)}, u32[]{:S(2)}, u32[]{:S(2)}) collective-permute-start(bf16[688,256]{1,0:T(8,128)(2,1)} %accumulate.19), channel_id=1, source_target_pairs={{0,8},{4,12},{8,16},{12,20},{16,24},{20,28},{24,0},{28,4},{1,9},{5... | collective-permute-start | bytes 1056776 | tf_op jit(solution)/shard_map/ppermute | solution.py:227
  198.3 16.4 %collective-permute-start.26 = (bf16[688,256]{1,0:T(8,128)(2,1)}, bf16[688,256]{1,0:T(8,128)(2,1)}, u32[]{:S(2)}, u32[]{:S(2)}) collective-permute-start(bf16[688,256]{1,0:T(8,128)(2,1)} %get-tuple-element.131.refs_1_), channel_id=1, source_target_pairs={{0,3},{1,2},{2,1},{3,0},{4,7},{5,6},{6,5},{7,4},{8,11},{9,10},{10,... | collective-permute-start | bytes 1056776 | tf_op jit(solution)/shard_map/ppermute | solution.py:221
  199.8 18.5 %collective-permute-start.33 = (bf16[688,256]{1,0:T(8,128)(2,1)}, bf16[688,256]{1,0:T(8,128)(2,1)}, u32[]{:S(2)}, u32[]{:S(2)}) collective-permute-start(bf16[688,256]{1,0:T(8,128)(2,1)} %get-tuple-element.131.refs_1_), channel_id=1, source_target_pairs={{0,1},{1,0},{2,3},{3,2},{4,5},{5,4},{6,7},{7,6},{8,9},{9,8},{10,11... | collective-permute-start | bytes 1056776 | tf_op jit(solution)/shard_map/ppermute | solution.py:221
  204.0 19.1 %collective-permute-start.34 = (bf16[688,256]{1,0:T(8,128)(2,1)}, bf16[688,256]{1,0:T(8,128)(2,1)}, u32[]{:S(2)}, u32[]{:S(2)}) collective-permute-start(bf16[688,256]{1,0:T(8,128)(2,1)} %get-tuple-element.131.refs_1_), channel_id=1, source_target_pairs={{0,2},{1,3},{2,0},{3,1},{4,6},{5,7},{6,4},{7,5},{8,10},{9,11},{10,... | collective-permute-start | bytes 1056776 | tf_op jit(solution)/shard_map/ppermute | solution.py:221
  208.6 17.2 %collective-permute-start.31 = (bf16[688,256]{1,0:T(8,128)(2,1)}, bf16[688,256]{1,0:T(8,128)(2,1)}, u32[]{:S(2)}, u32[]{:S(2)}) collective-permute-start(bf16[688,256]{1,0:T(8,128)(2,1)} %get-tuple-element.139.refs_2_), channel_id=1, source_target_pairs={{0,3},{1,2},{2,1},{3,0},{4,7},{5,6},{6,5},{7,4},{8,11},{9,10},{10,... | collective-permute-start | bytes 1056776 | tf_op jit(solution)/shard_map/ppermute | solution.py:221
  210.2 24.1 %collective-permute-start.36 = (bf16[688,256]{1,0:T(8,128)(2,1)}, bf16[688,256]{1,0:T(8,128)(2,1)}, u32[]{:S(2)}, u32[]{:S(2)}) collective-permute-start(bf16[688,256]{1,0:T(8,128)(2,1)} %get-tuple-element.139.refs_2_), channel_id=1, source_target_pairs={{0,2},{1,3},{2,0},{3,1},{4,6},{5,7},{6,4},{7,5},{8,10},{9,11},{10,... | collective-permute-start | bytes 1056776 | tf_op jit(solution)/shard_map/ppermute | solution.py:221
  214.8 19.5 %collective-permute-start.38 = (bf16[688,256]{1,0:T(8,128)(2,1)}, bf16[688,256]{1,0:T(8,128)(2,1)}, u32[]{:S(2)}, u32[]{:S(2)}) collective-permute-start(bf16[688,256]{1,0:T(8,128)(2,1)} %get-tuple-element.139.refs_2_), channel_id=1, source_target_pairs={{0,1},{1,0},{2,3},{3,2},{4,5},{5,4},{6,7},{7,6},{8,9},{9,8},{10,11... | collective-permute-start | bytes 1056776 | tf_op jit(solution)/shard_map/ppermute | solution.py:221
  223.1 17.9 %collective-permute-start.39 = (bf16[688,256]{1,0:T(8,128)(2,1)}, bf16[688,256]{1,0:T(8,128)(2,1)}, u32[]{:S(2)}, u32[]{:S(2)}) collective-permute-start(bf16[688,256]{1,0:T(8,128)(2,1)} %get-tuple-element.145.refs_3_), channel_id=1, source_target_pairs={{0,1},{1,0},{2,3},{3,2},{4,5},{5,4},{6,7},{7,6},{8,9},{9,8},{10,11... | collective-permute-start | bytes 1056776 | tf_op jit(solution)/shard_map/ppermute | solution.py:221
  223.6 24.3 %collective-permute-start.37 = (bf16[688,256]{1,0:T(8,128)(2,1)}, bf16[688,256]{1,0:T(8,128)(2,1)}, u32[]{:S(2)}, u32[]{:S(2)}) collective-permute-start(bf16[688,256]{1,0:T(8,128)(2,1)} %get-tuple-element.145.refs_3_), channel_id=1, source_target_pairs={{0,2},{1,3},{2,0},{3,1},{4,6},{5,7},{6,4},{7,5},{8,10},{9,11},{10,... | collective-permute-start | bytes 1056776 | tf_op jit(solution)/shard_map/ppermute | solution.py:221
  225.8 29.1 %collective-permute-start.35 = (bf16[688,256]{1,0:T(8,128)(2,1)}, bf16[688,256]{1,0:T(8,128)(2,1)}, u32[]{:S(2)}, u32[]{:S(2)}) collective-permute-start(bf16[688,256]{1,0:T(8,128)(2,1)} %get-tuple-element.145.refs_3_), channel_id=1, source_target_pairs={{0,3},{1,2},{2,1},{3,0},{4,7},{5,6},{6,5},{7,4},{8,11},{9,10},{10,... | collective-permute-start | bytes 1056776 | tf_op jit(solution)/shard_map/ppermute | solution.py:221

commit v5 on v4

v5 whole, which is shorter than its diff:
```python
import functools

import jax
import jax.numpy as jnp
from jax import lax
from jax.experimental import pallas as pl
from jax.experimental.pallas import tpu as pltpu
from jax.sharding import PartitionSpec as P

beta_first = 0.9
beta_second = 0.999
adam_count = 100.0
epsilon = 1e-08

F32 = jnp.float32
BF16 = jnp.bfloat16
COST = pl.CostEstimate(flops=1024, bytes_accessed=1 << 20, transcendentals=0)
PARAMS = pltpu.CompilerParams(vmem_limit_bytes=40 * 1024 * 1024)
RING_PARAMS = pltpu.CompilerParams(vmem_limit_bytes=64 * 1024 * 1024)


def transpose(value, block, begin=0, count=None, held=()):
    rows, columns = value.shape
    count = rows // block if count is None else count

    def kernel(value_ref, *refs):
        refs[-1][...] = value_ref[...].T

    return pl.pallas_call(
        kernel,
        out_shape=jax.ShapeDtypeStruct((columns, rows), value.dtype),
        grid=(count,),
        in_specs=[pl.BlockSpec((block, columns), lambda i: (begin + i, 0))]
        + [pl.BlockSpec(memory_space=pl.ANY)] * len(held),
        out_specs=pl.BlockSpec((columns, block), lambda i: (0, begin + i)),
        input_output_aliases={1: 0} if held else {},
        compiler_params=PARAMS,
        cost_estimate=COST,
        name="transpose",
    )(value, *held)


def plus(one, two):
    rows, width = one.shape
    block = pl.BlockSpec((rows // 2, width), lambda i: (i, 0))

    def kernel(one_ref, two_ref, out_ref):
        out_ref[...] = (one_ref[...].astype(F32) + two_ref[...].astype(F32)).astype(BF16)

    return pl.pallas_call(
        kernel,
        grid=(2,),
        out_shape=jax.ShapeDtypeStruct(one.shape, BF16),
        in_specs=[block, block],
        out_specs=block,
        compiler_params=RING_PARAMS,
        cost_estimate=COST,
        name="plus",
    )(one, two)


def gradient(grads_t, pieces, owners, cuts):
    _, owned, tokens = grads_t.shape
    rows, run = pieces[0].shape
    width = run * len(pieces) // 2
    count = owners.shape[0]

    def kernel(owners_ref, *refs):
        piece_refs, grads_ref, refs = refs[: len(pieces)], refs[len(pieces)], refs[len(pieces) + 1 :]
        out_refs, (whole_ref, held_ref, sems) = refs[:-3], refs[-3:]
        step = pl.program_id(0)

        def fetch(block):
            return pltpu.make_async_copy(grads_ref.at[owners_ref[block]], held_ref.at[block], sems.at[block])

        @pl.when(step == 0)
        def _():
            for block in range(count):
                fetch(block).start()
            for index, piece_ref in enumerate(piece_refs):
                row, column = index % 2 * rows, index // 2 * run
                whole_ref[row : row + rows, column : column + run] = piece_ref[...]

        fetch(step).wait()
        value = jnp.dot(held_ref[step], whole_ref[...], preferred_element_type=F32).astype(BF16)
        for out_ref, cut in zip(out_refs, cuts):
            out_ref[0] = value[cut]

    shapes = [(cut[0].stop - cut[0].start, cut[1].stop - cut[1].start) for cut in cuts]
    return pl.pallas_call(
        kernel,
        out_shape=[jax.ShapeDtypeStruct((count, *shape), BF16) for shape in shapes],
        grid_spec=pltpu.PrefetchScalarGridSpec(
            num_scalar_prefetch=1,
            grid=(count,),
            in_specs=[pl.BlockSpec((rows, run), lambda i, owners_ref: (0, 0))] * len(pieces)
            + [pl.BlockSpec(memory_space=pl.ANY)],
            out_specs=[pl.BlockSpec((1, *shape), lambda i, owners_ref: (i, 0, 0)) for shape in shapes],
            scratch_shapes=[
                pltpu.VMEM((tokens, width), BF16),
                pltpu.VMEM((count, owned, tokens), BF16),
                pltpu.SemaphoreType.DMA((count,)),
            ],
        ),
        compiler_params=RING_PARAMS,
        cost_estimate=COST,
        name="gradient",
    )(owners, *pieces, grads_t)


def accumulate(arrived, own, coming, hop):
    _, rows, width = own.shape

    def kernel(*refs):
        total = refs[0][0].astype(F32) + refs[1][0].astype(F32)
        if arrived:
            total = total + refs[2][...].astype(F32)
        refs[-1][...] = total.astype(BF16)

    block = pl.BlockSpec((1, rows, width), lambda i: (hop, 0, 0))
    return pl.pallas_call(
        kernel,
        grid=(1,),
        out_shape=jax.ShapeDtypeStruct((rows, width), BF16),
        in_specs=[block, block] + [pl.BlockSpec(memory_space=pltpu.VMEM)] * len(arrived),
        out_specs=pl.BlockSpec(memory_space=pltpu.VMEM),
        compiler_params=RING_PARAMS,
        cost_estimate=COST,
        name="accumulate",
    )(own, coming, *arrived)


def adam(pieces, first, second, held, begin):
    owned, rank = first.shape
    count, rows, _ = pieces[0][1].shape
    widths = [piece[0].shape[1] for piece in pieces]
    width = sum(widths)

    def kernel(*refs):
        first_ref, second_ref = refs[3 * len(pieces) : 3 * len(pieces) + 2]
        first_out, second_out, direction_out = refs[-3:]
        at = 0
        for index, size in enumerate(widths):
            arrived_ref, own_ref, other_ref = refs[3 * index : 3 * index + 3]
            columns = slice(at, at + size)
            at += size
            grad_low = arrived_ref[...].astype(F32) + own_ref[0].astype(F32) + other_ref[0].astype(F32)
            first_next = beta_first * first_ref[:, columns] + (1.0 - beta_first) * grad_low
            second_next = beta_second * second_ref[:, columns] + (1.0 - beta_second) * grad_low * grad_low
            first_out[:, columns] = first_next
            second_out[:, columns] = second_next
            bias_first = 1.0 - beta_first**adam_count
            bias_second = 1.0 - beta_second**adam_count
            direction = first_next / bias_first / (jnp.sqrt(second_next / bias_second) + epsilon)
            direction_out[:, columns] = direction.astype(BF16)

    rectangle = pl.BlockSpec((pl.Element(rows), pl.Element(width)), lambda i: begin)
    piece_specs = []
    for size in widths:
        piece_specs += [pl.BlockSpec(memory_space=pltpu.VMEM)]
        piece_specs += [pl.BlockSpec((1, rows, size), lambda i: (count - 1, 0, 0))] * 2
    inputs = len(piece_specs) + 2
    return pl.pallas_call(
        kernel,
        grid=(1,),
        out_shape=[
            jax.ShapeDtypeStruct((owned, rank), F32),
            jax.ShapeDtypeStruct((owned, rank), F32),
            jax.ShapeDtypeStruct((rows, width), BF16),
        ],
        in_specs=piece_specs + [rectangle, rectangle] + [pl.BlockSpec(memory_space=pl.ANY)] * len(held),
        out_specs=[rectangle, rectangle, pl.BlockSpec((rows, width), lambda i: (0, 0))],
        input_output_aliases={inputs + index: index for index in range(len(held))},
        compiler_params=RING_PARAMS,
        cost_estimate=COST,
        name="adam",
    )(*[array for piece in pieces for array in piece], first, second, *held)


def expand(targets, starts, rests, begin, basis_t, held, owned):
    rows, width = rests[0].shape
    rank, features = basis_t.shape
    count = len(starts)
    block = min(512, features)

    def kernel(targets_ref, basis_ref, *refs):
        start_refs, rest_refs = refs[:count], refs[count : 2 * count]
        out_ref, whole_ref = refs[-2:]

        @pl.when(pl.program_id(0) == 0)
        def _():
            for index in range(count):
                whole_ref[index, :, : rank - width] = start_refs[index][...]
                whole_ref[index, :, rank - width :] = rest_refs[index][...]

        for index in range(count):
            out_ref[targets_ref[index]] = jnp.dot(whole_ref[index], basis_ref[...], preferred_element_type=F32)

    return pl.pallas_call(
        kernel,
        out_shape=jax.ShapeDtypeStruct((count, owned, features), F32),
        grid_spec=pltpu.PrefetchScalarGridSpec(
            num_scalar_prefetch=1,
            grid=(features // block,),
            in_specs=[pl.BlockSpec((rank, block), lambda i, targets_ref: (0, i))]
            + [pl.BlockSpec((pl.Element(rows), pl.Element(rank - width)), lambda i, targets_ref: (begin, 0))] * count
            + [pl.BlockSpec((rows, width), lambda i, targets_ref: (0, 0))] * count
            + [pl.BlockSpec(memory_space=pl.ANY)] * len(held),
            out_specs=pl.BlockSpec(
                (pl.Element(count), pl.Element(rows), pl.Element(block)),
                lambda i, targets_ref: (0, begin, i * block),
            ),
            scratch_shapes=[pltpu.VMEM((count, rows, rank), BF16)],
        ),
        input_output_aliases={2 + 2 * count: 0} if held else {},
        compiler_params=RING_PARAMS,
        cost_estimate=COST,
        name="expand",
    )(targets, basis_t, *starts, *rests, *held)


def total_of(*terms):
    total = terms[0].astype(F32)
    for term in terms[1:]:
        total = total + term.astype(F32)
    return total.astype(BF16)


def after(value, *earlier):
    return lax.optimization_barrier((value, *jax.tree.leaves(earlier)))[0]


def local(activations, out_grads, projector, first_moment, second_moment):
    owned = first_moment.shape[1]
    features = activations[0]
    basis = projector[0]
    rank = basis.shape[1]
    tokens = features.shape[0]
    dp_count, fsdp_count = lax.axis_size("dp"), lax.axis_size("fsdp")
    dp, fsdp = lax.axis_index("dp"), lax.axis_index("fsdp")
    chips = dp_count // 2
    chip, core = dp // 2, dp % 2
    width = rank // 4

    offsets = [1 << bit for bit in range(fsdp_count.bit_length() - 1)]
    order = jnp.stack([fsdp ^ offset for offset in range(fsdp_count)]).astype(jnp.int32)
    hops = chips - 1
    ring_order = (chip - 1 - jnp.arange(chips, dtype=jnp.int32) + chips) % chips
    own_owners = (ring_order * 2 + core).astype(jnp.int32)
    other_owners = (ring_order * 2 + 1 - core).astype(jnp.int32)

    def across(value, offset):
        return lax.ppermute(value, "fsdp", [(index, index ^ offset) for index in range(fsdp_count)])

    def sibling(value):
        return lax.ppermute(value, "dp", [(index, index ^ 1) for index in range(dp_count)])

    def onward(value):
        return lax.ppermute(value, "dp", [(index, (index + 2) % dp_count) for index in range(dp_count)])

    def exchange(halves, step):
        return [across(half, offsets[step if index % 2 == 0 else -1 - step]) for index, half in enumerate(halves)]

    def add(halves, arrived, plus=total_of):
        return [plus(half, term) for half, term in zip(halves, arrived)]

    partial = jnp.dot(features, basis, preferred_element_type=F32).astype(BF16)
    low, high = partial[: tokens // 2], partial[tokens // 2 :]
    sums_0 = [low[:, :width], high[:, :width]]
    middle = (width + rank) // 2
    sums_1 = [half[:, run] for run in (slice(width, middle), slice(middle, rank)) for half in (low, high)]
    coming_0 = exchange(sums_0, 0)
    block = tokens // 4
    grads_t = transpose(after(out_grads[0], *sums_0), block, 0, 2)
    sums_0 = add(sums_0, [after(term, grads_t) for term in coming_0])
    for step in range(1, len(offsets) - 1):
        sums_0 = add(sums_0, exchange(sums_0, step))
    coming_0 = exchange(sums_0, len(offsets) - 1)
    grads_t = transpose(after(out_grads[0], *sums_0), block, 2, 2, (grads_t,)).reshape(dp_count, owned, tokens)
    sums_0 = add(sums_0, [after(term, grads_t) for term in coming_0])
    coming_1 = exchange([after(half, *sums_0) for half in sums_1], 0)

    cuts_0 = [(slice(0, owned), slice(0, width))]
    ends = [0, owned]
    if owned % 16 == 0:
        ends = [-(-owned * index // 48) * 16 for index in range(4)]
    rows_1 = [slice(*pair) for pair in zip(ends, ends[1:])]
    cuts_1 = [(rows, slice(0, rank - width)) for rows in rows_1]

    def ring(parts, stride, token, between, finish):
        events = sorted(
            (2 * hop + stride * part, part, hop)
            for part in range(len(parts))
            for hop in range(hops + (finish is not None))
        )
        arrived = [None] * len(parts)
        for number, (_, part, hop) in enumerate(events):
            if hop == hops:
                token = finish(part, after(arrived[part], token))
            else:
                own, coming = parts[part]
                before = () if arrived[part] is None else (arrived[part],)
                token = accumulate(before, after(own, token), coming, hop)
                arrived[part] = onward(token)
            if number in between:
                token = between[number](token)
        return token, arrived

    held = ()
    directions = []

    def step_of(pieces, begin):
        nonlocal held
        first_next, second_next, direction = adam(pieces, first_moment[0], second_moment[0], held, begin)
        held = (first_next, second_next)
        directions.append([direction])
        return direction

    def gather(part, *earlier):
        sent = after(directions[part][0], *earlier) if earlier else directions[part][0]
        directions[part] += [across(sent, offset) for offset in range(1, fsdp_count)]

    other = gradient(grads_t, sums_0, other_owners, cuts_0)
    coming = [sibling(value) for value in other]
    own = gradient(after(grads_t, *other), sums_0, own_owners, cuts_0)
    parts_0 = list(zip(own, coming))
    rest = {}

    def second_exchange(token):
        sums = add(sums_1, [after(term, token) for term in coming_1], plus)
        for step in range(1, len(offsets) - 1):
            sums = add(sums, exchange(sums, step), plus)
        rest["sums"], rest["coming"] = sums, exchange(sums, len(offsets) - 1)
        return sums[1]

    def start_rest(token):
        sums = add(rest["sums"], [after(term, token) for term in rest["coming"]], plus)
        rest["sums"] = sums
        rest["other"] = gradient(grads_t, sums, other_owners, cuts_1)
        return rest["other"][0]

    token, last_0 = ring(parts_0, 1, own[0], {0: second_exchange, 1: start_rest}, None)
    coming = [sibling(after(value, token)) for value in rest["other"]]
    own = gradient(after(grads_t, token), rest["sums"], own_owners, cuts_1)
    parts_1 = list(zip(own, coming))
    pieces = [(after(value, own[0]), *part) for value, part in zip(last_0, parts_0)]
    token = step_of(pieces, (0, 0))

    def turn_basis(token):
        rest["basis_t"] = transpose(after(basis, token), min(512, basis.shape[0]))
        return rest["basis_t"]

    def send_first(token):
        gather(0, token)
        return token

    def have_first(token):
        return [token, *directions[0]]

    def finish_1(part, arrived):
        token = step_of([(arrived, *parts_1[part])], (rows_1[part].start, width))
        gather(part + 1, *(directions[part - 1] if part > 1 else ()))
        return token

    first_send, first_wait = (1, 4)
    between = {2: turn_basis, first_send: send_first, first_wait: have_first}
    token, _ = ring(parts_1, 1.5, token, between, finish_1)

    update = ()
    for rows, gathered in zip(rows_1, directions[1:]):
        gathered = [after(gathered[0], token), *gathered[1:]]
        update = (expand(order, directions[0], gathered, rows.start, rest["basis_t"], update, owned),)
    return (update[0][None], held[0][None], held[1][None])


def solution(mesh):
    in_specs = (
        P(None, "dp", "fsdp"),
        P(None, "dp", "fsdp"),
        P(None, "fsdp", None),
        P(None, ("fsdp", "dp"), None),
        P(None, ("fsdp", "dp"), None),
    )
    out_specs = (
        P(None, None, "dp", "fsdp"),
        P(None, ("fsdp", "dp"), None),
        P(None, ("fsdp", "dp"), None),
    )
    return jax.shard_map(local, mesh=mesh, in_specs=in_specs, out_specs=out_specs, check_vma=False)
```

time: 263 us -> 234 us (0.89)
  waiting for transfers between devices: 86.5 us -> 37.7 us
  local copies, waits for them, and re-layouts: 4.8 us -> 19.7 us
  other arithmetic: 14.9 us -> 3.54 us
  Pallas kernels: 111 us -> 122 us
  starting transfers between devices: 36 us -> 41.1 us
    ppermute x20 -> x24, waiting for transfers between devices: 35.4 us -> 6.1 us  [across(): lax.ppermute(value, 'fsdp', [(index, index ^ offset) for index in range(f...]
    ppermute x15 -> x12, waiting for transfers between devices: 51.1 us -> 31.6 us  [onward(): lax.ppermute(value, 'dp', [(index, (index + 2) % dp_count) for index in r...]
    pallas_call x14 -> x24, Pallas kernels: 55.3 us -> 71.1 us  [the longest x4 31.4 us: gradient(): pl.pallas_call(kernel, out_shape=[jax.ShapeDtypeStruct((count, *shape), B...]
    unnamed x2 -> x12, local copies, waits for them, and re-layouts: 1.31 us -> 17.1 us
    convert_element_type x6 -> x3, other arithmetic: 13.8 us -> 1.74 us  [total_of(): return total.astype(BF16)]
    pallas_call x3, Pallas kernels: 15.4 us -> 9.93 us  [transpose(): pl.pallas_call(kernel, out_shape=jax.ShapeDtypeStruct((columns, rows), va...]
    ppermute x20 -> x24, starting transfers between devices: 25.6 us -> 29 us  [across(): lax.ppermute(value, 'fsdp', [(index, index ^ offset) for index in range(f...]
    ppermute x15 -> x12, starting transfers between devices: 9.4 us -> 11.5 us  [onward(): lax.ppermute(value, 'dp', [(index, (index + 2) % dp_count) for index in r...]
  transfers between devices with their start and end apart: 40 -> 40, of which waited for: 19 -> 9; matrix products, arithmetic and copies ran while one was open for 6% -> 2% of each run, Pallas kernels for 32% -> 45%
where the time goes in v5:
time: 234 us; the launch traced here: 233 us
  Pallas kernels  122 us (52%)
  starting transfers between devices  41.1 us (18%)
  waiting for transfers between devices  37.7 us (16%)
  local copies, waits for them, and re-layouts  19.7 us (8%)
  matrix products  7.95 us (3%)
  other arithmetic  3.54 us (2%)
    ppermute x12, waiting for transfers between devices, onward(): lax.ppermute(value, 'dp', [(index, (index + 2) % dp_count) for index in r...  31.6 us
    pallas_call x4, Pallas kernels, gradient(): pl.pallas_call(kernel, out_shape=[jax.ShapeDtypeStruct((count, *shape), B...  31.4 us
    ppermute x24, starting transfers between devices, across(): lax.ppermute(value, 'fsdp', [(index, index ^ offset) for index in range(f...  29 us
    pallas_call x3, Pallas kernels, expand(): pl.pallas_call(kernel, out_shape=jax.ShapeDtypeStruct((count, owned, feat...  28 us
    pallas_call x12, Pallas kernels, accumulate(): pl.pallas_call(kernel, grid=(1,), out_shape=jax.ShapeDtypeStruct((rows, w...  24.1 us
    unnamed x12, local copies, waits for them, and re-layouts  17.1 us
    pallas_call x8, Pallas kernels, plus(): pl.pallas_call(kernel, grid=(2,), out_shape=jax.ShapeDtypeStruct(one.shap...  15.6 us
    pallas_call x4, Pallas kernels, adam(): pl.pallas_call(kernel, grid=(1,), out_shape=[jax.ShapeDtypeStruct((owned,...  13.1 us
  transfers between devices with their start and end apart: 40, of which 9 were waited for; matrix products, arithmetic and copies ran while one was open for 2% of the time, Pallas kernels for 45%

profile of v5, /device:TPU:0, one launch (start us, length us, event | category | flops | bytes accessed | tf_op | source)
XLA Modules:
  0.0 232.9 jit_solution(2197518887557219729)
XLA Ops:
  0.6 8.0 %fusion.2 = bf16[1024,1024]{1,0:T(8,128)(2,1)S(1)} fusion(bf16[1,1024,2048]{2,1,0:T(8,128)(2,1)} %param.5, bf16[1,2048,1024]{2,1,0:T(8,128)(2,1)} %param.7), kind=kOutput, calls=%fused_computation.2 | convolution fusion | flops 4296015872 | bytes 10485760 | tf_op jit(solution)/shard_map/dot_general | solution.py:267
  8.7 3.0 %collective-permute-start.2 = (bf16[512,256]{1,0:T(8,128)(2,1)S(1)}, bf16[512,256]{1,0:T(8,128)(2,1)S(1)}, u32[]{:S(2)}, u32[]{:S(2)}) collective-permute-start(bf16[512,256]{1,0:T(8,128)(2,1)S(1)} %get-tuple-element.135), channel_id=1, source_target_pairs={{0,2},{1,3},{2,0},{3,1},{4,6},{5,7},{6,4},{7,5},{8,10},{9,11},{10,... | collective-permute-start | bytes 786440 | tf_op jit(solution)/shard_map/ppermute | solution.py:253
  11.7 1.5 collective-permute-start
  13.2 4.1 %transpose.5.refs_0_ = bf16[5504,1024]{1,0:T(8,128)(2,1)S(1)} custom-call(bf16[1024,5504]{1,0:T(8,128)(2,1)} %bitcast.25), custom_call_target="tpu_custom_call" | custom-call | flops 1024 | bytes 1048576 | tf_op jit(solution)/shard_map/transpose/pallas_call | solution.py:29
  17.4 4.3 %copy-done = bf16[5504,1024]{1,0:T(8,128)(2,1)} copy-done((bf16[5504,1024]{1,0:T(8,128)(2,1)}, bf16[5504,1024]{1,0:T(8,128)(2,1)S(1)}, u32[]{:S(2)}) %copy-start) | copy-done | bytes 11272216
  23.1 4.2 %copy-done.1 = bf16[5504,1024]{1,0:T(8,128)(2,1)S(1)} copy-done((bf16[5504,1024]{1,0:T(8,128)(2,1)S(1)}, bf16[5504,1024]{1,0:T(8,128)(2,1)}, u32[]{:S(2)}) %copy-start.1) | copy-done | bytes 11272216
  27.3 4.2 %transpose.6 = bf16[5504,1024]{1,0:T(8,128)(2,1)S(1)} custom-call(bf16[1024,5504]{1,0:T(8,128)(2,1)} %bitcast.26, bf16[5504,1024]{1,0:T(8,128)(2,1)S(1)} %copy-done.1), custom_call_target="tpu_custom_call", output_to_operand_aliasing={{}: (1, {})} | custom-call | flops 1024 | bytes 1048576 | tf_op jit(solution)/shard_map/transpose/pallas_call | solution.py:29
  31.5 4.3 %copy-done.2 = bf16[5504,1024]{1,0:T(8,128)(2,1)} copy-done((bf16[5504,1024]{1,0:T(8,128)(2,1)}, bf16[5504,1024]{1,0:T(8,128)(2,1)S(1)}, u32[]{:S(2)}) %copy-start.2) | copy-done | bytes 11272216
  37.4 6.2 %gradient.4 = bf16[4,688,256]{2,1,0:T(8,128)(2,1)} custom-call(s32[4]{0:T(128)} %add_subtract_fusion.owners_ref, bf16[512,256]{1,0:T(8,128)(2,1)} %add_convert_fusion.1.refs_0_, bf16[512,256]{1,0:T(8,128)(2,1)} %add_convert_fusion.refs_1_, bf16[8,688,1024]{2,1,0:T(8,128)(2,1)} %bitcast.19), custom_call_target="tpu_custom_call" | custom-call | flops 1024 | bytes 1048576 | tf_op jit(solution)/shard_map/gradient/pallas_call | solution.py:90
  43.7 2.6 %fusion.8 = (bf16[512,384]{1,0:T(8,128)(2,1)}, bf16[512,384]{1,0:T(8,128)(2,1)}, bf16[512,384]{1,0:T(8,128)(2,1)}, bf16[512,384]{1,0:T(8,128)(2,1)}) fusion(bf16[1024,1024]{1,0:T(8,128)(2,1)} %copy-done.5), kind=kLoop, calls=%fused_computation.16 | loop fusion | bytes 3145728 | tf_op jit(solution)/shard_map/slice | solution.py:271
  46.2 1.9 collective-permute-start.4
  48.2 1.5 collective-permute-start.7
  50.9 6.3 %gradient.5.refs_0_.refs_1_ = bf16[4,688,256]{2,1,0:T(8,128)(2,1)} custom-call(s32[4]{0:T(128)} %broadcast_add_fusion.owners_ref, bf16[512,256]{1,0:T(8,128)(2,1)} %add_convert_fusion.1.refs_0_, bf16[512,256]{1,0:T(8,128)(2,1)} %add_convert_fusion.refs_1_, bf16[8,688,1024]{2,1,0:T(8,128)(2,1)} %bitcast.20), custom_call_target="tpu_custom_call" | custom-call | flops 1024 | bytes 1048576 | tf_op jit(solution)/shard_map/gradient/pallas_call | solution.py:90
  57.2 1.9 accumulate.12
  59.1 2.0 collective-permute-start.8
  61.1 1.9 plus.8.one_ref
  63.0 1.5 collective-permute-start.6
  64.6 1.9 plus.9.one_ref
  66.5 1.5 collective-permute-start.9
  68.0 2.0 plus.12.one_ref
  70.5 1.9 plus.14.one_ref
  73.9 2.1 accumulate.13
  75.9 1.6 collective-permute-start.14
  77.5 1.9 plus.10.refs_0_
  79.4 2.0 plus.11.refs_1_
  81.4 3.6 %collective-permute-done.11.two_ref = bf16[512,384]{1,0:T(8,128)(2,1)} collective-permute-done((bf16[512,384]{1,0:T(8,128)(2,1)}, bf16[512,384]{1,0:T(8,128)(2,1)}, u32[]{:S(2)}, u32[]{:S(2)}) %collective-permute-start.11) | collective-permute-done | bytes 393248 | tf_op jit(solution)/shard_map/ppermute | solution.py:253
  85.0 2.0 plus.13.refs_2_
  87.0 2.0 plus.15.refs_3_
  88.9 9.4 %gradient.6 = (bf16[4,240,768]{2,1,0:T(8,128)(2,1)}, bf16[4,224,768]{2,1,0:T(8,128)(2,1)}, bf16[4,224,768]{2,1,0:T(8,128)(2,1)}) custom-call(s32[4]{0:T(128)} %add_subtract_fusion.owners_ref, bf16[512,384]{1,0:T(8,128)(2,1)} %plus.10.refs_0_, bf16[512,384]{1,0:T(8,128)(2,1)} %plus.11.refs_1_, bf16[512,384]{1,0:T(8,128)(2,1)} %plus.13.refs_2_, ...), custom_call_target="tpu_custom_call" | custom-call | flops 1024 | bytes 1048576 | tf_op jit(solution)/shard_map/gradient/pallas_call | solution.py:90
  98.4 2.1 accumulate.14
  100.9 1.6 collective-permute-start.15
  102.5 9.5 %gradient.7 = (bf16[4,240,768]{2,1,0:T(8,128)(2,1)}, bf16[4,224,768]{2,1,0:T(8,128)(2,1)}, bf16[4,224,768]{2,1,0:T(8,128)(2,1)}) custom-call(s32[4]{0:T(128)} %broadcast_add_fusion.owners_ref, bf16[512,384]{1,0:T(8,128)(2,1)} %plus.10.refs_0_, bf16[512,384]{1,0:T(8,128)(2,1)} %plus.11.refs_1_, bf16[512,384]{1,0:T(8,128)(2,1)} %plus.13.refs_2_, ...), custom_call_target="tpu_custom_call" | custom-call | flops 1024 | bytes 1048576 | tf_op jit(solution)/shard_map/gradient/pallas_call | solution.py:90
  112.0 1.7 collective-permute-done.15.refs_0_
  113.8 3.3 %adam.4 = (f32[688,1024]{1,0:T(8,128)}, f32[688,1024]{1,0:T(8,128)}, bf16[688,256]{1,0:T(8,128)(2,1)}) custom-call(bf16[688,256]{1,0:T(8,128)(2,1)} %collective-permute-done.15.refs_0_, bf16[4,688,256]{2,1,0:T(8,128)(2,1)} %gradient.5.refs_0_.refs_1_, bf16[4,688,256]{2,1,0:T(8,128)(2,1)} %collective-permute-done.5.refs_1_.refs_2_, f32[688,1024]{1,0:T(8,128)} %bitcast.27, ...), custom_call_target="tpu_custom_call" | custom-call | flops 1024 | bytes 1048576 | tf_op jit(solution)/shard_map/adam/pallas_call | solution.py:163
  117.0 1.9 accumulate.15
  118.9 1.9 accumulate.16
  120.9 1.5 collective-permute-start.21
  123.8 8.8 %collective-permute-done.18.refs_2_ = bf16[240,768]{1,0:T(8,128)(2,1)} collective-permute-done((bf16[240,768]{1,0:T(8,128)(2,1)}, bf16[240,768]{1,0:T(8,128)(2,1)}, u32[]{:S(2)}, u32[]{:S(2)}) %collective-permute-start.18) | collective-permute-done | bytes 368672 | tf_op jit(solution)/shard_map/ppermute | solution.py:259
  132.5 2.1 accumulate.17
  134.6 1.5 collective-permute-start.20
  136.7 2.2 copy-done.4
  138.9 1.6 transpose.7.basis_ref
  140.5 2.0 copy-done.3
  142.5 1.9 accumulate.18
  144.4 2.1 accumulate.19
  147.6 2.1 accumulate.20
  149.6 3.9 %collective-permute-start.25 = (bf16[240,768]{1,0:T(8,128)(2,1)}, bf16[240,768]{1,0:T(8,128)(2,1)}, u32[]{:S(2)}, u32[]{:S(2)}) collective-permute-start(bf16[240,768]{1,0:T(8,128)(2,1)} %accumulate.20), channel_id=1, source_target_pairs={{0,8},{4,12},{8,16},{12,20},{16,24},{20,28},{24,0},{28,4},{1,9},{5... | collective-permute-start | bytes 1105928 | tf_op jit(solution)/shard_map/ppermute | solution.py:259
  153.5 4.0 %collective-permute-done.26.refs_2_ = bf16[224,768]{1,0:T(8,128)(2,1)} collective-permute-done((bf16[224,768]{1,0:T(8,128)(2,1)}, bf16[224,768]{1,0:T(8,128)(2,1)}, u32[]{:S(2)}, u32[]{:S(2)}) %collective-permute-start.26) | collective-permute-done | bytes 344096 | tf_op jit(solution)/shard_map/ppermute | solution.py:259
  157.5 2.0 accumulate.21
  159.6 5.3 %collective-permute-done.27.refs_2_ = bf16[224,768]{1,0:T(8,128)(2,1)} collective-permute-done((bf16[224,768]{1,0:T(8,128)(2,1)}, bf16[224,768]{1,0:T(8,128)(2,1)}, u32[]{:S(2)}, u32[]{:S(2)}) %collective-permute-start.27) | collective-permute-done | bytes 344096 | tf_op jit(solution)/shard_map/ppermute | solution.py:259
  164.9 2.0 accumulate.22
  166.9 5.9 %collective-permute-done.25.refs_0_ = bf16[240,768]{1,0:T(8,128)(2,1)} collective-permute-done((bf16[240,768]{1,0:T(8,128)(2,1)}, bf16[240,768]{1,0:T(8,128)(2,1)}, u32[]{:S(2)}, u32[]{:S(2)}) %collective-permute-start.25) | collective-permute-done | bytes 368672 | tf_op jit(solution)/shard_map/ppermute | solution.py:259
  172.8 3.4 %adam.5 = (f32[688,1024]{1,0:T(8,128)}, f32[688,1024]{1,0:T(8,128)}, bf16[240,768]{1,0:T(8,128)(2,1)}) custom-call(bf16[240,768]{1,0:T(8,128)(2,1)} %collective-permute-done.25.refs_0_, bf16[4,240,768]{2,1,0:T(8,128)(2,1)} %get-tuple-element.107.refs_0_.refs_1_, ...), custom_call_target="tpu_custom_call", output_to_operand_aliasing={{0}: (5, {}), {1}: (6, {})} | custom-call | flops 1024 | bytes 1048576 | tf_op jit(solution)/shard_map/adam/pallas_call | solution.py:163
  177.6 1.5 collective-permute-start.32
  180.2 2.0 accumulate.23
  182.2 5.3 %collective-permute-done.30.refs_0_ = bf16[224,768]{1,0:T(8,128)(2,1)} collective-permute-done((bf16[224,768]{1,0:T(8,128)(2,1)}, bf16[224,768]{1,0:T(8,128)(2,1)}, u32[]{:S(2)}, u32[]{:S(2)}) %collective-permute-start.30) | collective-permute-done | bytes 344096 | tf_op jit(solution)/shard_map/ppermute | solution.py:259
  187.5 3.2 %adam.6 = (f32[688,1024]{1,0:T(8,128)}, f32[688,1024]{1,0:T(8,128)}, bf16[224,768]{1,0:T(8,128)(2,1)}) custom-call(bf16[224,768]{1,0:T(8,128)(2,1)} %collective-permute-done.30.refs_0_, bf16[4,224,768]{2,1,0:T(8,128)(2,1)} %get-tuple-element.109.refs_0_.refs_1_, ...), custom_call_target="tpu_custom_call", output_to_operand_aliasing={{0}: (5, {}), {1}: (6, {})} | custom-call | flops 1024 | bytes 1048576 | tf_op jit(solution)/shard_map/adam/pallas_call | solution.py:163
  193.5 3.2 %adam.7 = (f32[688,1024]{1,0:T(8,128)}, f32[688,1024]{1,0:T(8,128)}, bf16[224,768]{1,0:T(8,128)(2,1)}) custom-call(bf16[224,768]{1,0:T(8,128)(2,1)} %collective-permute-done.29.refs_0_, bf16[4,224,768]{2,1,0:T(8,128)(2,1)} %get-tuple-element.114.refs_0_.refs_1_, ...), custom_call_target="tpu_custom_call", output_to_operand_aliasing={{0}: (5, {}), {1}: (6, {})} | custom-call | flops 1024 | bytes 1048576 | tf_op jit(solution)/shard_map/adam/pallas_call | solution.py:163
  197.5 1.4 collective-permute-start.36
  200.3 2.5 %collective-permute-done.39.refs_7_ = bf16[224,768]{1,0:T(8,128)(2,1)} collective-permute-done((bf16[224,768]{1,0:T(8,128)(2,1)}, bf16[224,768]{1,0:T(8,128)(2,1)}, u32[]{:S(2)}, u32[]{:S(2)}) %collective-permute-start.39) | collective-permute-done | bytes 344096 | tf_op jit(solution)/shard_map/ppermute | solution.py:253
  202.7 1.5 collective-permute-start.34
  204.9 9.5 %expand.3.refs_8_ = f32[4,688,2048]{2,1,0:T(8,128)} custom-call(s32[4]{0:T(128)} %pad_add_fusion.targets_ref, bf16[1024,2048]{1,0:T(8,128)(2,1)} %copy-done.3, bf16[688,256]{1,0:T(8,128)(2,1)} %get-tuple-element.101.refs_0_, bf16[688,256]{1,0:T(8,128)(2,1)} %collective-permute-done.19.refs_1_, bf16[688,256]{1,0:T(8,128)(2,1)} %collective-permute-done.20.refs_2_, ...), custom_call_target="tpu_custom_call" | custom-call | flops 1024 | bytes 1048576 | tf_op jit(solution)/shard_map/expand/pallas_call | solution.py:199
  214.4 9.2 %expand.4.refs_8_ = f32[4,688,2048]{2,1,0:T(8,128)} custom-call(s32[4]{0:T(128)} %pad_add_fusion.targets_ref, bf16[1024,2048]{1,0:T(8,128)(2,1)} %copy-done.3, bf16[688,256]{1,0:T(8,128)(2,1)} %get-tuple-element.101.refs_0_, bf16[688,256]{1,0:T(8,128)(2,1)} %collective-permute-done.19.refs_1_, ...), custom_call_target="tpu_custom_call", output_to_operand_aliasing={{}: (10, {})} | custom-call | flops 1024 | bytes 1048576 | tf_op jit(solution)/shard_map/expand/pallas_call | solution.py:199
  223.7 9.2 %expand.5 = f32[4,688,2048]{2,1,0:T(8,128)} custom-call(s32[4]{0:T(128)} %pad_add_fusion.targets_ref, bf16[1024,2048]{1,0:T(8,128)(2,1)} %copy-done.3, bf16[688,256]{1,0:T(8,128)(2,1)} %get-tuple-element.101.refs_0_, bf16[688,256]{1,0:T(8,128)(2,1)} %collective-permute-done.19.refs_1_, ...), custom_call_target="tpu_custom_call", output_to_operand_aliasing={{}: (10, {})} | custom-call | flops 1024 | bytes 1048576 | tf_op jit(solution)/shard_map/expand/pallas_call | solution.py:199
  (71 shorter events, 17.9 us)
Async XLA Ops:
  8.6 13.1 %copy-start.5 = (bf16[1024,1024]{1,0:T(8,128)(2,1)}, bf16[1024,1024]{1,0:T(8,128)(2,1)S(1)}, u32[]{:S(2)}) copy-start(bf16[1024,1024]{1,0:T(8,128)(2,1)S(1)} %fusion.2) | copy-start | bytes 6291460
  8.7 13.0 %collective-permute-start.2 = (bf16[512,256]{1,0:T(8,128)(2,1)S(1)}, bf16[512,256]{1,0:T(8,128)(2,1)S(1)}, u32[]{:S(2)}, u32[]{:S(2)}) collective-permute-start(bf16[512,256]{1,0:T(8,128)(2,1)S(1)} %get-tuple-element.135), channel_id=1, source_target_pairs={{0,2},{1,3},{2,0},{3,1},{4,6},{5,7},{6,4},{7,5},{8,10},{9,11},{10,... | collective-permute-start | bytes 786440 | tf_op jit(solution)/shard_map/ppermute | solution.py:253
  11.7 10.0 %collective-permute-start = (bf16[512,256]{1,0:T(8,128)(2,1)S(1)}, bf16[512,256]{1,0:T(8,128)(2,1)S(1)}, u32[]{:S(2)}, u32[]{:S(2)}) collective-permute-start(bf16[512,256]{1,0:T(8,128)(2,1)S(1)} %get-tuple-element.136), channel_id=1, source_target_pairs={{0,1},{1,0},{2,3},{3,2},{4,5},{5,4},{6,7},{7,6},{8,9},{9,8},{10,11... | collective-permute-start | bytes 786440 | tf_op jit(solution)/shard_map/ppermute | solution.py:253
  17.4 4.3 %copy-start = (bf16[5504,1024]{1,0:T(8,128)(2,1)}, bf16[5504,1024]{1,0:T(8,128)(2,1)S(1)}, u32[]{:S(2)}) copy-start(bf16[5504,1024]{1,0:T(8,128)(2,1)S(1)} %transpose.5.refs_0_) | copy-start | bytes 33816580
  21.9 13.9 %collective-permute-start.3 = (bf16[512,256]{1,0:T(8,128)(2,1)S(1)}, bf16[512,256]{1,0:T(8,128)(2,1)S(1)}, u32[]{:S(2)}, u32[]{:S(2)}) collective-permute-start(bf16[512,256]{1,0:T(8,128)(2,1)S(1)} %get-tuple-element.133), channel_id=1, source_target_pairs={{0,1},{1,0},{2,3},{3,2},{4,5},{5,4},{6,7},{7,6},{8,9},{9,8},{10,11... | collective-permute-start | bytes 786440 | tf_op jit(solution)/shard_map/ppermute | solution.py:253
  22.5 14.1 %collective-permute-start.1 = (bf16[512,256]{1,0:T(8,128)(2,1)S(1)}, bf16[512,256]{1,0:T(8,128)(2,1)S(1)}, u32[]{:S(2)}, u32[]{:S(2)}) collective-permute-start(bf16[512,256]{1,0:T(8,128)(2,1)S(1)} %get-tuple-element.134), channel_id=1, source_target_pairs={{0,2},{1,3},{2,0},{3,1},{4,6},{5,7},{6,4},{7,5},{8,10},{9,11},{10,... | collective-permute-start | bytes 786440 | tf_op jit(solution)/shard_map/ppermute | solution.py:253
  23.1 4.2 %copy-start.1 = (bf16[5504,1024]{1,0:T(8,128)(2,1)S(1)}, bf16[5504,1024]{1,0:T(8,128)(2,1)}, u32[]{:S(2)}) copy-start(bf16[5504,1024]{1,0:T(8,128)(2,1)} %copy-done) | copy-start | bytes 33816580
  31.5 4.3 %copy-start.2 = (bf16[5504,1024]{1,0:T(8,128)(2,1)}, bf16[5504,1024]{1,0:T(8,128)(2,1)S(1)}, u32[]{:S(2)}) copy-start(bf16[5504,1024]{1,0:T(8,128)(2,1)S(1)} %transpose.6) | copy-start | bytes 33816580
  43.6 13.6 %collective-permute-start.5 = (bf16[4,688,256]{2,1,0:T(8,128)(2,1)}, bf16[4,688,256]{2,1,0:T(8,128)(2,1)}, u32[]{:S(2)}, u32[]{:S(2)}) collective-permute-start(bf16[4,688,256]{2,1,0:T(8,128)(2,1)} %gradient.4), channel_id=1, source_target_pairs={{0,4},{4,0},{8,12},{12,8},{16,20},{20,16},{24,28},{28,24},{1,5},{5... | collective-permute-start | bytes 4227080 | tf_op jit(solution)/shard_map/ppermute | solution.py:256
  46.2 14.8 %collective-permute-start.4 = (bf16[512,384]{1,0:T(8,128)(2,1)}, bf16[512,384]{1,0:T(8,128)(2,1)}, u32[]{:S(2)}, u32[]{:S(2)}) collective-permute-start(bf16[512,384]{1,0:T(8,128)(2,1)} %get-tuple-element.72.one_ref), channel_id=1, source_target_pairs={{0,1},{1,0},{2,3},{3,2},{4,5},{5,4},{6,7},{7,6},{8,9},{9,8},{10,11... | collective-permute-start | bytes 1179656 | tf_op jit(solution)/shard_map/ppermute | solution.py:253
  48.2 14.9 %collective-permute-start.7 = (bf16[512,384]{1,0:T(8,128)(2,1)}, bf16[512,384]{1,0:T(8,128)(2,1)}, u32[]{:S(2)}, u32[]{:S(2)}) collective-permute-start(bf16[512,384]{1,0:T(8,128)(2,1)} %get-tuple-element.76.one_ref), channel_id=1, source_target_pairs={{0,2},{1,3},{2,0},{3,1},{4,6},{5,7},{6,4},{7,5},{8,10},{9,11},{10,... | collective-permute-start | bytes 1179656 | tf_op jit(solution)/shard_map/ppermute | solution.py:253
  49.7 18.3 %collective-permute-start.10 = (bf16[512,384]{1,0:T(8,128)(2,1)}, bf16[512,384]{1,0:T(8,128)(2,1)}, u32[]{:S(2)}, u32[]{:S(2)}) collective-permute-start(bf16[512,384]{1,0:T(8,128)(2,1)} %get-tuple-element.81.one_ref), channel_id=1, source_target_pairs={{0,1},{1,0},{2,3},{3,2},{4,5},{5,4},{6,7},{7,6},{8,9},{9,8},{10,11... | collective-permute-start | bytes 1179656 | tf_op jit(solution)/shard_map/ppermute | solution.py:253
  50.2 20.3 %collective-permute-start.12 = (bf16[512,384]{1,0:T(8,128)(2,1)}, bf16[512,384]{1,0:T(8,128)(2,1)}, u32[]{:S(2)}, u32[]{:S(2)}) collective-permute-start(bf16[512,384]{1,0:T(8,128)(2,1)} %get-tuple-element.84.one_ref), channel_id=1, source_target_pairs={{0,2},{1,3},{2,0},{3,1},{4,6},{5,7},{6,4},{7,5},{8,10},{9,11},{10,... | collective-permute-start | bytes 1179656 | tf_op jit(solution)/shard_map/ppermute | solution.py:253
  59.1 14.7 %collective-permute-start.8 = (bf16[688,256]{1,0:T(8,128)(2,1)}, bf16[688,256]{1,0:T(8,128)(2,1)}, u32[]{:S(2)}, u32[]{:S(2)}) collective-permute-start(bf16[688,256]{1,0:T(8,128)(2,1)} %accumulate.12), channel_id=1, source_target_pairs={{0,8},{4,12},{8,16},{12,20},{16,24},{20,28},{24,0},{28,4},{1,9},{5... | collective-permute-start | bytes 1056776 | tf_op jit(solution)/shard_map/ppermute | solution.py:259
  63.0 14.4 %collective-permute-start.6 = (bf16[512,384]{1,0:T(8,128)(2,1)}, bf16[512,384]{1,0:T(8,128)(2,1)}, u32[]{:S(2)}, u32[]{:S(2)}) collective-permute-start(bf16[512,384]{1,0:T(8,128)(2,1)} %plus.8.one_ref), channel_id=1, source_target_pairs={{0,2},{1,3},{2,0},{3,1},{4,6},{5,7},{6,4},{7,5},{8,10},{9,11},{10,... | collective-permute-start | bytes 1179656 | tf_op jit(solution)/shard_map/ppermute | solution.py:253
  66.5 12.9 %collective-permute-start.9 = (bf16[512,384]{1,0:T(8,128)(2,1)}, bf16[512,384]{1,0:T(8,128)(2,1)}, u32[]{:S(2)}, u32[]{:S(2)}) collective-permute-start(bf16[512,384]{1,0:T(8,128)(2,1)} %plus.9.one_ref), channel_id=1, source_target_pairs={{0,1},{1,0},{2,3},{3,2},{4,5},{5,4},{6,7},{7,6},{8,9},{9,8},{10,11... | collective-permute-start | bytes 1179656 | tf_op jit(solution)/shard_map/ppermute | solution.py:253
  70.0 15.0 %collective-permute-start.11 = (bf16[512,384]{1,0:T(8,128)(2,1)}, bf16[512,384]{1,0:T(8,128)(2,1)}, u32[]{:S(2)}, u32[]{:S(2)}) collective-permute-start(bf16[512,384]{1,0:T(8,128)(2,1)} %plus.12.one_ref), channel_id=1, source_target_pairs={{0,2},{1,3},{2,0},{3,1},{4,6},{5,7},{6,4},{7,5},{8,10},{9,11},{10,... | collective-permute-start | bytes 1179656 | tf_op jit(solution)/shard_map/ppermute | solution.py:253
  72.4 14.5 %collective-permute-start.13 = (bf16[512,384]{1,0:T(8,128)(2,1)}, bf16[512,384]{1,0:T(8,128)(2,1)}, u32[]{:S(2)}, u32[]{:S(2)}) collective-permute-start(bf16[512,384]{1,0:T(8,128)(2,1)} %plus.14.one_ref), channel_id=1, source_target_pairs={{0,1},{1,0},{2,3},{3,2},{4,5},{5,4},{6,7},{7,6},{8,9},{9,8},{10,11... | collective-permute-start | bytes 1179656 | tf_op jit(solution)/shard_map/ppermute | solution.py:253
  75.9 22.4 %collective-permute-start.14 = (bf16[688,256]{1,0:T(8,128)(2,1)}, bf16[688,256]{1,0:T(8,128)(2,1)}, u32[]{:S(2)}, u32[]{:S(2)}) collective-permute-start(bf16[688,256]{1,0:T(8,128)(2,1)} %accumulate.13), channel_id=1, source_target_pairs={{0,8},{4,12},{8,16},{12,20},{16,24},{20,28},{24,0},{28,4},{1,9},{5... | collective-permute-start | bytes 1056776 | tf_op jit(solution)/shard_map/ppermute | solution.py:259
  100.4 16.6 %collective-permute-start.16 = (bf16[4,240,768]{2,1,0:T(8,128)(2,1)}, bf16[4,240,768]{2,1,0:T(8,128)(2,1)}, u32[]{:S(2)}, u32[]{:S(2)}) collective-permute-start(bf16[4,240,768]{2,1,0:T(8,128)(2,1)} %get-tuple-element.95), channel_id=1, source_target_pairs={{0,4},{4,0},{8,12},{12,8},{16,20},{20,16},{24,28},{28,24},{1,5},{5... | collective-permute-start | bytes 4423688 | tf_op jit(solution)/shard_map/ppermute | solution.py:256
  100.4 18.5 %collective-permute-start.17 = (bf16[4,224,768]{2,1,0:T(8,128)(2,1)}, bf16[4,224,768]{2,1,0:T(8,128)(2,1)}, u32[]{:S(2)}, u32[]{:S(2)}) collective-permute-start(bf16[4,224,768]{2,1,0:T(8,128)(2,1)} %get-tuple-element.98), channel_id=1, source_target_pairs={{0,4},{4,0},{8,12},{12,8},{16,20},{20,16},{24,28},{28,24},{1,5},{5... | collective-permute-start | bytes 4128776 | tf_op jit(solution)/shard_map/ppermute | solution.py:256
  100.9 35.2 %collective-permute-start.22 = (bf16[4,224,768]{2,1,0:T(8,128)(2,1)}, bf16[4,224,768]{2,1,0:T(8,128)(2,1)}, u32[]{:S(2)}, u32[]{:S(2)}) collective-permute-start(bf16[4,224,768]{2,1,0:T(8,128)(2,1)} %get-tuple-element.105), channel_id=1, source_target_pairs={{0,4},{4,0},{8,12},{12,8},{16,20},{20,16},{24,28},{28,24},{1,5},{5... | collective-permute-start | bytes 4128776 | tf_op jit(solution)/shard_map/ppermute | solution.py:256
  100.9 12.8 %collective-permute-start.15 = (bf16[688,256]{1,0:T(8,128)(2,1)}, bf16[688,256]{1,0:T(8,128)(2,1)}, u32[]{:S(2)}, u32[]{:S(2)}) collective-permute-start(bf16[688,256]{1,0:T(8,128)(2,1)} %accumulate.14), channel_id=1, source_target_pairs={{0,8},{4,12},{8,16},{12,20},{16,24},{20,28},{24,0},{28,4},{1,9},{5... | collective-permute-start | bytes 1056776 | tf_op jit(solution)/shard_map/ppermute | solution.py:259
  118.9 13.6 %collective-permute-start.18 = (bf16[240,768]{1,0:T(8,128)(2,1)}, bf16[240,768]{1,0:T(8,128)(2,1)}, u32[]{:S(2)}, u32[]{:S(2)}) collective-permute-start(bf16[240,768]{1,0:T(8,128)(2,1)} %accumulate.15), channel_id=1, source_target_pairs={{0,8},{4,12},{8,16},{12,20},{16,24},{20,28},{24,0},{28,4},{1,9},{5... | collective-permute-start | bytes 1105928 | tf_op jit(solution)/shard_map/ppermute | solution.py:259
  120.9 25.6 %collective-permute-start.21 = (bf16[688,256]{1,0:T(8,128)(2,1)}, bf16[688,256]{1,0:T(8,128)(2,1)}, u32[]{:S(2)}, u32[]{:S(2)}) collective-permute-start(bf16[688,256]{1,0:T(8,128)(2,1)} %get-tuple-element.101.refs_0_), channel_id=1, source_target_pairs={{0,3},{1,2},{2,1},{3,0},{4,7},{5,6},{6,5},{7,4},{8,11},{9,10},{10,... | collective-permute-start | bytes 1056776 | tf_op jit(solution)/shard_map/ppermute | solution.py:253
  122.3 22.0 %collective-permute-start.23 = (bf16[224,768]{1,0:T(8,128)(2,1)}, bf16[224,768]{1,0:T(8,128)(2,1)}, u32[]{:S(2)}, u32[]{:S(2)}) collective-permute-start(bf16[224,768]{1,0:T(8,128)(2,1)} %accumulate.16), channel_id=1, source_target_pairs={{0,8},{4,12},{8,16},{12,20},{16,24},{20,28},{24,0},{28,4},{1,9},{5... | collective-permute-start | bytes 1032200 | tf_op jit(solution)/shard_map/ppermute | solution.py:259
  134.6 12.9 %collective-permute-start.24 = (bf16[240,768]{1,0:T(8,128)(2,1)}, bf16[240,768]{1,0:T(8,128)(2,1)}, u32[]{:S(2)}, u32[]{:S(2)}) collective-permute-start(bf16[240,768]{1,0:T(8,128)(2,1)} %accumulate.17), channel_id=1, source_target_pairs={{0,8},{4,12},{8,16},{12,20},{16,24},{20,28},{24,0},{28,4},{1,9},{5... | collective-permute-start | bytes 1105928 | tf_op jit(solution)/shard_map/ppermute | solution.py:259
  134.6 12.9 %collective-permute-start.20 = (bf16[688,256]{1,0:T(8,128)(2,1)}, bf16[688,256]{1,0:T(8,128)(2,1)}, u32[]{:S(2)}, u32[]{:S(2)}) collective-permute-start(bf16[688,256]{1,0:T(8,128)(2,1)} %get-tuple-element.101.refs_0_), channel_id=1, source_target_pairs={{0,2},{1,3},{2,0},{3,1},{4,6},{5,7},{6,4},{7,5},{8,10},{9,11},{10,... | collective-permute-start | bytes 1056776 | tf_op jit(solution)/shard_map/ppermute | solution.py:253
  136.1 11.4 %collective-permute-start.19 = (bf16[688,256]{1,0:T(8,128)(2,1)}, bf16[688,256]{1,0:T(8,128)(2,1)}, u32[]{:S(2)}, u32[]{:S(2)}) collective-permute-start(bf16[688,256]{1,0:T(8,128)(2,1)} %get-tuple-element.101.refs_0_), channel_id=1, source_target_pairs={{0,1},{1,0},{2,3},{3,2},{4,5},{5,4},{6,7},{7,6},{8,9},{9,8},{10,11... | collective-permute-start | bytes 1056776 | tf_op jit(solution)/shard_map/ppermute | solution.py:253
  136.7 2.2 copy-start.4
  140.5 2.0 copy-start.3
  144.4 13.1 %collective-permute-start.26 = (bf16[224,768]{1,0:T(8,128)(2,1)}, bf16[224,768]{1,0:T(8,128)(2,1)}, u32[]{:S(2)}, u32[]{:S(2)}) collective-permute-start(bf16[224,768]{1,0:T(8,128)(2,1)} %accumulate.18), channel_id=1, source_target_pairs={{0,8},{4,12},{8,16},{12,20},{16,24},{20,28},{24,0},{28,4},{1,9},{5... | collective-permute-start | bytes 1032200 | tf_op jit(solution)/shard_map/ppermute | solution.py:259
  146.5 18.4 %collective-permute-start.27 = (bf16[224,768]{1,0:T(8,128)(2,1)}, bf16[224,768]{1,0:T(8,128)(2,1)}, u32[]{:S(2)}, u32[]{:S(2)}) collective-permute-start(bf16[224,768]{1,0:T(8,128)(2,1)} %accumulate.19), channel_id=1, source_target_pairs={{0,8},{4,12},{8,16},{12,20},{16,24},{20,28},{24,0},{28,4},{1,9},{5... | collective-permute-start | bytes 1032200 | tf_op jit(solution)/shard_map/ppermute | solution.py:259
  149.6 23.1 %collective-permute-start.25 = (bf16[240,768]{1,0:T(8,128)(2,1)}, bf16[240,768]{1,0:T(8,128)(2,1)}, u32[]{:S(2)}, u32[]{:S(2)}) collective-permute-start(bf16[240,768]{1,0:T(8,128)(2,1)} %accumulate.20), channel_id=1, source_target_pairs={{0,8},{4,12},{8,16},{12,20},{16,24},{20,28},{24,0},{28,4},{1,9},{5... | collective-permute-start | bytes 1105928 | tf_op jit(solution)/shard_map/ppermute | solution.py:259
  159.6 20.6 %collective-permute-start.28 = (bf16[224,768]{1,0:T(8,128)(2,1)}, bf16[224,768]{1,0:T(8,128)(2,1)}, u32[]{:S(2)}, u32[]{:S(2)}) collective-permute-start(bf16[224,768]{1,0:T(8,128)(2,1)} %accumulate.21), channel_id=1, source_target_pairs={{0,8},{4,12},{8,16},{12,20},{16,24},{20,28},{24,0},{28,4},{1,9},{5... | collective-permute-start | bytes 1032200 | tf_op jit(solution)/shard_map/ppermute | solution.py:259
  166.9 20.6 %collective-permute-start.30 = (bf16[224,768]{1,0:T(8,128)(2,1)}, bf16[224,768]{1,0:T(8,128)(2,1)}, u32[]{:S(2)}, u32[]{:S(2)}) collective-permute-start(bf16[224,768]{1,0:T(8,128)(2,1)} %accumulate.22), channel_id=1, source_target_pairs={{0,8},{4,12},{8,16},{12,20},{16,24},{20,28},{24,0},{28,4},{1,9},{5... | collective-permute-start | bytes 1032200 | tf_op jit(solution)/shard_map/ppermute | solution.py:259
  176.1 20.6 %collective-permute-start.33 = (bf16[240,768]{1,0:T(8,128)(2,1)}, bf16[240,768]{1,0:T(8,128)(2,1)}, u32[]{:S(2)}, u32[]{:S(2)}) collective-permute-start(bf16[240,768]{1,0:T(8,128)(2,1)} %get-tuple-element.126.refs_4_), channel_id=1, source_target_pairs={{0,3},{1,2},{2,1},{3,0},{4,7},{5,6},{6,5},{7,4},{8,11},{9,10},{10,... | collective-permute-start | bytes 1105928 | tf_op jit(solution)/shard_map/ppermute | solution.py:253
  177.6 19.9 %collective-permute-start.32 = (bf16[240,768]{1,0:T(8,128)(2,1)}, bf16[240,768]{1,0:T(8,128)(2,1)}, u32[]{:S(2)}, u32[]{:S(2)}) collective-permute-start(bf16[240,768]{1,0:T(8,128)(2,1)} %get-tuple-element.126.refs_4_), channel_id=1, source_target_pairs={{0,2},{1,3},{2,0},{3,1},{4,6},{5,7},{6,4},{7,5},{8,10},{9,11},{10,... | collective-permute-start | bytes 1105928 | tf_op jit(solution)/shard_map/ppermute | solution.py:253
  179.1 18.4 %collective-permute-start.31 = (bf16[240,768]{1,0:T(8,128)(2,1)}, bf16[240,768]{1,0:T(8,128)(2,1)}, u32[]{:S(2)}, u32[]{:S(2)}) collective-permute-start(bf16[240,768]{1,0:T(8,128)(2,1)} %get-tuple-element.126.refs_4_), channel_id=1, source_target_pairs={{0,1},{1,0},{2,3},{3,2},{4,5},{5,4},{6,7},{7,6},{8,9},{9,8},{10,11... | collective-permute-start | bytes 1105928 | tf_op jit(solution)/shard_map/ppermute | solution.py:253
  182.2 10.0 %collective-permute-start.29 = (bf16[224,768]{1,0:T(8,128)(2,1)}, bf16[224,768]{1,0:T(8,128)(2,1)}, u32[]{:S(2)}, u32[]{:S(2)}) collective-permute-start(bf16[224,768]{1,0:T(8,128)(2,1)} %accumulate.23), channel_id=1, source_target_pairs={{0,8},{4,12},{8,16},{12,20},{16,24},{20,28},{24,0},{28,4},{1,9},{5... | collective-permute-start | bytes 1032200 | tf_op jit(solution)/shard_map/ppermute | solution.py:259
  190.7 12.0 %collective-permute-start.39 = (bf16[224,768]{1,0:T(8,128)(2,1)}, bf16[224,768]{1,0:T(8,128)(2,1)}, u32[]{:S(2)}, u32[]{:S(2)}) collective-permute-start(bf16[224,768]{1,0:T(8,128)(2,1)} %get-tuple-element.125.refs_4_), channel_id=1, source_target_pairs={{0,3},{1,2},{2,1},{3,0},{4,7},{5,6},{6,5},{7,4},{8,11},{9,10},{10,... | collective-permute-start | bytes 1032200 | tf_op jit(solution)/shard_map/ppermute | solution.py:253
  192.2 22.2 %collective-permute-start.38 = (bf16[224,768]{1,0:T(8,128)(2,1)}, bf16[224,768]{1,0:T(8,128)(2,1)}, u32[]{:S(2)}, u32[]{:S(2)}) collective-permute-start(bf16[224,768]{1,0:T(8,128)(2,1)} %get-tuple-element.125.refs_4_), channel_id=1, source_target_pairs={{0,2},{1,3},{2,0},{3,1},{4,6},{5,7},{6,4},{7,5},{8,10},{9,11},{10,... | collective-permute-start | bytes 1032200 | tf_op jit(solution)/shard_map/ppermute | solution.py:253
  196.8 17.6 %collective-permute-start.37 = (bf16[224,768]{1,0:T(8,128)(2,1)}, bf16[224,768]{1,0:T(8,128)(2,1)}, u32[]{:S(2)}, u32[]{:S(2)}) collective-permute-start(bf16[224,768]{1,0:T(8,128)(2,1)} %get-tuple-element.125.refs_4_), channel_id=1, source_target_pairs={{0,1},{1,0},{2,3},{3,2},{4,5},{5,4},{6,7},{7,6},{8,9},{9,8},{10,11... | collective-permute-start | bytes 1032200 | tf_op jit(solution)/shard_map/ppermute | solution.py:253
  197.5 26.2 %collective-permute-start.36 = (bf16[224,768]{1,0:T(8,128)(2,1)}, bf16[224,768]{1,0:T(8,128)(2,1)}, u32[]{:S(2)}, u32[]{:S(2)}) collective-permute-start(bf16[224,768]{1,0:T(8,128)(2,1)} %get-tuple-element.124.refs_4_), channel_id=1, source_target_pairs={{0,3},{1,2},{2,1},{3,0},{4,7},{5,6},{6,5},{7,4},{8,11},{9,10},{10,... | collective-permute-start | bytes 1032200 | tf_op jit(solution)/shard_map/ppermute | solution.py:253
  198.9 24.7 %collective-permute-start.35 = (bf16[224,768]{1,0:T(8,128)(2,1)}, bf16[224,768]{1,0:T(8,128)(2,1)}, u32[]{:S(2)}, u32[]{:S(2)}) collective-permute-start(bf16[224,768]{1,0:T(8,128)(2,1)} %get-tuple-element.124.refs_4_), channel_id=1, source_target_pairs={{0,2},{1,3},{2,0},{3,1},{4,6},{5,7},{6,4},{7,5},{8,10},{9,11},{10,... | collective-permute-start | bytes 1032200 | tf_op jit(solution)/shard_map/ppermute | solution.py:253
  202.7 20.9 %collective-permute-start.34 = (bf16[224,768]{1,0:T(8,128)(2,1)}, bf16[224,768]{1,0:T(8,128)(2,1)}, u32[]{:S(2)}, u32[]{:S(2)}) collective-permute-start(bf16[224,768]{1,0:T(8,128)(2,1)} %get-tuple-element.124.refs_4_), channel_id=1, source_target_pairs={{0,1},{1,0},{2,3},{3,2},{4,5},{5,4},{6,7},{7,6},{8,9},{9,8},{10,11... | collective-permute-start | bytes 1032200 | tf_op jit(solution)/shard_map/ppermute | solution.py:253

commit v6 on v5

--- a/solution.py
+++ b/solution.py
@@ -15,11 +15,11 @@
 F32 = jnp.float32
 BF16 = jnp.bfloat16
 COST = pl.CostEstimate(flops=1024, bytes_accessed=1 << 20, transcendentals=0)
-PARAMS = pltpu.CompilerParams(vmem_limit_bytes=40 * 1024 * 1024)
+PARAMS = pltpu.CompilerParams(vmem_limit_bytes=58 * 1024 * 1024)
 RING_PARAMS = pltpu.CompilerParams(vmem_limit_bytes=64 * 1024 * 1024)
 
 
-def transpose(value, block, begin=0, count=None, held=()):
+def transpose(value, block, begin=0, count=None, held=(), params=PARAMS):
     rows, columns = value.shape
     count = rows // block if count is None else count
 
@@ -34,29 +34,31 @@
         + [pl.BlockSpec(memory_space=pl.ANY)] * len(held),
         out_specs=pl.BlockSpec((columns, block), lambda i: (0, begin + i)),
         input_output_aliases={1: 0} if held else {},
-        compiler_params=PARAMS,
+        compiler_params=params,
         cost_estimate=COST,
         name="transpose",
     )(value, *held)
 
 
-def plus(one, two):
-    rows, width = one.shape
+def plus(ones, twos):
+    rows, width = ones[0].shape
     block = pl.BlockSpec((rows // 2, width), lambda i: (i, 0))
-
-    def kernel(one_ref, two_ref, out_ref):
-        out_ref[...] = (one_ref[...].astype(F32) + two_ref[...].astype(F32)).astype(BF16)
+    count = len(ones)
+
+    def kernel(*refs):
+        for one_ref, two_ref, out_ref in zip(refs, refs[count:], refs[2 * count :]):
+            out_ref[...] = (one_ref[...].astype(F32) + two_ref[...].astype(F32)).astype(BF16)
 
     return pl.pallas_call(
         kernel,
         grid=(2,),
-        out_shape=jax.ShapeDtypeStruct(one.shape, BF16),
-        in_specs=[block, block],
-        out_specs=block,
+        out_shape=[jax.ShapeDtypeStruct((rows, width), BF16)] * count,
+        in_specs=[block] * (2 * count),
+        out_specs=[block] * count,
         compiler_params=RING_PARAMS,
         cost_estimate=COST,
         name="plus",
-    )(one, two)
+    )(*ones, *twos)
 
 
 def gradient(grads_t, pieces, owners, cuts):
@@ -108,73 +110,77 @@
     )(owners, *pieces, grads_t)
 
 
-def accumulate(arrived, own, coming, hop):
+def accumulate(places, arrived, own, coming, hop):
     _, rows, width = own.shape
 
-    def kernel(*refs):
-        total = refs[0][0].astype(F32) + refs[1][0].astype(F32)
+    def kernel(places_ref, own_ref, coming_ref, *refs):
+        total = own_ref[0].astype(F32) + coming_ref[0].astype(F32)
         if arrived:
-            total = total + refs[2][...].astype(F32)
+            total = total + refs[0][...].astype(F32)
         refs[-1][...] = total.astype(BF16)
 
-    block = pl.BlockSpec((1, rows, width), lambda i: (hop, 0, 0))
-    return pl.pallas_call(
-        kernel,
-        grid=(1,),
+    return pl.pallas_call(
+        kernel,
         out_shape=jax.ShapeDtypeStruct((rows, width), BF16),
-        in_specs=[block, block] + [pl.BlockSpec(memory_space=pltpu.VMEM)] * len(arrived),
-        out_specs=pl.BlockSpec(memory_space=pltpu.VMEM),
+        grid_spec=pltpu.PrefetchScalarGridSpec(
+            num_scalar_prefetch=1,
+            grid=(1,),
+            in_specs=[
+                pl.BlockSpec((1, rows, width), lambda i, places_ref: (places_ref[0, hop], 0, 0)),
+                pl.BlockSpec((1, rows, width), lambda i, places_ref: (places_ref[1, hop], 0, 0)),
+            ]
+            + [pl.BlockSpec(memory_space=pltpu.VMEM)] * len(arrived),
+            out_specs=pl.BlockSpec(memory_space=pltpu.VMEM),
+        ),
         compiler_params=RING_PARAMS,
         cost_estimate=COST,
         name="accumulate",
-    )(own, coming, *arrived)
-
-
-def adam(pieces, first, second, held, begin):
+    )(places, own, coming, *arrived)
+
+
+def adam(places, arrived, own, coming, first, second, held, begin):
     owned, rank = first.shape
-    count, rows, _ = pieces[0][1].shape
-    widths = [piece[0].shape[1] for piece in pieces]
-    width = sum(widths)
-
-    def kernel(*refs):
-        first_ref, second_ref = refs[3 * len(pieces) : 3 * len(pieces) + 2]
+    rows, width = arrived.shape
+    last = places.shape[1] - 1
+
+    def kernel(places_ref, arrived_ref, own_ref, coming_ref, first_ref, second_ref, *refs):
         first_out, second_out, direction_out = refs[-3:]
-        at = 0
-        for index, size in enumerate(widths):
-            arrived_ref, own_ref, other_ref = refs[3 * index : 3 * index + 3]
-            columns = slice(at, at + size)
-            at += size
-            grad_low = arrived_ref[...].astype(F32) + own_ref[0].astype(F32) + other_ref[0].astype(F32)
-            first_next = beta_first * first_ref[:, columns] + (1.0 - beta_first) * grad_low
-            second_next = beta_second * second_ref[:, columns] + (1.0 - beta_second) * grad_low * grad_low
-            first_out[:, columns] = first_next
-            second_out[:, columns] = second_next
-            bias_first = 1.0 - beta_first**adam_count
-            bias_second = 1.0 - beta_second**adam_count
-            direction = first_next / bias_first / (jnp.sqrt(second_next / bias_second) + epsilon)
-            direction_out[:, columns] = direction.astype(BF16)
-
-    rectangle = pl.BlockSpec((pl.Element(rows), pl.Element(width)), lambda i: begin)
-    piece_specs = []
-    for size in widths:
-        piece_specs += [pl.BlockSpec(memory_space=pltpu.VMEM)]
-        piece_specs += [pl.BlockSpec((1, rows, size), lambda i: (count - 1, 0, 0))] * 2
-    inputs = len(piece_specs) + 2
-    return pl.pallas_call(
-        kernel,
-        grid=(1,),
+        grad_low = arrived_ref[...].astype(F32) + own_ref[0].astype(F32) + coming_ref[0].astype(F32)
+        first_next = beta_first * first_ref[...] + (1.0 - beta_first) * grad_low
+        second_next = beta_second * second_ref[...] + (1.0 - beta_second) * grad_low * grad_low
+        first_out[...] = first_next
+        second_out[...] = second_next
+        bias_first = 1.0 - beta_first**adam_count
+        bias_second = 1.0 - beta_second**adam_count
+        direction = first_next / bias_first / (jnp.sqrt(second_next / bias_second) + epsilon)
+        direction_out[...] = direction.astype(BF16)
+
+    rectangle = pl.BlockSpec((pl.Element(rows), pl.Element(width)), lambda i, places_ref: begin)
+    return pl.pallas_call(
+        kernel,
         out_shape=[
             jax.ShapeDtypeStruct((owned, rank), F32),
             jax.ShapeDtypeStruct((owned, rank), F32),
             jax.ShapeDtypeStruct((rows, width), BF16),
         ],
-        in_specs=piece_specs + [rectangle, rectangle] + [pl.BlockSpec(memory_space=pl.ANY)] * len(held),
-        out_specs=[rectangle, rectangle, pl.BlockSpec((rows, width), lambda i: (0, 0))],
-        input_output_aliases={inputs + index: index for index in range(len(held))},
+        grid_spec=pltpu.PrefetchScalarGridSpec(
+            num_scalar_prefetch=1,
+            grid=(1,),
+            in_specs=[
+                pl.BlockSpec(memory_space=pltpu.VMEM),
+                pl.BlockSpec((1, rows, width), lambda i, places_ref: (places_ref[0, last], 0, 0)),
+                pl.BlockSpec((1, rows, width), lambda i, places_ref: (places_ref[1, last], 0, 0)),
+                rectangle,
+                rectangle,
+            ]
+            + [pl.BlockSpec(memory_space=pl.ANY)] * len(held),
+            out_specs=[rectangle, rectangle, pl.BlockSpec((rows, width), lambda i, places_ref: (0, 0))],
+        ),
+        input_output_aliases={6 + index: index for index in range(len(held))},
         compiler_params=RING_PARAMS,
         cost_estimate=COST,
         name="adam",
-    )(*[array for piece in pieces for array in piece], first, second, *held)
+    )(places, arrived, own, coming, first, second, *held)
 
 
 def expand(targets, starts, rests, begin, basis_t, held, owned):
@@ -190,11 +196,13 @@
         @pl.when(pl.program_id(0) == 0)
         def _():
             for index in range(count):
-                whole_ref[index, :, : rank - width] = start_refs[index][...]
-                whole_ref[index, :, rank - width :] = rest_refs[index][...]
-
+                here = slice(index * rows, (index + 1) * rows)
+                whole_ref[here, : rank - width] = start_refs[index][...]
+                whole_ref[here, rank - width :] = rest_refs[index][...]
+
+        value = jnp.dot(whole_ref[...], basis_ref[...], preferred_element_type=F32)
         for index in range(count):
-            out_ref[targets_ref[index]] = jnp.dot(whole_ref[index], basis_ref[...], preferred_element_type=F32)
+            out_ref[targets_ref[index]] = value[index * rows : (index + 1) * rows]
 
     return pl.pallas_call(
         kernel,
@@ -210,7 +218,7 @@
                 (pl.Element(count), pl.Element(rows), pl.Element(block)),
                 lambda i, targets_ref: (0, begin, i * block),
             ),
-            scratch_shapes=[pltpu.VMEM((count, rows, rank), BF16)],
+            scratch_shapes=[pltpu.VMEM((count * rows, rank), BF16)],
         ),
         input_output_aliases={2 + 2 * count: 0} if held else {},
         compiler_params=RING_PARAMS,
@@ -261,17 +269,29 @@
     def exchange(halves, step):
         return [across(half, offsets[step if index % 2 == 0 else -1 - step]) for index, half in enumerate(halves)]
 
-    def add(halves, arrived, plus=total_of):
-        return [plus(half, term) for half, term in zip(halves, arrived)]
-
-    partial = jnp.dot(features, basis, preferred_element_type=F32).astype(BF16)
-    low, high = partial[: tokens // 2], partial[tokens // 2 :]
-    sums_0 = [low[:, :width], high[:, :width]]
+    def add(halves, arrived):
+        return [total_of(half, term) for half, term in zip(halves, arrived)]
+
+    def add_pairs(pieces, arrived):
+        return [
+            total
+            for index in range(0, len(pieces), 2)
+            for total in plus(pieces[index : index + 2], arrived[index : index + 2])
+        ]
+
+    def projected(features, columns):
+        return [
+            jnp.dot(half, basis[:, columns], preferred_element_type=F32).astype(BF16)
+            for half in (features[: tokens // 2], features[tokens // 2 :])
+        ]
+
+    sums_0 = projected(features, slice(0, width))
     middle = (width + rank) // 2
-    sums_1 = [half[:, run] for run in (slice(width, middle), slice(middle, rank)) for half in (low, high)]
+    later = after(features, *sums_0)
+    sums_1 = projected(later, slice(width, middle)) + projected(later, slice(middle, rank))
     coming_0 = exchange(sums_0, 0)
     block = tokens // 4
-    grads_t = transpose(after(out_grads[0], *sums_0), block, 0, 2)
+    grads_t = transpose(after(out_grads[0], *sums_1), block, 0, 2)
     sums_0 = add(sums_0, [after(term, grads_t) for term in coming_0])
     for step in range(1, len(offsets) - 1):
         sums_0 = add(sums_0, exchange(sums_0, step))
@@ -280,14 +300,13 @@
     sums_0 = add(sums_0, [after(term, grads_t) for term in coming_0])
     coming_1 = exchange([after(half, *sums_0) for half in sums_1], 0)
 
-    cuts_0 = [(slice(0, owned), slice(0, width))]
     ends = [0, owned]
     if owned % 16 == 0:
         ends = [-(-owned * index // 48) * 16 for index in range(4)]
     rows_1 = [slice(*pair) for pair in zip(ends, ends[1:])]
     cuts_1 = [(rows, slice(0, rank - width)) for rows in rows_1]
 
-    def ring(parts, stride, token, between, finish):
+    def ring(places, parts, stride, token, between, finish):
         events = sorted(
             (2 * hop + stride * part, part, hop)
             for part in range(len(parts))
@@ -300,7 +319,7 @@
             else:
                 own, coming = parts[part]
                 before = () if arrived[part] is None else (arrived[part],)
-                token = accumulate(before, after(own, token), coming, hop)
+                token = accumulate(places, before, after(own, token), coming, hop)
                 arrived[part] = onward(token)
             if number in between:
                 token = between[number](token)
@@ -309,9 +328,11 @@
     held = ()
     directions = []
 
-    def step_of(pieces, begin):
+    def step_of(places, arrived, part, begin):
         nonlocal held
-        first_next, second_next, direction = adam(pieces, first_moment[0], second_moment[0], held, begin)
+        first_next, second_next, direction = adam(
+            places, arrived, *part, first_moment[0], second_moment[0], held, begin
+        )
         held = (first_next, second_next)
         directions.append([direction])
         return direction
@@ -320,51 +341,52 @@
         sent = after(directions[part][0], *earlier) if earlier else directions[part][0]
         directions[part] += [across(sent, offset) for offset in range(1, fsdp_count)]
 
-    other = gradient(grads_t, sums_0, other_owners, cuts_0)
-    coming = [sibling(value) for value in other]
-    own = gradient(after(grads_t, *other), sums_0, own_owners, cuts_0)
-    parts_0 = list(zip(own, coming))
+    whole = jnp.concatenate(sums_0)
+    product = jnp.dot(grads_t.reshape(dp_count * owned, tokens), whole, preferred_element_type=F32).astype(BF16)
+    pairs = product.reshape(chips, 2, owned, width)
+    coming = sibling(lax.dynamic_slice_in_dim(pairs, 1 - core, 1, axis=1)[:, 0])
+    part_0 = (product.reshape(dp_count, owned, width), coming)
+    places_0 = jnp.stack([own_owners, ring_order])
+    places_1 = jnp.stack([jnp.arange(chips, dtype=jnp.int32)] * 2)
     rest = {}
 
     def second_exchange(token):
-        sums = add(sums_1, [after(term, token) for term in coming_1], plus)
+        sums = add_pairs(sums_1, [after(term, token) for term in coming_1])
         for step in range(1, len(offsets) - 1):
-            sums = add(sums, exchange(sums, step), plus)
+            sums = add_pairs(sums, exchange(sums, step))
         rest["sums"], rest["coming"] = sums, exchange(sums, len(offsets) - 1)
         return sums[1]
 
     def start_rest(token):
-        sums = add(rest["sums"], [after(term, token) for term in rest["coming"]], plus)
+        sums = add_pairs(rest["sums"], [after(term, token) for term in rest["coming"]])
         rest["sums"] = sums
         rest["other"] = gradient(grads_t, sums, other_owners, cuts_1)
         return rest["other"][0]
 
-    token, last_0 = ring(parts_0, 1, own[0], {0: second_exchange, 1: start_rest}, None)
+    token, last_0 = ring(places_0, [part_0], 1, product, {0: second_exchange, 1: start_rest}, None)
     coming = [sibling(after(value, token)) for value in rest["other"]]
     own = gradient(after(grads_t, token), rest["sums"], own_owners, cuts_1)
     parts_1 = list(zip(own, coming))
-    pieces = [(after(value, own[0]), *part) for value, part in zip(last_0, parts_0)]
-    token = step_of(pieces, (0, 0))
+
+    def finish_0(token):
+        direction = step_of(places_0, after(last_0[0], token), part_0, (0, 0))
+        gather(0)
+        return direction
 
     def turn_basis(token):
-        rest["basis_t"] = transpose(after(basis, token), min(512, basis.shape[0]))
+        rest["basis_t"] = transpose(after(basis, token), min(512, basis.shape[0]), params=RING_PARAMS)
         return rest["basis_t"]
-
-    def send_first(token):
-        gather(0, token)
-        return token
 
     def have_first(token):
         return [token, *directions[0]]
 
     def finish_1(part, arrived):
-        token = step_of([(arrived, *parts_1[part])], (rows_1[part].start, width))
+        token = step_of(places_1, arrived, parts_1[part], (rows_1[part].start, width))
         gather(part + 1, *(directions[part - 1] if part > 1 else ()))
         return token
 
-    first_send, first_wait = (1, 4)
-    between = {2: turn_basis, first_send: send_first, first_wait: have_first}
-    token, _ = ring(parts_1, 1.5, token, between, finish_1)
+    between = {1: finish_0, 2: turn_basis, 4: have_first}
+    token, _ = ring(places_1, parts_1, 1.5, [own[0], *last_0], between, finish_1)
 
     update = ()
     for rows, gathered in zip(rows_1, directions[1:]):

time: 234 us -> 226 us (0.966)
  local copies, waits for them, and re-layouts: 19.7 us -> 1.62 us
  matrix products: 7.95 us -> 20.4 us
  Pallas kernels: 122 us -> 119 us
  waiting for transfers between devices: 37.7 us -> 40.2 us
    unnamed x12 -> x6, local copies, waits for them, and re-layouts: 17.1 us -> 1.53 us
    ppermute x24, waiting for transfers between devices: 6.1 us -> 19.6 us  [across(): lax.ppermute(value, 'fsdp', [(index, index ^ offset) for index in range(f...]
    pallas_call x4 -> x2, Pallas kernels: 31.4 us -> 18.9 us  [gradient(): pl.pallas_call(kernel, out_shape=[jax.ShapeDtypeStruct((count, *shape), B...]
    dot_general x1 -> x7, matrix products: 7.95 us -> 20.4 us  [the longest x6 13.1 us: projected(): jnp.dot(half, basis[:, columns], preferred_element_type=F32).astype(BF16)]
    ppermute x12, waiting for transfers between devices: 31.6 us -> 20.7 us  [onward(): lax.ppermute(value, 'dp', [(index, (index + 2) % dp_count) for index in r...]
    pallas_call x3, Pallas kernels: 9.93 us -> 15.4 us  [transpose(): pl.pallas_call(kernel, out_shape=jax.ShapeDtypeStruct((columns, rows), va...]
    pallas_call x24 -> x20, Pallas kernels: 52.8 us -> 57.2 us  [the longest x12 32.4 us: accumulate(): pl.pallas_call(kernel, out_shape=jax.ShapeDtypeStruct((rows, width), BF16...]
    slice x2 -> x0, local copies, waits for them, and re-layouts: 2.64 us -> none  [the longest x1 2.57 us: local(): half[:, run]]
  transfers between devices with their start and end apart: 40 -> 40, of which waited for: 9 -> 15; matrix products, arithmetic and copies ran while one was open for 2% -> 6% of each run, Pallas kernels for 45% -> 48%
where the time goes in v6:
time: 226 us; the launch traced here: 224 us
  Pallas kernels  119 us (53%)
  waiting for transfers between devices  40.2 us (18%)
  starting transfers between devices  39.2 us (17%)
  matrix products  20.4 us (9%)
  other arithmetic  2.71 us (1%)
    pallas_call x12, Pallas kernels, accumulate(): pl.pallas_call(kernel, out_shape=jax.ShapeDtypeStruct((rows, width), BF16...  32.4 us
    pallas_call x3, Pallas kernels, expand(): pl.pallas_call(kernel, out_shape=jax.ShapeDtypeStruct((count, owned, feat...  27.9 us
    ppermute x24, starting transfers between devices, across(): lax.ppermute(value, 'fsdp', [(index, index ^ offset) for index in range(f...  27 us
    ppermute x12, waiting for transfers between devices, onward(): lax.ppermute(value, 'dp', [(index, (index + 2) % dp_count) for index in r...  20.7 us
    ppermute x24, waiting for transfers between devices, across(): lax.ppermute(value, 'fsdp', [(index, index ^ offset) for index in range(f...  19.6 us
    pallas_call x2, Pallas kernels, gradient(): pl.pallas_call(kernel, out_shape=[jax.ShapeDtypeStruct((count, *shape), B...  18.9 us
    pallas_call x4, Pallas kernels, adam(): pl.pallas_call(kernel, out_shape=[jax.ShapeDtypeStruct((owned, rank), F32...  15.7 us
    pallas_call x3, Pallas kernels, transpose(): pl.pallas_call(kernel, out_shape=jax.ShapeDtypeStruct((columns, rows), va...  15.4 us
  transfers between devices with their start and end apart: 40, of which 15 were waited for; matrix products, arithmetic and copies ran while one was open for 6% of the time, Pallas kernels for 48%

profile of v6, /device:TPU:0, one launch (start us, length us, event | category | flops | bytes accessed | tf_op | source)
XLA Modules:
  0.0 224.3 jit_solution(446321351189129631)
XLA Ops:
  0.6 2.7 %fusion.38 = bf16[512,256]{1,0:T(8,128)(2,1)S(1)} fusion(bf16[1,1024,2048]{2,1,0:T(8,128)(2,1)} %param.5, bf16[2048,1024]{1,0:T(8,128)(2,1)} %bitcast.50), kind=kOutput, calls=%fused_computation.24 | convolution fusion | flops 537001984 | bytes 3407872 | tf_op jit(solution)/shard_map/dot_general | solution.py:284
  3.4 3.0 %collective-permute-start = (bf16[512,256]{1,0:T(8,128)(2,1)S(1)}, bf16[512,256]{1,0:T(8,128)(2,1)S(1)}, u32[]{:S(2)}, u32[]{:S(2)}) collective-permute-start(bf16[512,256]{1,0:T(8,128)(2,1)S(1)} %fusion.38), channel_id=1, source_target_pairs={{0,1},{1,0},{2,3},{3,2},{4,5},{5,4},{6,7},{7,6},{8,9},{9,8},{10,11... | collective-permute-start | bytes 786440 | tf_op jit(solution)/shard_map/ppermute | solution.py:261
  6.4 2.3 %fusion.41 = bf16[512,256]{1,0:T(8,128)(2,1)S(1)} fusion(bf16[1,1024,2048]{2,1,0:T(8,128)(2,1)} %param.5, bf16[2048,1024]{1,0:T(8,128)(2,1)S(1)} %bitcast.52), kind=kOutput, calls=%fused_computation.25 | convolution fusion | flops 537001984 | bytes 3407872 | tf_op jit(solution)/shard_map/dot_general | solution.py:284
  8.7 1.6 collective-permute-start.2
  10.3 2.0 fusion.23.refs_0_
  12.3 2.0 fusion.33.refs_1_
  14.3 2.0 fusion.28.refs_1_
  16.3 2.0 fusion.18.refs_0_
  18.3 5.1 %transpose.5.refs_0_ = bf16[5504,1024]{1,0:T(8,128)(2,1)} custom-call(bf16[1024,5504]{1,0:T(8,128)(2,1)} %bitcast.38), custom_call_target="tpu_custom_call" | custom-call | flops 1024 | bytes 1048576 | tf_op jit(solution)/shard_map/transpose/pallas_call | solution.py:29
  24.7 5.1 %transpose.6 = bf16[5504,1024]{1,0:T(8,128)(2,1)} custom-call(bf16[1024,5504]{1,0:T(8,128)(2,1)} %bitcast.39, bf16[5504,1024]{1,0:T(8,128)(2,1)} %transpose.5.refs_0_), custom_call_target="tpu_custom_call", output_to_operand_aliasing={{}: (1, {})} | custom-call | flops 1024 | bytes 1048576 | tf_op jit(solution)/shard_map/transpose/pallas_call | solution.py:29
  29.7 1.3 collective-permute-done.1
  31.5 7.3 %convolution_convert_fusion = bf16[5504,256]{1,0:T(8,128)(2,1)S(1)} fusion(bf16[5504,1024]{1,0:T(8,128)(2,1)} %transpose.6, bf16[512,256]{1,0:T(8,128)(2,1)S(1)} %get-tuple-element.147, bf16[512,256]{1,0:T(8,128)(2,1)S(1)} %get-tuple-element.148), kind=kOutput, calls=%fused_computation | convolution fusion | flops 2888138752 | bytes 14614528 | tf_op jit(solution)/shard_map/dot_general | solution.py:345
  38.8 1.5 copy-done
  41.4 1.5 collective-permute-start.6
  42.9 1.2 collective-permute-start.10
  45.3 2.6 %accumulate.12 = bf16[688,256]{1,0:T(8,128)(2,1)} custom-call(s32[2,4]{1,0:T(2,128)} %pad_add_fusion.1.places_ref, bf16[8,688,256]{2,1,0:T(8,128)(2,1)} %bitcast.34, bf16[4,688,256]{2,1,0:T(8,128)(2,1)} %collective-permute-done.5.coming_ref), custom_call_target="tpu_custom_call" | custom-call | flops 1024 | bytes 1048576 | tf_op jit(solution)/shard_map/accumulate/pallas_call | solution.py:122
  47.9 1.6 collective-permute-start.8
  49.4 4.3 %collective-permute-done.6.refs_3_ = bf16[512,384]{1,0:T(8,128)(2,1)} collective-permute-done((bf16[512,384]{1,0:T(8,128)(2,1)}, bf16[512,384]{1,0:T(8,128)(2,1)}, u32[]{:S(2)}, u32[]{:S(2)}) %collective-permute-start.6) | collective-permute-done | bytes 393248 | tf_op jit(solution)/shard_map/ppermute | solution.py:261
  53.7 2.3 %plus.4 = (bf16[512,384]{1,0:T(8,128)(2,1)}, bf16[512,384]{1,0:T(8,128)(2,1)}) custom-call(bf16[512,384]{1,0:T(8,128)(2,1)} %fusion.18.refs_0_, bf16[512,384]{1,0:T(8,128)(2,1)} %fusion.28.refs_1_, bf16[512,384]{1,0:T(8,128)(2,1)} %collective-permute-done.4.refs_2_, bf16[512,384]{1,0:T(8,128)(2,1)} %collective-permute-done.6.refs_3_), custom_call_target="tpu_custom_call" | custom-call | flops 1024 | bytes 1048576 | tf_op jit(solution)/shard_map/plus/pallas_call | solution.py:52
  56.0 5.4 %collective-permute-done.11.refs_3_ = bf16[512,384]{1,0:T(8,128)(2,1)} collective-permute-done((bf16[512,384]{1,0:T(8,128)(2,1)}, bf16[512,384]{1,0:T(8,128)(2,1)}, u32[]{:S(2)}, u32[]{:S(2)}) %collective-permute-start.11) | collective-permute-done | bytes 393248 | tf_op jit(solution)/shard_map/ppermute | solution.py:261
  61.4 1.5 collective-permute-start.7
  62.9 1.2 collective-permute-start.9
  64.1 2.3 %plus.6 = (bf16[512,384]{1,0:T(8,128)(2,1)}, bf16[512,384]{1,0:T(8,128)(2,1)}) custom-call(bf16[512,384]{1,0:T(8,128)(2,1)} %fusion.23.refs_0_, bf16[512,384]{1,0:T(8,128)(2,1)} %fusion.33.refs_1_, bf16[512,384]{1,0:T(8,128)(2,1)} %collective-permute-done.10.refs_2_, bf16[512,384]{1,0:T(8,128)(2,1)} %collective-permute-done.11.refs_3_), custom_call_target="tpu_custom_call" | custom-call | flops 1024 | bytes 1048576 | tf_op jit(solution)/shard_map/plus/pallas_call | solution.py:52
  67.7 2.8 %accumulate.13 = bf16[688,256]{1,0:T(8,128)(2,1)} custom-call(s32[2,4]{1,0:T(2,128)} %pad_add_fusion.1.places_ref, bf16[8,688,256]{2,1,0:T(8,128)(2,1)} %bitcast.35, bf16[4,688,256]{2,1,0:T(8,128)(2,1)} %collective-permute-done.5.coming_ref, bf16[688,256]{1,0:T(8,128)(2,1)} %collective-permute-done.8.refs_0_), custom_call_target="tpu_custom_call" | custom-call | flops 1024 | bytes 1048576 | tf_op jit(solution)/shard_map/accumulate/pallas_call | solution.py:122
  70.4 1.6 collective-permute-start.14
  73.7 1.5 collective-permute-done.9.refs_3_
  75.3 2.3 %plus.5 = (bf16[512,384]{1,0:T(8,128)(2,1)}, bf16[512,384]{1,0:T(8,128)(2,1)}) custom-call(bf16[512,384]{1,0:T(8,128)(2,1)} %get-tuple-element.85.refs_0_, bf16[512,384]{1,0:T(8,128)(2,1)} %get-tuple-element.86.refs_1_, bf16[512,384]{1,0:T(8,128)(2,1)} %collective-permute-done.7.refs_2_, bf16[512,384]{1,0:T(8,128)(2,1)} %collective-permute-done.9.refs_3_), custom_call_target="tpu_custom_call" | custom-call | flops 1024 | bytes 1048576 | tf_op jit(solution)/shard_map/plus/pallas_call | solution.py:52
  77.6 2.9 %collective-permute-done.12.refs_2_ = bf16[512,384]{1,0:T(8,128)(2,1)} collective-permute-done((bf16[512,384]{1,0:T(8,128)(2,1)}, bf16[512,384]{1,0:T(8,128)(2,1)}, u32[]{:S(2)}, u32[]{:S(2)}) %collective-permute-start.12) | collective-permute-done | bytes 393248 | tf_op jit(solution)/shard_map/ppermute | solution.py:261
  80.5 1.2 collective-permute-done.13.refs_3_
  81.7 2.3 %plus.7 = (bf16[512,384]{1,0:T(8,128)(2,1)}, bf16[512,384]{1,0:T(8,128)(2,1)}) custom-call(bf16[512,384]{1,0:T(8,128)(2,1)} %get-tuple-element.96.refs_0_, bf16[512,384]{1,0:T(8,128)(2,1)} %get-tuple-element.97.refs_1_, bf16[512,384]{1,0:T(8,128)(2,1)} %collective-permute-done.12.refs_2_, bf16[512,384]{1,0:T(8,128)(2,1)} %collective-permute-done.13.refs_3_), custom_call_target="tpu_custom_call" | custom-call | flops 1024 | bytes 1048576 | tf_op jit(solution)/shard_map/plus/pallas_call | solution.py:52
  84.0 9.4 %gradient.2 = (bf16[4,240,768]{2,1,0:T(8,128)(2,1)}, bf16[4,224,768]{2,1,0:T(8,128)(2,1)}, bf16[4,224,768]{2,1,0:T(8,128)(2,1)}) custom-call(s32[4]{0:T(128)} %get-tuple-element.143.owners_ref, bf16[512,384]{1,0:T(8,128)(2,1)} %get-tuple-element.90.refs_0_, bf16[512,384]{1,0:T(8,128)(2,1)} %get-tuple-element.91.refs_1_, ...), custom_call_target="tpu_custom_call" | custom-call | flops 1024 | bytes 1048576 | tf_op jit(solution)/shard_map/gradient/pallas_call | solution.py:92
  93.4 2.8 %accumulate.14 = bf16[688,256]{1,0:T(8,128)(2,1)} custom-call(s32[2,4]{1,0:T(2,128)} %pad_add_fusion.1.places_ref, bf16[8,688,256]{2,1,0:T(8,128)(2,1)} %bitcast.36, bf16[4,688,256]{2,1,0:T(8,128)(2,1)} %collective-permute-done.5.coming_ref, bf16[688,256]{1,0:T(8,128)(2,1)} %collective-permute-done.14.refs_0_), custom_call_target="tpu_custom_call" | custom-call | flops 1024 | bytes 1048576 | tf_op jit(solution)/shard_map/accumulate/pallas_call | solution.py:122
  96.7 1.6 collective-permute-start.15
  98.9 9.5 %gradient.3 = (bf16[4,240,768]{2,1,0:T(8,128)(2,1)}, bf16[4,224,768]{2,1,0:T(8,128)(2,1)}, bf16[4,224,768]{2,1,0:T(8,128)(2,1)}) custom-call(s32[4]{0:T(128)} %get-tuple-element.144.owners_ref, bf16[512,384]{1,0:T(8,128)(2,1)} %get-tuple-element.90.refs_0_, bf16[512,384]{1,0:T(8,128)(2,1)} %get-tuple-element.91.refs_1_, ...), custom_call_target="tpu_custom_call" | custom-call | flops 1024 | bytes 1048576 | tf_op jit(solution)/shard_map/gradient/pallas_call | solution.py:92
  109.5 2.6 %accumulate.15 = bf16[240,768]{1,0:T(8,128)(2,1)} custom-call(s32[2,4]{1,0:T(2,128)} %pad_add_fusion.places_ref, bf16[4,240,768]{2,1,0:T(8,128)(2,1)} %get-tuple-element.121.own_ref, bf16[4,240,768]{2,1,0:T(8,128)(2,1)} %collective-permute-done.16.coming_ref), custom_call_target="tpu_custom_call" | custom-call | flops 1024 | bytes 1048576 | tf_op jit(solution)/shard_map/accumulate/pallas_call | solution.py:122
  112.5 2.6 %accumulate.16 = bf16[224,768]{1,0:T(8,128)(2,1)} custom-call(s32[2,4]{1,0:T(2,128)} %pad_add_fusion.places_ref, bf16[4,224,768]{2,1,0:T(8,128)(2,1)} %get-tuple-element.123.own_ref, bf16[4,224,768]{2,1,0:T(8,128)(2,1)} %collective-permute-done.17.coming_ref), custom_call_target="tpu_custom_call" | custom-call | flops 1024 | bytes 1048576 | tf_op jit(solution)/shard_map/accumulate/pallas_call | solution.py:122
  115.1 3.9 %adam.4 = (f32[688,1024]{1,0:T(8,128)}, f32[688,1024]{1,0:T(8,128)}, bf16[688,256]{1,0:T(8,128)(2,1)}) custom-call(s32[2,4]{1,0:T(2,128)} %pad_add_fusion.1.places_ref, bf16[688,256]{1,0:T(8,128)(2,1)} %collective-permute-done.15.arrived_ref, bf16[8,688,256]{2,1,0:T(8,128)(2,1)} %bitcast.37, bf16[4,688,256]{2,1,0:T(8,128)(2,1)} %collective-permute-done.5.coming_ref, ...), custom_call_target="tpu_custom_call" | custom-call | flops 1024 | bytes 1048576 | tf_op jit(solution)/shard_map/adam/pallas_call | solution.py:159
  120.2 1.6 collective-permute-start.23
  121.8 2.7 %collective-permute-done.18.refs_0_ = bf16[240,768]{1,0:T(8,128)(2,1)} collective-permute-done((bf16[240,768]{1,0:T(8,128)(2,1)}, bf16[240,768]{1,0:T(8,128)(2,1)}, u32[]{:S(2)}, u32[]{:S(2)}) %collective-permute-start.18) | collective-permute-done | bytes 368672 | tf_op jit(solution)/shard_map/ppermute | solution.py:267
  124.6 2.8 %accumulate.17 = bf16[240,768]{1,0:T(8,128)(2,1)} custom-call(s32[2,4]{1,0:T(2,128)} %pad_add_fusion.places_ref, bf16[4,240,768]{2,1,0:T(8,128)(2,1)} %get-tuple-element.121.own_ref, bf16[4,240,768]{2,1,0:T(8,128)(2,1)} %collective-permute-done.16.coming_ref, bf16[240,768]{1,0:T(8,128)(2,1)} %collective-permute-done.18.refs_0_), custom_call_target="tpu_custom_call" | custom-call | flops 1024 | bytes 1048576 | tf_op jit(solution)/shard_map/accumulate/pallas_call | solution.py:122
  127.8 1.2 collective-permute-start.19
  129.0 5.3 %transpose.7.basis_ref = bf16[1024,2048]{1,0:T(8,128)(2,1)} custom-call(bf16[2048,1024]{1,0:T(8,128)(2,1)} %bitcast.51), custom_call_target="tpu_custom_call" | custom-call | flops 1024 | bytes 1048576 | tf_op jit(solution)/shard_map/transpose/pallas_call | solution.py:29
  134.4 2.6 %accumulate.18 = bf16[224,768]{1,0:T(8,128)(2,1)} custom-call(s32[2,4]{1,0:T(2,128)} %pad_add_fusion.places_ref, bf16[4,224,768]{2,1,0:T(8,128)(2,1)} %get-tuple-element.128.own_ref, bf16[4,224,768]{2,1,0:T(8,128)(2,1)} %collective-permute-done.22.coming_ref), custom_call_target="tpu_custom_call" | custom-call | flops 1024 | bytes 1048576 | tf_op jit(solution)/shard_map/accumulate/pallas_call | solution.py:122
  137.8 2.7 %accumulate.19 = bf16[224,768]{1,0:T(8,128)(2,1)} custom-call(s32[2,4]{1,0:T(2,128)} %pad_add_fusion.places_ref, bf16[4,224,768]{2,1,0:T(8,128)(2,1)} %get-tuple-element.123.own_ref, bf16[4,224,768]{2,1,0:T(8,128)(2,1)} %collective-permute-done.17.coming_ref, bf16[224,768]{1,0:T(8,128)(2,1)} %collective-permute-done.23.refs_0_), custom_call_target="tpu_custom_call" | custom-call | flops 1024 | bytes 1048576 | tf_op jit(solution)/shard_map/accumulate/pallas_call | solution.py:122
  140.9 2.8 %accumulate.20 = bf16[240,768]{1,0:T(8,128)(2,1)} custom-call(s32[2,4]{1,0:T(2,128)} %pad_add_fusion.places_ref, bf16[4,240,768]{2,1,0:T(8,128)(2,1)} %get-tuple-element.121.own_ref, bf16[4,240,768]{2,1,0:T(8,128)(2,1)} %collective-permute-done.16.coming_ref, bf16[240,768]{1,0:T(8,128)(2,1)} %collective-permute-done.24.refs_0_), custom_call_target="tpu_custom_call" | custom-call | flops 1024 | bytes 1048576 | tf_op jit(solution)/shard_map/accumulate/pallas_call | solution.py:122
  143.7 3.7 %collective-permute-start.25 = (bf16[240,768]{1,0:T(8,128)(2,1)}, bf16[240,768]{1,0:T(8,128)(2,1)}, u32[]{:S(2)}, u32[]{:S(2)}) collective-permute-start(bf16[240,768]{1,0:T(8,128)(2,1)} %accumulate.20), channel_id=1, source_target_pairs={{0,8},{4,12},{8,16},{12,20},{16,24},{20,28},{24,0},{28,4},{1,9},{5... | collective-permute-start | bytes 1105928 | tf_op jit(solution)/shard_map/ppermute | solution.py:267
  147.4 2.6 %collective-permute-done.26.refs_0_ = bf16[224,768]{1,0:T(8,128)(2,1)} collective-permute-done((bf16[224,768]{1,0:T(8,128)(2,1)}, bf16[224,768]{1,0:T(8,128)(2,1)}, u32[]{:S(2)}, u32[]{:S(2)}) %collective-permute-start.26) | collective-permute-done | bytes 344096 | tf_op jit(solution)/shard_map/ppermute | solution.py:267
  150.1 2.7 %accumulate.21 = bf16[224,768]{1,0:T(8,128)(2,1)} custom-call(s32[2,4]{1,0:T(2,128)} %pad_add_fusion.places_ref, bf16[4,224,768]{2,1,0:T(8,128)(2,1)} %get-tuple-element.128.own_ref, bf16[4,224,768]{2,1,0:T(8,128)(2,1)} %collective-permute-done.22.coming_ref, bf16[224,768]{1,0:T(8,128)(2,1)} %collective-permute-done.26.refs_0_), custom_call_target="tpu_custom_call" | custom-call | flops 1024 | bytes 1048576 | tf_op jit(solution)/shard_map/accumulate/pallas_call | solution.py:122
  152.8 4.6 %collective-permute-done.27.refs_0_ = bf16[224,768]{1,0:T(8,128)(2,1)} collective-permute-done((bf16[224,768]{1,0:T(8,128)(2,1)}, bf16[224,768]{1,0:T(8,128)(2,1)}, u32[]{:S(2)}, u32[]{:S(2)}) %collective-permute-start.27) | collective-permute-done | bytes 344096 | tf_op jit(solution)/shard_map/ppermute | solution.py:267
  157.4 2.7 %accumulate.22 = bf16[224,768]{1,0:T(8,128)(2,1)} custom-call(s32[2,4]{1,0:T(2,128)} %pad_add_fusion.places_ref, bf16[4,224,768]{2,1,0:T(8,128)(2,1)} %get-tuple-element.123.own_ref, bf16[4,224,768]{2,1,0:T(8,128)(2,1)} %collective-permute-done.17.coming_ref, bf16[224,768]{1,0:T(8,128)(2,1)} %collective-permute-done.27.refs_0_), custom_call_target="tpu_custom_call" | custom-call | flops 1024 | bytes 1048576 | tf_op jit(solution)/shard_map/accumulate/pallas_call | solution.py:122
  160.2 5.2 %collective-permute-done.25.arrived_ref = bf16[240,768]{1,0:T(8,128)(2,1)} collective-permute-done((bf16[240,768]{1,0:T(8,128)(2,1)}, bf16[240,768]{1,0:T(8,128)(2,1)}, u32[]{:S(2)}, u32[]{:S(2)}) %collective-permute-start.25) | collective-permute-done | bytes 368672 | tf_op jit(solution)/shard_map/ppermute | solution.py:267
  165.3 4.0 %adam.5 = (f32[688,1024]{1,0:T(8,128)}, f32[688,1024]{1,0:T(8,128)}, bf16[240,768]{1,0:T(8,128)(2,1)}) custom-call(s32[2,4]{1,0:T(2,128)} %pad_add_fusion.places_ref, bf16[240,768]{1,0:T(8,128)(2,1)} %collective-permute-done.25.arrived_ref, bf16[4,240,768]{2,1,0:T(8,128)(2,1)} %get-tuple-element.121.own_ref, ...), custom_call_target="tpu_custom_call", output_to_operand_aliasing={{0}: (6, {}), {1}: (7, {})} | custom-call | flops 1024 | bytes 1048576 | tf_op jit(solution)/shard_map/adam/pallas_call | solution.py:159
  169.3 1.8 collective-permute-start.33
  171.6 1.2 collective-permute-start.31
  172.8 2.7 %accumulate.23 = bf16[224,768]{1,0:T(8,128)(2,1)} custom-call(s32[2,4]{1,0:T(2,128)} %pad_add_fusion.places_ref, bf16[4,224,768]{2,1,0:T(8,128)(2,1)} %get-tuple-element.128.own_ref, bf16[4,224,768]{2,1,0:T(8,128)(2,1)} %collective-permute-done.22.coming_ref, bf16[224,768]{1,0:T(8,128)(2,1)} %collective-permute-done.28.refs_0_), custom_call_target="tpu_custom_call" | custom-call | flops 1024 | bytes 1048576 | tf_op jit(solution)/shard_map/accumulate/pallas_call | solution.py:122
  175.6 4.3 %collective-permute-done.30.arrived_ref = bf16[224,768]{1,0:T(8,128)(2,1)} collective-permute-done((bf16[224,768]{1,0:T(8,128)(2,1)}, bf16[224,768]{1,0:T(8,128)(2,1)}, u32[]{:S(2)}, u32[]{:S(2)}) %collective-permute-start.30) | collective-permute-done | bytes 344096 | tf_op jit(solution)/shard_map/ppermute | solution.py:267
  179.8 3.9 %adam.6 = (f32[688,1024]{1,0:T(8,128)}, f32[688,1024]{1,0:T(8,128)}, bf16[224,768]{1,0:T(8,128)(2,1)}) custom-call(s32[2,4]{1,0:T(2,128)} %pad_add_fusion.places_ref, bf16[224,768]{1,0:T(8,128)(2,1)} %collective-permute-done.30.arrived_ref, bf16[4,224,768]{2,1,0:T(8,128)(2,1)} %get-tuple-element.123.own_ref, ...), custom_call_target="tpu_custom_call", output_to_operand_aliasing={{0}: (6, {}), {1}: (7, {})} | custom-call | flops 1024 | bytes 1048576 | tf_op jit(solution)/shard_map/adam/pallas_call | solution.py:159
  183.7 1.8 collective-permute-start.39
  186.7 3.9 %adam.7 = (f32[688,1024]{1,0:T(8,128)}, f32[688,1024]{1,0:T(8,128)}, bf16[224,768]{1,0:T(8,128)(2,1)}) custom-call(s32[2,4]{1,0:T(2,128)} %pad_add_fusion.places_ref, bf16[224,768]{1,0:T(8,128)(2,1)} %collective-permute-done.29.arrived_ref, bf16[4,224,768]{2,1,0:T(8,128)(2,1)} %get-tuple-element.128.own_ref, ...), custom_call_target="tpu_custom_call", output_to_operand_aliasing={{0}: (6, {}), {1}: (7, {})} | custom-call | flops 1024 | bytes 1048576 | tf_op jit(solution)/shard_map/adam/pallas_call | solution.py:159
  191.2 1.7 collective-permute-start.36
  194.1 1.4 collective-permute-done.39.refs_7_
  196.4 9.5 %expand.3.refs_8_ = f32[4,688,2048]{2,1,0:T(8,128)} custom-call(s32[4]{0:T(128)} %pad_add_fusion.2.targets_ref, bf16[1024,2048]{1,0:T(8,128)(2,1)} %transpose.7.basis_ref, bf16[688,256]{1,0:T(8,128)(2,1)} %get-tuple-element.113.refs_0_, bf16[688,256]{1,0:T(8,128)(2,1)} %collective-permute-done.19.refs_1_, bf16[688,256]{1,0:T(8,128)(2,1)} %collective-permute-done.20.refs_2_, ...), custom_call_target="tpu_custom_call" | custom-call | flops 1024 | bytes 1048576 | tf_op jit(solution)/shard_map/expand/pallas_call | solution.py:207
  205.9 9.2 %expand.4.refs_8_ = f32[4,688,2048]{2,1,0:T(8,128)} custom-call(s32[4]{0:T(128)} %pad_add_fusion.2.targets_ref, bf16[1024,2048]{1,0:T(8,128)(2,1)} %transpose.7.basis_ref, bf16[688,256]{1,0:T(8,128)(2,1)} %get-tuple-element.113.refs_0_, bf16[688,256]{1,0:T(8,128)(2,1)} %collective-permute-done.19.refs_1_, ...), custom_call_target="tpu_custom_call", output_to_operand_aliasing={{}: (10, {})} | custom-call | flops 1024 | bytes 1048576 | tf_op jit(solution)/shard_map/expand/pallas_call | solution.py:207
  215.2 9.2 %expand.5 = f32[4,688,2048]{2,1,0:T(8,128)} custom-call(s32[4]{0:T(128)} %pad_add_fusion.2.targets_ref, bf16[1024,2048]{1,0:T(8,128)(2,1)} %transpose.7.basis_ref, bf16[688,256]{1,0:T(8,128)(2,1)} %get-tuple-element.113.refs_0_, bf16[688,256]{1,0:T(8,128)(2,1)} %collective-permute-done.19.refs_1_, ...), custom_call_target="tpu_custom_call", output_to_operand_aliasing={{}: (10, {})} | custom-call | flops 1024 | bytes 1048576 | tf_op jit(solution)/shard_map/expand/pallas_call | solution.py:207
  (67 shorter events, 16.9 us)
Async XLA Ops:
  0.6 5.8 %copy-start.1 = (bf16[1,2048,1024]{2,1,0:T(8,128)(2,1)S(1)}, bf16[1,2048,1024]{2,1,0:T(8,128)(2,1)}, u32[]{:S(2)}) copy-start(bf16[1,2048,1024]{2,1,0:T(8,128)(2,1)} %param.7) | copy-start | bytes 12582916
  3.4 6.9 %copy-start.2 = (bf16[1,1024,2048]{2,1,0:T(8,128)(2,1)S(1)}, bf16[1,1024,2048]{2,1,0:T(8,128)(2,1)}, u32[]{:S(2)}) copy-start(bf16[1,1024,2048]{2,1,0:T(8,128)(2,1)} %param.5) | copy-start | bytes 12582916
  3.4 20.0 %collective-permute-start = (bf16[512,256]{1,0:T(8,128)(2,1)S(1)}, bf16[512,256]{1,0:T(8,128)(2,1)S(1)}, u32[]{:S(2)}, u32[]{:S(2)}) collective-permute-start(bf16[512,256]{1,0:T(8,128)(2,1)S(1)} %fusion.38), channel_id=1, source_target_pairs={{0,1},{1,0},{2,3},{3,2},{4,5},{5,4},{6,7},{7,6},{8,9},{9,8},{10,11... | collective-permute-start | bytes 786440 | tf_op jit(solution)/shard_map/ppermute | solution.py:261
  8.7 14.7 %collective-permute-start.2 = (bf16[512,256]{1,0:T(8,128)(2,1)S(1)}, bf16[512,256]{1,0:T(8,128)(2,1)S(1)}, u32[]{:S(2)}, u32[]{:S(2)}) collective-permute-start(bf16[512,256]{1,0:T(8,128)(2,1)S(1)} %fusion.41), channel_id=1, source_target_pairs={{0,2},{1,3},{2,0},{3,1},{4,6},{5,7},{6,4},{7,5},{8,10},{9,11},{10,... | collective-permute-start | bytes 786440 | tf_op jit(solution)/shard_map/ppermute | solution.py:261
  23.5 7.5 %collective-permute-start.1 = (bf16[512,256]{1,0:T(8,128)(2,1)S(1)}, bf16[512,256]{1,0:T(8,128)(2,1)S(1)}, u32[]{:S(2)}, u32[]{:S(2)}) collective-permute-start(bf16[512,256]{1,0:T(8,128)(2,1)S(1)} %add_convert_fusion.3), channel_id=1, source_target_pairs={{0,2},{1,3},{2,0},{3,1},{4,6},{5,7},{6,4},{7,5},{8,10},{9,11},{10,... | collective-permute-start | bytes 786440 | tf_op jit(solution)/shard_map/ppermute | solution.py:261
  24.1 7.3 %collective-permute-start.3 = (bf16[512,256]{1,0:T(8,128)(2,1)S(1)}, bf16[512,256]{1,0:T(8,128)(2,1)S(1)}, u32[]{:S(2)}, u32[]{:S(2)}) collective-permute-start(bf16[512,256]{1,0:T(8,128)(2,1)S(1)} %add_convert_fusion.2), channel_id=1, source_target_pairs={{0,1},{1,0},{2,3},{3,2},{4,5},{5,4},{6,7},{7,6},{8,9},{9,8},{10,11... | collective-permute-start | bytes 786440 | tf_op jit(solution)/shard_map/ppermute | solution.py:261
  38.8 1.5 copy-start
  40.4 4.8 %collective-permute-start.5 = (bf16[4,688,256]{2,1,0:T(8,128)(2,1)S(1)}, bf16[4,688,256]{2,1,0:T(8,128)(2,1)}, u32[]{:S(2)}, u32[]{:S(2)}) collective-permute-start(bf16[4,688,256]{2,1,0:T(8,128)(2,1)S(1)} %dynamic-slice_bitcast_fusion), channel_id=1, source_target_pairs={{0,4},{4,0},{8,12},{12,8},{16,20},{20,16},{24,28},{28,24},{1,5},{5... | collective-permute-start | bytes 4227080 | tf_op jit(solution)/shard_map/ppermute | solution.py:264
  40.6 13.1 %collective-permute-start.4 = (bf16[512,384]{1,0:T(8,128)(2,1)}, bf16[512,384]{1,0:T(8,128)(2,1)}, u32[]{:S(2)}, u32[]{:S(2)}) collective-permute-start(bf16[512,384]{1,0:T(8,128)(2,1)} %fusion.18.refs_0_), channel_id=1, source_target_pairs={{0,1},{1,0},{2,3},{3,2},{4,5},{5,4},{6,7},{7,6},{8,9},{9,8},{10,11... | collective-permute-start | bytes 1179656 | tf_op jit(solution)/shard_map/ppermute | solution.py:261
  41.4 12.3 %collective-permute-start.6 = (bf16[512,384]{1,0:T(8,128)(2,1)}, bf16[512,384]{1,0:T(8,128)(2,1)}, u32[]{:S(2)}, u32[]{:S(2)}) collective-permute-start(bf16[512,384]{1,0:T(8,128)(2,1)} %fusion.28.refs_1_), channel_id=1, source_target_pairs={{0,2},{1,3},{2,0},{3,1},{4,6},{5,7},{6,4},{7,5},{8,10},{9,11},{10,... | collective-permute-start | bytes 1179656 | tf_op jit(solution)/shard_map/ppermute | solution.py:261
  42.9 21.2 %collective-permute-start.10 = (bf16[512,384]{1,0:T(8,128)(2,1)}, bf16[512,384]{1,0:T(8,128)(2,1)}, u32[]{:S(2)}, u32[]{:S(2)}) collective-permute-start(bf16[512,384]{1,0:T(8,128)(2,1)} %fusion.23.refs_0_), channel_id=1, source_target_pairs={{0,1},{1,0},{2,3},{3,2},{4,5},{5,4},{6,7},{7,6},{8,9},{9,8},{10,11... | collective-permute-start | bytes 1179656 | tf_op jit(solution)/shard_map/ppermute | solution.py:261
  44.2 17.2 %collective-permute-start.11 = (bf16[512,384]{1,0:T(8,128)(2,1)}, bf16[512,384]{1,0:T(8,128)(2,1)}, u32[]{:S(2)}, u32[]{:S(2)}) collective-permute-start(bf16[512,384]{1,0:T(8,128)(2,1)} %fusion.33.refs_1_), channel_id=1, source_target_pairs={{0,2},{1,3},{2,0},{3,1},{4,6},{5,7},{6,4},{7,5},{8,10},{9,11},{10,... | collective-permute-start | bytes 1179656 | tf_op jit(solution)/shard_map/ppermute | solution.py:261
  47.9 19.8 %collective-permute-start.8 = (bf16[688,256]{1,0:T(8,128)(2,1)}, bf16[688,256]{1,0:T(8,128)(2,1)}, u32[]{:S(2)}, u32[]{:S(2)}) collective-permute-start(bf16[688,256]{1,0:T(8,128)(2,1)} %accumulate.12), channel_id=1, source_target_pairs={{0,8},{4,12},{8,16},{12,20},{16,24},{20,28},{24,0},{28,4},{1,9},{5... | collective-permute-start | bytes 1056776 | tf_op jit(solution)/shard_map/ppermute | solution.py:267
  61.4 12.4 %collective-permute-start.7 = (bf16[512,384]{1,0:T(8,128)(2,1)}, bf16[512,384]{1,0:T(8,128)(2,1)}, u32[]{:S(2)}, u32[]{:S(2)}) collective-permute-start(bf16[512,384]{1,0:T(8,128)(2,1)} %get-tuple-element.85.refs_0_), channel_id=1, source_target_pairs={{0,2},{1,3},{2,0},{3,1},{4,6},{5,7},{6,4},{7,5},{8,10},{9,11},{10,... | collective-permute-start | bytes 1179656 | tf_op jit(solution)/shard_map/ppermute | solution.py:261
  62.9 12.4 %collective-permute-start.9 = (bf16[512,384]{1,0:T(8,128)(2,1)}, bf16[512,384]{1,0:T(8,128)(2,1)}, u32[]{:S(2)}, u32[]{:S(2)}) collective-permute-start(bf16[512,384]{1,0:T(8,128)(2,1)} %get-tuple-element.86.refs_1_), channel_id=1, source_target_pairs={{0,1},{1,0},{2,3},{3,2},{4,5},{5,4},{6,7},{7,6},{8,9},{9,8},{10,11... | collective-permute-start | bytes 1179656 | tf_op jit(solution)/shard_map/ppermute | solution.py:261
  66.4 14.1 %collective-permute-start.12 = (bf16[512,384]{1,0:T(8,128)(2,1)}, bf16[512,384]{1,0:T(8,128)(2,1)}, u32[]{:S(2)}, u32[]{:S(2)}) collective-permute-start(bf16[512,384]{1,0:T(8,128)(2,1)} %get-tuple-element.96.refs_0_), channel_id=1, source_target_pairs={{0,2},{1,3},{2,0},{3,1},{4,6},{5,7},{6,4},{7,5},{8,10},{9,11},{10,... | collective-permute-start | bytes 1179656 | tf_op jit(solution)/shard_map/ppermute | solution.py:261
  66.9 14.8 %collective-permute-start.13 = (bf16[512,384]{1,0:T(8,128)(2,1)}, bf16[512,384]{1,0:T(8,128)(2,1)}, u32[]{:S(2)}, u32[]{:S(2)}) collective-permute-start(bf16[512,384]{1,0:T(8,128)(2,1)} %get-tuple-element.97.refs_1_), channel_id=1, source_target_pairs={{0,1},{1,0},{2,3},{3,2},{4,5},{5,4},{6,7},{7,6},{8,9},{9,8},{10,11... | collective-permute-start | bytes 1179656 | tf_op jit(solution)/shard_map/ppermute | solution.py:261
  70.4 23.0 %collective-permute-start.14 = (bf16[688,256]{1,0:T(8,128)(2,1)}, bf16[688,256]{1,0:T(8,128)(2,1)}, u32[]{:S(2)}, u32[]{:S(2)}) collective-permute-start(bf16[688,256]{1,0:T(8,128)(2,1)} %accumulate.13), channel_id=1, source_target_pairs={{0,8},{4,12},{8,16},{12,20},{16,24},{20,28},{24,0},{28,4},{1,9},{5... | collective-permute-start | bytes 1056776 | tf_op jit(solution)/shard_map/ppermute | solution.py:267
  96.2 13.3 %collective-permute-start.16 = (bf16[4,240,768]{2,1,0:T(8,128)(2,1)}, bf16[4,240,768]{2,1,0:T(8,128)(2,1)}, u32[]{:S(2)}, u32[]{:S(2)}) collective-permute-start(bf16[4,240,768]{2,1,0:T(8,128)(2,1)} %get-tuple-element.108), channel_id=1, source_target_pairs={{0,4},{4,0},{8,12},{12,8},{16,20},{20,16},{24,28},{28,24},{1,5},{5... | collective-permute-start | bytes 4423688 | tf_op jit(solution)/shard_map/ppermute | solution.py:264
  96.2 16.4 %collective-permute-start.17 = (bf16[4,224,768]{2,1,0:T(8,128)(2,1)}, bf16[4,224,768]{2,1,0:T(8,128)(2,1)}, u32[]{:S(2)}, u32[]{:S(2)}) collective-permute-start(bf16[4,224,768]{2,1,0:T(8,128)(2,1)} %get-tuple-element.111), channel_id=1, source_target_pairs={{0,4},{4,0},{8,12},{12,8},{16,20},{20,16},{24,28},{28,24},{1,5},{5... | collective-permute-start | bytes 4128776 | tf_op jit(solution)/shard_map/ppermute | solution.py:264
  96.7 31.1 %collective-permute-start.22 = (bf16[4,224,768]{2,1,0:T(8,128)(2,1)}, bf16[4,224,768]{2,1,0:T(8,128)(2,1)}, u32[]{:S(2)}, u32[]{:S(2)}) collective-permute-start(bf16[4,224,768]{2,1,0:T(8,128)(2,1)} %get-tuple-element.119), channel_id=1, source_target_pairs={{0,4},{4,0},{8,12},{12,8},{16,20},{20,16},{24,28},{28,24},{1,5},{5... | collective-permute-start | bytes 4128776 | tf_op jit(solution)/shard_map/ppermute | solution.py:264
  96.7 12.8 %collective-permute-start.15 = (bf16[688,256]{1,0:T(8,128)(2,1)}, bf16[688,256]{1,0:T(8,128)(2,1)}, u32[]{:S(2)}, u32[]{:S(2)}) collective-permute-start(bf16[688,256]{1,0:T(8,128)(2,1)} %accumulate.14), channel_id=1, source_target_pairs={{0,8},{4,12},{8,16},{12,20},{16,24},{20,28},{24,0},{28,4},{1,9},{5... | collective-permute-start | bytes 1056776 | tf_op jit(solution)/shard_map/ppermute | solution.py:267
  112.1 12.4 %collective-permute-start.18 = (bf16[240,768]{1,0:T(8,128)(2,1)}, bf16[240,768]{1,0:T(8,128)(2,1)}, u32[]{:S(2)}, u32[]{:S(2)}) collective-permute-start(bf16[240,768]{1,0:T(8,128)(2,1)} %accumulate.15), channel_id=1, source_target_pairs={{0,8},{4,12},{8,16},{12,20},{16,24},{20,28},{24,0},{28,4},{1,9},{5... | collective-permute-start | bytes 1105928 | tf_op jit(solution)/shard_map/ppermute | solution.py:267
  119.1 21.5 %collective-permute-start.21 = (bf16[688,256]{1,0:T(8,128)(2,1)}, bf16[688,256]{1,0:T(8,128)(2,1)}, u32[]{:S(2)}, u32[]{:S(2)}) collective-permute-start(bf16[688,256]{1,0:T(8,128)(2,1)} %get-tuple-element.113.refs_0_), channel_id=1, source_target_pairs={{0,3},{1,2},{2,1},{3,0},{4,7},{5,6},{6,5},{7,4},{8,11},{9,10},{10,... | collective-permute-start | bytes 1056776 | tf_op jit(solution)/shard_map/ppermute | solution.py:261
  120.2 16.7 %collective-permute-start.23 = (bf16[224,768]{1,0:T(8,128)(2,1)}, bf16[224,768]{1,0:T(8,128)(2,1)}, u32[]{:S(2)}, u32[]{:S(2)}) collective-permute-start(bf16[224,768]{1,0:T(8,128)(2,1)} %accumulate.16), channel_id=1, source_target_pairs={{0,8},{4,12},{8,16},{12,20},{16,24},{20,28},{24,0},{28,4},{1,9},{5... | collective-permute-start | bytes 1032200 | tf_op jit(solution)/shard_map/ppermute | solution.py:267
  127.3 13.6 %collective-permute-start.24 = (bf16[240,768]{1,0:T(8,128)(2,1)}, bf16[240,768]{1,0:T(8,128)(2,1)}, u32[]{:S(2)}, u32[]{:S(2)}) collective-permute-start(bf16[240,768]{1,0:T(8,128)(2,1)} %accumulate.17), channel_id=1, source_target_pairs={{0,8},{4,12},{8,16},{12,20},{16,24},{20,28},{24,0},{28,4},{1,9},{5... | collective-permute-start | bytes 1105928 | tf_op jit(solution)/shard_map/ppermute | solution.py:267
  127.3 13.6 %collective-permute-start.20 = (bf16[688,256]{1,0:T(8,128)(2,1)}, bf16[688,256]{1,0:T(8,128)(2,1)}, u32[]{:S(2)}, u32[]{:S(2)}) collective-permute-start(bf16[688,256]{1,0:T(8,128)(2,1)} %get-tuple-element.113.refs_0_), channel_id=1, source_target_pairs={{0,2},{1,3},{2,0},{3,1},{4,6},{5,7},{6,4},{7,5},{8,10},{9,11},{10,... | collective-permute-start | bytes 1056776 | tf_op jit(solution)/shard_map/ppermute | solution.py:261
  127.8 13.1 %collective-permute-start.19 = (bf16[688,256]{1,0:T(8,128)(2,1)}, bf16[688,256]{1,0:T(8,128)(2,1)}, u32[]{:S(2)}, u32[]{:S(2)}) collective-permute-start(bf16[688,256]{1,0:T(8,128)(2,1)} %get-tuple-element.113.refs_0_), channel_id=1, source_target_pairs={{0,1},{1,0},{2,3},{3,2},{4,5},{5,4},{6,7},{7,6},{8,9},{9,8},{10,11... | collective-permute-start | bytes 1056776 | tf_op jit(solution)/shard_map/ppermute | solution.py:261
  137.0 13.1 %collective-permute-start.26 = (bf16[224,768]{1,0:T(8,128)(2,1)}, bf16[224,768]{1,0:T(8,128)(2,1)}, u32[]{:S(2)}, u32[]{:S(2)}) collective-permute-start(bf16[224,768]{1,0:T(8,128)(2,1)} %accumulate.18), channel_id=1, source_target_pairs={{0,8},{4,12},{8,16},{12,20},{16,24},{20,28},{24,0},{28,4},{1,9},{5... | collective-permute-start | bytes 1032200 | tf_op jit(solution)/shard_map/ppermute | solution.py:267
  140.5 16.9 %collective-permute-start.27 = (bf16[224,768]{1,0:T(8,128)(2,1)}, bf16[224,768]{1,0:T(8,128)(2,1)}, u32[]{:S(2)}, u32[]{:S(2)}) collective-permute-start(bf16[224,768]{1,0:T(8,128)(2,1)} %accumulate.19), channel_id=1, source_target_pairs={{0,8},{4,12},{8,16},{12,20},{16,24},{20,28},{24,0},{28,4},{1,9},{5... | collective-permute-start | bytes 1032200 | tf_op jit(solution)/shard_map/ppermute | solution.py:267
  143.7 21.6 %collective-permute-start.25 = (bf16[240,768]{1,0:T(8,128)(2,1)}, bf16[240,768]{1,0:T(8,128)(2,1)}, u32[]{:S(2)}, u32[]{:S(2)}) collective-permute-start(bf16[240,768]{1,0:T(8,128)(2,1)} %accumulate.20), channel_id=1, source_target_pairs={{0,8},{4,12},{8,16},{12,20},{16,24},{20,28},{24,0},{28,4},{1,9},{5... | collective-permute-start | bytes 1105928 | tf_op jit(solution)/shard_map/ppermute | solution.py:267
  152.8 20.0 %collective-permute-start.28 = (bf16[224,768]{1,0:T(8,128)(2,1)}, bf16[224,768]{1,0:T(8,128)(2,1)}, u32[]{:S(2)}, u32[]{:S(2)}) collective-permute-start(bf16[224,768]{1,0:T(8,128)(2,1)} %accumulate.21), channel_id=1, source_target_pairs={{0,8},{4,12},{8,16},{12,20},{16,24},{20,28},{24,0},{28,4},{1,9},{5... | collective-permute-start | bytes 1032200 | tf_op jit(solution)/shard_map/ppermute | solution.py:267
  160.2 19.7 %collective-permute-start.30 = (bf16[224,768]{1,0:T(8,128)(2,1)}, bf16[224,768]{1,0:T(8,128)(2,1)}, u32[]{:S(2)}, u32[]{:S(2)}) collective-permute-start(bf16[224,768]{1,0:T(8,128)(2,1)} %accumulate.22), channel_id=1, source_target_pairs={{0,8},{4,12},{8,16},{12,20},{16,24},{20,28},{24,0},{28,4},{1,9},{5... | collective-permute-start | bytes 1032200 | tf_op jit(solution)/shard_map/ppermute | solution.py:267
  169.3 21.3 %collective-permute-start.33 = (bf16[240,768]{1,0:T(8,128)(2,1)}, bf16[240,768]{1,0:T(8,128)(2,1)}, u32[]{:S(2)}, u32[]{:S(2)}) collective-permute-start(bf16[240,768]{1,0:T(8,128)(2,1)} %get-tuple-element.140.refs_4_), channel_id=1, source_target_pairs={{0,3},{1,2},{2,1},{3,0},{4,7},{5,6},{6,5},{7,4},{8,11},{9,10},{10,... | collective-permute-start | bytes 1105928 | tf_op jit(solution)/shard_map/ppermute | solution.py:261
  171.1 20.1 %collective-permute-start.32 = (bf16[240,768]{1,0:T(8,128)(2,1)}, bf16[240,768]{1,0:T(8,128)(2,1)}, u32[]{:S(2)}, u32[]{:S(2)}) collective-permute-start(bf16[240,768]{1,0:T(8,128)(2,1)} %get-tuple-element.140.refs_4_), channel_id=1, source_target_pairs={{0,2},{1,3},{2,0},{3,1},{4,6},{5,7},{6,4},{7,5},{8,10},{9,11},{10,... | collective-permute-start | bytes 1105928 | tf_op jit(solution)/shard_map/ppermute | solution.py:261
  171.6 19.6 %collective-permute-start.31 = (bf16[240,768]{1,0:T(8,128)(2,1)}, bf16[240,768]{1,0:T(8,128)(2,1)}, u32[]{:S(2)}, u32[]{:S(2)}) collective-permute-start(bf16[240,768]{1,0:T(8,128)(2,1)} %get-tuple-element.140.refs_4_), channel_id=1, source_target_pairs={{0,1},{1,0},{2,3},{3,2},{4,5},{5,4},{6,7},{7,6},{8,9},{9,8},{10,11... | collective-permute-start | bytes 1105928 | tf_op jit(solution)/shard_map/ppermute | solution.py:261
  175.6 9.9 %collective-permute-start.29 = (bf16[224,768]{1,0:T(8,128)(2,1)}, bf16[224,768]{1,0:T(8,128)(2,1)}, u32[]{:S(2)}, u32[]{:S(2)}) collective-permute-start(bf16[224,768]{1,0:T(8,128)(2,1)} %accumulate.23), channel_id=1, source_target_pairs={{0,8},{4,12},{8,16},{12,20},{16,24},{20,28},{24,0},{28,4},{1,9},{5... | collective-permute-start | bytes 1032200 | tf_op jit(solution)/shard_map/ppermute | solution.py:267
  183.7 11.8 %collective-permute-start.39 = (bf16[224,768]{1,0:T(8,128)(2,1)}, bf16[224,768]{1,0:T(8,128)(2,1)}, u32[]{:S(2)}, u32[]{:S(2)}) collective-permute-start(bf16[224,768]{1,0:T(8,128)(2,1)} %get-tuple-element.139.refs_4_), channel_id=1, source_target_pairs={{0,3},{1,2},{2,1},{3,0},{4,7},{5,6},{6,5},{7,4},{8,11},{9,10},{10,... | collective-permute-start | bytes 1032200 | tf_op jit(solution)/shard_map/ppermute | solution.py:261
  185.5 20.4 %collective-permute-start.38 = (bf16[224,768]{1,0:T(8,128)(2,1)}, bf16[224,768]{1,0:T(8,128)(2,1)}, u32[]{:S(2)}, u32[]{:S(2)}) collective-permute-start(bf16[224,768]{1,0:T(8,128)(2,1)} %get-tuple-element.139.refs_4_), channel_id=1, source_target_pairs={{0,2},{1,3},{2,0},{3,1},{4,6},{5,7},{6,4},{7,5},{8,10},{9,11},{10,... | collective-permute-start | bytes 1032200 | tf_op jit(solution)/shard_map/ppermute | solution.py:261
  190.6 15.3 %collective-permute-start.37 = (bf16[224,768]{1,0:T(8,128)(2,1)}, bf16[224,768]{1,0:T(8,128)(2,1)}, u32[]{:S(2)}, u32[]{:S(2)}) collective-permute-start(bf16[224,768]{1,0:T(8,128)(2,1)} %get-tuple-element.139.refs_4_), channel_id=1, source_target_pairs={{0,1},{1,0},{2,3},{3,2},{4,5},{5,4},{6,7},{7,6},{8,9},{9,8},{10,11... | collective-permute-start | bytes 1032200 | tf_op jit(solution)/shard_map/ppermute | solution.py:261
  191.2 24.0 %collective-permute-start.36 = (bf16[224,768]{1,0:T(8,128)(2,1)}, bf16[224,768]{1,0:T(8,128)(2,1)}, u32[]{:S(2)}, u32[]{:S(2)}) collective-permute-start(bf16[224,768]{1,0:T(8,128)(2,1)} %get-tuple-element.138.refs_4_), channel_id=1, source_target_pairs={{0,3},{1,2},{2,1},{3,0},{4,7},{5,6},{6,5},{7,4},{8,11},{9,10},{10,... | collective-permute-start | bytes 1032200 | tf_op jit(solution)/shard_map/ppermute | solution.py:261
  192.9 22.2 %collective-permute-start.35 = (bf16[224,768]{1,0:T(8,128)(2,1)}, bf16[224,768]{1,0:T(8,128)(2,1)}, u32[]{:S(2)}, u32[]{:S(2)}) collective-permute-start(bf16[224,768]{1,0:T(8,128)(2,1)} %get-tuple-element.138.refs_4_), channel_id=1, source_target_pairs={{0,2},{1,3},{2,0},{3,1},{4,6},{5,7},{6,4},{7,5},{8,10},{9,11},{10,... | collective-permute-start | bytes 1032200 | tf_op jit(solution)/shard_map/ppermute | solution.py:261
  195.5 19.6 %collective-permute-start.34 = (bf16[224,768]{1,0:T(8,128)(2,1)}, bf16[224,768]{1,0:T(8,128)(2,1)}, u32[]{:S(2)}, u32[]{:S(2)}) collective-permute-start(bf16[224,768]{1,0:T(8,128)(2,1)} %get-tuple-element.138.refs_4_), channel_id=1, source_target_pairs={{0,1},{1,0},{2,3},{3,2},{4,5},{5,4},{6,7},{7,6},{8,9},{9,8},{10,11... | collective-permute-start | bytes 1032200 | tf_op jit(solution)/shard_map/ppermute | solution.py:261

commit v7 on v0

v7 whole, which is shorter than its diff:
```python
import functools

import jax
import jax.numpy as jnp
from jax import lax
from jax.experimental import pallas as pl
from jax.experimental.pallas import tpu as pltpu
from jax.sharding import PartitionSpec as P

beta_first = 0.9
beta_second = 0.999
adam_count = 100.0
epsilon = 1e-08

F32 = jnp.float32
BF16 = jnp.bfloat16
COST = pl.CostEstimate(flops=1024, bytes_accessed=1 << 20, transcendentals=0)
PARAMS = pltpu.CompilerParams(vmem_limit_bytes=58 * 1024 * 1024)
RING_PARAMS = pltpu.CompilerParams(vmem_limit_bytes=64 * 1024 * 1024)


def turn(core, grads, owned):
    tokens, columns = grads.shape
    chips = columns // (2 * owned)
    block = tokens // 4

    def kernel(core_ref, grads_ref, out_ref):
        for parity in range(2):

            @pl.when(core_ref[0] == parity)
            def _(parity=parity):
                for chip in range(chips):
                    begin = (2 * chip + parity) * owned
                    low = begin // 128 * 128
                    high = min(-(-(begin + owned) // 128) * 128, columns)
                    value = grads_ref[:, low:high].T
                    out_ref[chip] = value[begin - low : begin - low + owned]

    return pl.pallas_call(
        kernel,
        out_shape=jax.ShapeDtypeStruct((chips, owned, tokens), BF16),
        grid_spec=pltpu.PrefetchScalarGridSpec(
            num_scalar_prefetch=1,
            grid=(4,),
            in_specs=[pl.BlockSpec((block, columns), lambda i, core_ref: (i, 0))],
            out_specs=pl.BlockSpec((chips, owned, block), lambda i, core_ref: (0, 0, i)),
        ),
        compiler_params=PARAMS,
        cost_estimate=COST,
        name="turn",
    )(core, grads)


def plus(ones, twos, runs=1):
    rows, width = ones[0].shape
    count, size = len(ones), width // runs
    block = pl.BlockSpec((rows // 2, width), lambda i: (i, 0))

    def kernel(*refs):
        for index in range(count):
            total = (refs[index][...].astype(F32) + refs[count + index][...].astype(F32)).astype(BF16)
            for run in range(runs):
                refs[(2 + run) * count + index][...] = total[:, run * size : (run + 1) * size]

    return pl.pallas_call(
        kernel,
        grid=(2,),
        out_shape=[jax.ShapeDtypeStruct((rows, size), BF16)] * (count * runs),
        in_specs=[block] * (2 * count),
        out_specs=[pl.BlockSpec((rows // 2, size), lambda i: (i, 0))] * (count * runs),
        compiler_params=RING_PARAMS,
        cost_estimate=COST,
        name="plus",
    )(*ones, *twos)


def gradient(stacks, pieces, order, cuts=None):
    _, owned, tokens = stacks[0].shape
    rows, width = pieces[0].shape
    count = order.shape[0]

    def kernel(order_ref, *refs):
        piece_refs = refs[: len(pieces)]
        stack_refs = refs[len(pieces) : len(pieces) + 2]
        out_refs, (whole_ref, held_ref, sems) = refs[len(pieces) + 2 : -3], refs[-3:]
        step = pl.program_id(0)

        def fetch(block, side):
            return pltpu.make_async_copy(
                stack_refs[side].at[order_ref[block]],
                held_ref.at[block, :, pl.ds(side * tokens, tokens)],
                sems.at[block, side],
            )

        @pl.when(step == 0)
        def _():
            for block in range(count):
                for side in range(2):
                    fetch(block, side).start()
            for index, piece_ref in enumerate(piece_refs):
                whole_ref[index * rows : (index + 1) * rows, :] = piece_ref[...]

        for side in range(2):
            fetch(step, side).wait()
        value = jnp.dot(held_ref[step], whole_ref[...], preferred_element_type=F32).astype(BF16)
        if cuts is None:
            out_refs[0][0] = value
        else:
            for out_ref, cut in zip(out_refs, cuts):
                out_ref[...] = value[cut]

    if cuts is None:
        out_shape = [jax.ShapeDtypeStruct((count, owned, width), BF16)]
        out_specs = [pl.BlockSpec((1, owned, width), lambda i, order_ref: (i, 0, 0))]
    else:
        out_shape = [jax.ShapeDtypeStruct((cut.stop - cut.start, width), BF16) for cut in cuts]
        out_specs = [pl.BlockSpec(out.shape, lambda i, order_ref: (0, 0)) for out in out_shape]
    results = pl.pallas_call(
        kernel,
        out_shape=out_shape,
        grid_spec=pltpu.PrefetchScalarGridSpec(
            num_scalar_prefetch=1,
            grid=(count,),
            in_specs=[pl.BlockSpec((rows, width), lambda i, order_ref: (0, 0))] * len(pieces)
            + [pl.BlockSpec(memory_space=pl.ANY)] * 2,
            out_specs=out_specs,
            scratch_shapes=[
                pltpu.VMEM((2 * tokens, width), BF16),
                pltpu.VMEM((count, owned, 2 * tokens), BF16),
                pltpu.SemaphoreType.DMA((count, 2)),
            ],
        ),
        compiler_params=RING_PARAMS,
        cost_estimate=COST,
        name="gradient",
    )(order, *pieces, *stacks)
    return results[0] if cuts is None else results


def part_of(stack, block, rows):
    shape = (pl.Element(1), pl.Element(rows.stop - rows.start), pl.Element(stack.shape[2]))
    return pl.BlockSpec(shape, lambda i: (block, rows.start, 0))


def accumulate(arrived, own, block, rows):
    def kernel(own_ref, arrived_ref, out_ref):
        out_ref[...] = (own_ref[0].astype(F32) + arrived_ref[...].astype(F32)).astype(BF16)

    return pl.pallas_call(
        kernel,
        grid=(1,),
        out_shape=jax.ShapeDtypeStruct(arrived.shape, BF16),
        in_specs=[part_of(own, block, rows), pl.BlockSpec(memory_space=pltpu.VMEM)],
        out_specs=pl.BlockSpec(memory_space=pltpu.VMEM),
        compiler_params=RING_PARAMS,
        cost_estimate=COST,
        name="accumulate",
    )(own, arrived)


def adam(arrived, stacks, block, rows, first, second, held, column):
    owned, rank = first.shape
    height, width = arrived.shape

    def kernel(arrived_ref, first_ref, second_ref, *refs):
        first_out, second_out, direction_out = refs[-3:]
        grad_low = arrived_ref[...].astype(F32)
        for stack_ref in refs[: len(stacks)]:
            grad_low = grad_low + stack_ref[0].astype(F32)
        first_next = beta_first * first_ref[...] + (1.0 - beta_first) * grad_low
        second_next = beta_second * second_ref[...] + (1.0 - beta_second) * grad_low * grad_low
        first_out[...] = first_next
        second_out[...] = second_next
        bias_first = 1.0 - beta_first**adam_count
        bias_second = 1.0 - beta_second**adam_count
        direction = first_next / bias_first / (jnp.sqrt(second_next / bias_second) + epsilon)
        direction_out[...] = direction.astype(BF16)

    rectangle = pl.BlockSpec((pl.Element(height), pl.Element(width)), lambda i: (rows.start, column))
    return pl.pallas_call(
        kernel,
        grid=(1,),
        out_shape=[
            jax.ShapeDtypeStruct((owned, rank), F32),
            jax.ShapeDtypeStruct((owned, rank), F32),
            jax.ShapeDtypeStruct((height, width), BF16),
        ],
        in_specs=[pl.BlockSpec(memory_space=pltpu.VMEM), rectangle, rectangle]
        + [part_of(stack, block, rows) for stack in stacks]
        + [pl.BlockSpec(memory_space=pl.ANY)] * len(held),
        out_specs=[rectangle, rectangle, pl.BlockSpec((height, width), lambda i: (0, 0))],
        input_output_aliases={3 + len(stacks) + index: index for index in range(len(held))},
        compiler_params=RING_PARAMS,
        cost_estimate=COST,
        name="adam",
    )(arrived, first, second, *stacks, *held)


def expand(targets, starts, rests, rows, owned, basis, held):
    count = len(starts)
    begin = starts[0].shape[1]
    height, width = rests[0].shape
    features, rank = basis.shape
    block = min(512, features)

    def kernel(targets_ref, basis_ref, *refs):
        start_refs, rest_refs, (out_ref, whole_ref) = refs[:count], refs[count : 2 * count], refs[-2:]

        @pl.when(pl.program_id(0) == 0)
        def _():
            for index in range(count):
                here = slice(index * height, (index + 1) * height)
                whole_ref[here, :begin] = start_refs[index][...]
                whole_ref[here, begin:] = rest_refs[index][...]

        value = lax.dot_general(
            whole_ref[...], basis_ref[...], (((1,), (1,)), ((), ())), preferred_element_type=F32
        )
        for index in range(count):
            out_ref[targets_ref[index]] = value[index * height : (index + 1) * height]

    return pl.pallas_call(
        kernel,
        out_shape=jax.ShapeDtypeStruct((count, owned, features), F32),
        grid_spec=pltpu.PrefetchScalarGridSpec(
            num_scalar_prefetch=1,
            grid=(features // block,),
            in_specs=[pl.BlockSpec((block, rank), lambda i, targets_ref: (i, 0))]
            + [pl.BlockSpec((height, begin), lambda i, targets_ref: (0, 0))] * count
            + [pl.BlockSpec((height, width), lambda i, targets_ref: (0, 0))] * count
            + [pl.BlockSpec(memory_space=pl.ANY)] * len(held),
            out_specs=pl.BlockSpec(
                (pl.Element(count), pl.Element(height), pl.Element(block)),
                lambda i, targets_ref: (0, rows.start, i * block),
            ),
            scratch_shapes=[pltpu.VMEM((count * height, rank), BF16)],
        ),
        input_output_aliases={2 + 2 * count: 0} if held else {},
        compiler_params=RING_PARAMS,
        cost_estimate=COST,
        name="expand",
    )(targets, basis, *starts, *rests, *held)


def total_of(*terms):
    total = terms[0].astype(F32)
    for term in terms[1:]:
        total = total + term.astype(F32)
    return total.astype(BF16)


def after(value, *earlier):
    return lax.optimization_barrier((value, *jax.tree.leaves(earlier)))[0]


def local(activations, out_grads, projector, first_moment, second_moment):
    owned = first_moment.shape[1]
    features = activations[0]
    basis = projector[0]
    rank = basis.shape[1]
    tokens = features.shape[0]
    dp_count, fsdp_count = lax.axis_size("dp"), lax.axis_size("fsdp")
    dp, fsdp = lax.axis_index("dp"), lax.axis_index("fsdp")
    chips = dp_count // 2
    chip, core = dp // 2, dp % 2
    width = rank * 3 // 8

    offsets = [1 << bit for bit in range(fsdp_count.bit_length() - 1)]
    order = jnp.stack([fsdp ^ offset for offset in range(fsdp_count)]).astype(jnp.int32)
    hops = chips - 1
    ring_order = (chip - 1 - jnp.arange(chips, dtype=jnp.int32) + chips) % chips

    def across(value, offset):
        return lax.ppermute(value, "fsdp", [(index, index ^ offset) for index in range(fsdp_count)])

    def sibling(value):
        return lax.ppermute(value, "dp", [(index, index ^ 1) for index in range(dp_count)])

    def onward(value):
        return lax.ppermute(value, "dp", [(index, (index + 2) % dp_count) for index in range(dp_count)])

    def exchange(halves, step):
        return [across(half, offsets[step if index % 2 == 0 else -1 - step]) for index, half in enumerate(halves)]

    def add(halves, arrived):
        return [total_of(half, term) for half, term in zip(halves, arrived)]

    def add_pairs(pieces, arrived):
        return [
            total
            for index in range(0, len(pieces), 2)
            for total in plus(pieces[index : index + 2], arrived[index : index + 2])
        ]

    def projected(features, columns):
        partial = jnp.dot(features, basis[:, columns], preferred_element_type=F32).astype(BF16)
        return [partial[: tokens // 2], partial[tokens // 2 :]]

    grads = out_grads[0]
    others_grads = sibling(grads)
    sums_0 = projected(features, slice(0, width))
    coming_0 = exchange(sums_0, 0)
    sums_1 = projected(after(features, *sums_0), slice(width, rank))
    parity = jnp.reshape(core, (1,)).astype(jnp.int32)
    mine = turn(parity, after(grads, *sums_1), owned)
    sums_0 = add(sums_0, [after(term, mine) for term in coming_0])
    for step in range(1, len(offsets) - 1):
        sums_0 = add(sums_0, exchange(sums_0, step))
    coming_0 = exchange(sums_0, len(offsets) - 1)
    theirs = turn(parity, after(others_grads, *sums_0), owned)
    stacks = [mine, theirs]
    sums_0 = add(sums_0, [after(term, theirs) for term in coming_0])
    both_0 = sums_0 + [sibling(half) for half in sums_0]
    coming_1 = exchange([after(half, *sums_0) for half in sums_1], 0)

    product = gradient(stacks, both_0, jnp.arange(chips, dtype=jnp.int32))
    lines = [list(range(parity, dp_count, 2)) for parity in range(2)]
    mine_0 = lax.psum_scatter(
        product.reshape(chips * owned, width), "dp", scatter_dimension=0, axis_index_groups=lines, tiled=True
    )

    sums_1 = add_pairs(sums_1, [after(term, product) for term in coming_1])
    for step in range(1, len(offsets)):
        sums_1 = add_pairs(sums_1, exchange(sums_1, step))
    both_1 = sums_1 + [sibling(half) for half in sums_1]

    held = ()

    def step_of(arrived, stacks, block, rows, column):
        nonlocal held
        first_next, second_next, direction = adam(
            arrived, stacks, block, rows, first_moment[0], second_moment[0], held, column
        )
        held = (first_next, second_next)
        return direction

    ends = [0, owned]
    if owned % 16 == 0:
        ends = [-(-owned * index // 48) * 16 for index in range(4)]
    parts = [slice(*pair) for pair in zip(ends, ends[1:])]
    count = len(parts)

    leaving = gradient(stacks, both_1, ring_order[:1], parts)
    arrived = [onward(value) for value in leaving]
    others = gradient([after(stacks[0], *leaving), stacks[1]], both_1, ring_order[1:])

    token = others
    directions = []

    starts = [[] for _ in parts]
    stages = [(part, step) for part in range(count) for step in range(len(offsets))]
    reached = []

    def spread(token):
        part, step = stages.pop(0)
        rows = parts[part]
        if step == 0:
            starts[part].append(step_of(after(mine_0[rows], token), (), 0, rows, 0))
        starts[part].extend([across(after(piece, token), offsets[step]) for piece in starts[part]])
        return starts[part]

    events = sorted((2 * hop + 1.5 * part, part, hop) for part in range(count) for hop in range(1, chips))
    for number, (_, part, hop) in enumerate(events):
        rows = parts[part]
        if number >= 2 and (reached or stages):
            token = [token, *reached]
            reached = spread(token) if stages else []
        if hop < hops:
            token = accumulate(after(arrived[part], token), others, hop - 1, rows)
            arrived[part] = onward(token)
            continue
        token = step_of(after(arrived[part], token), (others,), hop - 1, rows, width)
        sent = after(token, directions[part - 2]) if part > 1 else token
        directions.append([token] + [across(sent, offset) for offset in range(1, fsdp_count)])
    while stages:
        spread(token)

    update = ()
    for rows, start, pieces in zip(parts, starts, directions):
        pieces = [after(pieces[0], token), *pieces[1:]]
        update = (expand(order, start, pieces, rows, owned, basis, update),)
    return (update[0][None], held[0][None], held[1][None])


def solution(mesh):
    in_specs = (
        P(None, "dp", "fsdp"),
        P(None, "dp", "fsdp"),
        P(None, "fsdp", None),
        P(None, ("fsdp", "dp"), None),
        P(None, ("fsdp", "dp"), None),
    )
    out_specs = (
        P(None, None, "dp", "fsdp"),
        P(None, ("fsdp", "dp"), None),
        P(None, ("fsdp", "dp"), None),
    )
    return jax.shard_map(local, mesh=mesh, in_specs=in_specs, out_specs=out_specs, check_vma=False)
```

time: 344 us -> 253 us (0.74)
  waiting for transfers between devices: 239 us -> 74.7 us
  Pallas kernels: 0 us -> 105 us
  matrix products: 48.2 us -> 8.56 us
  starting transfers between devices: 0.3 us -> 38.8 us
  local copies, waits for them, and re-layouts: 33.8 us -> 8.39 us
  other arithmetic: 7.76 us -> 1.54 us
    unnamed x4 -> x1, waiting for transfers between devices: 109 us -> 0.02 us
    pallas_call x0 -> x22, Pallas kernels: none -> 105 us  [the longest x3 30.8 us: gradient(): pl.pallas_call(kernel, out_shape=out_shape, grid_spec=pltpu.PrefetchScala...]
    ppermute x0 -> x40, waiting for transfers between devices: none -> 74.7 us  [the longest x26 60.3 us: across(): lax.ppermute(value, 'fsdp', [(index, index ^ offset) for index in range(f...]
    psum x1 -> x0, waiting for transfers between devices: 72.4 us -> none  [local(): projected = lax.psum(partial_value.astype(jnp.bfloat16), 'fsdp')]
    all_gather x1 -> x0, waiting for transfers between devices: 57.6 us -> none  [local(): lax.all_gather(direction, 'fsdp', axis=0, tiled=True)]
    dot_general x3 -> x2, matrix products: 48.2 us -> 8.56 us  [projected(): jnp.dot(features, basis[:, columns], preferred_element_type=F32)]
    ppermute x0 -> x40, starting transfers between devices: none -> 38.8 us  [the longest x26 28.1 us: across(): lax.ppermute(value, 'fsdp', [(index, index ^ offset) for index in range(f...]
    unnamed x8 -> x10, local copies, waits for them, and re-layouts: 31.2 us -> 1.19 us
  transfers between devices with their start and end apart: 3 -> 41, of which waited for: 3 -> 19; matrix products, arithmetic and copies ran while one was open for 3% -> 7% of each run, Pallas kernels for 0% -> 34%
where the time goes in v7:
time: 253 us; the launch traced here: 252 us
  Pallas kernels  105 us (42%)
  waiting for transfers between devices  74.7 us (30%)
  starting transfers between devices  38.8 us (15%)
  between operations  14.2 us (6%)
  matrix products  8.56 us (3%)
  local copies, waits for them, and re-layouts  8.39 us (3%)
    ppermute x26, waiting for transfers between devices, across(): lax.ppermute(value, 'fsdp', [(index, index ^ offset) for index in range(f...  60.3 us
    pallas_call x3, Pallas kernels, gradient(): pl.pallas_call(kernel, out_shape=out_shape, grid_spec=pltpu.PrefetchScala...  30.8 us
    pallas_call x3, Pallas kernels, expand(): pl.pallas_call(kernel, out_shape=jax.ShapeDtypeStruct((count, owned, feat...  28.2 us
    ppermute x26, starting transfers between devices, across(): lax.ppermute(value, 'fsdp', [(index, index ^ offset) for index in range(f...  28.1 us
    pallas_call x6, Pallas kernels, adam(): pl.pallas_call(kernel, grid=(1,), out_shape=[jax.ShapeDtypeStruct((owned,...  15.1 us
    pallas_call x2, Pallas kernels, turn(): pl.pallas_call(kernel, out_shape=jax.ShapeDtypeStruct((chips, owned, toke...  15.1 us
    pallas_call x6, Pallas kernels, accumulate(): pl.pallas_call(kernel, grid=(1,), out_shape=jax.ShapeDtypeStruct(arrived....  11 us
    ppermute x9, waiting for transfers between devices, onward(): lax.ppermute(value, 'dp', [(index, (index + 2) % dp_count) for index in r...  10.9 us
  transfers between devices with their start and end apart: 41, of which 19 were waited for; matrix products, arithmetic and copies ran while one was open for 7% of the time, Pallas kernels for 34%

profile of v7, /device:TPU:0, one launch (start us, length us, event | category | flops | bytes accessed | tf_op | source)
XLA Modules:
  0.0 251.6 jit_solution(14354863945581276644)
XLA Ops:
  7.7 5.1 %fusion.7 = bf16[1024,384]{1,0:T(8,128)(2,1)S(1)} fusion(bf16[2048,1024]{1,0:T(8,128)(2,1)} %bitcast.33, bf16[1,1024,2048]{2,1,0:T(8,128)(2,1)} %param.5), kind=kOutput, calls=%fused_computation.5 | convolution fusion | flops 1611005952 | bytes 6553600 | tf_op jit(solution)/shard_map/dot_general | solution.py:296
  13.7 2.5 %collective-permute-start.3 = (bf16[512,384]{1,0:T(8,128)(2,1)}, bf16[512,384]{1,0:T(8,128)(2,1)S(1)}, u32[]{:S(2)}, u32[]{:S(2)}) collective-permute-start(bf16[512,384]{1,0:T(8,128)(2,1)} %get-tuple-element.131), channel_id=1, source_target_pairs={{0,2},{1,3},{2,0},{3,1},{4,6},{5,7},{6,4},{7,5},{8,10},{9,11},{10,... | collective-permute-start | bytes 1179656 | tf_op jit(solution)/shard_map/ppermute | solution.py:274
  16.3 1.5 collective-permute-start
  17.8 3.4 %fusion.2 = bf16[1024,640]{1,0:T(8,128)(2,1)S(1)} fusion(bf16[1024,2048]{1,0:T(8,128)(2,1)S(1)} %bitcast.42, bf16[2048,1024]{1,0:T(8,128)(2,1)S(1)} %bitcast.37), kind=kOutput, calls=%fused_computation.2 | convolution fusion | flops 2685009920 | bytes 8126464 | tf_op jit(solution)/shard_map/dot_general | solution.py:296
  21.2 1.2 fusion.12
  22.4 7.5 %turn.2.refs_4_ = bf16[4,688,1024]{2,1,0:T(8,128)(2,1)} custom-call(s32[1]{0:T(128)} %bitcast.6.core_ref, bf16[1024,5504]{1,0:T(8,128)(2,1)} %bitcast.39), custom_call_target="tpu_custom_call" | custom-call | flops 1024 | bytes 1048576 | tf_op jit(solution)/shard_map/turn/pallas_call | solution.py:39
  30.7 7.6 %turn.3.refs_5_ = bf16[4,688,1024]{2,1,0:T(8,128)(2,1)} custom-call(s32[1]{0:T(128)} %bitcast.6.core_ref, bf16[1024,5504]{1,0:T(8,128)(2,1)} %collective-permute-done.2.grads_ref), custom_call_target="tpu_custom_call" | custom-call | flops 1024 | bytes 1048576 | tf_op jit(solution)/shard_map/turn/pallas_call | solution.py:39
  38.3 2.8 %collective-permute-done.4 = bf16[512,384]{1,0:T(8,128)(2,1)S(1)} collective-permute-done((bf16[512,384]{1,0:T(8,128)(2,1)S(1)}, bf16[512,384]{1,0:T(8,128)(2,1)S(1)}, u32[]{:S(2)}, u32[]{:S(2)}) %collective-permute-start.4) | collective-permute-done | bytes 393248 | tf_op jit(solution)/shard_map/ppermute | solution.py:274
  42.0 1.2 collective-permute-done.5.refs_2_
  44.5 11.2 %gradient.3 = bf16[4,688,384]{2,1,0:T(8,128)(2,1)} custom-call(s32[4]{0:T(128)} %iota.6.order_ref, bf16[512,384]{1,0:T(8,128)(2,1)} %copy-done.2, bf16[512,384]{1,0:T(8,128)(2,1)} %copy-done.1, bf16[512,384]{1,0:T(8,128)(2,1)} %copy-done.3, bf16[512,384]{1,0:T(8,128)(2,1)} %collective-permute-done.6.refs_3_, bf16[4,688,1024]{2,1,0:T(8,128)(2,1)} %turn.2.refs_4_, ...), custom_call_target="tpu_custom_call" | custom-call | flops 1024 | bytes 1048576 | tf_op jit(solution)/shard_map/gradient/pallas_call | solution.py:118
  55.8 1.6 collective-permute-start.7
  57.8 15.1 %collective-permute-done.7.refs_2_ = bf16[512,640]{1,0:T(8,128)(2,1)} collective-permute-done((bf16[512,640]{1,0:T(8,128)(2,1)}, bf16[512,640]{1,0:T(8,128)(2,1)}, u32[]{:S(2)}, u32[]{:S(2)}) %collective-permute-start.7) | collective-permute-done | bytes 655392 | tf_op jit(solution)/shard_map/ppermute | solution.py:274
  72.9 1.2 collective-permute-done.8.refs_3_
  74.1 2.6 %plus.2 = (bf16[512,640]{1,0:T(8,128)(2,1)}, bf16[512,640]{1,0:T(8,128)(2,1)}) custom-call(bf16[512,640]{1,0:T(8,128)(2,1)} %get-tuple-element.72.refs_0_, bf16[512,640]{1,0:T(8,128)(2,1)} %get-tuple-element.74.refs_1_, bf16[512,640]{1,0:T(8,128)(2,1)} %collective-permute-done.7.refs_2_, bf16[512,640]{1,0:T(8,128)(2,1)} %collective-permute-done.8.refs_3_), custom_call_target="tpu_custom_call" | custom-call | flops 1024 | bytes 1048576 | tf_op jit(solution)/shard_map/plus/pallas_call | solution.py:65
  77.7 15.0 %collective-permute-done.9.refs_2_ = bf16[512,640]{1,0:T(8,128)(2,1)} collective-permute-done((bf16[512,640]{1,0:T(8,128)(2,1)}, bf16[512,640]{1,0:T(8,128)(2,1)}, u32[]{:S(2)}, u32[]{:S(2)}) %collective-permute-start.9) | collective-permute-done | bytes 655392 | tf_op jit(solution)/shard_map/ppermute | solution.py:274
  92.9 2.6 %plus.3 = (bf16[512,640]{1,0:T(8,128)(2,1)}, bf16[512,640]{1,0:T(8,128)(2,1)}) custom-call(bf16[512,640]{1,0:T(8,128)(2,1)} %get-tuple-element.76.refs_0_, bf16[512,640]{1,0:T(8,128)(2,1)} %get-tuple-element.77.refs_1_, bf16[512,640]{1,0:T(8,128)(2,1)} %collective-permute-done.9.refs_2_, bf16[512,640]{1,0:T(8,128)(2,1)} %collective-permute-done.10.refs_3_), custom_call_target="tpu_custom_call" | custom-call | flops 1024 | bytes 1048576 | tf_op jit(solution)/shard_map/plus/pallas_call | solution.py:65
  96.5 1.4 collective-permute-done.11.refs_2_
  97.9 0.9 collective-permute-done.12.refs_3_
  98.9 7.3 %gradient.4 = (bf16[240,640]{1,0:T(8,128)(2,1)}, bf16[224,640]{1,0:T(8,128)(2,1)}, bf16[224,640]{1,0:T(8,128)(2,1)}) custom-call(s32[1]{0:T(128)} %bitcast.41, bf16[512,640]{1,0:T(8,128)(2,1)} %get-tuple-element.78.refs_0_, bf16[512,640]{1,0:T(8,128)(2,1)} %get-tuple-element.79.refs_1_, bf16[512,640]{1,0:T(8,128)(2,1)} %collective-permute-done.11.refs_2_, ...), custom_call_target="tpu_custom_call" | custom-call | flops 1024 | bytes 1048576 | tf_op jit(solution)/shard_map/gradient/pallas_call | solution.py:118
  106.2 1.6 collective-permute-start.13
  107.9 1.6 collective-permute-start.15
  109.4 1.2 slice.40.order_ref
  110.7 12.2 %gradient.5.own_ref.refs_0_ = bf16[3,688,640]{2,1,0:T(8,128)(2,1)} custom-call(s32[3]{0:T(128)} %slice.40.order_ref, bf16[512,640]{1,0:T(8,128)(2,1)} %get-tuple-element.78.refs_0_, bf16[512,640]{1,0:T(8,128)(2,1)} %get-tuple-element.79.refs_1_, bf16[512,640]{1,0:T(8,128)(2,1)} %collective-permute-done.11.refs_2_, ...), custom_call_target="tpu_custom_call" | custom-call | flops 1024 | bytes 1048576 | tf_op jit(solution)/shard_map/gradient/pallas_call | solution.py:118
  122.9 1.9 accumulate.6
  124.7 1.6 collective-permute-start.14
  126.3 1.8 accumulate.7
  128.1 1.6 slice.51.arrived_ref
  129.8 2.3 adam.6
  132.9 1.5 collective-permute-start.17
  134.4 1.2 collective-permute-done.14.arrived_ref
  135.6 1.9 accumulate.8
  138.2 1.5 collective-permute-start.20
  140.2 1.8 fusion.14
  142.0 2.6 %collective-permute-done.18.arrived_ref = bf16[224,640]{1,0:T(8,128)(2,1)} collective-permute-done((bf16[224,640]{1,0:T(8,128)(2,1)}, bf16[224,640]{1,0:T(8,128)(2,1)}, u32[]{:S(2)}, u32[]{:S(2)}) %collective-permute-start.18) | collective-permute-done | bytes 286752 | tf_op jit(solution)/shard_map/ppermute | solution.py:280
  144.6 1.8 accumulate.9
  146.4 0.9 collective-permute-done.21.refs_3_
  147.3 2.2 adam.7
  151.0 1.3 collective-permute-start.26
  152.3 1.8 accumulate.10
  154.2 1.1 collective-permute-done.22.refs_1_
  155.3 1.5 collective-permute-start.23
  158.1 4.4 %collective-permute-done.16.arrived_ref = bf16[240,640]{1,0:T(8,128)(2,1)} collective-permute-done((bf16[240,640]{1,0:T(8,128)(2,1)}, bf16[240,640]{1,0:T(8,128)(2,1)}, u32[]{:S(2)}, u32[]{:S(2)}) %collective-permute-start.16) | collective-permute-done | bytes 307232 | tf_op jit(solution)/shard_map/ppermute | solution.py:280
  162.5 2.9 %adam.8 = (f32[688,1024]{1,0:T(8,128)}, f32[688,1024]{1,0:T(8,128)}, bf16[240,640]{1,0:T(8,128)(2,1)}) custom-call(bf16[240,640]{1,0:T(8,128)(2,1)} %collective-permute-done.16.arrived_ref, f32[688,1024]{1,0:T(8,128)} %bitcast.21, f32[688,1024]{1,0:T(8,128)} %bitcast.27, ...), custom_call_target="tpu_custom_call", output_to_operand_aliasing={{0}: (4, {}), {1}: (5, {})} | custom-call | flops 1024 | bytes 1048576 | tf_op jit(solution)/shard_map/adam/pallas_call | solution.py:180
  165.4 2.7 %collective-permute-done.26.arrived_ref = bf16[224,640]{1,0:T(8,128)(2,1)} collective-permute-done((bf16[224,640]{1,0:T(8,128)(2,1)}, bf16[224,640]{1,0:T(8,128)(2,1)}, u32[]{:S(2)}, u32[]{:S(2)}) %collective-permute-start.26) | collective-permute-done | bytes 286752 | tf_op jit(solution)/shard_map/ppermute | solution.py:280
  168.1 1.8 accumulate.11
  169.9 2.2 adam.9
  172.1 1.4 collective-permute-start.25
  173.5 6.2 %collective-permute-done.25.refs_1_ = bf16[224,384]{1,0:T(8,128)(2,1)} collective-permute-done((bf16[224,384]{1,0:T(8,128)(2,1)}, bf16[224,384]{1,0:T(8,128)(2,1)}, u32[]{:S(2)}, u32[]{:S(2)}) %collective-permute-start.25) | collective-permute-done | bytes 172064 | tf_op jit(solution)/shard_map/ppermute | solution.py:274
  179.8 1.5 collective-permute-start.27
  181.3 1.3 collective-permute-start.33
  182.6 1.5 collective-permute-start.32
  184.8 2.8 %adam.10 = (f32[688,1024]{1,0:T(8,128)}, f32[688,1024]{1,0:T(8,128)}, bf16[224,640]{1,0:T(8,128)(2,1)}) custom-call(bf16[224,640]{1,0:T(8,128)(2,1)} %collective-permute-done.30.arrived_ref, f32[688,1024]{1,0:T(8,128)} %bitcast.23, f32[688,1024]{1,0:T(8,128)} %bitcast.29, ...), custom_call_target="tpu_custom_call", output_to_operand_aliasing={{0}: (4, {}), {1}: (5, {})} | custom-call | flops 1024 | bytes 1048576 | tf_op jit(solution)/shard_map/adam/pallas_call | solution.py:180
  187.5 1.3 collective-permute-start.39
  188.9 2.8 %collective-permute-done.27.refs_2_ = bf16[224,384]{1,0:T(8,128)(2,1)} collective-permute-done((bf16[224,384]{1,0:T(8,128)(2,1)}, bf16[224,384]{1,0:T(8,128)(2,1)}, u32[]{:S(2)}, u32[]{:S(2)}) %collective-permute-start.27) | collective-permute-done | bytes 172064 | tf_op jit(solution)/shard_map/ppermute | solution.py:274
  191.6 1.2 collective-permute-start.28
  192.8 14.0 %collective-permute-done.28.refs_3_ = bf16[224,384]{1,0:T(8,128)(2,1)} collective-permute-done((bf16[224,384]{1,0:T(8,128)(2,1)}, bf16[224,384]{1,0:T(8,128)(2,1)}, u32[]{:S(2)}, u32[]{:S(2)}) %collective-permute-start.28) | collective-permute-done | bytes 172064 | tf_op jit(solution)/shard_map/ppermute | solution.py:274
  206.9 1.4 collective-permute-start.38
  208.3 2.8 %adam.11 = (f32[688,1024]{1,0:T(8,128)}, f32[688,1024]{1,0:T(8,128)}, bf16[224,640]{1,0:T(8,128)(2,1)}) custom-call(bf16[224,640]{1,0:T(8,128)(2,1)} %collective-permute-done.29.arrived_ref, f32[688,1024]{1,0:T(8,128)} %bitcast.24, f32[688,1024]{1,0:T(8,128)} %bitcast.30, ...), custom_call_target="tpu_custom_call", output_to_operand_aliasing={{0}: (4, {}), {1}: (5, {})} | custom-call | flops 1024 | bytes 1048576 | tf_op jit(solution)/shard_map/adam/pallas_call | solution.py:180
  211.1 1.3 collective-permute-start.37
  213.1 1.4 collective-permute-start.35
  214.6 1.3 collective-permute-start.34
  216.5 9.6 %expand.3.refs_8_ = f32[4,688,2048]{2,1,0:T(8,128)} custom-call(s32[4]{0:T(128)} %pad_add_fusion.targets_ref, bf16[2048,1024]{1,0:T(8,128)(2,1)} %bitcast.34, bf16[240,384]{1,0:T(8,128)(2,1)} %get-tuple-element.91.refs_0_, bf16[240,384]{1,0:T(8,128)(2,1)} %collective-permute-done.19.refs_1_, bf16[240,384]{1,0:T(8,128)(2,1)} %collective-permute-done.20.refs_2_, ...), custom_call_target="tpu_custom_call" | custom-call | flops 1024 | bytes 1048576 | tf_op jit(solution)/shard_map/expand/pallas_call | solution.py:222
  226.2 9.3 %expand.4.refs_8_ = f32[4,688,2048]{2,1,0:T(8,128)} custom-call(s32[4]{0:T(128)} %pad_add_fusion.targets_ref, bf16[2048,1024]{1,0:T(8,128)(2,1)} %bitcast.35, bf16[224,384]{1,0:T(8,128)(2,1)} %get-tuple-element.103.refs_0_, bf16[224,384]{1,0:T(8,128)(2,1)} %collective-permute-done.22.refs_1_, ...), custom_call_target="tpu_custom_call", output_to_operand_aliasing={{}: (10, {})} | custom-call | flops 1024 | bytes 1048576 | tf_op jit(solution)/shard_map/expand/pallas_call | solution.py:222
  235.5 9.3 %expand.5 = f32[4,688,2048]{2,1,0:T(8,128)} custom-call(s32[4]{0:T(128)} %pad_add_fusion.targets_ref, bf16[2048,1024]{1,0:T(8,128)(2,1)} %bitcast.36, bf16[224,384]{1,0:T(8,128)(2,1)} %get-tuple-element.111.refs_0_, bf16[224,384]{1,0:T(8,128)(2,1)} %collective-permute-done.25.refs_1_, ...), custom_call_target="tpu_custom_call", output_to_operand_aliasing={{}: (10, {})} | custom-call | flops 1024 | bytes 1048576 | tf_op jit(solution)/shard_map/expand/pallas_call | solution.py:222
  (64 shorter events, 14.1 us)
Async XLA Ops:
  7.2 121.0 %reduce-scatter.2.cloned.1.call-start = ((), (), s32[]{:S(2)}) async-start(), calls=%async_computation.1 | async-start | bytes 2641920 | tf_op jit(solution)/shard_map/reduce_scatter | solution.py:318
  7.2 23.5 %collective-permute-start.2 = (bf16[1024,5504]{1,0:T(8,128)(2,1)}, bf16[1024,5504]{1,0:T(8,128)(2,1)}, u32[]{:S(2)}, u32[]{:S(2)}) collective-permute-start(bf16[1024,5504]{1,0:T(8,128)(2,1)} %bitcast.38), channel_id=1, source_target_pairs={{0,4},{4,0},{8,12},{12,8},{16,20},{20,16},{24,28},{28,24},{1,5},{5... | collective-permute-start | bytes 33816584 | tf_op jit(solution)/shard_map/ppermute | solution.py:277
  7.7 10.0 %copy-start = (bf16[1,2048,1024]{2,1,0:T(8,128)(2,1)S(1)}, bf16[1,2048,1024]{2,1,0:T(8,128)(2,1)}, u32[]{:S(2)}) copy-start(bf16[1,2048,1024]{2,1,0:T(8,128)(2,1)} %param.7) | copy-start | bytes 12582916
  7.7 10.0 %copy-start.4 = (bf16[1,1024,2048]{2,1,0:T(8,128)(2,1)S(1)}, bf16[1,1024,2048]{2,1,0:T(8,128)(2,1)}, u32[]{:S(2)}) copy-start(bf16[1,1024,2048]{2,1,0:T(8,128)(2,1)} %param.5) | copy-start | bytes 12582916
  13.7 16.2 %collective-permute-start.3 = (bf16[512,384]{1,0:T(8,128)(2,1)}, bf16[512,384]{1,0:T(8,128)(2,1)S(1)}, u32[]{:S(2)}, u32[]{:S(2)}) collective-permute-start(bf16[512,384]{1,0:T(8,128)(2,1)} %get-tuple-element.131), channel_id=1, source_target_pairs={{0,2},{1,3},{2,0},{3,1},{4,6},{5,7},{6,4},{7,5},{8,10},{9,11},{10,... | collective-permute-start | bytes 1179656 | tf_op jit(solution)/shard_map/ppermute | solution.py:274
  16.3 13.6 %collective-permute-start = (bf16[512,384]{1,0:T(8,128)(2,1)S(1)}, bf16[512,384]{1,0:T(8,128)(2,1)S(1)}, u32[]{:S(2)}, u32[]{:S(2)}) collective-permute-start(bf16[512,384]{1,0:T(8,128)(2,1)S(1)} %get-tuple-element.132), channel_id=1, source_target_pairs={{0,1},{1,0},{2,3},{3,2},{4,5},{5,4},{6,7},{7,6},{8,9},{9,8},{10,11... | collective-permute-start | bytes 1179656 | tf_op jit(solution)/shard_map/ppermute | solution.py:274
  30.1 11.0 %collective-permute-start.4 = (bf16[512,384]{1,0:T(8,128)(2,1)S(1)}, bf16[512,384]{1,0:T(8,128)(2,1)S(1)}, u32[]{:S(2)}, u32[]{:S(2)}) collective-permute-start(bf16[512,384]{1,0:T(8,128)(2,1)S(1)} %get-tuple-element.129), channel_id=1, source_target_pairs={{0,1},{1,0},{2,3},{3,2},{4,5},{5,4},{6,7},{7,6},{8,9},{9,8},{10,11... | collective-permute-start | bytes 1179656 | tf_op jit(solution)/shard_map/ppermute | solution.py:274
  30.7 10.6 %collective-permute-start.1 = (bf16[512,384]{1,0:T(8,128)(2,1)S(1)}, bf16[512,384]{1,0:T(8,128)(2,1)S(1)}, u32[]{:S(2)}, u32[]{:S(2)}) collective-permute-start(bf16[512,384]{1,0:T(8,128)(2,1)S(1)} %get-tuple-element.130), channel_id=1, source_target_pairs={{0,2},{1,3},{2,0},{3,1},{4,6},{5,7},{6,4},{7,5},{8,10},{9,11},{10,... | collective-permute-start | bytes 1179656 | tf_op jit(solution)/shard_map/ppermute | solution.py:274
  41.2 0.8 copy-start.1
  41.4 2.5 %copy-start.2 = (bf16[512,384]{1,0:T(8,128)(2,1)}, bf16[512,384]{1,0:T(8,128)(2,1)S(1)}, u32[]{:S(2)}) copy-start(bf16[512,384]{1,0:T(8,128)(2,1)S(1)} %add_convert_fusion.1.refs_0_) | copy-start | bytes 1179652
  41.4 1.8 collective-permute-start.5
  42.0 2.0 collective-permute-start.6
  43.2 0.7 copy-start.3
  55.8 17.2 %collective-permute-start.7 = (bf16[512,640]{1,0:T(8,128)(2,1)}, bf16[512,640]{1,0:T(8,128)(2,1)}, u32[]{:S(2)}, u32[]{:S(2)}) collective-permute-start(bf16[512,640]{1,0:T(8,128)(2,1)} %get-tuple-element.72.refs_0_), channel_id=1, source_target_pairs={{0,1},{1,0},{2,3},{3,2},{4,5},{5,4},{6,7},{7,6},{8,9},{9,8},{10,11... | collective-permute-start | bytes 1966088 | tf_op jit(solution)/shard_map/ppermute | solution.py:274
  57.3 16.8 %collective-permute-start.8 = (bf16[512,640]{1,0:T(8,128)(2,1)}, bf16[512,640]{1,0:T(8,128)(2,1)}, u32[]{:S(2)}, u32[]{:S(2)}) collective-permute-start(bf16[512,640]{1,0:T(8,128)(2,1)} %get-tuple-element.74.refs_1_), channel_id=1, source_target_pairs={{0,2},{1,3},{2,0},{3,1},{4,6},{5,7},{6,4},{7,5},{8,10},{9,11},{10,... | collective-permute-start | bytes 1966088 | tf_op jit(solution)/shard_map/ppermute | solution.py:274
  76.8 15.9 %collective-permute-start.9 = (bf16[512,640]{1,0:T(8,128)(2,1)}, bf16[512,640]{1,0:T(8,128)(2,1)}, u32[]{:S(2)}, u32[]{:S(2)}) collective-permute-start(bf16[512,640]{1,0:T(8,128)(2,1)} %get-tuple-element.76.refs_0_), channel_id=1, source_target_pairs={{0,2},{1,3},{2,0},{3,1},{4,6},{5,7},{6,4},{7,5},{8,10},{9,11},{10,... | collective-permute-start | bytes 1966088 | tf_op jit(solution)/shard_map/ppermute | solution.py:274
  77.3 15.6 %collective-permute-start.10 = (bf16[512,640]{1,0:T(8,128)(2,1)}, bf16[512,640]{1,0:T(8,128)(2,1)}, u32[]{:S(2)}, u32[]{:S(2)}) collective-permute-start(bf16[512,640]{1,0:T(8,128)(2,1)} %get-tuple-element.77.refs_1_), channel_id=1, source_target_pairs={{0,1},{1,0},{2,3},{3,2},{4,5},{5,4},{6,7},{7,6},{8,9},{9,8},{10,11... | collective-permute-start | bytes 1966088 | tf_op jit(solution)/shard_map/ppermute | solution.py:274
  95.5 2.4 collective-permute-start.11
  95.5 3.4 %collective-permute-start.12 = (bf16[512,640]{1,0:T(8,128)(2,1)}, bf16[512,640]{1,0:T(8,128)(2,1)}, u32[]{:S(2)}, u32[]{:S(2)}) collective-permute-start(bf16[512,640]{1,0:T(8,128)(2,1)} %get-tuple-element.79.refs_1_), channel_id=1, source_target_pairs={{0,4},{4,0},{8,12},{12,8},{16,20},{20,16},{24,28},{28,24},{1,5},{5... | collective-permute-start | bytes 1966088 | tf_op jit(solution)/shard_map/ppermute | solution.py:277
  106.2 16.7 %collective-permute-start.13 = (bf16[240,640]{1,0:T(8,128)(2,1)}, bf16[240,640]{1,0:T(8,128)(2,1)}, u32[]{:S(2)}, u32[]{:S(2)}) collective-permute-start(bf16[240,640]{1,0:T(8,128)(2,1)} %get-tuple-element.80), channel_id=1, source_target_pairs={{0,8},{4,12},{8,16},{12,20},{16,24},{20,28},{24,0},{28,4},{1,9},{5... | collective-permute-start | bytes 921608 | tf_op jit(solution)/shard_map/ppermute | solution.py:280
  107.9 18.5 %collective-permute-start.15 = (bf16[224,640]{1,0:T(8,128)(2,1)}, bf16[224,640]{1,0:T(8,128)(2,1)}, u32[]{:S(2)}, u32[]{:S(2)}) collective-permute-start(bf16[224,640]{1,0:T(8,128)(2,1)} %get-tuple-element.81), channel_id=1, source_target_pairs={{0,8},{4,12},{8,16},{12,20},{16,24},{20,28},{24,0},{28,4},{1,9},{5... | collective-permute-start | bytes 860168 | tf_op jit(solution)/shard_map/ppermute | solution.py:280
  124.7 10.9 %collective-permute-start.14 = (bf16[240,640]{1,0:T(8,128)(2,1)}, bf16[240,640]{1,0:T(8,128)(2,1)}, u32[]{:S(2)}, u32[]{:S(2)}) collective-permute-start(bf16[240,640]{1,0:T(8,128)(2,1)} %accumulate.6), channel_id=1, source_target_pairs={{0,8},{4,12},{8,16},{12,20},{16,24},{20,28},{24,0},{28,4},{1,9},{5... | collective-permute-start | bytes 921608 | tf_op jit(solution)/shard_map/ppermute | solution.py:280
  132.0 6.1 %collective-permute-start.19 = (bf16[240,384]{1,0:T(8,128)(2,1)}, bf16[240,384]{1,0:T(8,128)(2,1)}, u32[]{:S(2)}, u32[]{:S(2)}) collective-permute-start(bf16[240,384]{1,0:T(8,128)(2,1)} %get-tuple-element.91.refs_0_), channel_id=1, source_target_pairs={{0,1},{1,0},{2,3},{3,2},{4,5},{5,4},{6,7},{7,6},{8,9},{9,8},{10,11... | collective-permute-start | bytes 552968 | tf_op jit(solution)/shard_map/ppermute | solution.py:274
  132.7 11.9 %collective-permute-start.18 = (bf16[224,640]{1,0:T(8,128)(2,1)}, bf16[224,640]{1,0:T(8,128)(2,1)}, u32[]{:S(2)}, u32[]{:S(2)}) collective-permute-start(bf16[224,640]{1,0:T(8,128)(2,1)} %get-tuple-element.82), channel_id=1, source_target_pairs={{0,8},{4,12},{8,16},{12,20},{16,24},{20,28},{24,0},{28,4},{1,9},{5... | collective-permute-start | bytes 860168 | tf_op jit(solution)/shard_map/ppermute | solution.py:280
  132.9 19.4 %collective-permute-start.17 = (bf16[224,640]{1,0:T(8,128)(2,1)}, bf16[224,640]{1,0:T(8,128)(2,1)}, u32[]{:S(2)}, u32[]{:S(2)}) collective-permute-start(bf16[224,640]{1,0:T(8,128)(2,1)} %accumulate.7), channel_id=1, source_target_pairs={{0,8},{4,12},{8,16},{12,20},{16,24},{20,28},{24,0},{28,4},{1,9},{5... | collective-permute-start | bytes 860168 | tf_op jit(solution)/shard_map/ppermute | solution.py:280
  138.2 8.2 %collective-permute-start.20 = (bf16[240,384]{1,0:T(8,128)(2,1)}, bf16[240,384]{1,0:T(8,128)(2,1)}, u32[]{:S(2)}, u32[]{:S(2)}) collective-permute-start(bf16[240,384]{1,0:T(8,128)(2,1)} %get-tuple-element.91.refs_0_), channel_id=1, source_target_pairs={{0,2},{1,3},{2,0},{3,1},{4,6},{5,7},{6,4},{7,5},{8,10},{9,11},{10,... | collective-permute-start | bytes 552968 | tf_op jit(solution)/shard_map/ppermute | solution.py:274
  139.6 7.7 %collective-permute-start.21 = (bf16[240,384]{1,0:T(8,128)(2,1)}, bf16[240,384]{1,0:T(8,128)(2,1)}, u32[]{:S(2)}, u32[]{:S(2)}) collective-permute-start(bf16[240,384]{1,0:T(8,128)(2,1)} %collective-permute-done.19.refs_1_), channel_id=1, source_target_pairs={{0,2},{1,3},{2,0},{3,1},{4,6},{5,7},{6,4},{7,5},{8,10},{9,11},{10,... | collective-permute-start | bytes 552968 | tf_op jit(solution)/shard_map/ppermute | solution.py:274
  149.5 5.7 %collective-permute-start.22 = (bf16[224,384]{1,0:T(8,128)(2,1)}, bf16[224,384]{1,0:T(8,128)(2,1)}, u32[]{:S(2)}, u32[]{:S(2)}) collective-permute-start(bf16[224,384]{1,0:T(8,128)(2,1)} %get-tuple-element.103.refs_0_), channel_id=1, source_target_pairs={{0,1},{1,0},{2,3},{3,2},{4,5},{5,4},{6,7},{7,6},{8,9},{9,8},{10,11... | collective-permute-start | bytes 516104 | tf_op jit(solution)/shard_map/ppermute | solution.py:274
  150.2 12.3 %collective-permute-start.16 = (bf16[240,640]{1,0:T(8,128)(2,1)}, bf16[240,640]{1,0:T(8,128)(2,1)}, u32[]{:S(2)}, u32[]{:S(2)}) collective-permute-start(bf16[240,640]{1,0:T(8,128)(2,1)} %accumulate.8), channel_id=1, source_target_pairs={{0,8},{4,12},{8,16},{12,20},{16,24},{20,28},{24,0},{28,4},{1,9},{5... | collective-permute-start | bytes 921608 | tf_op jit(solution)/shard_map/ppermute | solution.py:280
  151.0 17.1 %collective-permute-start.26 = (bf16[224,640]{1,0:T(8,128)(2,1)}, bf16[224,640]{1,0:T(8,128)(2,1)}, u32[]{:S(2)}, u32[]{:S(2)}) collective-permute-start(bf16[224,640]{1,0:T(8,128)(2,1)} %accumulate.9), channel_id=1, source_target_pairs={{0,8},{4,12},{8,16},{12,20},{16,24},{20,28},{24,0},{28,4},{1,9},{5... | collective-permute-start | bytes 860168 | tf_op jit(solution)/shard_map/ppermute | solution.py:280
  155.3 12.8 %collective-permute-start.23 = (bf16[224,384]{1,0:T(8,128)(2,1)}, bf16[224,384]{1,0:T(8,128)(2,1)}, u32[]{:S(2)}, u32[]{:S(2)}) collective-permute-start(bf16[224,384]{1,0:T(8,128)(2,1)} %get-tuple-element.103.refs_0_), channel_id=1, source_target_pairs={{0,2},{1,3},{2,0},{3,1},{4,6},{5,7},{6,4},{7,5},{8,10},{9,11},{10,... | collective-permute-start | bytes 516104 | tf_op jit(solution)/shard_map/ppermute | solution.py:274
  156.8 11.3 %collective-permute-start.24 = (bf16[224,384]{1,0:T(8,128)(2,1)}, bf16[224,384]{1,0:T(8,128)(2,1)}, u32[]{:S(2)}, u32[]{:S(2)}) collective-permute-start(bf16[224,384]{1,0:T(8,128)(2,1)} %collective-permute-done.22.refs_1_), channel_id=1, source_target_pairs={{0,2},{1,3},{2,0},{3,1},{4,6},{5,7},{6,4},{7,5},{8,10},{9,11},{10,... | collective-permute-start | bytes 516104 | tf_op jit(solution)/shard_map/ppermute | solution.py:274
  157.3 26.8 %collective-permute-start.30 = (bf16[224,640]{1,0:T(8,128)(2,1)}, bf16[224,640]{1,0:T(8,128)(2,1)}, u32[]{:S(2)}, u32[]{:S(2)}) collective-permute-start(bf16[224,640]{1,0:T(8,128)(2,1)} %accumulate.10), channel_id=1, source_target_pairs={{0,8},{4,12},{8,16},{12,20},{16,24},{20,28},{24,0},{28,4},{1,9},{5... | collective-permute-start | bytes 860168 | tf_op jit(solution)/shard_map/ppermute | solution.py:280
  169.9 17.6 %collective-permute-start.29 = (bf16[224,640]{1,0:T(8,128)(2,1)}, bf16[224,640]{1,0:T(8,128)(2,1)}, u32[]{:S(2)}, u32[]{:S(2)}) collective-permute-start(bf16[224,640]{1,0:T(8,128)(2,1)} %accumulate.11), channel_id=1, source_target_pairs={{0,8},{4,12},{8,16},{12,20},{16,24},{20,28},{24,0},{28,4},{1,9},{5... | collective-permute-start | bytes 860168 | tf_op jit(solution)/shard_map/ppermute | solution.py:280
  172.1 7.6 %collective-permute-start.25 = (bf16[224,384]{1,0:T(8,128)(2,1)}, bf16[224,384]{1,0:T(8,128)(2,1)}, u32[]{:S(2)}, u32[]{:S(2)}) collective-permute-start(bf16[224,384]{1,0:T(8,128)(2,1)} %get-tuple-element.111.refs_0_), channel_id=1, source_target_pairs={{0,1},{1,0},{2,3},{3,2},{4,5},{5,4},{6,7},{7,6},{8,9},{9,8},{10,11... | collective-permute-start | bytes 516104 | tf_op jit(solution)/shard_map/ppermute | solution.py:274
  179.8 11.9 %collective-permute-start.27 = (bf16[224,384]{1,0:T(8,128)(2,1)}, bf16[224,384]{1,0:T(8,128)(2,1)}, u32[]{:S(2)}, u32[]{:S(2)}) collective-permute-start(bf16[224,384]{1,0:T(8,128)(2,1)} %get-tuple-element.111.refs_0_), channel_id=1, source_target_pairs={{0,2},{1,3},{2,0},{3,1},{4,6},{5,7},{6,4},{7,5},{8,10},{9,11},{10,... | collective-permute-start | bytes 516104 | tf_op jit(solution)/shard_map/ppermute | solution.py:274
  181.3 29.8 %collective-permute-start.33 = (bf16[240,640]{1,0:T(8,128)(2,1)}, bf16[240,640]{1,0:T(8,128)(2,1)}, u32[]{:S(2)}, u32[]{:S(2)}) collective-permute-start(bf16[240,640]{1,0:T(8,128)(2,1)} %get-tuple-element.124.refs_4_), channel_id=1, source_target_pairs={{0,3},{1,2},{2,1},{3,0},{4,7},{5,6},{6,5},{7,4},{8,11},{9,10},{10,... | collective-permute-start | bytes 921608 | tf_op jit(solution)/shard_map/ppermute | solution.py:274
  182.6 29.8 %collective-permute-start.32 = (bf16[240,640]{1,0:T(8,128)(2,1)}, bf16[240,640]{1,0:T(8,128)(2,1)}, u32[]{:S(2)}, u32[]{:S(2)}) collective-permute-start(bf16[240,640]{1,0:T(8,128)(2,1)} %get-tuple-element.124.refs_4_), channel_id=1, source_target_pairs={{0,2},{1,3},{2,0},{3,1},{4,6},{5,7},{6,4},{7,5},{8,10},{9,11},{10,... | collective-permute-start | bytes 921608 | tf_op jit(solution)/shard_map/ppermute | solution.py:274
  184.1 28.3 %collective-permute-start.31 = (bf16[240,640]{1,0:T(8,128)(2,1)}, bf16[240,640]{1,0:T(8,128)(2,1)}, u32[]{:S(2)}, u32[]{:S(2)}) collective-permute-start(bf16[240,640]{1,0:T(8,128)(2,1)} %get-tuple-element.124.refs_4_), channel_id=1, source_target_pairs={{0,1},{1,0},{2,3},{3,2},{4,5},{5,4},{6,7},{7,6},{8,9},{9,8},{10,11... | collective-permute-start | bytes 921608 | tf_op jit(solution)/shard_map/ppermute | solution.py:274
  187.5 27.0 %collective-permute-start.39 = (bf16[224,640]{1,0:T(8,128)(2,1)}, bf16[224,640]{1,0:T(8,128)(2,1)}, u32[]{:S(2)}, u32[]{:S(2)}) collective-permute-start(bf16[224,640]{1,0:T(8,128)(2,1)} %get-tuple-element.123.refs_4_), channel_id=1, source_target_pairs={{0,3},{1,2},{2,1},{3,0},{4,7},{5,6},{6,5},{7,4},{8,11},{9,10},{10,... | collective-permute-start | bytes 860168 | tf_op jit(solution)/shard_map/ppermute | solution.py:274
  191.6 15.2 %collective-permute-start.28 = (bf16[224,384]{1,0:T(8,128)(2,1)}, bf16[224,384]{1,0:T(8,128)(2,1)}, u32[]{:S(2)}, u32[]{:S(2)}) collective-permute-start(bf16[224,384]{1,0:T(8,128)(2,1)} %collective-permute-done.25.refs_1_), channel_id=1, source_target_pairs={{0,2},{1,3},{2,0},{3,1},{4,6},{5,7},{6,4},{7,5},{8,10},{9,11},{10,... | collective-permute-start | bytes 516104 | tf_op jit(solution)/shard_map/ppermute | solution.py:274
  206.9 19.3 %collective-permute-start.38 = (bf16[224,640]{1,0:T(8,128)(2,1)}, bf16[224,640]{1,0:T(8,128)(2,1)}, u32[]{:S(2)}, u32[]{:S(2)}) collective-permute-start(bf16[224,640]{1,0:T(8,128)(2,1)} %get-tuple-element.123.refs_4_), channel_id=1, source_target_pairs={{0,2},{1,3},{2,0},{3,1},{4,6},{5,7},{6,4},{7,5},{8,10},{9,11},{10,... | collective-permute-start | bytes 860168 | tf_op jit(solution)/shard_map/ppermute | solution.py:274
  211.1 15.1 %collective-permute-start.37 = (bf16[224,640]{1,0:T(8,128)(2,1)}, bf16[224,640]{1,0:T(8,128)(2,1)}, u32[]{:S(2)}, u32[]{:S(2)}) collective-permute-start(bf16[224,640]{1,0:T(8,128)(2,1)} %get-tuple-element.123.refs_4_), channel_id=1, source_target_pairs={{0,1},{1,0},{2,3},{3,2},{4,5},{5,4},{6,7},{7,6},{8,9},{9,8},{10,11... | collective-permute-start | bytes 860168 | tf_op jit(solution)/shard_map/ppermute | solution.py:274
  212.4 23.1 %collective-permute-start.36 = (bf16[224,640]{1,0:T(8,128)(2,1)}, bf16[224,640]{1,0:T(8,128)(2,1)}, u32[]{:S(2)}, u32[]{:S(2)}) collective-permute-start(bf16[224,640]{1,0:T(8,128)(2,1)} %get-tuple-element.122.refs_4_), channel_id=1, source_target_pairs={{0,3},{1,2},{2,1},{3,0},{4,7},{5,6},{6,5},{7,4},{8,11},{9,10},{10,... | collective-permute-start | bytes 860168 | tf_op jit(solution)/shard_map/ppermute | solution.py:274
  213.1 22.3 %collective-permute-start.35 = (bf16[224,640]{1,0:T(8,128)(2,1)}, bf16[224,640]{1,0:T(8,128)(2,1)}, u32[]{:S(2)}, u32[]{:S(2)}) collective-permute-start(bf16[224,640]{1,0:T(8,128)(2,1)} %get-tuple-element.122.refs_4_), channel_id=1, source_target_pairs={{0,2},{1,3},{2,0},{3,1},{4,6},{5,7},{6,4},{7,5},{8,10},{9,11},{10,... | collective-permute-start | bytes 860168 | tf_op jit(solution)/shard_map/ppermute | solution.py:274
  214.6 20.9 %collective-permute-start.34 = (bf16[224,640]{1,0:T(8,128)(2,1)}, bf16[224,640]{1,0:T(8,128)(2,1)}, u32[]{:S(2)}, u32[]{:S(2)}) collective-permute-start(bf16[224,640]{1,0:T(8,128)(2,1)} %get-tuple-element.122.refs_4_), channel_id=1, source_target_pairs={{0,1},{1,0},{2,3},{3,2},{4,5},{5,4},{6,7},{7,6},{8,9},{9,8},{10,11... | collective-permute-start | bytes 860168 | tf_op jit(solution)/shard_map/ppermute | solution.py:274
Sparse Core Ops, SparseCore 0:
  55.9 44.6 reduce-scatter.1

commit v8 on v7

--- a/solution.py
+++ b/solution.py
@@ -76,7 +76,8 @@
 
 def gradient(stacks, pieces, order, cuts=None):
     _, owned, tokens = stacks[0].shape
-    rows, width = pieces[0].shape
+    rows, run = pieces[0].shape
+    width = run * len(pieces) // 4
     count = order.shape[0]
 
     def kernel(order_ref, *refs):
@@ -98,7 +99,9 @@
                 for side in range(2):
                     fetch(block, side).start()
             for index, piece_ref in enumerate(piece_refs):
-                whole_ref[index * rows : (index + 1) * rows, :] = piece_ref[...]
+                side, place = divmod(index, len(pieces) // 2)
+                row, column = side * tokens + place % 2 * rows, place // 2 * run
+                whole_ref[row : row + rows, column : column + run] = piece_ref[...]
 
         for side in range(2):
             fetch(step, side).wait()
@@ -121,7 +124,7 @@
         grid_spec=pltpu.PrefetchScalarGridSpec(
             num_scalar_prefetch=1,
             grid=(count,),
-            in_specs=[pl.BlockSpec((rows, width), lambda i, order_ref: (0, 0))] * len(pieces)
+            in_specs=[pl.BlockSpec((rows, run), lambda i, order_ref: (0, 0))] * len(pieces)
             + [pl.BlockSpec(memory_space=pl.ANY)] * 2,
             out_specs=out_specs,
             scratch_shapes=[
@@ -158,15 +161,13 @@
     )(own, arrived)
 
 
-def adam(arrived, stacks, block, rows, first, second, held, column):
+def adam(arrived, stack, block, rows, first, second, held, column):
     owned, rank = first.shape
     height, width = arrived.shape
 
-    def kernel(arrived_ref, first_ref, second_ref, *refs):
+    def kernel(arrived_ref, stack_ref, first_ref, second_ref, *refs):
         first_out, second_out, direction_out = refs[-3:]
-        grad_low = arrived_ref[...].astype(F32)
-        for stack_ref in refs[: len(stacks)]:
-            grad_low = grad_low + stack_ref[0].astype(F32)
+        grad_low = arrived_ref[...].astype(F32) + stack_ref[0].astype(F32)
         first_next = beta_first * first_ref[...] + (1.0 - beta_first) * grad_low
         second_next = beta_second * second_ref[...] + (1.0 - beta_second) * grad_low * grad_low
         first_out[...] = first_next
@@ -185,20 +186,19 @@
             jax.ShapeDtypeStruct((owned, rank), F32),
             jax.ShapeDtypeStruct((height, width), BF16),
         ],
-        in_specs=[pl.BlockSpec(memory_space=pltpu.VMEM), rectangle, rectangle]
-        + [part_of(stack, block, rows) for stack in stacks]
+        in_specs=[pl.BlockSpec(memory_space=pltpu.VMEM), part_of(stack, block, rows), rectangle, rectangle]
         + [pl.BlockSpec(memory_space=pl.ANY)] * len(held),
         out_specs=[rectangle, rectangle, pl.BlockSpec((height, width), lambda i: (0, 0))],
-        input_output_aliases={3 + len(stacks) + index: index for index in range(len(held))},
+        input_output_aliases={4 + index: index for index in range(len(held))},
         compiler_params=RING_PARAMS,
         cost_estimate=COST,
         name="adam",
-    )(arrived, first, second, *stacks, *held)
-
-
-def expand(targets, starts, rests, rows, owned, basis, held):
+    )(arrived, stack, first, second, *held)
+
+
+def expand(targets, starts, rests, rows, basis, held):
     count = len(starts)
-    begin = starts[0].shape[1]
+    owned, begin = starts[0].shape
     height, width = rests[0].shape
     features, rank = basis.shape
     block = min(512, features)
@@ -226,7 +226,7 @@
             num_scalar_prefetch=1,
             grid=(features // block,),
             in_specs=[pl.BlockSpec((block, rank), lambda i, targets_ref: (i, 0))]
-            + [pl.BlockSpec((height, begin), lambda i, targets_ref: (0, 0))] * count
+            + [pl.BlockSpec((pl.Element(height), pl.Element(begin)), lambda i, targets_ref: (rows.start, 0))] * count
             + [pl.BlockSpec((height, width), lambda i, targets_ref: (0, 0))] * count
             + [pl.BlockSpec(memory_space=pl.ANY)] * len(held),
             out_specs=pl.BlockSpec(
@@ -263,7 +263,7 @@
     dp, fsdp = lax.axis_index("dp"), lax.axis_index("fsdp")
     chips = dp_count // 2
     chip, core = dp // 2, dp % 2
-    width = rank * 3 // 8
+    width = rank // 4
 
     offsets = [1 << bit for bit in range(fsdp_count.bit_length() - 1)]
     order = jnp.stack([fsdp ^ offset for offset in range(fsdp_count)]).astype(jnp.int32)
@@ -307,32 +307,28 @@
     for step in range(1, len(offsets) - 1):
         sums_0 = add(sums_0, exchange(sums_0, step))
     coming_0 = exchange(sums_0, len(offsets) - 1)
+    coming_1 = exchange([after(half, *sums_0) for half in sums_1], 0)
     theirs = turn(parity, after(others_grads, *sums_0), owned)
     stacks = [mine, theirs]
     sums_0 = add(sums_0, [after(term, theirs) for term in coming_0])
     both_0 = sums_0 + [sibling(half) for half in sums_0]
-    coming_1 = exchange([after(half, *sums_0) for half in sums_1], 0)
-
-    product = gradient(stacks, both_0, jnp.arange(chips, dtype=jnp.int32))
-    lines = [list(range(parity, dp_count, 2)) for parity in range(2)]
-    mine_0 = lax.psum_scatter(
-        product.reshape(chips * owned, width), "dp", scatter_dimension=0, axis_index_groups=lines, tiled=True
-    )
-
-    sums_1 = add_pairs(sums_1, [after(term, product) for term in coming_1])
-    for step in range(1, len(offsets)):
+
+    whole = slice(0, owned)
+    leaving = gradient(stacks, both_0, ring_order[:1], [whole])
+    arrived_0 = onward(leaving[0])
+    others_0 = gradient([after(mine, *leaving), theirs], both_0, ring_order[1:])
+
+    sums_1 = plus(sums_1, [after(term, others_0) for term in coming_1], 2)
+    coming_1 = exchange(sums_1, 1)
+    for hop in range(1, hops - 1):
+        token = accumulate(after(arrived_0, sums_1), others_0, hop - 1, whole)
+        arrived_0 = onward(token)
+    sums_1 = add_pairs(sums_1, [after(term, token) for term in coming_1])
+    for step in range(2, len(offsets)):
         sums_1 = add_pairs(sums_1, exchange(sums_1, step))
     both_1 = sums_1 + [sibling(half) for half in sums_1]
-
-    held = ()
-
-    def step_of(arrived, stacks, block, rows, column):
-        nonlocal held
-        first_next, second_next, direction = adam(
-            arrived, stacks, block, rows, first_moment[0], second_moment[0], held, column
-        )
-        held = (first_next, second_next)
-        return direction
+    token = accumulate(after(arrived_0, sums_1), others_0, hops - 2, whole)
+    arrived_0 = onward(token)
 
     ends = [0, owned]
     if owned % 16 == 0:
@@ -340,45 +336,52 @@
     parts = [slice(*pair) for pair in zip(ends, ends[1:])]
     count = len(parts)
 
-    leaving = gradient(stacks, both_1, ring_order[:1], parts)
+    leaving = gradient([after(mine, token), theirs], both_1, ring_order[:1], parts)
     arrived = [onward(value) for value in leaving]
-    others = gradient([after(stacks[0], *leaving), stacks[1]], both_1, ring_order[1:])
-
+    others = gradient([after(mine, *leaving), theirs], both_1, ring_order[1:])
+
+    held = ()
+
+    def step_of(arrived, stack, rows, column):
+        nonlocal held
+        first_next, second_next, direction = adam(
+            arrived, stack, hops - 1, rows, first_moment[0], second_moment[0], held, column
+        )
+        held = (first_next, second_next)
+        return direction
+
+    starts = []
     token = others
+    stages = list(offsets)
+
+    def spread(token):
+        offset = stages.pop(0)
+        starts.extend([across(after(piece, token), offset) for piece in starts])
+
     directions = []
-
-    starts = [[] for _ in parts]
-    stages = [(part, step) for part in range(count) for step in range(len(offsets))]
-    reached = []
-
-    def spread(token):
-        part, step = stages.pop(0)
-        rows = parts[part]
-        if step == 0:
-            starts[part].append(step_of(after(mine_0[rows], token), (), 0, rows, 0))
-        starts[part].extend([across(after(piece, token), offsets[step]) for piece in starts[part]])
-        return starts[part]
-
     events = sorted((2 * hop + 1.5 * part, part, hop) for part in range(count) for hop in range(1, chips))
     for number, (_, part, hop) in enumerate(events):
         rows = parts[part]
-        if number >= 2 and (reached or stages):
-            token = [token, *reached]
-            reached = spread(token) if stages else []
+        if number == 1:
+            starts.append(step_of(after(arrived_0, token), others_0, whole, 0))
+        if number in (1, 3, 5):
+            token = [token, *starts]
+            if stages:
+                spread(token)
         if hop < hops:
             token = accumulate(after(arrived[part], token), others, hop - 1, rows)
             arrived[part] = onward(token)
             continue
-        token = step_of(after(arrived[part], token), (others,), hop - 1, rows, width)
+        token = step_of(after(arrived[part], token), others, rows, width)
         sent = after(token, directions[part - 2]) if part > 1 else token
         directions.append([token] + [across(sent, offset) for offset in range(1, fsdp_count)])
     while stages:
         spread(token)
 
     update = ()
-    for rows, start, pieces in zip(parts, starts, directions):
+    for rows, pieces in zip(parts, directions):
         pieces = [after(pieces[0], token), *pieces[1:]]
-        update = (expand(order, start, pieces, rows, owned, basis, update),)
+        update = (expand(order, starts, pieces, rows, basis, update),)
     return (update[0][None], held[0][None], held[1][None])
 
 

time: 253 us -> 218 us (0.86)
  waiting for transfers between devices: 74.7 us -> 55.8 us
  between operations: 14.2 us -> 0.84 us
  Pallas kernels: 105 us -> 111 us
  local copies, waits for them, and re-layouts: 8.39 us -> 3.31 us
  starting transfers between devices: 38.8 us -> 35.2 us
    ppermute x26 -> x22, waiting for transfers between devices: 60.3 us -> 0.62 us  [across(): lax.ppermute(value, 'fsdp', [(index, index ^ offset) for index in range(f...]
    ppermute x9 -> x12, waiting for transfers between devices: 10.9 us -> 54.3 us  [onward(): lax.ppermute(value, 'dp', [(index, (index + 2) % dp_count) for index in r...]
    pallas_call x6 -> x8, Pallas kernels: 11 us -> 15.3 us  [accumulate(): pl.pallas_call(kernel, grid=(1,), out_shape=jax.ShapeDtypeStruct(arrived....]
    slice x3 -> x1, local copies, waits for them, and re-layouts: 4.63 us -> 0.65 us  [local(): others_0 = gradient([after(mine, *leaving), theirs], both_0, ring_order[1:])]
    ppermute x26 -> x22, starting transfers between devices: 28.1 us -> 25.4 us  [across(): lax.ppermute(value, 'fsdp', [(index, index ^ offset) for index in range(f...]
    pallas_call x6 -> x4, Pallas kernels: 15.1 us -> 12.4 us  [adam(): pl.pallas_call(kernel, grid=(1,), out_shape=[jax.ShapeDtypeStruct((owned,...]
    ppermute x5 -> x7, waiting for transfers between devices: 3.53 us -> 0.87 us  [sibling(): lax.ppermute(value, 'dp', [(index, index ^ 1) for index in range(dp_count)])]
    pallas_call x2 -> x3, Pallas kernels: 5.23 us -> 7.37 us  [plus(): pl.pallas_call(kernel, grid=(2,), out_shape=[jax.ShapeDtypeStruct((rows,...]
  transfers between devices with their start and end apart: 41 -> 41, of which waited for: 19 -> 16; matrix products, arithmetic and copies ran while one was open for 7% -> 6% of each run, Pallas kernels for 34% -> 42%
where the time goes in v8:
time: 218 us; the launch traced here: 217 us
  Pallas kernels  111 us (51%)
  waiting for transfers between devices  55.8 us (26%)
  starting transfers between devices  35.2 us (16%)
  matrix products  10.3 us (5%)
  local copies, waits for them, and re-layouts  3.31 us (2%)
    ppermute x12, waiting for transfers between devices, onward(): lax.ppermute(value, 'dp', [(index, (index + 2) % dp_count) for index in r...  54.3 us
    pallas_call x4, Pallas kernels, gradient(): pl.pallas_call(kernel, out_shape=out_shape, grid_spec=pltpu.PrefetchScala...  32.4 us
    pallas_call x3, Pallas kernels, expand(): pl.pallas_call(kernel, out_shape=jax.ShapeDtypeStruct((count, owned, feat...  28.2 us
    ppermute x22, starting transfers between devices, across(): lax.ppermute(value, 'fsdp', [(index, index ^ offset) for index in range(f...  25.4 us
    pallas_call x8, Pallas kernels, accumulate(): pl.pallas_call(kernel, grid=(1,), out_shape=jax.ShapeDtypeStruct(arrived....  15.3 us
    pallas_call x2, Pallas kernels, turn(): pl.pallas_call(kernel, out_shape=jax.ShapeDtypeStruct((chips, owned, toke...  15.1 us
    pallas_call x4, Pallas kernels, adam(): pl.pallas_call(kernel, grid=(1,), out_shape=[jax.ShapeDtypeStruct((owned,...  12.4 us
    dot_general x2, matrix products, projected(): jnp.dot(features, basis[:, columns], preferred_element_type=F32)  10.3 us
  transfers between devices with their start and end apart: 41, of which 16 were waited for; matrix products, arithmetic and copies ran while one was open for 6% of the time, Pallas kernels for 42%

profile of v8, /device:TPU:0, one launch (start us, length us, event | category | flops | bytes accessed | tf_op | source)
XLA Modules:
  0.0 217.0 jit_solution(8051543228767413492)
XLA Ops:
  1.1 3.7 %convolution_convert_fusion = bf16[1024,256]{1,0:T(8,128)(2,1)S(1)} fusion(bf16[2048,1024]{1,0:T(8,128)(2,1)} %bitcast.26, bf16[1,1024,2048]{2,1,0:T(8,128)(2,1)} %param.5), kind=kOutput, calls=%fused_computation.3 | convolution fusion | flops 1074003968 | bytes 5767168 | tf_op jit(solution)/shard_map/dot_general | solution.py:296
  4.9 2.6 %collective-permute-start.3 = (bf16[512,256]{1,0:T(8,128)(2,1)S(1)}, bf16[512,256]{1,0:T(8,128)(2,1)S(1)}, u32[]{:S(2)}, u32[]{:S(2)}) collective-permute-start(bf16[512,256]{1,0:T(8,128)(2,1)S(1)} %get-tuple-element.127), channel_id=1, source_target_pairs={{0,2},{1,3},{2,0},{3,1},{4,6},{5,7},{6,4},{7,5},{8,10},{9,11},{10,... | collective-permute-start | bytes 786440 | tf_op jit(solution)/shard_map/ppermute | solution.py:274
  7.5 1.5 collective-permute-start
  9.0 6.6 %fusion.2 = bf16[1024,768]{1,0:T(8,128)(2,1)S(1)} fusion(bf16[1024,2048]{1,0:T(8,128)(2,1)} %bitcast.37, bf16[2048,1024]{1,0:T(8,128)(2,1)} %bitcast.27), kind=kOutput, calls=%fused_computation.2 | convolution fusion | flops 3222011904 | bytes 8912896 | tf_op jit(solution)/shard_map/dot_general | solution.py:296
  15.6 1.2 fusion.8
  16.8 7.5 %turn.2.refs_4_.refs_8_ = bf16[4,688,1024]{2,1,0:T(8,128)(2,1)} custom-call(s32[1]{0:T(128)} %bitcast.6.core_ref, bf16[1024,5504]{1,0:T(8,128)(2,1)} %bitcast.34), custom_call_target="tpu_custom_call" | custom-call | flops 1024 | bytes 1048576 | tf_op jit(solution)/shard_map/turn/pallas_call | solution.py:39
  24.5 0.6 collective-permute-start.4
  25.2 1.9 collective-permute-start.9
  27.1 1.5 collective-permute-start.8
  28.6 7.6 %turn.3.refs_5_.refs_9_ = bf16[4,688,1024]{2,1,0:T(8,128)(2,1)} custom-call(s32[1]{0:T(128)} %bitcast.6.core_ref, bf16[1024,5504]{1,0:T(8,128)(2,1)} %collective-permute-done.2.grads_ref), custom_call_target="tpu_custom_call" | custom-call | flops 1024 | bytes 1048576 | tf_op jit(solution)/shard_map/turn/pallas_call | solution.py:39
  36.4 0.5 copy-done
  37.0 0.7 slice.26.order_ref
  37.9 0.6 collective-permute-done.6.refs_3_
  38.6 0.7 copy-done.3
  39.3 5.3 %gradient.4 = bf16[688,256]{1,0:T(8,128)(2,1)} custom-call(s32[1]{0:T(128)} %bitcast.35, bf16[512,256]{1,0:T(8,128)(2,1)} %copy-done.1, bf16[512,256]{1,0:T(8,128)(2,1)} %copy-done, bf16[512,256]{1,0:T(8,128)(2,1)} %copy-done.2, bf16[512,256]{1,0:T(8,128)(2,1)} %copy-done.3, bf16[4,688,1024]{2,1,0:T(8,128)(2,1)} %turn.2.refs_4_.refs_8_, ...), custom_call_target="tpu_custom_call" | custom-call | flops 1024 | bytes 1048576 | tf_op jit(solution)/shard_map/gradient/pallas_call | solution.py:121
  44.6 7.2 %gradient.5.own_ref.stack_ref = bf16[3,688,256]{2,1,0:T(8,128)(2,1)} custom-call(s32[3]{0:T(128)} %slice.26.order_ref, bf16[512,256]{1,0:T(8,128)(2,1)} %copy-done.1, bf16[512,256]{1,0:T(8,128)(2,1)} %copy-done, bf16[512,256]{1,0:T(8,128)(2,1)} %copy-done.2, bf16[512,256]{1,0:T(8,128)(2,1)} %copy-done.3, bf16[4,688,1024]{2,1,0:T(8,128)(2,1)} %turn.2.refs_4_.refs_8_, ...), custom_call_target="tpu_custom_call" | custom-call | flops 1024 | bytes 1048576 | tf_op jit(solution)/shard_map/gradient/pallas_call | solution.py:121
  51.8 2.8 %plus.3 = (bf16[512,384]{1,0:T(8,128)(2,1)}, bf16[512,384]{1,0:T(8,128)(2,1)}, bf16[512,384]{1,0:T(8,128)(2,1)}, bf16[512,384]{1,0:T(8,128)(2,1)}) custom-call(bf16[512,768]{1,0:T(8,128)(2,1)} %get-tuple-element.71.refs_0_, bf16[512,768]{1,0:T(8,128)(2,1)} %get-tuple-element.73.refs_1_, bf16[512,768]{1,0:T(8,128)(2,1)} %collective-permute-done.8.refs_2_, ...), custom_call_target="tpu_custom_call" | custom-call | flops 1024 | bytes 1048576 | tf_op jit(solution)/shard_map/plus/pallas_call | solution.py:65
  55.3 1.9 collective-permute-start.13
  57.2 1.5 collective-permute-start.14
  58.7 1.6 collective-permute-start.7
  60.3 9.8 %collective-permute-done.7.arrived_ref = bf16[688,256]{1,0:T(8,128)(2,1)} collective-permute-done((bf16[688,256]{1,0:T(8,128)(2,1)}, bf16[688,256]{1,0:T(8,128)(2,1)}, u32[]{:S(2)}, u32[]{:S(2)}) %collective-permute-start.7) | collective-permute-done | bytes 352288 | tf_op jit(solution)/shard_map/ppermute | solution.py:280
  70.1 1.9 accumulate.8
  72.0 2.3 %plus.4 = (bf16[512,384]{1,0:T(8,128)(2,1)}, bf16[512,384]{1,0:T(8,128)(2,1)}) custom-call(bf16[512,384]{1,0:T(8,128)(2,1)} %get-tuple-element.75.refs_0_, bf16[512,384]{1,0:T(8,128)(2,1)} %get-tuple-element.76.refs_1_, bf16[512,384]{1,0:T(8,128)(2,1)} %collective-permute-done.11.refs_2_, bf16[512,384]{1,0:T(8,128)(2,1)} %collective-permute-done.12.refs_3_), custom_call_target="tpu_custom_call" | custom-call | flops 1024 | bytes 1048576 | tf_op jit(solution)/shard_map/plus/pallas_call | solution.py:65
  74.8 2.3 %plus.5 = (bf16[512,384]{1,0:T(8,128)(2,1)}, bf16[512,384]{1,0:T(8,128)(2,1)}) custom-call(bf16[512,384]{1,0:T(8,128)(2,1)} %get-tuple-element.77.refs_0_, bf16[512,384]{1,0:T(8,128)(2,1)} %get-tuple-element.78.refs_1_, bf16[512,384]{1,0:T(8,128)(2,1)} %collective-permute-done.13.refs_2_, bf16[512,384]{1,0:T(8,128)(2,1)} %collective-permute-done.14.refs_3_), custom_call_target="tpu_custom_call" | custom-call | flops 1024 | bytes 1048576 | tf_op jit(solution)/shard_map/plus/pallas_call | solution.py:65
  77.6 1.6 collective-permute-start.10
  79.2 10.8 %collective-permute-done.10.arrived_ref = bf16[688,256]{1,0:T(8,128)(2,1)} collective-permute-done((bf16[688,256]{1,0:T(8,128)(2,1)}, bf16[688,256]{1,0:T(8,128)(2,1)}, u32[]{:S(2)}, u32[]{:S(2)}) %collective-permute-start.10) | collective-permute-done | bytes 352288 | tf_op jit(solution)/shard_map/ppermute | solution.py:280
  90.0 1.9 accumulate.9
  92.0 7.5 %gradient.6 = (bf16[240,768]{1,0:T(8,128)(2,1)}, bf16[224,768]{1,0:T(8,128)(2,1)}, bf16[224,768]{1,0:T(8,128)(2,1)}) custom-call(s32[1]{0:T(128)} %bitcast.36, bf16[512,384]{1,0:T(8,128)(2,1)} %get-tuple-element.82.refs_0_, bf16[512,384]{1,0:T(8,128)(2,1)} %get-tuple-element.83.refs_1_, bf16[512,384]{1,0:T(8,128)(2,1)} %get-tuple-element.86.refs_2_, ...), custom_call_target="tpu_custom_call" | custom-call | flops 1024 | bytes 1048576 | tf_op jit(solution)/shard_map/gradient/pallas_call | solution.py:121
  99.6 1.3 collective-permute-start.15
  100.8 1.6 collective-permute-start.23
  102.4 12.5 %gradient.7.own_ref.stack_ref = bf16[3,688,768]{2,1,0:T(8,128)(2,1)} custom-call(s32[3]{0:T(128)} %slice.26.order_ref, bf16[512,384]{1,0:T(8,128)(2,1)} %get-tuple-element.82.refs_0_, bf16[512,384]{1,0:T(8,128)(2,1)} %get-tuple-element.83.refs_1_, bf16[512,384]{1,0:T(8,128)(2,1)} %get-tuple-element.86.refs_2_, bf16[512,384]{1,0:T(8,128)(2,1)} %get-tuple-element.87.refs_3_, ...), custom_call_target="tpu_custom_call" | custom-call | flops 1024 | bytes 1048576 | tf_op jit(solution)/shard_map/gradient/pallas_call | solution.py:121
  114.9 1.9 accumulate.10
  116.8 2.1 collective-permute-start.22
  118.9 1.8 collective-permute-done.15.arrived_ref
  120.7 3.1 %adam.4 = (f32[688,1024]{1,0:T(8,128)}, f32[688,1024]{1,0:T(8,128)}, bf16[688,256]{1,0:T(8,128)(2,1)}) custom-call(bf16[688,256]{1,0:T(8,128)(2,1)} %collective-permute-done.15.arrived_ref, bf16[3,688,256]{2,1,0:T(8,128)(2,1)} %gradient.5.own_ref.stack_ref, f32[688,1024]{1,0:T(8,128)} %bitcast.18, f32[688,1024]{1,0:T(8,128)} %bitcast.22), custom_call_target="tpu_custom_call" | custom-call | flops 1024 | bytes 1048576 | tf_op jit(solution)/shard_map/adam/pallas_call | solution.py:181
  124.4 3.7 %collective-permute-done.23.arrived_ref = bf16[224,768]{1,0:T(8,128)(2,1)} collective-permute-done((bf16[224,768]{1,0:T(8,128)(2,1)}, bf16[224,768]{1,0:T(8,128)(2,1)}, u32[]{:S(2)}, u32[]{:S(2)}) %collective-permute-start.23) | collective-permute-done | bytes 344096 | tf_op jit(solution)/shard_map/ppermute | solution.py:280
  128.1 1.9 accumulate.11
  130.0 6.0 %collective-permute-done.22.arrived_ref = bf16[240,768]{1,0:T(8,128)(2,1)} collective-permute-done((bf16[240,768]{1,0:T(8,128)(2,1)}, bf16[240,768]{1,0:T(8,128)(2,1)}, u32[]{:S(2)}, u32[]{:S(2)}) %collective-permute-start.22) | collective-permute-done | bytes 368672 | tf_op jit(solution)/shard_map/ppermute | solution.py:280
  136.0 1.9 accumulate.12
  137.9 1.5 collective-permute-start.24
  140.0 3.4 %collective-permute-done.26.arrived_ref = bf16[224,768]{1,0:T(8,128)(2,1)} collective-permute-done((bf16[224,768]{1,0:T(8,128)(2,1)}, bf16[224,768]{1,0:T(8,128)(2,1)}, u32[]{:S(2)}, u32[]{:S(2)}) %collective-permute-start.26) | collective-permute-done | bytes 344096 | tf_op jit(solution)/shard_map/ppermute | solution.py:280
  143.4 1.9 accumulate.13
  145.3 5.5 %collective-permute-done.29.arrived_ref = bf16[224,768]{1,0:T(8,128)(2,1)} collective-permute-done((bf16[224,768]{1,0:T(8,128)(2,1)}, bf16[224,768]{1,0:T(8,128)(2,1)}, u32[]{:S(2)}, u32[]{:S(2)}) %collective-permute-start.29) | collective-permute-done | bytes 344096 | tf_op jit(solution)/shard_map/ppermute | solution.py:280
  150.8 1.9 accumulate.14
  152.7 6.0 %collective-permute-done.28.arrived_ref = bf16[240,768]{1,0:T(8,128)(2,1)} collective-permute-done((bf16[240,768]{1,0:T(8,128)(2,1)}, bf16[240,768]{1,0:T(8,128)(2,1)}, u32[]{:S(2)}, u32[]{:S(2)}) %collective-permute-start.28) | collective-permute-done | bytes 368672 | tf_op jit(solution)/shard_map/ppermute | solution.py:280
  158.7 3.1 %adam.5 = (f32[688,1024]{1,0:T(8,128)}, f32[688,1024]{1,0:T(8,128)}, bf16[240,768]{1,0:T(8,128)(2,1)}) custom-call(bf16[240,768]{1,0:T(8,128)(2,1)} %collective-permute-done.28.arrived_ref, bf16[3,688,768]{2,1,0:T(8,128)(2,1)} %gradient.7.own_ref.stack_ref, f32[688,1024]{1,0:T(8,128)} %bitcast.19, ...), custom_call_target="tpu_custom_call", output_to_operand_aliasing={{0}: (4, {}), {1}: (5, {})} | custom-call | flops 1024 | bytes 1048576 | tf_op jit(solution)/shard_map/adam/pallas_call | solution.py:181
  161.8 1.5 collective-permute-start.34
  163.8 1.5 collective-permute-start.32
  165.3 0.7 collective-permute-done.27.arrived_ref
  166.0 1.9 accumulate.15
  167.9 5.5 %collective-permute-done.31.arrived_ref = bf16[224,768]{1,0:T(8,128)(2,1)} collective-permute-done((bf16[224,768]{1,0:T(8,128)(2,1)}, bf16[224,768]{1,0:T(8,128)(2,1)}, u32[]{:S(2)}, u32[]{:S(2)}) %collective-permute-start.31) | collective-permute-done | bytes 344096 | tf_op jit(solution)/shard_map/ppermute | solution.py:280
  173.4 3.1 %adam.6 = (f32[688,1024]{1,0:T(8,128)}, f32[688,1024]{1,0:T(8,128)}, bf16[224,768]{1,0:T(8,128)(2,1)}) custom-call(bf16[224,768]{1,0:T(8,128)(2,1)} %collective-permute-done.31.arrived_ref, bf16[3,688,768]{2,1,0:T(8,128)(2,1)} %gradient.7.own_ref.stack_ref, f32[688,1024]{1,0:T(8,128)} %bitcast.20, ...), custom_call_target="tpu_custom_call", output_to_operand_aliasing={{0}: (4, {}), {1}: (5, {})} | custom-call | flops 1024 | bytes 1048576 | tf_op jit(solution)/shard_map/adam/pallas_call | solution.py:181
  176.4 1.5 collective-permute-start.40
  178.0 1.1 collective-permute-done.30.arrived_ref
  179.0 1.5 collective-permute-start.39
  180.5 3.1 %adam.7 = (f32[688,1024]{1,0:T(8,128)}, f32[688,1024]{1,0:T(8,128)}, bf16[224,768]{1,0:T(8,128)(2,1)}) custom-call(bf16[224,768]{1,0:T(8,128)(2,1)} %collective-permute-done.30.arrived_ref, bf16[3,688,768]{2,1,0:T(8,128)(2,1)} %gradient.7.own_ref.stack_ref, f32[688,1024]{1,0:T(8,128)} %bitcast.21, ...), custom_call_target="tpu_custom_call", output_to_operand_aliasing={{0}: (4, {}), {1}: (5, {})} | custom-call | flops 1024 | bytes 1048576 | tf_op jit(solution)/shard_map/adam/pallas_call | solution.py:181
  183.6 0.6 collective-permute-start.38
  184.2 1.4 collective-permute-start.37
  185.6 1.5 collective-permute-start.36
  187.1 0.6 collective-permute-start.35
  187.7 0.6 pad_add_fusion.targets_ref
  188.3 9.6 %expand.3.refs_8_ = f32[4,688,2048]{2,1,0:T(8,128)} custom-call(s32[4]{0:T(128)} %pad_add_fusion.targets_ref, bf16[2048,1024]{1,0:T(8,128)(2,1)} %bitcast.28, bf16[688,256]{1,0:T(8,128)(2,1)} %get-tuple-element.100.refs_0_, bf16[688,256]{1,0:T(8,128)(2,1)} %collective-permute-done.21.refs_1_, bf16[688,256]{1,0:T(8,128)(2,1)} %collective-permute-done.24.refs_2_, ...), custom_call_target="tpu_custom_call" | custom-call | flops 1024 | bytes 1048576 | tf_op jit(solution)/shard_map/expand/pallas_call | solution.py:222
  197.9 9.3 %expand.4.refs_8_ = f32[4,688,2048]{2,1,0:T(8,128)} custom-call(s32[4]{0:T(128)} %pad_add_fusion.targets_ref, bf16[2048,1024]{1,0:T(8,128)(2,1)} %bitcast.29, bf16[688,256]{1,0:T(8,128)(2,1)} %get-tuple-element.100.refs_0_, bf16[688,256]{1,0:T(8,128)(2,1)} %collective-permute-done.21.refs_1_, ...), custom_call_target="tpu_custom_call", output_to_operand_aliasing={{}: (10, {})} | custom-call | flops 1024 | bytes 1048576 | tf_op jit(solution)/shard_map/expand/pallas_call | solution.py:222
  207.7 9.3 %expand.5 = f32[4,688,2048]{2,1,0:T(8,128)} custom-call(s32[4]{0:T(128)} %pad_add_fusion.targets_ref, bf16[2048,1024]{1,0:T(8,128)(2,1)} %bitcast.30, bf16[688,256]{1,0:T(8,128)(2,1)} %get-tuple-element.100.refs_0_, bf16[688,256]{1,0:T(8,128)(2,1)} %collective-permute-done.21.refs_1_, ...), custom_call_target="tpu_custom_call", output_to_operand_aliasing={{}: (10, {})} | custom-call | flops 1024 | bytes 1048576 | tf_op jit(solution)/shard_map/expand/pallas_call | solution.py:222
  (62 shorter events, 5.3 us)
Async XLA Ops:
  0.6 28.0 %collective-permute-start.2 = (bf16[1024,5504]{1,0:T(8,128)(2,1)}, bf16[1024,5504]{1,0:T(8,128)(2,1)}, u32[]{:S(2)}, u32[]{:S(2)}) collective-permute-start(bf16[1024,5504]{1,0:T(8,128)(2,1)} %bitcast.33), channel_id=1, source_target_pairs={{0,4},{4,0},{8,12},{12,8},{16,20},{20,16},{24,28},{28,24},{1,5},{5... | collective-permute-start | bytes 33816584 | tf_op jit(solution)/shard_map/ppermute | solution.py:277
  4.9 19.4 %collective-permute-start.3 = (bf16[512,256]{1,0:T(8,128)(2,1)S(1)}, bf16[512,256]{1,0:T(8,128)(2,1)S(1)}, u32[]{:S(2)}, u32[]{:S(2)}) collective-permute-start(bf16[512,256]{1,0:T(8,128)(2,1)S(1)} %get-tuple-element.127), channel_id=1, source_target_pairs={{0,2},{1,3},{2,0},{3,1},{4,6},{5,7},{6,4},{7,5},{8,10},{9,11},{10,... | collective-permute-start | bytes 786440 | tf_op jit(solution)/shard_map/ppermute | solution.py:274
  7.5 16.8 %collective-permute-start = (bf16[512,256]{1,0:T(8,128)(2,1)S(1)}, bf16[512,256]{1,0:T(8,128)(2,1)S(1)}, u32[]{:S(2)}, u32[]{:S(2)}) collective-permute-start(bf16[512,256]{1,0:T(8,128)(2,1)S(1)} %get-tuple-element.128), channel_id=1, source_target_pairs={{0,1},{1,0},{2,3},{3,2},{4,5},{5,4},{6,7},{7,6},{8,9},{9,8},{10,11... | collective-permute-start | bytes 786440 | tf_op jit(solution)/shard_map/ppermute | solution.py:274
  24.5 11.7 %collective-permute-start.4 = (bf16[512,256]{1,0:T(8,128)(2,1)S(1)}, bf16[512,256]{1,0:T(8,128)(2,1)S(1)}, u32[]{:S(2)}, u32[]{:S(2)}) collective-permute-start(bf16[512,256]{1,0:T(8,128)(2,1)S(1)} %get-tuple-element.125), channel_id=1, source_target_pairs={{0,1},{1,0},{2,3},{3,2},{4,5},{5,4},{6,7},{7,6},{8,9},{9,8},{10,11... | collective-permute-start | bytes 786440 | tf_op jit(solution)/shard_map/ppermute | solution.py:274
  25.1 11.1 %collective-permute-start.1 = (bf16[512,256]{1,0:T(8,128)(2,1)S(1)}, bf16[512,256]{1,0:T(8,128)(2,1)S(1)}, u32[]{:S(2)}, u32[]{:S(2)}) collective-permute-start(bf16[512,256]{1,0:T(8,128)(2,1)S(1)} %get-tuple-element.126), channel_id=1, source_target_pairs={{0,2},{1,3},{2,0},{3,1},{4,6},{5,7},{6,4},{7,5},{8,10},{9,11},{10,... | collective-permute-start | bytes 786440 | tf_op jit(solution)/shard_map/ppermute | solution.py:274
  25.2 26.6 %collective-permute-start.9 = (bf16[512,768]{1,0:T(8,128)(2,1)}, bf16[512,768]{1,0:T(8,128)(2,1)}, u32[]{:S(2)}, u32[]{:S(2)}) collective-permute-start(bf16[512,768]{1,0:T(8,128)(2,1)} %get-tuple-element.73.refs_1_), channel_id=1, source_target_pairs={{0,2},{1,3},{2,0},{3,1},{4,6},{5,7},{6,4},{7,5},{8,10},{9,11},{10,... | collective-permute-start | bytes 2359304 | tf_op jit(solution)/shard_map/ppermute | solution.py:274
  27.1 24.7 %collective-permute-start.8 = (bf16[512,768]{1,0:T(8,128)(2,1)}, bf16[512,768]{1,0:T(8,128)(2,1)}, u32[]{:S(2)}, u32[]{:S(2)}) collective-permute-start(bf16[512,768]{1,0:T(8,128)(2,1)} %get-tuple-element.71.refs_0_), channel_id=1, source_target_pairs={{0,1},{1,0},{2,3},{3,2},{4,5},{5,4},{6,7},{7,6},{8,9},{9,8},{10,11... | collective-permute-start | bytes 2359304 | tf_op jit(solution)/shard_map/ppermute | solution.py:274
  36.2 0.7 copy-start
  36.3 2.2 %copy-start.1 = (bf16[512,256]{1,0:T(8,128)(2,1)}, bf16[512,256]{1,0:T(8,128)(2,1)S(1)}, u32[]{:S(2)}) copy-start(bf16[512,256]{1,0:T(8,128)(2,1)S(1)} %add_convert_fusion.1.refs_0_) | copy-start | bytes 786436
  36.3 1.6 collective-permute-start.5
  37.0 1.5 collective-permute-start.6
  37.0 1.5 copy-start.4
  37.9 0.7 copy-start.2
  38.6 0.7 copy-start.3
  54.6 17.3 %collective-permute-start.11 = (bf16[512,384]{1,0:T(8,128)(2,1)}, bf16[512,384]{1,0:T(8,128)(2,1)}, u32[]{:S(2)}, u32[]{:S(2)}) collective-permute-start(bf16[512,384]{1,0:T(8,128)(2,1)} %get-tuple-element.75.refs_0_), channel_id=1, source_target_pairs={{0,2},{1,3},{2,0},{3,1},{4,6},{5,7},{6,4},{7,5},{8,10},{9,11},{10,... | collective-permute-start | bytes 1179656 | tf_op jit(solution)/shard_map/ppermute | solution.py:274
  55.2 16.8 %collective-permute-start.12 = (bf16[512,384]{1,0:T(8,128)(2,1)}, bf16[512,384]{1,0:T(8,128)(2,1)}, u32[]{:S(2)}, u32[]{:S(2)}) collective-permute-start(bf16[512,384]{1,0:T(8,128)(2,1)} %get-tuple-element.76.refs_1_), channel_id=1, source_target_pairs={{0,1},{1,0},{2,3},{3,2},{4,5},{5,4},{6,7},{7,6},{8,9},{9,8},{10,11... | collective-permute-start | bytes 1179656 | tf_op jit(solution)/shard_map/ppermute | solution.py:274
  55.3 19.5 %collective-permute-start.13 = (bf16[512,384]{1,0:T(8,128)(2,1)}, bf16[512,384]{1,0:T(8,128)(2,1)}, u32[]{:S(2)}, u32[]{:S(2)}) collective-permute-start(bf16[512,384]{1,0:T(8,128)(2,1)} %get-tuple-element.77.refs_0_), channel_id=1, source_target_pairs={{0,2},{1,3},{2,0},{3,1},{4,6},{5,7},{6,4},{7,5},{8,10},{9,11},{10,... | collective-permute-start | bytes 1179656 | tf_op jit(solution)/shard_map/ppermute | solution.py:274
  57.2 17.6 %collective-permute-start.14 = (bf16[512,384]{1,0:T(8,128)(2,1)}, bf16[512,384]{1,0:T(8,128)(2,1)}, u32[]{:S(2)}, u32[]{:S(2)}) collective-permute-start(bf16[512,384]{1,0:T(8,128)(2,1)} %get-tuple-element.78.refs_1_), channel_id=1, source_target_pairs={{0,1},{1,0},{2,3},{3,2},{4,5},{5,4},{6,7},{7,6},{8,9},{9,8},{10,11... | collective-permute-start | bytes 1179656 | tf_op jit(solution)/shard_map/ppermute | solution.py:274
  58.7 11.4 %collective-permute-start.7 = (bf16[688,256]{1,0:T(8,128)(2,1)}, bf16[688,256]{1,0:T(8,128)(2,1)}, u32[]{:S(2)}, u32[]{:S(2)}) collective-permute-start(bf16[688,256]{1,0:T(8,128)(2,1)} %gradient.4), channel_id=1, source_target_pairs={{0,8},{4,12},{8,16},{12,20},{16,24},{20,28},{24,0},{28,4},{1,9},{5... | collective-permute-start | bytes 1056776 | tf_op jit(solution)/shard_map/ppermute | solution.py:280
  74.3 17.7 %collective-permute-start.16 = (bf16[512,384]{1,0:T(8,128)(2,1)}, bf16[512,384]{1,0:T(8,128)(2,1)}, u32[]{:S(2)}, u32[]{:S(2)}) collective-permute-start(bf16[512,384]{1,0:T(8,128)(2,1)} %get-tuple-element.82.refs_0_), channel_id=1, source_target_pairs={{0,4},{4,0},{8,12},{12,8},{16,20},{20,16},{24,28},{28,24},{1,5},{5... | collective-permute-start | bytes 1179656 | tf_op jit(solution)/shard_map/ppermute | solution.py:277
  74.3 17.7 %collective-permute-start.17 = (bf16[512,384]{1,0:T(8,128)(2,1)}, bf16[512,384]{1,0:T(8,128)(2,1)}, u32[]{:S(2)}, u32[]{:S(2)}) collective-permute-start(bf16[512,384]{1,0:T(8,128)(2,1)} %get-tuple-element.83.refs_1_), channel_id=1, source_target_pairs={{0,4},{4,0},{8,12},{12,8},{16,20},{20,16},{24,28},{28,24},{1,5},{5... | collective-permute-start | bytes 1179656 | tf_op jit(solution)/shard_map/ppermute | solution.py:277
  77.1 14.9 %collective-permute-start.18 = (bf16[512,384]{1,0:T(8,128)(2,1)}, bf16[512,384]{1,0:T(8,128)(2,1)}, u32[]{:S(2)}, u32[]{:S(2)}) collective-permute-start(bf16[512,384]{1,0:T(8,128)(2,1)} %get-tuple-element.86.refs_2_), channel_id=1, source_target_pairs={{0,4},{4,0},{8,12},{12,8},{16,20},{20,16},{24,28},{28,24},{1,5},{5... | collective-permute-start | bytes 1179656 | tf_op jit(solution)/shard_map/ppermute | solution.py:277
  77.1 14.8 %collective-permute-start.19 = (bf16[512,384]{1,0:T(8,128)(2,1)}, bf16[512,384]{1,0:T(8,128)(2,1)}, u32[]{:S(2)}, u32[]{:S(2)}) collective-permute-start(bf16[512,384]{1,0:T(8,128)(2,1)} %get-tuple-element.87.refs_3_), channel_id=1, source_target_pairs={{0,4},{4,0},{8,12},{12,8},{16,20},{20,16},{24,28},{28,24},{1,5},{5... | collective-permute-start | bytes 1179656 | tf_op jit(solution)/shard_map/ppermute | solution.py:277
  77.6 12.4 %collective-permute-start.10 = (bf16[688,256]{1,0:T(8,128)(2,1)}, bf16[688,256]{1,0:T(8,128)(2,1)}, u32[]{:S(2)}, u32[]{:S(2)}) collective-permute-start(bf16[688,256]{1,0:T(8,128)(2,1)} %accumulate.8), channel_id=1, source_target_pairs={{0,8},{4,12},{8,16},{12,20},{16,24},{20,28},{24,0},{28,4},{1,9},{5... | collective-permute-start | bytes 1056776 | tf_op jit(solution)/shard_map/ppermute | solution.py:280
  99.5 15.4 %collective-permute-start.20 = (bf16[240,768]{1,0:T(8,128)(2,1)}, bf16[240,768]{1,0:T(8,128)(2,1)}, u32[]{:S(2)}, u32[]{:S(2)}) collective-permute-start(bf16[240,768]{1,0:T(8,128)(2,1)} %get-tuple-element.90), channel_id=1, source_target_pairs={{0,8},{4,12},{8,16},{12,20},{16,24},{20,28},{24,0},{28,4},{1,9},{5... | collective-permute-start | bytes 1105928 | tf_op jit(solution)/shard_map/ppermute | solution.py:280
  99.6 21.2 %collective-permute-start.15 = (bf16[688,256]{1,0:T(8,128)(2,1)}, bf16[688,256]{1,0:T(8,128)(2,1)}, u32[]{:S(2)}, u32[]{:S(2)}) collective-permute-start(bf16[688,256]{1,0:T(8,128)(2,1)} %accumulate.9), channel_id=1, source_target_pairs={{0,8},{4,12},{8,16},{12,20},{16,24},{20,28},{24,0},{28,4},{1,9},{5... | collective-permute-start | bytes 1056776 | tf_op jit(solution)/shard_map/ppermute | solution.py:280
  100.8 27.3 %collective-permute-start.23 = (bf16[224,768]{1,0:T(8,128)(2,1)}, bf16[224,768]{1,0:T(8,128)(2,1)}, u32[]{:S(2)}, u32[]{:S(2)}) collective-permute-start(bf16[224,768]{1,0:T(8,128)(2,1)} %get-tuple-element.91), channel_id=1, source_target_pairs={{0,8},{4,12},{8,16},{12,20},{16,24},{20,28},{24,0},{28,4},{1,9},{5... | collective-permute-start | bytes 1032200 | tf_op jit(solution)/shard_map/ppermute | solution.py:280
  116.8 19.2 %collective-permute-start.22 = (bf16[240,768]{1,0:T(8,128)(2,1)}, bf16[240,768]{1,0:T(8,128)(2,1)}, u32[]{:S(2)}, u32[]{:S(2)}) collective-permute-start(bf16[240,768]{1,0:T(8,128)(2,1)} %accumulate.10), channel_id=1, source_target_pairs={{0,8},{4,12},{8,16},{12,20},{16,24},{20,28},{24,0},{28,4},{1,9},{5... | collective-permute-start | bytes 1105928 | tf_op jit(solution)/shard_map/ppermute | solution.py:280
  123.8 14.1 %collective-permute-start.21 = (bf16[688,256]{1,0:T(8,128)(2,1)}, bf16[688,256]{1,0:T(8,128)(2,1)}, u32[]{:S(2)}, u32[]{:S(2)}) collective-permute-start(bf16[688,256]{1,0:T(8,128)(2,1)} %get-tuple-element.100.refs_0_), channel_id=1, source_target_pairs={{0,1},{1,0},{2,3},{3,2},{4,5},{5,4},{6,7},{7,6},{8,9},{9,8},{10,11... | collective-permute-start | bytes 1056776 | tf_op jit(solution)/shard_map/ppermute | solution.py:274
  124.4 19.0 %collective-permute-start.26 = (bf16[224,768]{1,0:T(8,128)(2,1)}, bf16[224,768]{1,0:T(8,128)(2,1)}, u32[]{:S(2)}, u32[]{:S(2)}) collective-permute-start(bf16[224,768]{1,0:T(8,128)(2,1)} %get-tuple-element.92), channel_id=1, source_target_pairs={{0,8},{4,12},{8,16},{12,20},{16,24},{20,28},{24,0},{28,4},{1,9},{5... | collective-permute-start | bytes 1032200 | tf_op jit(solution)/shard_map/ppermute | solution.py:280
  130.0 20.7 %collective-permute-start.29 = (bf16[224,768]{1,0:T(8,128)(2,1)}, bf16[224,768]{1,0:T(8,128)(2,1)}, u32[]{:S(2)}, u32[]{:S(2)}) collective-permute-start(bf16[224,768]{1,0:T(8,128)(2,1)} %accumulate.11), channel_id=1, source_target_pairs={{0,8},{4,12},{8,16},{12,20},{16,24},{20,28},{24,0},{28,4},{1,9},{5... | collective-permute-start | bytes 1032200 | tf_op jit(solution)/shard_map/ppermute | solution.py:280
  137.9 20.7 %collective-permute-start.28 = (bf16[240,768]{1,0:T(8,128)(2,1)}, bf16[240,768]{1,0:T(8,128)(2,1)}, u32[]{:S(2)}, u32[]{:S(2)}) collective-permute-start(bf16[240,768]{1,0:T(8,128)(2,1)} %accumulate.12), channel_id=1, source_target_pairs={{0,8},{4,12},{8,16},{12,20},{16,24},{20,28},{24,0},{28,4},{1,9},{5... | collective-permute-start | bytes 1105928 | tf_op jit(solution)/shard_map/ppermute | solution.py:280
  137.9 14.7 %collective-permute-start.24 = (bf16[688,256]{1,0:T(8,128)(2,1)}, bf16[688,256]{1,0:T(8,128)(2,1)}, u32[]{:S(2)}, u32[]{:S(2)}) collective-permute-start(bf16[688,256]{1,0:T(8,128)(2,1)} %get-tuple-element.100.refs_0_), channel_id=1, source_target_pairs={{0,2},{1,3},{2,0},{3,1},{4,6},{5,7},{6,4},{7,5},{8,10},{9,11},{10,... | collective-permute-start | bytes 1056776 | tf_op jit(solution)/shard_map/ppermute | solution.py:274
  139.5 13.2 %collective-permute-start.25 = (bf16[688,256]{1,0:T(8,128)(2,1)}, bf16[688,256]{1,0:T(8,128)(2,1)}, u32[]{:S(2)}, u32[]{:S(2)}) collective-permute-start(bf16[688,256]{1,0:T(8,128)(2,1)} %collective-permute-done.21.refs_1_), channel_id=1, source_target_pairs={{0,2},{1,3},{2,0},{3,1},{4,6},{5,7},{6,4},{7,5},{8,10},{9,11},{10,... | collective-permute-start | bytes 1056776 | tf_op jit(solution)/shard_map/ppermute | solution.py:274
  145.3 20.7 %collective-permute-start.27 = (bf16[224,768]{1,0:T(8,128)(2,1)}, bf16[224,768]{1,0:T(8,128)(2,1)}, u32[]{:S(2)}, u32[]{:S(2)}) collective-permute-start(bf16[224,768]{1,0:T(8,128)(2,1)} %accumulate.13), channel_id=1, source_target_pairs={{0,8},{4,12},{8,16},{12,20},{16,24},{20,28},{24,0},{28,4},{1,9},{5... | collective-permute-start | bytes 1032200 | tf_op jit(solution)/shard_map/ppermute | solution.py:280
  152.7 20.7 %collective-permute-start.31 = (bf16[224,768]{1,0:T(8,128)(2,1)}, bf16[224,768]{1,0:T(8,128)(2,1)}, u32[]{:S(2)}, u32[]{:S(2)}) collective-permute-start(bf16[224,768]{1,0:T(8,128)(2,1)} %accumulate.14), channel_id=1, source_target_pairs={{0,8},{4,12},{8,16},{12,20},{16,24},{20,28},{24,0},{28,4},{1,9},{5... | collective-permute-start | bytes 1032200 | tf_op jit(solution)/shard_map/ppermute | solution.py:280
  161.8 21.8 %collective-permute-start.34 = (bf16[240,768]{1,0:T(8,128)(2,1)}, bf16[240,768]{1,0:T(8,128)(2,1)}, u32[]{:S(2)}, u32[]{:S(2)}) collective-permute-start(bf16[240,768]{1,0:T(8,128)(2,1)} %get-tuple-element.120.refs_4_), channel_id=1, source_target_pairs={{0,3},{1,2},{2,1},{3,0},{4,7},{5,6},{6,5},{7,4},{8,11},{9,10},{10,... | collective-permute-start | bytes 1105928 | tf_op jit(solution)/shard_map/ppermute | solution.py:274
  163.3 20.9 %collective-permute-start.33 = (bf16[240,768]{1,0:T(8,128)(2,1)}, bf16[240,768]{1,0:T(8,128)(2,1)}, u32[]{:S(2)}, u32[]{:S(2)}) collective-permute-start(bf16[240,768]{1,0:T(8,128)(2,1)} %get-tuple-element.120.refs_4_), channel_id=1, source_target_pairs={{0,2},{1,3},{2,0},{3,1},{4,6},{5,7},{6,4},{7,5},{8,10},{9,11},{10,... | collective-permute-start | bytes 1105928 | tf_op jit(solution)/shard_map/ppermute | solution.py:274
  163.8 20.4 %collective-permute-start.32 = (bf16[240,768]{1,0:T(8,128)(2,1)}, bf16[240,768]{1,0:T(8,128)(2,1)}, u32[]{:S(2)}, u32[]{:S(2)}) collective-permute-start(bf16[240,768]{1,0:T(8,128)(2,1)} %get-tuple-element.120.refs_4_), channel_id=1, source_target_pairs={{0,1},{1,0},{2,3},{3,2},{4,5},{5,4},{6,7},{7,6},{8,9},{9,8},{10,11... | collective-permute-start | bytes 1105928 | tf_op jit(solution)/shard_map/ppermute | solution.py:274
  167.9 11.1 %collective-permute-start.30 = (bf16[224,768]{1,0:T(8,128)(2,1)}, bf16[224,768]{1,0:T(8,128)(2,1)}, u32[]{:S(2)}, u32[]{:S(2)}) collective-permute-start(bf16[224,768]{1,0:T(8,128)(2,1)} %accumulate.15), channel_id=1, source_target_pairs={{0,8},{4,12},{8,16},{12,20},{16,24},{20,28},{24,0},{28,4},{1,9},{5... | collective-permute-start | bytes 1032200 | tf_op jit(solution)/shard_map/ppermute | solution.py:280
  176.4 10.7 %collective-permute-start.40 = (bf16[224,768]{1,0:T(8,128)(2,1)}, bf16[224,768]{1,0:T(8,128)(2,1)}, u32[]{:S(2)}, u32[]{:S(2)}) collective-permute-start(bf16[224,768]{1,0:T(8,128)(2,1)} %get-tuple-element.119.refs_4_), channel_id=1, source_target_pairs={{0,3},{1,2},{2,1},{3,0},{4,7},{5,6},{6,5},{7,4},{8,11},{9,10},{10,... | collective-permute-start | bytes 1032200 | tf_op jit(solution)/shard_map/ppermute | solution.py:274
  179.0 18.9 %collective-permute-start.39 = (bf16[224,768]{1,0:T(8,128)(2,1)}, bf16[224,768]{1,0:T(8,128)(2,1)}, u32[]{:S(2)}, u32[]{:S(2)}) collective-permute-start(bf16[224,768]{1,0:T(8,128)(2,1)} %get-tuple-element.119.refs_4_), channel_id=1, source_target_pairs={{0,2},{1,3},{2,0},{3,1},{4,6},{5,7},{6,4},{7,5},{8,10},{9,11},{10,... | collective-permute-start | bytes 1032200 | tf_op jit(solution)/shard_map/ppermute | solution.py:274
  183.6 14.3 %collective-permute-start.38 = (bf16[224,768]{1,0:T(8,128)(2,1)}, bf16[224,768]{1,0:T(8,128)(2,1)}, u32[]{:S(2)}, u32[]{:S(2)}) collective-permute-start(bf16[224,768]{1,0:T(8,128)(2,1)} %get-tuple-element.119.refs_4_), channel_id=1, source_target_pairs={{0,1},{1,0},{2,3},{3,2},{4,5},{5,4},{6,7},{7,6},{8,9},{9,8},{10,11... | collective-permute-start | bytes 1032200 | tf_op jit(solution)/shard_map/ppermute | solution.py:274
  184.2 23.0 %collective-permute-start.37 = (bf16[224,768]{1,0:T(8,128)(2,1)}, bf16[224,768]{1,0:T(8,128)(2,1)}, u32[]{:S(2)}, u32[]{:S(2)}) collective-permute-start(bf16[224,768]{1,0:T(8,128)(2,1)} %get-tuple-element.118.refs_4_), channel_id=1, source_target_pairs={{0,3},{1,2},{2,1},{3,0},{4,7},{5,6},{6,5},{7,4},{8,11},{9,10},{10,... | collective-permute-start | bytes 1032200 | tf_op jit(solution)/shard_map/ppermute | solution.py:274
  185.6 22.0 %collective-permute-start.36 = (bf16[224,768]{1,0:T(8,128)(2,1)}, bf16[224,768]{1,0:T(8,128)(2,1)}, u32[]{:S(2)}, u32[]{:S(2)}) collective-permute-start(bf16[224,768]{1,0:T(8,128)(2,1)} %get-tuple-element.118.refs_4_), channel_id=1, source_target_pairs={{0,2},{1,3},{2,0},{3,1},{4,6},{5,7},{6,4},{7,5},{8,10},{9,11},{10,... | collective-permute-start | bytes 1032200 | tf_op jit(solution)/shard_map/ppermute | solution.py:274
  187.1 20.6 %collective-permute-start.35 = (bf16[224,768]{1,0:T(8,128)(2,1)}, bf16[224,768]{1,0:T(8,128)(2,1)}, u32[]{:S(2)}, u32[]{:S(2)}) collective-permute-start(bf16[224,768]{1,0:T(8,128)(2,1)} %get-tuple-element.118.refs_4_), channel_id=1, source_target_pairs={{0,1},{1,0},{2,3},{3,2},{4,5},{5,4},{6,7},{7,6},{8,9},{9,8},{10,11... | collective-permute-start | bytes 1032200 | tf_op jit(solution)/shard_map/ppermute | solution.py:274

commit v9 on v8

--- a/solution.py
+++ b/solution.py
@@ -316,19 +316,17 @@
     whole = slice(0, owned)
     leaving = gradient(stacks, both_0, ring_order[:1], [whole])
     arrived_0 = onward(leaving[0])
-    others_0 = gradient([after(mine, *leaving), theirs], both_0, ring_order[1:])
-
-    sums_1 = plus(sums_1, [after(term, others_0) for term in coming_1], 2)
+    sums_1 = plus(sums_1, [after(term, *leaving) for term in coming_1], 2)
     coming_1 = exchange(sums_1, 1)
+    others_0 = gradient([after(mine, *sums_1), theirs], both_0, ring_order[1:])
+    token = others_0
     for hop in range(1, hops - 1):
-        token = accumulate(after(arrived_0, sums_1), others_0, hop - 1, whole)
+        token = accumulate(after(arrived_0, token), others_0, hop - 1, whole)
         arrived_0 = onward(token)
     sums_1 = add_pairs(sums_1, [after(term, token) for term in coming_1])
     for step in range(2, len(offsets)):
         sums_1 = add_pairs(sums_1, exchange(sums_1, step))
     both_1 = sums_1 + [sibling(half) for half in sums_1]
-    token = accumulate(after(arrived_0, sums_1), others_0, hops - 2, whole)
-    arrived_0 = onward(token)
 
     ends = [0, owned]
     if owned % 16 == 0:
@@ -336,9 +334,11 @@
     parts = [slice(*pair) for pair in zip(ends, ends[1:])]
     count = len(parts)
 
-    leaving = gradient([after(mine, token), theirs], both_1, ring_order[:1], parts)
+    leaving = gradient(stacks, both_1, ring_order[:1], parts)
     arrived = [onward(value) for value in leaving]
-    others = gradient([after(mine, *leaving), theirs], both_1, ring_order[1:])
+    token = accumulate(after(arrived_0, *leaving), others_0, hops - 2, whole)
+    arrived_0 = onward(token)
+    others = gradient([after(mine, token), theirs], both_1, ring_order[1:])
 
     held = ()
 

time: 218 us -> 204 us (0.936)
  waiting for transfers between devices: 55.8 us -> 36.1 us
  starting transfers between devices: 35.2 us -> 39.8 us
    ppermute x12, waiting for transfers between devices: 54.3 us -> 27 us  [onward(): lax.ppermute(value, 'dp', [(index, (index + 2) % dp_count) for index in r...]
    ppermute x22, waiting for transfers between devices: 0.62 us -> 7.59 us  [across(): lax.ppermute(value, 'fsdp', [(index, index ^ offset) for index in range(f...]
    ppermute x22, starting transfers between devices: 25.4 us -> 27.9 us  [across(): lax.ppermute(value, 'fsdp', [(index, index ^ offset) for index in range(f...]
  transfers between devices with their start and end apart: 41 -> 41, of which waited for: 16 -> 14; matrix products, arithmetic and copies ran while one was open for 6% -> 7% of each run, Pallas kernels for 42% -> 49%
where the time goes in v9:
time: 204 us; the launch traced here: 203 us
  Pallas kernels  111 us (54%)
  starting transfers between devices  39.8 us (20%)
  waiting for transfers between devices  36.1 us (18%)
  matrix products  10.3 us (5%)
  local copies, waits for them, and re-layouts  3.99 us (2%)
    pallas_call x4, Pallas kernels, gradient(): pl.pallas_call(kernel, out_shape=out_shape, grid_spec=pltpu.PrefetchScala...  32.4 us
    pallas_call x3, Pallas kernels, expand(): pl.pallas_call(kernel, out_shape=jax.ShapeDtypeStruct((count, owned, feat...  28.2 us
    ppermute x22, starting transfers between devices, across(): lax.ppermute(value, 'fsdp', [(index, index ^ offset) for index in range(f...  27.9 us
    ppermute x12, waiting for transfers between devices, onward(): lax.ppermute(value, 'dp', [(index, (index + 2) % dp_count) for index in r...  27 us
    pallas_call x8, Pallas kernels, accumulate(): pl.pallas_call(kernel, grid=(1,), out_shape=jax.ShapeDtypeStruct(arrived....  15.4 us
    pallas_call x2, Pallas kernels, turn(): pl.pallas_call(kernel, out_shape=jax.ShapeDtypeStruct((chips, owned, toke...  15.1 us
    pallas_call x4, Pallas kernels, adam(): pl.pallas_call(kernel, grid=(1,), out_shape=[jax.ShapeDtypeStruct((owned,...  12.4 us
    dot_general x2, matrix products, projected(): jnp.dot(features, basis[:, columns], preferred_element_type=F32)  10.3 us
  transfers between devices with their start and end apart: 41, of which 14 were waited for; matrix products, arithmetic and copies ran while one was open for 7% of the time, Pallas kernels for 49%

profile of v9, /device:TPU:0, one launch (start us, length us, event | category | flops | bytes accessed | tf_op | source)
XLA Modules:
  0.0 203.3 jit_solution(11116197868450813126)
XLA Ops:
  1.1 3.7 %convolution_convert_fusion = bf16[1024,256]{1,0:T(8,128)(2,1)S(1)} fusion(bf16[2048,1024]{1,0:T(8,128)(2,1)} %bitcast.26, bf16[1,1024,2048]{2,1,0:T(8,128)(2,1)} %param.5), kind=kOutput, calls=%fused_computation.3 | convolution fusion | flops 1074003968 | bytes 5767168 | tf_op jit(solution)/shard_map/dot_general | solution.py:296
  4.9 2.6 %collective-permute-start.3 = (bf16[512,256]{1,0:T(8,128)(2,1)S(1)}, bf16[512,256]{1,0:T(8,128)(2,1)S(1)}, u32[]{:S(2)}, u32[]{:S(2)}) collective-permute-start(bf16[512,256]{1,0:T(8,128)(2,1)S(1)} %get-tuple-element.125), channel_id=1, source_target_pairs={{0,2},{1,3},{2,0},{3,1},{4,6},{5,7},{6,4},{7,5},{8,10},{9,11},{10,... | collective-permute-start | bytes 786440 | tf_op jit(solution)/shard_map/ppermute | solution.py:274
  7.5 1.5 collective-permute-start
  9.0 6.6 %fusion.2 = bf16[1024,768]{1,0:T(8,128)(2,1)S(1)} fusion(bf16[1024,2048]{1,0:T(8,128)(2,1)} %bitcast.37, bf16[2048,1024]{1,0:T(8,128)(2,1)} %bitcast.27), kind=kOutput, calls=%fused_computation.2 | convolution fusion | flops 3222011904 | bytes 8912896 | tf_op jit(solution)/shard_map/dot_general | solution.py:296
  15.6 1.2 fusion.8
  16.8 7.5 %turn.2.refs_4_.refs_8_ = bf16[4,688,1024]{2,1,0:T(8,128)(2,1)} custom-call(s32[1]{0:T(128)} %bitcast.6.core_ref, bf16[1024,5504]{1,0:T(8,128)(2,1)} %bitcast.34), custom_call_target="tpu_custom_call" | custom-call | flops 1024 | bytes 1048576 | tf_op jit(solution)/shard_map/turn/pallas_call | solution.py:39
  24.5 0.6 collective-permute-start.4
  25.2 1.9 collective-permute-start.8
  27.1 1.5 collective-permute-start.7
  28.6 7.6 %turn.3.refs_5_.refs_9_ = bf16[4,688,1024]{2,1,0:T(8,128)(2,1)} custom-call(s32[1]{0:T(128)} %bitcast.6.core_ref, bf16[1024,5504]{1,0:T(8,128)(2,1)} %collective-permute-done.2.grads_ref), custom_call_target="tpu_custom_call" | custom-call | flops 1024 | bytes 1048576 | tf_op jit(solution)/shard_map/turn/pallas_call | solution.py:39
  38.6 0.7 copy-done.3
  39.4 5.3 %gradient.4 = bf16[688,256]{1,0:T(8,128)(2,1)} custom-call(s32[1]{0:T(128)} %bitcast.35, bf16[512,256]{1,0:T(8,128)(2,1)} %copy-done.1, bf16[512,256]{1,0:T(8,128)(2,1)} %copy-done, bf16[512,256]{1,0:T(8,128)(2,1)} %copy-done.2, bf16[512,256]{1,0:T(8,128)(2,1)} %copy-done.3, bf16[4,688,1024]{2,1,0:T(8,128)(2,1)} %turn.2.refs_4_.refs_8_, ...), custom_call_target="tpu_custom_call" | custom-call | flops 1024 | bytes 1048576 | tf_op jit(solution)/shard_map/gradient/pallas_call | solution.py:121
  44.6 5.3 %collective-permute-done.8.refs_3_ = bf16[512,768]{1,0:T(8,128)(2,1)} collective-permute-done((bf16[512,768]{1,0:T(8,128)(2,1)}, bf16[512,768]{1,0:T(8,128)(2,1)}, u32[]{:S(2)}, u32[]{:S(2)}) %collective-permute-start.8) | collective-permute-done | bytes 786464 | tf_op jit(solution)/shard_map/ppermute | solution.py:274
  49.9 2.8 %plus.3 = (bf16[512,384]{1,0:T(8,128)(2,1)}, bf16[512,384]{1,0:T(8,128)(2,1)}, bf16[512,384]{1,0:T(8,128)(2,1)}, bf16[512,384]{1,0:T(8,128)(2,1)}) custom-call(bf16[512,768]{1,0:T(8,128)(2,1)} %get-tuple-element.69.refs_0_, bf16[512,768]{1,0:T(8,128)(2,1)} %get-tuple-element.71.refs_1_, bf16[512,768]{1,0:T(8,128)(2,1)} %collective-permute-done.7.refs_2_, ...), custom_call_target="tpu_custom_call" | custom-call | flops 1024 | bytes 1048576 | tf_op jit(solution)/shard_map/plus/pallas_call | solution.py:65
  53.1 1.6 collective-permute-start.12
  54.7 1.5 collective-permute-start.13
  56.8 1.6 collective-permute-start.9
  58.4 1.3 slice.26.order_ref
  59.7 7.2 %gradient.5.own_ref.stack_ref = bf16[3,688,256]{2,1,0:T(8,128)(2,1)} custom-call(s32[3]{0:T(128)} %slice.26.order_ref, bf16[512,256]{1,0:T(8,128)(2,1)} %copy-done.1, bf16[512,256]{1,0:T(8,128)(2,1)} %copy-done, bf16[512,256]{1,0:T(8,128)(2,1)} %copy-done.2, bf16[512,256]{1,0:T(8,128)(2,1)} %copy-done.3, bf16[4,688,1024]{2,1,0:T(8,128)(2,1)} %turn.2.refs_4_.refs_8_, ...), custom_call_target="tpu_custom_call" | custom-call | flops 1024 | bytes 1048576 | tf_op jit(solution)/shard_map/gradient/pallas_call | solution.py:121
  66.9 2.0 accumulate.8
  68.8 2.3 %plus.4 = (bf16[512,384]{1,0:T(8,128)(2,1)}, bf16[512,384]{1,0:T(8,128)(2,1)}) custom-call(bf16[512,384]{1,0:T(8,128)(2,1)} %get-tuple-element.73.refs_0_, bf16[512,384]{1,0:T(8,128)(2,1)} %get-tuple-element.74.refs_1_, bf16[512,384]{1,0:T(8,128)(2,1)} %collective-permute-done.11.refs_2_, bf16[512,384]{1,0:T(8,128)(2,1)} %collective-permute-done.12.refs_3_), custom_call_target="tpu_custom_call" | custom-call | flops 1024 | bytes 1048576 | tf_op jit(solution)/shard_map/plus/pallas_call | solution.py:65
  71.6 2.3 %plus.5 = (bf16[512,384]{1,0:T(8,128)(2,1)}, bf16[512,384]{1,0:T(8,128)(2,1)}) custom-call(bf16[512,384]{1,0:T(8,128)(2,1)} %get-tuple-element.75.refs_0_, bf16[512,384]{1,0:T(8,128)(2,1)} %get-tuple-element.76.refs_1_, bf16[512,384]{1,0:T(8,128)(2,1)} %collective-permute-done.13.refs_2_, bf16[512,384]{1,0:T(8,128)(2,1)} %collective-permute-done.14.refs_3_), custom_call_target="tpu_custom_call" | custom-call | flops 1024 | bytes 1048576 | tf_op jit(solution)/shard_map/plus/pallas_call | solution.py:65
  74.4 1.6 collective-permute-start.10
  76.5 7.5 %gradient.6 = (bf16[240,768]{1,0:T(8,128)(2,1)}, bf16[224,768]{1,0:T(8,128)(2,1)}, bf16[224,768]{1,0:T(8,128)(2,1)}) custom-call(s32[1]{0:T(128)} %bitcast.36, bf16[512,384]{1,0:T(8,128)(2,1)} %get-tuple-element.81.refs_0_, bf16[512,384]{1,0:T(8,128)(2,1)} %get-tuple-element.82.refs_1_, bf16[512,384]{1,0:T(8,128)(2,1)} %get-tuple-element.85.refs_2_, ...), custom_call_target="tpu_custom_call" | custom-call | flops 1024 | bytes 1048576 | tf_op jit(solution)/shard_map/gradient/pallas_call | solution.py:121
  84.0 1.6 collective-permute-start.20
  85.7 1.1 collective-permute-done.10.arrived_ref
  86.7 1.9 accumulate.9
  89.2 1.4 collective-permute-start.23
  90.6 12.5 %gradient.7.own_ref.stack_ref = bf16[3,688,768]{2,1,0:T(8,128)(2,1)} custom-call(s32[3]{0:T(128)} %slice.26.order_ref, bf16[512,384]{1,0:T(8,128)(2,1)} %get-tuple-element.81.refs_0_, bf16[512,384]{1,0:T(8,128)(2,1)} %get-tuple-element.82.refs_1_, bf16[512,384]{1,0:T(8,128)(2,1)} %get-tuple-element.85.refs_2_, bf16[512,384]{1,0:T(8,128)(2,1)} %get-tuple-element.86.refs_3_, ...), custom_call_target="tpu_custom_call" | custom-call | flops 1024 | bytes 1048576 | tf_op jit(solution)/shard_map/gradient/pallas_call | solution.py:121
  103.1 1.9 accumulate.10
  105.0 0.8 collective-permute-start.22
  105.8 3.1 %adam.4 = (f32[688,1024]{1,0:T(8,128)}, f32[688,1024]{1,0:T(8,128)}, bf16[688,256]{1,0:T(8,128)(2,1)}) custom-call(bf16[688,256]{1,0:T(8,128)(2,1)} %collective-permute-done.19.arrived_ref, bf16[3,688,256]{2,1,0:T(8,128)(2,1)} %gradient.5.own_ref.stack_ref, f32[688,1024]{1,0:T(8,128)} %bitcast.18, f32[688,1024]{1,0:T(8,128)} %bitcast.22), custom_call_target="tpu_custom_call" | custom-call | flops 1024 | bytes 1048576 | tf_op jit(solution)/shard_map/adam/pallas_call | solution.py:181
  109.0 1.4 collective-permute-start.21
  110.4 2.2 %collective-permute-start.26 = (bf16[224,768]{1,0:T(8,128)(2,1)}, bf16[224,768]{1,0:T(8,128)(2,1)}, u32[]{:S(2)}, u32[]{:S(2)}) collective-permute-start(bf16[224,768]{1,0:T(8,128)(2,1)} %get-tuple-element.89), channel_id=1, source_target_pairs={{0,8},{4,12},{8,16},{12,20},{16,24},{20,28},{24,0},{28,4},{1,9},{5... | collective-permute-start | bytes 1032200 | tf_op jit(solution)/shard_map/ppermute | solution.py:280
  112.6 1.9 accumulate.11
  115.0 5.4 %collective-permute-done.22.arrived_ref = bf16[240,768]{1,0:T(8,128)(2,1)} collective-permute-done((bf16[240,768]{1,0:T(8,128)(2,1)}, bf16[240,768]{1,0:T(8,128)(2,1)}, u32[]{:S(2)}, u32[]{:S(2)}) %collective-permute-start.22) | collective-permute-done | bytes 368672 | tf_op jit(solution)/shard_map/ppermute | solution.py:280
  120.4 1.9 accumulate.12
  122.4 1.4 collective-permute-start.24
  123.8 0.6 collective-permute-start.25
  124.4 3.4 %collective-permute-done.26.arrived_ref = bf16[224,768]{1,0:T(8,128)(2,1)} collective-permute-done((bf16[224,768]{1,0:T(8,128)(2,1)}, bf16[224,768]{1,0:T(8,128)(2,1)}, u32[]{:S(2)}, u32[]{:S(2)}) %collective-permute-start.26) | collective-permute-done | bytes 344096 | tf_op jit(solution)/shard_map/ppermute | solution.py:280
  127.8 1.9 accumulate.13
  129.7 5.5 %collective-permute-done.29.arrived_ref = bf16[224,768]{1,0:T(8,128)(2,1)} collective-permute-done((bf16[224,768]{1,0:T(8,128)(2,1)}, bf16[224,768]{1,0:T(8,128)(2,1)}, u32[]{:S(2)}, u32[]{:S(2)}) %collective-permute-start.29) | collective-permute-done | bytes 344096 | tf_op jit(solution)/shard_map/ppermute | solution.py:280
  135.2 1.9 accumulate.14
  137.1 1.8 collective-permute-done.25.refs_3_
  138.9 4.2 %collective-permute-done.28.arrived_ref = bf16[240,768]{1,0:T(8,128)(2,1)} collective-permute-done((bf16[240,768]{1,0:T(8,128)(2,1)}, bf16[240,768]{1,0:T(8,128)(2,1)}, u32[]{:S(2)}, u32[]{:S(2)}) %collective-permute-start.28) | collective-permute-done | bytes 368672 | tf_op jit(solution)/shard_map/ppermute | solution.py:280
  143.1 3.1 %adam.5 = (f32[688,1024]{1,0:T(8,128)}, f32[688,1024]{1,0:T(8,128)}, bf16[240,768]{1,0:T(8,128)(2,1)}) custom-call(bf16[240,768]{1,0:T(8,128)(2,1)} %collective-permute-done.28.arrived_ref, bf16[3,688,768]{2,1,0:T(8,128)(2,1)} %gradient.7.own_ref.stack_ref, f32[688,1024]{1,0:T(8,128)} %bitcast.19, ...), custom_call_target="tpu_custom_call", output_to_operand_aliasing={{0}: (4, {}), {1}: (5, {})} | custom-call | flops 1024 | bytes 1048576 | tf_op jit(solution)/shard_map/adam/pallas_call | solution.py:181
  146.2 2.3 %collective-permute-start.34 = (bf16[240,768]{1,0:T(8,128)(2,1)}, bf16[240,768]{1,0:T(8,128)(2,1)}, u32[]{:S(2)}, u32[]{:S(2)}) collective-permute-start(bf16[240,768]{1,0:T(8,128)(2,1)} %get-tuple-element.118.refs_4_), channel_id=1, source_target_pairs={{0,3},{1,2},{2,1},{3,0},{4,7},{5,6},{6,5},{7,4},{8,11},{9,10},{10,... | collective-permute-start | bytes 1105928 | tf_op jit(solution)/shard_map/ppermute | solution.py:274
  148.5 0.7 collective-permute-start.33
  149.7 0.7 collective-permute-done.27.arrived_ref
  150.5 1.9 accumulate.15
  152.4 5.5 %collective-permute-done.31.arrived_ref = bf16[224,768]{1,0:T(8,128)(2,1)} collective-permute-done((bf16[224,768]{1,0:T(8,128)(2,1)}, bf16[224,768]{1,0:T(8,128)(2,1)}, u32[]{:S(2)}, u32[]{:S(2)}) %collective-permute-start.31) | collective-permute-done | bytes 344096 | tf_op jit(solution)/shard_map/ppermute | solution.py:280
  157.8 3.0 %adam.6 = (f32[688,1024]{1,0:T(8,128)}, f32[688,1024]{1,0:T(8,128)}, bf16[224,768]{1,0:T(8,128)(2,1)}) custom-call(bf16[224,768]{1,0:T(8,128)(2,1)} %collective-permute-done.31.arrived_ref, bf16[3,688,768]{2,1,0:T(8,128)(2,1)} %gradient.7.own_ref.stack_ref, f32[688,1024]{1,0:T(8,128)} %bitcast.20, ...), custom_call_target="tpu_custom_call", output_to_operand_aliasing={{0}: (4, {}), {1}: (5, {})} | custom-call | flops 1024 | bytes 1048576 | tf_op jit(solution)/shard_map/adam/pallas_call | solution.py:181
  160.9 2.3 %collective-permute-start.40 = (bf16[224,768]{1,0:T(8,128)(2,1)}, bf16[224,768]{1,0:T(8,128)(2,1)}, u32[]{:S(2)}, u32[]{:S(2)}) collective-permute-start(bf16[224,768]{1,0:T(8,128)(2,1)} %get-tuple-element.117.refs_4_), channel_id=1, source_target_pairs={{0,3},{1,2},{2,1},{3,0},{4,7},{5,6},{6,5},{7,4},{8,11},{9,10},{10,... | collective-permute-start | bytes 1032200 | tf_op jit(solution)/shard_map/ppermute | solution.py:274
  163.2 1.3 collective-permute-done.30.arrived_ref
  164.4 1.5 collective-permute-start.39
  165.9 3.1 %adam.7 = (f32[688,1024]{1,0:T(8,128)}, f32[688,1024]{1,0:T(8,128)}, bf16[224,768]{1,0:T(8,128)(2,1)}) custom-call(bf16[224,768]{1,0:T(8,128)(2,1)} %collective-permute-done.30.arrived_ref, bf16[3,688,768]{2,1,0:T(8,128)(2,1)} %gradient.7.own_ref.stack_ref, f32[688,1024]{1,0:T(8,128)} %bitcast.21, ...), custom_call_target="tpu_custom_call", output_to_operand_aliasing={{0}: (4, {}), {1}: (5, {})} | custom-call | flops 1024 | bytes 1048576 | tf_op jit(solution)/shard_map/adam/pallas_call | solution.py:181
  168.9 1.4 collective-permute-start.38
  170.4 0.6 collective-permute-start.37
  171.0 1.5 collective-permute-start.36
  172.9 1.5 collective-permute-start.35
  174.4 0.7 pad_add_fusion.targets_ref
  175.1 9.6 %expand.3.refs_8_ = f32[4,688,2048]{2,1,0:T(8,128)} custom-call(s32[4]{0:T(128)} %pad_add_fusion.targets_ref, bf16[2048,1024]{1,0:T(8,128)(2,1)} %bitcast.28, bf16[688,256]{1,0:T(8,128)(2,1)} %get-tuple-element.98.refs_0_, bf16[688,256]{1,0:T(8,128)(2,1)} %collective-permute-done.21.refs_1_, bf16[688,256]{1,0:T(8,128)(2,1)} %collective-permute-done.24.refs_2_, ...), custom_call_target="tpu_custom_call" | custom-call | flops 1024 | bytes 1048576 | tf_op jit(solution)/shard_map/expand/pallas_call | solution.py:222
  184.7 9.3 %expand.4.refs_8_ = f32[4,688,2048]{2,1,0:T(8,128)} custom-call(s32[4]{0:T(128)} %pad_add_fusion.targets_ref, bf16[2048,1024]{1,0:T(8,128)(2,1)} %bitcast.29, bf16[688,256]{1,0:T(8,128)(2,1)} %get-tuple-element.98.refs_0_, bf16[688,256]{1,0:T(8,128)(2,1)} %collective-permute-done.21.refs_1_, ...), custom_call_target="tpu_custom_call", output_to_operand_aliasing={{}: (10, {})} | custom-call | flops 1024 | bytes 1048576 | tf_op jit(solution)/shard_map/expand/pallas_call | solution.py:222
  194.0 9.3 %expand.5 = f32[4,688,2048]{2,1,0:T(8,128)} custom-call(s32[4]{0:T(128)} %pad_add_fusion.targets_ref, bf16[2048,1024]{1,0:T(8,128)(2,1)} %bitcast.30, bf16[688,256]{1,0:T(8,128)(2,1)} %get-tuple-element.98.refs_0_, bf16[688,256]{1,0:T(8,128)(2,1)} %collective-permute-done.21.refs_1_, ...), custom_call_target="tpu_custom_call", output_to_operand_aliasing={{}: (10, {})} | custom-call | flops 1024 | bytes 1048576 | tf_op jit(solution)/shard_map/expand/pallas_call | solution.py:222
  (60 shorter events, 7.8 us)
Async XLA Ops:
  0.6 28.0 %collective-permute-start.2 = (bf16[1024,5504]{1,0:T(8,128)(2,1)}, bf16[1024,5504]{1,0:T(8,128)(2,1)}, u32[]{:S(2)}, u32[]{:S(2)}) collective-permute-start(bf16[1024,5504]{1,0:T(8,128)(2,1)} %bitcast.33), channel_id=1, source_target_pairs={{0,4},{4,0},{8,12},{12,8},{16,20},{20,16},{24,28},{28,24},{1,5},{5... | collective-permute-start | bytes 33816584 | tf_op jit(solution)/shard_map/ppermute | solution.py:277
  4.9 19.4 %collective-permute-start.3 = (bf16[512,256]{1,0:T(8,128)(2,1)S(1)}, bf16[512,256]{1,0:T(8,128)(2,1)S(1)}, u32[]{:S(2)}, u32[]{:S(2)}) collective-permute-start(bf16[512,256]{1,0:T(8,128)(2,1)S(1)} %get-tuple-element.125), channel_id=1, source_target_pairs={{0,2},{1,3},{2,0},{3,1},{4,6},{5,7},{6,4},{7,5},{8,10},{9,11},{10,... | collective-permute-start | bytes 786440 | tf_op jit(solution)/shard_map/ppermute | solution.py:274
  7.5 16.8 %collective-permute-start = (bf16[512,256]{1,0:T(8,128)(2,1)S(1)}, bf16[512,256]{1,0:T(8,128)(2,1)S(1)}, u32[]{:S(2)}, u32[]{:S(2)}) collective-permute-start(bf16[512,256]{1,0:T(8,128)(2,1)S(1)} %get-tuple-element.126), channel_id=1, source_target_pairs={{0,1},{1,0},{2,3},{3,2},{4,5},{5,4},{6,7},{7,6},{8,9},{9,8},{10,11... | collective-permute-start | bytes 786440 | tf_op jit(solution)/shard_map/ppermute | solution.py:274
  24.5 11.7 %collective-permute-start.4 = (bf16[512,256]{1,0:T(8,128)(2,1)S(1)}, bf16[512,256]{1,0:T(8,128)(2,1)S(1)}, u32[]{:S(2)}, u32[]{:S(2)}) collective-permute-start(bf16[512,256]{1,0:T(8,128)(2,1)S(1)} %get-tuple-element.123), channel_id=1, source_target_pairs={{0,1},{1,0},{2,3},{3,2},{4,5},{5,4},{6,7},{7,6},{8,9},{9,8},{10,11... | collective-permute-start | bytes 786440 | tf_op jit(solution)/shard_map/ppermute | solution.py:274
  25.1 11.1 %collective-permute-start.1 = (bf16[512,256]{1,0:T(8,128)(2,1)S(1)}, bf16[512,256]{1,0:T(8,128)(2,1)S(1)}, u32[]{:S(2)}, u32[]{:S(2)}) collective-permute-start(bf16[512,256]{1,0:T(8,128)(2,1)S(1)} %get-tuple-element.124), channel_id=1, source_target_pairs={{0,2},{1,3},{2,0},{3,1},{4,6},{5,7},{6,4},{7,5},{8,10},{9,11},{10,... | collective-permute-start | bytes 786440 | tf_op jit(solution)/shard_map/ppermute | solution.py:274
  25.2 24.7 %collective-permute-start.8 = (bf16[512,768]{1,0:T(8,128)(2,1)}, bf16[512,768]{1,0:T(8,128)(2,1)}, u32[]{:S(2)}, u32[]{:S(2)}) collective-permute-start(bf16[512,768]{1,0:T(8,128)(2,1)} %get-tuple-element.71.refs_1_), channel_id=1, source_target_pairs={{0,2},{1,3},{2,0},{3,1},{4,6},{5,7},{6,4},{7,5},{8,10},{9,11},{10,... | collective-permute-start | bytes 2359304 | tf_op jit(solution)/shard_map/ppermute | solution.py:274
  27.1 22.8 %collective-permute-start.7 = (bf16[512,768]{1,0:T(8,128)(2,1)}, bf16[512,768]{1,0:T(8,128)(2,1)}, u32[]{:S(2)}, u32[]{:S(2)}) collective-permute-start(bf16[512,768]{1,0:T(8,128)(2,1)} %get-tuple-element.69.refs_0_), channel_id=1, source_target_pairs={{0,1},{1,0},{2,3},{3,2},{4,5},{5,4},{6,7},{7,6},{8,9},{9,8},{10,11... | collective-permute-start | bytes 2359304 | tf_op jit(solution)/shard_map/ppermute | solution.py:274
  36.2 0.7 copy-start
  36.3 2.1 %copy-start.1 = (bf16[512,256]{1,0:T(8,128)(2,1)}, bf16[512,256]{1,0:T(8,128)(2,1)S(1)}, u32[]{:S(2)}) copy-start(bf16[512,256]{1,0:T(8,128)(2,1)S(1)} %add_convert_fusion.1.refs_0_) | copy-start | bytes 786436
  36.3 1.6 collective-permute-start.5
  36.9 1.5 collective-permute-start.6
  37.9 0.7 copy-start.2
  38.6 0.7 copy-start.3
  52.7 16.1 %collective-permute-start.11 = (bf16[512,384]{1,0:T(8,128)(2,1)}, bf16[512,384]{1,0:T(8,128)(2,1)}, u32[]{:S(2)}, u32[]{:S(2)}) collective-permute-start(bf16[512,384]{1,0:T(8,128)(2,1)} %get-tuple-element.73.refs_0_), channel_id=1, source_target_pairs={{0,2},{1,3},{2,0},{3,1},{4,6},{5,7},{6,4},{7,5},{8,10},{9,11},{10,... | collective-permute-start | bytes 1179656 | tf_op jit(solution)/shard_map/ppermute | solution.py:274
  53.1 15.8 %collective-permute-start.12 = (bf16[512,384]{1,0:T(8,128)(2,1)}, bf16[512,384]{1,0:T(8,128)(2,1)}, u32[]{:S(2)}, u32[]{:S(2)}) collective-permute-start(bf16[512,384]{1,0:T(8,128)(2,1)} %get-tuple-element.74.refs_1_), channel_id=1, source_target_pairs={{0,1},{1,0},{2,3},{3,2},{4,5},{5,4},{6,7},{7,6},{8,9},{9,8},{10,11... | collective-permute-start | bytes 1179656 | tf_op jit(solution)/shard_map/ppermute | solution.py:274
  54.7 16.9 %collective-permute-start.13 = (bf16[512,384]{1,0:T(8,128)(2,1)}, bf16[512,384]{1,0:T(8,128)(2,1)}, u32[]{:S(2)}, u32[]{:S(2)}) collective-permute-start(bf16[512,384]{1,0:T(8,128)(2,1)} %get-tuple-element.75.refs_0_), channel_id=1, source_target_pairs={{0,2},{1,3},{2,0},{3,1},{4,6},{5,7},{6,4},{7,5},{8,10},{9,11},{10,... | collective-permute-start | bytes 1179656 | tf_op jit(solution)/shard_map/ppermute | solution.py:274
  56.2 15.4 %collective-permute-start.14 = (bf16[512,384]{1,0:T(8,128)(2,1)}, bf16[512,384]{1,0:T(8,128)(2,1)}, u32[]{:S(2)}, u32[]{:S(2)}) collective-permute-start(bf16[512,384]{1,0:T(8,128)(2,1)} %get-tuple-element.76.refs_1_), channel_id=1, source_target_pairs={{0,1},{1,0},{2,3},{3,2},{4,5},{5,4},{6,7},{7,6},{8,9},{9,8},{10,11... | collective-permute-start | bytes 1179656 | tf_op jit(solution)/shard_map/ppermute | solution.py:274
  56.8 10.1 %collective-permute-start.9 = (bf16[688,256]{1,0:T(8,128)(2,1)}, bf16[688,256]{1,0:T(8,128)(2,1)}, u32[]{:S(2)}, u32[]{:S(2)}) collective-permute-start(bf16[688,256]{1,0:T(8,128)(2,1)} %gradient.4), channel_id=1, source_target_pairs={{0,8},{4,12},{8,16},{12,20},{16,24},{20,28},{24,0},{28,4},{1,9},{5... | collective-permute-start | bytes 1056776 | tf_op jit(solution)/shard_map/ppermute | solution.py:280
  71.1 4.9 %collective-permute-start.15 = (bf16[512,384]{1,0:T(8,128)(2,1)}, bf16[512,384]{1,0:T(8,128)(2,1)}, u32[]{:S(2)}, u32[]{:S(2)}) collective-permute-start(bf16[512,384]{1,0:T(8,128)(2,1)} %get-tuple-element.81.refs_0_), channel_id=1, source_target_pairs={{0,4},{4,0},{8,12},{12,8},{16,20},{20,16},{24,28},{28,24},{1,5},{5... | collective-permute-start | bytes 1179656 | tf_op jit(solution)/shard_map/ppermute | solution.py:277
  71.1 4.9 %collective-permute-start.16 = (bf16[512,384]{1,0:T(8,128)(2,1)}, bf16[512,384]{1,0:T(8,128)(2,1)}, u32[]{:S(2)}, u32[]{:S(2)}) collective-permute-start(bf16[512,384]{1,0:T(8,128)(2,1)} %get-tuple-element.82.refs_1_), channel_id=1, source_target_pairs={{0,4},{4,0},{8,12},{12,8},{16,20},{20,16},{24,28},{28,24},{1,5},{5... | collective-permute-start | bytes 1179656 | tf_op jit(solution)/shard_map/ppermute | solution.py:277
  73.9 2.1 %collective-permute-start.17 = (bf16[512,384]{1,0:T(8,128)(2,1)}, bf16[512,384]{1,0:T(8,128)(2,1)}, u32[]{:S(2)}, u32[]{:S(2)}) collective-permute-start(bf16[512,384]{1,0:T(8,128)(2,1)} %get-tuple-element.85.refs_2_), channel_id=1, source_target_pairs={{0,4},{4,0},{8,12},{12,8},{16,20},{20,16},{24,28},{28,24},{1,5},{5... | collective-permute-start | bytes 1179656 | tf_op jit(solution)/shard_map/ppermute | solution.py:277
  74.0 2.6 %collective-permute-start.18 = (bf16[512,384]{1,0:T(8,128)(2,1)}, bf16[512,384]{1,0:T(8,128)(2,1)}, u32[]{:S(2)}, u32[]{:S(2)}) collective-permute-start(bf16[512,384]{1,0:T(8,128)(2,1)} %get-tuple-element.86.refs_3_), channel_id=1, source_target_pairs={{0,4},{4,0},{8,12},{12,8},{16,20},{20,16},{24,28},{28,24},{1,5},{5... | collective-permute-start | bytes 1179656 | tf_op jit(solution)/shard_map/ppermute | solution.py:277
  74.4 12.3 %collective-permute-start.10 = (bf16[688,256]{1,0:T(8,128)(2,1)}, bf16[688,256]{1,0:T(8,128)(2,1)}, u32[]{:S(2)}, u32[]{:S(2)}) collective-permute-start(bf16[688,256]{1,0:T(8,128)(2,1)} %accumulate.8), channel_id=1, source_target_pairs={{0,8},{4,12},{8,16},{12,20},{16,24},{20,28},{24,0},{28,4},{1,9},{5... | collective-permute-start | bytes 1056776 | tf_op jit(solution)/shard_map/ppermute | solution.py:280
  84.0 19.0 %collective-permute-start.20 = (bf16[240,768]{1,0:T(8,128)(2,1)}, bf16[240,768]{1,0:T(8,128)(2,1)}, u32[]{:S(2)}, u32[]{:S(2)}) collective-permute-start(bf16[240,768]{1,0:T(8,128)(2,1)} %get-tuple-element.87), channel_id=1, source_target_pairs={{0,8},{4,12},{8,16},{12,20},{16,24},{20,28},{24,0},{28,4},{1,9},{5... | collective-permute-start | bytes 1105928 | tf_op jit(solution)/shard_map/ppermute | solution.py:280
  88.7 17.2 %collective-permute-start.19 = (bf16[688,256]{1,0:T(8,128)(2,1)}, bf16[688,256]{1,0:T(8,128)(2,1)}, u32[]{:S(2)}, u32[]{:S(2)}) collective-permute-start(bf16[688,256]{1,0:T(8,128)(2,1)} %accumulate.9), channel_id=1, source_target_pairs={{0,8},{4,12},{8,16},{12,20},{16,24},{20,28},{24,0},{28,4},{1,9},{5... | collective-permute-start | bytes 1056776 | tf_op jit(solution)/shard_map/ppermute | solution.py:280
  89.2 23.4 %collective-permute-start.23 = (bf16[224,768]{1,0:T(8,128)(2,1)}, bf16[224,768]{1,0:T(8,128)(2,1)}, u32[]{:S(2)}, u32[]{:S(2)}) collective-permute-start(bf16[224,768]{1,0:T(8,128)(2,1)} %get-tuple-element.88), channel_id=1, source_target_pairs={{0,8},{4,12},{8,16},{12,20},{16,24},{20,28},{24,0},{28,4},{1,9},{5... | collective-permute-start | bytes 1032200 | tf_op jit(solution)/shard_map/ppermute | solution.py:280
  105.0 15.4 %collective-permute-start.22 = (bf16[240,768]{1,0:T(8,128)(2,1)}, bf16[240,768]{1,0:T(8,128)(2,1)}, u32[]{:S(2)}, u32[]{:S(2)}) collective-permute-start(bf16[240,768]{1,0:T(8,128)(2,1)} %accumulate.10), channel_id=1, source_target_pairs={{0,8},{4,12},{8,16},{12,20},{16,24},{20,28},{24,0},{28,4},{1,9},{5... | collective-permute-start | bytes 1105928 | tf_op jit(solution)/shard_map/ppermute | solution.py:280
  109.0 13.4 %collective-permute-start.21 = (bf16[688,256]{1,0:T(8,128)(2,1)}, bf16[688,256]{1,0:T(8,128)(2,1)}, u32[]{:S(2)}, u32[]{:S(2)}) collective-permute-start(bf16[688,256]{1,0:T(8,128)(2,1)} %get-tuple-element.98.refs_0_), channel_id=1, source_target_pairs={{0,1},{1,0},{2,3},{3,2},{4,5},{5,4},{6,7},{7,6},{8,9},{9,8},{10,11... | collective-permute-start | bytes 1056776 | tf_op jit(solution)/shard_map/ppermute | solution.py:274
  110.4 17.4 %collective-permute-start.26 = (bf16[224,768]{1,0:T(8,128)(2,1)}, bf16[224,768]{1,0:T(8,128)(2,1)}, u32[]{:S(2)}, u32[]{:S(2)}) collective-permute-start(bf16[224,768]{1,0:T(8,128)(2,1)} %get-tuple-element.89), channel_id=1, source_target_pairs={{0,8},{4,12},{8,16},{12,20},{16,24},{20,28},{24,0},{28,4},{1,9},{5... | collective-permute-start | bytes 1032200 | tf_op jit(solution)/shard_map/ppermute | solution.py:280
  114.5 20.7 %collective-permute-start.29 = (bf16[224,768]{1,0:T(8,128)(2,1)}, bf16[224,768]{1,0:T(8,128)(2,1)}, u32[]{:S(2)}, u32[]{:S(2)}) collective-permute-start(bf16[224,768]{1,0:T(8,128)(2,1)} %accumulate.11), channel_id=1, source_target_pairs={{0,8},{4,12},{8,16},{12,20},{16,24},{20,28},{24,0},{28,4},{1,9},{5... | collective-permute-start | bytes 1032200 | tf_op jit(solution)/shard_map/ppermute | solution.py:280
  122.4 20.7 %collective-permute-start.28 = (bf16[240,768]{1,0:T(8,128)(2,1)}, bf16[240,768]{1,0:T(8,128)(2,1)}, u32[]{:S(2)}, u32[]{:S(2)}) collective-permute-start(bf16[240,768]{1,0:T(8,128)(2,1)} %accumulate.12), channel_id=1, source_target_pairs={{0,8},{4,12},{8,16},{12,20},{16,24},{20,28},{24,0},{28,4},{1,9},{5... | collective-permute-start | bytes 1105928 | tf_op jit(solution)/shard_map/ppermute | solution.py:280
  122.4 14.7 %collective-permute-start.24 = (bf16[688,256]{1,0:T(8,128)(2,1)}, bf16[688,256]{1,0:T(8,128)(2,1)}, u32[]{:S(2)}, u32[]{:S(2)}) collective-permute-start(bf16[688,256]{1,0:T(8,128)(2,1)} %get-tuple-element.98.refs_0_), channel_id=1, source_target_pairs={{0,2},{1,3},{2,0},{3,1},{4,6},{5,7},{6,4},{7,5},{8,10},{9,11},{10,... | collective-permute-start | bytes 1056776 | tf_op jit(solution)/shard_map/ppermute | solution.py:274
  123.8 15.1 %collective-permute-start.25 = (bf16[688,256]{1,0:T(8,128)(2,1)}, bf16[688,256]{1,0:T(8,128)(2,1)}, u32[]{:S(2)}, u32[]{:S(2)}) collective-permute-start(bf16[688,256]{1,0:T(8,128)(2,1)} %collective-permute-done.21.refs_1_), channel_id=1, source_target_pairs={{0,2},{1,3},{2,0},{3,1},{4,6},{5,7},{6,4},{7,5},{8,10},{9,11},{10,... | collective-permute-start | bytes 1056776 | tf_op jit(solution)/shard_map/ppermute | solution.py:274
  129.7 20.7 %collective-permute-start.27 = (bf16[224,768]{1,0:T(8,128)(2,1)}, bf16[224,768]{1,0:T(8,128)(2,1)}, u32[]{:S(2)}, u32[]{:S(2)}) collective-permute-start(bf16[224,768]{1,0:T(8,128)(2,1)} %accumulate.13), channel_id=1, source_target_pairs={{0,8},{4,12},{8,16},{12,20},{16,24},{20,28},{24,0},{28,4},{1,9},{5... | collective-permute-start | bytes 1032200 | tf_op jit(solution)/shard_map/ppermute | solution.py:280
  137.1 20.7 %collective-permute-start.31 = (bf16[224,768]{1,0:T(8,128)(2,1)}, bf16[224,768]{1,0:T(8,128)(2,1)}, u32[]{:S(2)}, u32[]{:S(2)}) collective-permute-start(bf16[224,768]{1,0:T(8,128)(2,1)} %accumulate.14), channel_id=1, source_target_pairs={{0,8},{4,12},{8,16},{12,20},{16,24},{20,28},{24,0},{28,4},{1,9},{5... | collective-permute-start | bytes 1032200 | tf_op jit(solution)/shard_map/ppermute | solution.py:280
  146.2 22.7 %collective-permute-start.34 = (bf16[240,768]{1,0:T(8,128)(2,1)}, bf16[240,768]{1,0:T(8,128)(2,1)}, u32[]{:S(2)}, u32[]{:S(2)}) collective-permute-start(bf16[240,768]{1,0:T(8,128)(2,1)} %get-tuple-element.118.refs_4_), channel_id=1, source_target_pairs={{0,3},{1,2},{2,1},{3,0},{4,7},{5,6},{6,5},{7,4},{8,11},{9,10},{10,... | collective-permute-start | bytes 1105928 | tf_op jit(solution)/shard_map/ppermute | solution.py:274
  148.5 21.9 %collective-permute-start.33 = (bf16[240,768]{1,0:T(8,128)(2,1)}, bf16[240,768]{1,0:T(8,128)(2,1)}, u32[]{:S(2)}, u32[]{:S(2)}) collective-permute-start(bf16[240,768]{1,0:T(8,128)(2,1)} %get-tuple-element.118.refs_4_), channel_id=1, source_target_pairs={{0,2},{1,3},{2,0},{3,1},{4,6},{5,7},{6,4},{7,5},{8,10},{9,11},{10,... | collective-permute-start | bytes 1105928 | tf_op jit(solution)/shard_map/ppermute | solution.py:274
  149.2 21.2 %collective-permute-start.32 = (bf16[240,768]{1,0:T(8,128)(2,1)}, bf16[240,768]{1,0:T(8,128)(2,1)}, u32[]{:S(2)}, u32[]{:S(2)}) collective-permute-start(bf16[240,768]{1,0:T(8,128)(2,1)} %get-tuple-element.118.refs_4_), channel_id=1, source_target_pairs={{0,1},{1,0},{2,3},{3,2},{4,5},{5,4},{6,7},{7,6},{8,9},{9,8},{10,11... | collective-permute-start | bytes 1105928 | tf_op jit(solution)/shard_map/ppermute | solution.py:274
  152.4 12.1 %collective-permute-start.30 = (bf16[224,768]{1,0:T(8,128)(2,1)}, bf16[224,768]{1,0:T(8,128)(2,1)}, u32[]{:S(2)}, u32[]{:S(2)}) collective-permute-start(bf16[224,768]{1,0:T(8,128)(2,1)} %accumulate.15), channel_id=1, source_target_pairs={{0,8},{4,12},{8,16},{12,20},{16,24},{20,28},{24,0},{28,4},{1,9},{5... | collective-permute-start | bytes 1032200 | tf_op jit(solution)/shard_map/ppermute | solution.py:280
  160.9 12.0 %collective-permute-start.40 = (bf16[224,768]{1,0:T(8,128)(2,1)}, bf16[224,768]{1,0:T(8,128)(2,1)}, u32[]{:S(2)}, u32[]{:S(2)}) collective-permute-start(bf16[224,768]{1,0:T(8,128)(2,1)} %get-tuple-element.117.refs_4_), channel_id=1, source_target_pairs={{0,3},{1,2},{2,1},{3,0},{4,7},{5,6},{6,5},{7,4},{8,11},{9,10},{10,... | collective-permute-start | bytes 1032200 | tf_op jit(solution)/shard_map/ppermute | solution.py:274
  164.4 20.3 %collective-permute-start.39 = (bf16[224,768]{1,0:T(8,128)(2,1)}, bf16[224,768]{1,0:T(8,128)(2,1)}, u32[]{:S(2)}, u32[]{:S(2)}) collective-permute-start(bf16[224,768]{1,0:T(8,128)(2,1)} %get-tuple-element.117.refs_4_), channel_id=1, source_target_pairs={{0,2},{1,3},{2,0},{3,1},{4,6},{5,7},{6,4},{7,5},{8,10},{9,11},{10,... | collective-permute-start | bytes 1032200 | tf_op jit(solution)/shard_map/ppermute | solution.py:274
  168.9 15.8 %collective-permute-start.38 = (bf16[224,768]{1,0:T(8,128)(2,1)}, bf16[224,768]{1,0:T(8,128)(2,1)}, u32[]{:S(2)}, u32[]{:S(2)}) collective-permute-start(bf16[224,768]{1,0:T(8,128)(2,1)} %get-tuple-element.117.refs_4_), channel_id=1, source_target_pairs={{0,1},{1,0},{2,3},{3,2},{4,5},{5,4},{6,7},{7,6},{8,9},{9,8},{10,11... | collective-permute-start | bytes 1032200 | tf_op jit(solution)/shard_map/ppermute | solution.py:274
  170.4 23.6 %collective-permute-start.37 = (bf16[224,768]{1,0:T(8,128)(2,1)}, bf16[224,768]{1,0:T(8,128)(2,1)}, u32[]{:S(2)}, u32[]{:S(2)}) collective-permute-start(bf16[224,768]{1,0:T(8,128)(2,1)} %get-tuple-element.116.refs_4_), channel_id=1, source_target_pairs={{0,3},{1,2},{2,1},{3,0},{4,7},{5,6},{6,5},{7,4},{8,11},{9,10},{10,... | collective-permute-start | bytes 1032200 | tf_op jit(solution)/shard_map/ppermute | solution.py:274
  171.0 23.0 %collective-permute-start.36 = (bf16[224,768]{1,0:T(8,128)(2,1)}, bf16[224,768]{1,0:T(8,128)(2,1)}, u32[]{:S(2)}, u32[]{:S(2)}) collective-permute-start(bf16[224,768]{1,0:T(8,128)(2,1)} %get-tuple-element.116.refs_4_), channel_id=1, source_target_pairs={{0,2},{1,3},{2,0},{3,1},{4,6},{5,7},{6,4},{7,5},{8,10},{9,11},{10,... | collective-permute-start | bytes 1032200 | tf_op jit(solution)/shard_map/ppermute | solution.py:274
  172.9 21.1 %collective-permute-start.35 = (bf16[224,768]{1,0:T(8,128)(2,1)}, bf16[224,768]{1,0:T(8,128)(2,1)}, u32[]{:S(2)}, u32[]{:S(2)}) collective-permute-start(bf16[224,768]{1,0:T(8,128)(2,1)} %get-tuple-element.116.refs_4_), channel_id=1, source_target_pairs={{0,1},{1,0},{2,3},{3,2},{4,5},{5,4},{6,7},{7,6},{8,9},{9,8},{10,11... | collective-permute-start | bytes 1032200 | tf_op jit(solution)/shard_map/ppermute | solution.py:274

commit v10 on v9

--- a/solution.py
+++ b/solution.py
@@ -74,11 +74,10 @@
     )(*ones, *twos)
 
 
-def gradient(stacks, pieces, order, cuts=None):
+def gradient(stacks, pieces, order, begin, count, cuts=None):
     _, owned, tokens = stacks[0].shape
     rows, run = pieces[0].shape
     width = run * len(pieces) // 4
-    count = order.shape[0]
 
     def kernel(order_ref, *refs):
         piece_refs = refs[: len(pieces)]
@@ -88,7 +87,7 @@
 
         def fetch(block, side):
             return pltpu.make_async_copy(
-                stack_refs[side].at[order_ref[block]],
+                stack_refs[side].at[order_ref[begin + block]],
                 held_ref.at[block, :, pl.ds(side * tokens, tokens)],
                 sems.at[block, side],
             )
@@ -300,7 +299,11 @@
     others_grads = sibling(grads)
     sums_0 = projected(features, slice(0, width))
     coming_0 = exchange(sums_0, 0)
-    sums_1 = projected(after(features, *sums_0), slice(width, rank))
+    later = after(features, *sums_0)
+    sums_1 = [
+        jnp.dot(half, basis[:, width:], preferred_element_type=F32).astype(BF16)
+        for half in (later[: tokens // 2], later[tokens // 2 :])
+    ]
     parity = jnp.reshape(core, (1,)).astype(jnp.int32)
     mine = turn(parity, after(grads, *sums_1), owned)
     sums_0 = add(sums_0, [after(term, mine) for term in coming_0])
@@ -314,11 +317,11 @@
     both_0 = sums_0 + [sibling(half) for half in sums_0]
 
     whole = slice(0, owned)
-    leaving = gradient(stacks, both_0, ring_order[:1], [whole])
+    leaving = gradient(stacks, both_0, ring_order, 0, 1, [whole])
     arrived_0 = onward(leaving[0])
     sums_1 = plus(sums_1, [after(term, *leaving) for term in coming_1], 2)
     coming_1 = exchange(sums_1, 1)
-    others_0 = gradient([after(mine, *sums_1), theirs], both_0, ring_order[1:])
+    others_0 = gradient([after(mine, *sums_1), theirs], both_0, ring_order, 1, hops)
     token = others_0
     for hop in range(1, hops - 1):
         token = accumulate(after(arrived_0, token), others_0, hop - 1, whole)
@@ -334,11 +337,11 @@
     parts = [slice(*pair) for pair in zip(ends, ends[1:])]
     count = len(parts)
 
-    leaving = gradient(stacks, both_1, ring_order[:1], parts)
+    leaving = gradient(stacks, both_1, ring_order, 0, 1, parts)
     arrived = [onward(value) for value in leaving]
     token = accumulate(after(arrived_0, *leaving), others_0, hops - 2, whole)
     arrived_0 = onward(token)
-    others = gradient([after(mine, token), theirs], both_1, ring_order[1:])
+    others = gradient([after(mine, token), theirs], both_1, ring_order, 1, hops)
 
     held = ()
 
@@ -362,9 +365,11 @@
     events = sorted((2 * hop + 1.5 * part, part, hop) for part in range(count) for hop in range(1, chips))
     for number, (_, part, hop) in enumerate(events):
         rows = parts[part]
-        if number == 1:
+        if number == 0:
+            token = [token, *arrived]
+        if number == 2:
             starts.append(step_of(after(arrived_0, token), others_0, whole, 0))
-        if number in (1, 3, 5):
+        if number in (2, 4, 6):
             token = [token, *starts]
             if stages:
                 spread(token)

time: 204 us -> 205 us (level)
  waiting for transfers between devices: 36.1 us -> 40.5 us
  local copies, waits for them, and re-layouts: 3.99 us -> 1.39 us
    dot_general x2 -> x1, matrix products: 10.3 us -> 3.88 us  [projected(): jnp.dot(features, basis[:, columns], preferred_element_type=F32)]
    dot_general x0 -> x2, matrix products: none -> 5.44 us  [local(): jnp.dot(half, basis[:, width:], preferred_element_type=F32).astype(BF16)]
    ppermute x12, waiting for transfers between devices: 27 us -> 31.7 us  [onward(): lax.ppermute(value, 'dp', [(index, (index + 2) % dp_count) for index in r...]
    ppermute x12, starting transfers between devices: 10.3 us -> 14.1 us  [onward(): lax.ppermute(value, 'dp', [(index, (index + 2) % dp_count) for index in r...]
    ppermute x22, starting transfers between devices: 27.9 us -> 24.5 us  [across(): lax.ppermute(value, 'fsdp', [(index, index ^ offset) for index in range(f...]
  transfers between devices with their start and end apart: 41 -> 41, of which waited for: 14 -> 14; matrix products, arithmetic and copies ran while one was open for 7% -> 5% of each run, Pallas kernels for 49% -> 48%
where the time goes in v10:
time: 205 us; the launch traced here: 204 us
  Pallas kernels  111 us (54%)
  waiting for transfers between devices  40.5 us (20%)
  starting transfers between devices  40.2 us (20%)
  matrix products  9.32 us (5%)
    pallas_call x4, Pallas kernels, gradient(): pl.pallas_call(kernel, out_shape=out_shape, grid_spec=pltpu.PrefetchScala...  32.4 us
    ppermute x12, waiting for transfers between devices, onward(): lax.ppermute(value, 'dp', [(index, (index + 2) % dp_count) for index in r...  31.7 us
    pallas_call x3, Pallas kernels, expand(): pl.pallas_call(kernel, out_shape=jax.ShapeDtypeStruct((count, owned, feat...  28.2 us
    ppermute x22, starting transfers between devices, across(): lax.ppermute(value, 'fsdp', [(index, index ^ offset) for index in range(f...  24.5 us
    pallas_call x8, Pallas kernels, accumulate(): pl.pallas_call(kernel, grid=(1,), out_shape=jax.ShapeDtypeStruct(arrived....  15.4 us
    pallas_call x2, Pallas kernels, turn(): pl.pallas_call(kernel, out_shape=jax.ShapeDtypeStruct((chips, owned, toke...  15.1 us
    ppermute x12, starting transfers between devices, onward(): lax.ppermute(value, 'dp', [(index, (index + 2) % dp_count) for index in r...  14.1 us
    pallas_call x4, Pallas kernels, adam(): pl.pallas_call(kernel, grid=(1,), out_shape=[jax.ShapeDtypeStruct((owned,...  12.4 us
  transfers between devices with their start and end apart: 41, of which 14 were waited for; matrix products, arithmetic and copies ran while one was open for 5% of the time, Pallas kernels for 48%

profile of v10, /device:TPU:0, one launch (start us, length us, event | category | flops | bytes accessed | tf_op | source)
XLA Modules:
  0.0 204.4 jit_solution(8933239608699023768)
XLA Ops:
  1.2 3.9 %convolution_convert_fusion = bf16[1024,256]{1,0:T(8,128)(2,1)S(1)} fusion(bf16[2048,1024]{1,0:T(8,128)(2,1)} %bitcast.24, bf16[1,1024,2048]{2,1,0:T(8,128)(2,1)} %param.5), kind=kOutput, calls=%fused_computation.8 | convolution fusion | flops 1074003968 | bytes 5767168 | tf_op jit(solution)/shard_map/dot_general | solution.py:295
  5.1 2.6 %collective-permute-start.3 = (bf16[512,256]{1,0:T(8,128)(2,1)S(1)}, bf16[512,256]{1,0:T(8,128)(2,1)S(1)}, u32[]{:S(2)}, u32[]{:S(2)}) collective-permute-start(bf16[512,256]{1,0:T(8,128)(2,1)S(1)} %get-tuple-element.123), channel_id=1, source_target_pairs={{0,2},{1,3},{2,0},{3,1},{4,6},{5,7},{6,4},{7,5},{8,10},{9,11},{10,... | collective-permute-start | bytes 786440 | tf_op jit(solution)/shard_map/ppermute | solution.py:273
  7.7 1.5 collective-permute-start
  9.2 2.7 %fusion.11.refs_1_ = bf16[512,768]{1,0:T(8,128)(2,1)} fusion(bf16[2048,1024]{1,0:T(8,128)(2,1)S(1)} %bitcast.28, bf16[1024,2048]{1,0:T(8,128)(2,1)S(1)} %bitcast.34), kind=kOutput, calls=%fused_computation.7 | convolution fusion | flops 1611005952 | bytes 6029312 | tf_op jit(solution)/shard_map/dot_general | solution.py:304
  11.9 2.7 %fusion.6.refs_0_ = bf16[512,768]{1,0:T(8,128)(2,1)} fusion(bf16[2048,1024]{1,0:T(8,128)(2,1)S(1)} %bitcast.29, bf16[1024,2048]{1,0:T(8,128)(2,1)S(1)} %bitcast.35), kind=kOutput, calls=%fused_computation.6 | convolution fusion | flops 1611005952 | bytes 6029312 | tf_op jit(solution)/shard_map/dot_general | solution.py:304
  14.6 7.5 %turn.2.refs_4_.refs_8_ = bf16[4,688,1024]{2,1,0:T(8,128)(2,1)} custom-call(s32[1]{0:T(128)} %bitcast.6.core_ref, bf16[1024,5504]{1,0:T(8,128)(2,1)} %bitcast.33), custom_call_target="tpu_custom_call" | custom-call | flops 1024 | bytes 1048576 | tf_op jit(solution)/shard_map/turn/pallas_call | solution.py:39
  23.4 1.5 collective-permute-start.8
  24.9 1.5 collective-permute-start.7
  26.4 7.6 %turn.3.refs_5_.refs_9_ = bf16[4,688,1024]{2,1,0:T(8,128)(2,1)} custom-call(s32[1]{0:T(128)} %bitcast.6.core_ref, bf16[1024,5504]{1,0:T(8,128)(2,1)} %collective-permute-done.2.grads_ref), custom_call_target="tpu_custom_call" | custom-call | flops 1024 | bytes 1048576 | tf_op jit(solution)/shard_map/turn/pallas_call | solution.py:39
  35.7 0.7 copy-done.3
  36.5 5.3 %gradient.4 = bf16[688,256]{1,0:T(8,128)(2,1)} custom-call(s32[4]{0:T(128)} %and_select_fusion.order_ref, bf16[512,256]{1,0:T(8,128)(2,1)} %copy-done.2, bf16[512,256]{1,0:T(8,128)(2,1)} %copy-done.1, bf16[512,256]{1,0:T(8,128)(2,1)} %copy-done.3, bf16[512,256]{1,0:T(8,128)(2,1)} %collective-permute-done.6.refs_3_, ...), custom_call_target="tpu_custom_call" | custom-call | flops 1024 | bytes 1048576 | tf_op jit(solution)/shard_map/gradient/pallas_call | solution.py:120
  41.7 5.9 %collective-permute-done.8.refs_3_ = bf16[512,768]{1,0:T(8,128)(2,1)} collective-permute-done((bf16[512,768]{1,0:T(8,128)(2,1)}, bf16[512,768]{1,0:T(8,128)(2,1)}, u32[]{:S(2)}, u32[]{:S(2)}) %collective-permute-start.8) | collective-permute-done | bytes 786464 | tf_op jit(solution)/shard_map/ppermute | solution.py:273
  47.7 2.8 %plus.3 = (bf16[512,384]{1,0:T(8,128)(2,1)}, bf16[512,384]{1,0:T(8,128)(2,1)}, bf16[512,384]{1,0:T(8,128)(2,1)}, bf16[512,384]{1,0:T(8,128)(2,1)}) custom-call(bf16[512,768]{1,0:T(8,128)(2,1)} %fusion.6.refs_0_, bf16[512,768]{1,0:T(8,128)(2,1)} %fusion.11.refs_1_, bf16[512,768]{1,0:T(8,128)(2,1)} %collective-permute-done.7.refs_2_, ...), custom_call_target="tpu_custom_call" | custom-call | flops 1024 | bytes 1048576 | tf_op jit(solution)/shard_map/plus/pallas_call | solution.py:65
  50.5 1.1 collective-permute-start.11
  51.6 0.9 collective-permute-start.12
  52.5 1.5 collective-permute-start.13
  54.5 1.6 collective-permute-start.9
  56.1 7.2 %gradient.5.own_ref.stack_ref = bf16[3,688,256]{2,1,0:T(8,128)(2,1)} custom-call(s32[4]{0:T(128)} %and_select_fusion.order_ref, bf16[512,256]{1,0:T(8,128)(2,1)} %copy-done.2, bf16[512,256]{1,0:T(8,128)(2,1)} %copy-done.1, bf16[512,256]{1,0:T(8,128)(2,1)} %copy-done.3, bf16[512,256]{1,0:T(8,128)(2,1)} %collective-permute-done.6.refs_3_, ...), custom_call_target="tpu_custom_call" | custom-call | flops 1024 | bytes 1048576 | tf_op jit(solution)/shard_map/gradient/pallas_call | solution.py:120
  63.3 1.2 collective-permute-done.9.arrived_ref
  64.5 2.0 accumulate.8
  66.5 2.3 %plus.4 = (bf16[512,384]{1,0:T(8,128)(2,1)}, bf16[512,384]{1,0:T(8,128)(2,1)}) custom-call(bf16[512,384]{1,0:T(8,128)(2,1)} %get-tuple-element.73.refs_0_, bf16[512,384]{1,0:T(8,128)(2,1)} %get-tuple-element.74.refs_1_, bf16[512,384]{1,0:T(8,128)(2,1)} %collective-permute-done.11.refs_2_, bf16[512,384]{1,0:T(8,128)(2,1)} %collective-permute-done.12.refs_3_), custom_call_target="tpu_custom_call" | custom-call | flops 1024 | bytes 1048576 | tf_op jit(solution)/shard_map/plus/pallas_call | solution.py:65
  69.2 1.2 collective-permute-done.14.refs_3_
  70.4 2.3 %plus.5 = (bf16[512,384]{1,0:T(8,128)(2,1)}, bf16[512,384]{1,0:T(8,128)(2,1)}) custom-call(bf16[512,384]{1,0:T(8,128)(2,1)} %get-tuple-element.75.refs_0_, bf16[512,384]{1,0:T(8,128)(2,1)} %get-tuple-element.76.refs_1_, bf16[512,384]{1,0:T(8,128)(2,1)} %collective-permute-done.13.refs_2_, bf16[512,384]{1,0:T(8,128)(2,1)} %collective-permute-done.14.refs_3_), custom_call_target="tpu_custom_call" | custom-call | flops 1024 | bytes 1048576 | tf_op jit(solution)/shard_map/plus/pallas_call | solution.py:65
  73.2 1.6 collective-permute-start.10
  75.3 7.5 %gradient.6 = (bf16[240,768]{1,0:T(8,128)(2,1)}, bf16[224,768]{1,0:T(8,128)(2,1)}, bf16[224,768]{1,0:T(8,128)(2,1)}) custom-call(s32[4]{0:T(128)} %and_select_fusion.order_ref, bf16[512,384]{1,0:T(8,128)(2,1)} %get-tuple-element.81.refs_0_, bf16[512,384]{1,0:T(8,128)(2,1)} %get-tuple-element.82.refs_1_, bf16[512,384]{1,0:T(8,128)(2,1)} %get-tuple-element.85.refs_2_, ...), custom_call_target="tpu_custom_call" | custom-call | flops 1024 | bytes 1048576 | tf_op jit(solution)/shard_map/gradient/pallas_call | solution.py:120
  82.8 1.6 collective-permute-start.21
  84.4 1.6 collective-permute-start.20
  86.0 1.6 collective-permute-start.22
  87.6 1.9 accumulate.9
  89.8 12.5 %gradient.7.own_ref.stack_ref = bf16[3,688,768]{2,1,0:T(8,128)(2,1)} custom-call(s32[4]{0:T(128)} %and_select_fusion.order_ref, bf16[512,384]{1,0:T(8,128)(2,1)} %get-tuple-element.81.refs_0_, bf16[512,384]{1,0:T(8,128)(2,1)} %get-tuple-element.82.refs_1_, bf16[512,384]{1,0:T(8,128)(2,1)} %get-tuple-element.85.refs_2_, ...), custom_call_target="tpu_custom_call" | custom-call | flops 1024 | bytes 1048576 | tf_op jit(solution)/shard_map/gradient/pallas_call | solution.py:120
  102.2 1.6 collective-permute-done.20.arrived_ref
  103.8 7.4 %collective-permute-done.22.arrived_ref = bf16[224,768]{1,0:T(8,128)(2,1)} collective-permute-done((bf16[224,768]{1,0:T(8,128)(2,1)}, bf16[224,768]{1,0:T(8,128)(2,1)}, u32[]{:S(2)}, u32[]{:S(2)}) %collective-permute-start.22) | collective-permute-done | bytes 344096 | tf_op jit(solution)/shard_map/ppermute | solution.py:279
  111.2 1.9 accumulate.10
  113.1 1.9 accumulate.11
  115.0 3.7 %collective-permute-done.19.arrived_ref = bf16[688,256]{1,0:T(8,128)(2,1)} collective-permute-done((bf16[688,256]{1,0:T(8,128)(2,1)}, bf16[688,256]{1,0:T(8,128)(2,1)}, u32[]{:S(2)}, u32[]{:S(2)}) %collective-permute-start.19) | collective-permute-done | bytes 352288 | tf_op jit(solution)/shard_map/ppermute | solution.py:279
  118.7 3.1 %adam.4 = (f32[688,1024]{1,0:T(8,128)}, f32[688,1024]{1,0:T(8,128)}, bf16[688,256]{1,0:T(8,128)(2,1)}) custom-call(bf16[688,256]{1,0:T(8,128)(2,1)} %collective-permute-done.19.arrived_ref, bf16[3,688,256]{2,1,0:T(8,128)(2,1)} %gradient.5.own_ref.stack_ref, f32[688,1024]{1,0:T(8,128)} %bitcast.16, f32[688,1024]{1,0:T(8,128)} %bitcast.20), custom_call_target="tpu_custom_call" | custom-call | flops 1024 | bytes 1048576 | tf_op jit(solution)/shard_map/adam/pallas_call | solution.py:180
  122.4 3.8 %collective-permute-done.24.arrived_ref = bf16[240,768]{1,0:T(8,128)(2,1)} collective-permute-done((bf16[240,768]{1,0:T(8,128)(2,1)}, bf16[240,768]{1,0:T(8,128)(2,1)}, u32[]{:S(2)}, u32[]{:S(2)}) %collective-permute-start.24) | collective-permute-done | bytes 368672 | tf_op jit(solution)/shard_map/ppermute | solution.py:279
  126.2 1.9 accumulate.12
  128.3 1.9 accumulate.13
  130.2 0.7 collective-permute-done.23.refs_1_
  131.3 0.9 collective-permute-start.27
  132.2 1.7 collective-permute-start.26
  133.8 0.8 collective-permute-done.29.arrived_ref
  134.7 1.9 accumulate.14
  136.6 0.8 collective-permute-start.31
  137.3 5.2 %collective-permute-done.28.arrived_ref = bf16[240,768]{1,0:T(8,128)(2,1)} collective-permute-done((bf16[240,768]{1,0:T(8,128)(2,1)}, bf16[240,768]{1,0:T(8,128)(2,1)}, u32[]{:S(2)}, u32[]{:S(2)}) %collective-permute-start.28) | collective-permute-done | bytes 368672 | tf_op jit(solution)/shard_map/ppermute | solution.py:279
  142.6 3.1 %adam.5 = (f32[688,1024]{1,0:T(8,128)}, f32[688,1024]{1,0:T(8,128)}, bf16[240,768]{1,0:T(8,128)(2,1)}) custom-call(bf16[240,768]{1,0:T(8,128)(2,1)} %collective-permute-done.28.arrived_ref, bf16[3,688,768]{2,1,0:T(8,128)(2,1)} %gradient.7.own_ref.stack_ref, f32[688,1024]{1,0:T(8,128)} %bitcast.17, ...), custom_call_target="tpu_custom_call", output_to_operand_aliasing={{0}: (4, {}), {1}: (5, {})} | custom-call | flops 1024 | bytes 1048576 | tf_op jit(solution)/shard_map/adam/pallas_call | solution.py:180
  145.7 1.2 collective-permute-start.34
  146.9 3.0 %collective-permute-done.27.arrived_ref = bf16[224,768]{1,0:T(8,128)(2,1)} collective-permute-done((bf16[224,768]{1,0:T(8,128)(2,1)}, bf16[224,768]{1,0:T(8,128)(2,1)}, u32[]{:S(2)}, u32[]{:S(2)}) %collective-permute-start.27) | collective-permute-done | bytes 344096 | tf_op jit(solution)/shard_map/ppermute | solution.py:279
  149.9 1.2 collective-permute-start.33
  151.7 1.9 accumulate.15
  153.6 4.1 %collective-permute-start.30 = (bf16[224,768]{1,0:T(8,128)(2,1)}, bf16[224,768]{1,0:T(8,128)(2,1)}, u32[]{:S(2)}, u32[]{:S(2)}) collective-permute-start(bf16[224,768]{1,0:T(8,128)(2,1)} %accumulate.15), channel_id=1, source_target_pairs={{0,8},{4,12},{8,16},{12,20},{16,24},{20,28},{24,0},{28,4},{1,9},{5... | collective-permute-start | bytes 1032200 | tf_op jit(solution)/shard_map/ppermute | solution.py:279
  157.7 3.0 %adam.6 = (f32[688,1024]{1,0:T(8,128)}, f32[688,1024]{1,0:T(8,128)}, bf16[224,768]{1,0:T(8,128)(2,1)}) custom-call(bf16[224,768]{1,0:T(8,128)(2,1)} %collective-permute-done.31.arrived_ref, bf16[3,688,768]{2,1,0:T(8,128)(2,1)} %gradient.7.own_ref.stack_ref, f32[688,1024]{1,0:T(8,128)} %bitcast.18, ...), custom_call_target="tpu_custom_call", output_to_operand_aliasing={{0}: (4, {}), {1}: (5, {})} | custom-call | flops 1024 | bytes 1048576 | tf_op jit(solution)/shard_map/adam/pallas_call | solution.py:180
  160.8 1.4 collective-permute-start.40
  162.1 4.9 %collective-permute-done.30.arrived_ref = bf16[224,768]{1,0:T(8,128)(2,1)} collective-permute-done((bf16[224,768]{1,0:T(8,128)(2,1)}, bf16[224,768]{1,0:T(8,128)(2,1)}, u32[]{:S(2)}, u32[]{:S(2)}) %collective-permute-start.30) | collective-permute-done | bytes 344096 | tf_op jit(solution)/shard_map/ppermute | solution.py:279
  167.1 1.0 collective-permute-start.39
  168.1 3.1 %adam.7 = (f32[688,1024]{1,0:T(8,128)}, f32[688,1024]{1,0:T(8,128)}, bf16[224,768]{1,0:T(8,128)(2,1)}) custom-call(bf16[224,768]{1,0:T(8,128)(2,1)} %collective-permute-done.30.arrived_ref, bf16[3,688,768]{2,1,0:T(8,128)(2,1)} %gradient.7.own_ref.stack_ref, f32[688,1024]{1,0:T(8,128)} %bitcast.19, ...), custom_call_target="tpu_custom_call", output_to_operand_aliasing={{0}: (4, {}), {1}: (5, {})} | custom-call | flops 1024 | bytes 1048576 | tf_op jit(solution)/shard_map/adam/pallas_call | solution.py:180
  171.2 0.8 collective-permute-start.38
  172.0 1.6 collective-permute-start.37
  173.6 1.0 collective-permute-start.36
  174.7 0.8 collective-permute-start.35
  176.1 9.6 %expand.3.refs_8_ = f32[4,688,2048]{2,1,0:T(8,128)} custom-call(s32[4]{0:T(128)} %pad_add_fusion.targets_ref, bf16[2048,1024]{1,0:T(8,128)(2,1)} %bitcast.25, bf16[688,256]{1,0:T(8,128)(2,1)} %get-tuple-element.99.refs_0_, bf16[688,256]{1,0:T(8,128)(2,1)} %collective-permute-done.23.refs_1_, bf16[688,256]{1,0:T(8,128)(2,1)} %collective-permute-done.25.refs_2_, ...), custom_call_target="tpu_custom_call" | custom-call | flops 1024 | bytes 1048576 | tf_op jit(solution)/shard_map/expand/pallas_call | solution.py:221
  185.8 9.3 %expand.4.refs_8_ = f32[4,688,2048]{2,1,0:T(8,128)} custom-call(s32[4]{0:T(128)} %pad_add_fusion.targets_ref, bf16[2048,1024]{1,0:T(8,128)(2,1)} %bitcast.26, bf16[688,256]{1,0:T(8,128)(2,1)} %get-tuple-element.99.refs_0_, bf16[688,256]{1,0:T(8,128)(2,1)} %collective-permute-done.23.refs_1_, ...), custom_call_target="tpu_custom_call", output_to_operand_aliasing={{}: (10, {})} | custom-call | flops 1024 | bytes 1048576 | tf_op jit(solution)/shard_map/expand/pallas_call | solution.py:221
  195.1 9.3 %expand.5 = f32[4,688,2048]{2,1,0:T(8,128)} custom-call(s32[4]{0:T(128)} %pad_add_fusion.targets_ref, bf16[2048,1024]{1,0:T(8,128)(2,1)} %bitcast.27, bf16[688,256]{1,0:T(8,128)(2,1)} %get-tuple-element.99.refs_0_, bf16[688,256]{1,0:T(8,128)(2,1)} %collective-permute-done.23.refs_1_, ...), custom_call_target="tpu_custom_call", output_to_operand_aliasing={{}: (10, {})} | custom-call | flops 1024 | bytes 1048576 | tf_op jit(solution)/shard_map/expand/pallas_call | solution.py:221
  (61 shorter events, 8.2 us)
Async XLA Ops:
  0.6 25.8 %collective-permute-start.2 = (bf16[1024,5504]{1,0:T(8,128)(2,1)}, bf16[1024,5504]{1,0:T(8,128)(2,1)}, u32[]{:S(2)}, u32[]{:S(2)}) collective-permute-start(bf16[1024,5504]{1,0:T(8,128)(2,1)} %bitcast.32), channel_id=1, source_target_pairs={{0,4},{4,0},{8,12},{12,8},{16,20},{20,16},{24,28},{28,24},{1,5},{5... | collective-permute-start | bytes 33816584 | tf_op jit(solution)/shard_map/ppermute | solution.py:276
  1.1 8.0 %copy-start = (bf16[1,2048,1024]{2,1,0:T(8,128)(2,1)S(1)}, bf16[1,2048,1024]{2,1,0:T(8,128)(2,1)}, u32[]{:S(2)}) copy-start(bf16[1,2048,1024]{2,1,0:T(8,128)(2,1)} %param.7) | copy-start | bytes 12582916
  1.1 8.0 %copy-start.4 = (bf16[1,1024,2048]{2,1,0:T(8,128)(2,1)S(1)}, bf16[1,1024,2048]{2,1,0:T(8,128)(2,1)}, u32[]{:S(2)}) copy-start(bf16[1,1024,2048]{2,1,0:T(8,128)(2,1)} %param.5) | copy-start | bytes 12582916
  5.1 17.0 %collective-permute-start.3 = (bf16[512,256]{1,0:T(8,128)(2,1)S(1)}, bf16[512,256]{1,0:T(8,128)(2,1)S(1)}, u32[]{:S(2)}, u32[]{:S(2)}) collective-permute-start(bf16[512,256]{1,0:T(8,128)(2,1)S(1)} %get-tuple-element.123), channel_id=1, source_target_pairs={{0,2},{1,3},{2,0},{3,1},{4,6},{5,7},{6,4},{7,5},{8,10},{9,11},{10,... | collective-permute-start | bytes 786440 | tf_op jit(solution)/shard_map/ppermute | solution.py:273
  7.7 14.4 %collective-permute-start = (bf16[512,256]{1,0:T(8,128)(2,1)S(1)}, bf16[512,256]{1,0:T(8,128)(2,1)S(1)}, u32[]{:S(2)}, u32[]{:S(2)}) collective-permute-start(bf16[512,256]{1,0:T(8,128)(2,1)S(1)} %get-tuple-element.124), channel_id=1, source_target_pairs={{0,1},{1,0},{2,3},{3,2},{4,5},{5,4},{6,7},{7,6},{8,9},{9,8},{10,11... | collective-permute-start | bytes 786440 | tf_op jit(solution)/shard_map/ppermute | solution.py:273
  22.3 11.7 %collective-permute-start.4 = (bf16[512,256]{1,0:T(8,128)(2,1)S(1)}, bf16[512,256]{1,0:T(8,128)(2,1)S(1)}, u32[]{:S(2)}, u32[]{:S(2)}) collective-permute-start(bf16[512,256]{1,0:T(8,128)(2,1)S(1)} %get-tuple-element.121), channel_id=1, source_target_pairs={{0,1},{1,0},{2,3},{3,2},{4,5},{5,4},{6,7},{7,6},{8,9},{9,8},{10,11... | collective-permute-start | bytes 786440 | tf_op jit(solution)/shard_map/ppermute | solution.py:273
  22.9 11.1 %collective-permute-start.1 = (bf16[512,256]{1,0:T(8,128)(2,1)S(1)}, bf16[512,256]{1,0:T(8,128)(2,1)S(1)}, u32[]{:S(2)}, u32[]{:S(2)}) collective-permute-start(bf16[512,256]{1,0:T(8,128)(2,1)S(1)} %get-tuple-element.122), channel_id=1, source_target_pairs={{0,2},{1,3},{2,0},{3,1},{4,6},{5,7},{6,4},{7,5},{8,10},{9,11},{10,... | collective-permute-start | bytes 786440 | tf_op jit(solution)/shard_map/ppermute | solution.py:273
  23.4 24.3 %collective-permute-start.8 = (bf16[512,768]{1,0:T(8,128)(2,1)}, bf16[512,768]{1,0:T(8,128)(2,1)}, u32[]{:S(2)}, u32[]{:S(2)}) collective-permute-start(bf16[512,768]{1,0:T(8,128)(2,1)} %fusion.11.refs_1_), channel_id=1, source_target_pairs={{0,2},{1,3},{2,0},{3,1},{4,6},{5,7},{6,4},{7,5},{8,10},{9,11},{10,... | collective-permute-start | bytes 2359304 | tf_op jit(solution)/shard_map/ppermute | solution.py:273
  24.9 22.8 %collective-permute-start.7 = (bf16[512,768]{1,0:T(8,128)(2,1)}, bf16[512,768]{1,0:T(8,128)(2,1)}, u32[]{:S(2)}, u32[]{:S(2)}) collective-permute-start(bf16[512,768]{1,0:T(8,128)(2,1)} %fusion.6.refs_0_), channel_id=1, source_target_pairs={{0,1},{1,0},{2,3},{3,2},{4,5},{5,4},{6,7},{7,6},{8,9},{9,8},{10,11... | collective-permute-start | bytes 2359304 | tf_op jit(solution)/shard_map/ppermute | solution.py:273
  34.0 0.7 copy-start.1
  34.1 0.7 copy-start.2
  34.1 1.6 collective-permute-start.5
  34.7 1.7 collective-permute-start.6
  35.7 0.7 copy-start.3
  50.5 16.0 %collective-permute-start.11 = (bf16[512,384]{1,0:T(8,128)(2,1)}, bf16[512,384]{1,0:T(8,128)(2,1)}, u32[]{:S(2)}, u32[]{:S(2)}) collective-permute-start(bf16[512,384]{1,0:T(8,128)(2,1)} %get-tuple-element.73.refs_0_), channel_id=1, source_target_pairs={{0,2},{1,3},{2,0},{3,1},{4,6},{5,7},{6,4},{7,5},{8,10},{9,11},{10,... | collective-permute-start | bytes 1179656 | tf_op jit(solution)/shard_map/ppermute | solution.py:273
  51.6 14.9 %collective-permute-start.12 = (bf16[512,384]{1,0:T(8,128)(2,1)}, bf16[512,384]{1,0:T(8,128)(2,1)}, u32[]{:S(2)}, u32[]{:S(2)}) collective-permute-start(bf16[512,384]{1,0:T(8,128)(2,1)} %get-tuple-element.74.refs_1_), channel_id=1, source_target_pairs={{0,1},{1,0},{2,3},{3,2},{4,5},{5,4},{6,7},{7,6},{8,9},{9,8},{10,11... | collective-permute-start | bytes 1179656 | tf_op jit(solution)/shard_map/ppermute | solution.py:273
  52.5 16.8 %collective-permute-start.13 = (bf16[512,384]{1,0:T(8,128)(2,1)}, bf16[512,384]{1,0:T(8,128)(2,1)}, u32[]{:S(2)}, u32[]{:S(2)}) collective-permute-start(bf16[512,384]{1,0:T(8,128)(2,1)} %get-tuple-element.75.refs_0_), channel_id=1, source_target_pairs={{0,2},{1,3},{2,0},{3,1},{4,6},{5,7},{6,4},{7,5},{8,10},{9,11},{10,... | collective-permute-start | bytes 1179656 | tf_op jit(solution)/shard_map/ppermute | solution.py:273
  54.0 16.4 %collective-permute-start.14 = (bf16[512,384]{1,0:T(8,128)(2,1)}, bf16[512,384]{1,0:T(8,128)(2,1)}, u32[]{:S(2)}, u32[]{:S(2)}) collective-permute-start(bf16[512,384]{1,0:T(8,128)(2,1)} %get-tuple-element.76.refs_1_), channel_id=1, source_target_pairs={{0,1},{1,0},{2,3},{3,2},{4,5},{5,4},{6,7},{7,6},{8,9},{9,8},{10,11... | collective-permute-start | bytes 1179656 | tf_op jit(solution)/shard_map/ppermute | solution.py:273
  54.5 10.0 %collective-permute-start.9 = (bf16[688,256]{1,0:T(8,128)(2,1)}, bf16[688,256]{1,0:T(8,128)(2,1)}, u32[]{:S(2)}, u32[]{:S(2)}) collective-permute-start(bf16[688,256]{1,0:T(8,128)(2,1)} %gradient.4), channel_id=1, source_target_pairs={{0,8},{4,12},{8,16},{12,20},{16,24},{20,28},{24,0},{28,4},{1,9},{5... | collective-permute-start | bytes 1056776 | tf_op jit(solution)/shard_map/ppermute | solution.py:279
  68.7 6.0 %collective-permute-start.15 = (bf16[512,384]{1,0:T(8,128)(2,1)}, bf16[512,384]{1,0:T(8,128)(2,1)}, u32[]{:S(2)}, u32[]{:S(2)}) collective-permute-start(bf16[512,384]{1,0:T(8,128)(2,1)} %get-tuple-element.81.refs_0_), channel_id=1, source_target_pairs={{0,4},{4,0},{8,12},{12,8},{16,20},{20,16},{24,28},{28,24},{1,5},{5... | collective-permute-start | bytes 1179656 | tf_op jit(solution)/shard_map/ppermute | solution.py:276
  68.7 6.0 %collective-permute-start.16 = (bf16[512,384]{1,0:T(8,128)(2,1)}, bf16[512,384]{1,0:T(8,128)(2,1)}, u32[]{:S(2)}, u32[]{:S(2)}) collective-permute-start(bf16[512,384]{1,0:T(8,128)(2,1)} %get-tuple-element.82.refs_1_), channel_id=1, source_target_pairs={{0,4},{4,0},{8,12},{12,8},{16,20},{20,16},{24,28},{28,24},{1,5},{5... | collective-permute-start | bytes 1179656 | tf_op jit(solution)/shard_map/ppermute | solution.py:276
  72.7 2.1 %collective-permute-start.17 = (bf16[512,384]{1,0:T(8,128)(2,1)}, bf16[512,384]{1,0:T(8,128)(2,1)}, u32[]{:S(2)}, u32[]{:S(2)}) collective-permute-start(bf16[512,384]{1,0:T(8,128)(2,1)} %get-tuple-element.85.refs_2_), channel_id=1, source_target_pairs={{0,4},{4,0},{8,12},{12,8},{16,20},{20,16},{24,28},{28,24},{1,5},{5... | collective-permute-start | bytes 1179656 | tf_op jit(solution)/shard_map/ppermute | solution.py:276
  72.7 2.6 %collective-permute-start.18 = (bf16[512,384]{1,0:T(8,128)(2,1)}, bf16[512,384]{1,0:T(8,128)(2,1)}, u32[]{:S(2)}, u32[]{:S(2)}) collective-permute-start(bf16[512,384]{1,0:T(8,128)(2,1)} %get-tuple-element.86.refs_3_), channel_id=1, source_target_pairs={{0,4},{4,0},{8,12},{12,8},{16,20},{20,16},{24,28},{28,24},{1,5},{5... | collective-permute-start | bytes 1179656 | tf_op jit(solution)/shard_map/ppermute | solution.py:276
  73.2 14.4 %collective-permute-start.10 = (bf16[688,256]{1,0:T(8,128)(2,1)}, bf16[688,256]{1,0:T(8,128)(2,1)}, u32[]{:S(2)}, u32[]{:S(2)}) collective-permute-start(bf16[688,256]{1,0:T(8,128)(2,1)} %accumulate.8), channel_id=1, source_target_pairs={{0,8},{4,12},{8,16},{12,20},{16,24},{20,28},{24,0},{28,4},{1,9},{5... | collective-permute-start | bytes 1056776 | tf_op jit(solution)/shard_map/ppermute | solution.py:279
  82.8 28.3 %collective-permute-start.21 = (bf16[240,768]{1,0:T(8,128)(2,1)}, bf16[240,768]{1,0:T(8,128)(2,1)}, u32[]{:S(2)}, u32[]{:S(2)}) collective-permute-start(bf16[240,768]{1,0:T(8,128)(2,1)} %get-tuple-element.87), channel_id=1, source_target_pairs={{0,8},{4,12},{8,16},{12,20},{16,24},{20,28},{24,0},{28,4},{1,9},{5... | collective-permute-start | bytes 1105928 | tf_op jit(solution)/shard_map/ppermute | solution.py:279
  84.4 19.4 %collective-permute-start.20 = (bf16[224,768]{1,0:T(8,128)(2,1)}, bf16[224,768]{1,0:T(8,128)(2,1)}, u32[]{:S(2)}, u32[]{:S(2)}) collective-permute-start(bf16[224,768]{1,0:T(8,128)(2,1)} %get-tuple-element.88), channel_id=1, source_target_pairs={{0,8},{4,12},{8,16},{12,20},{16,24},{20,28},{24,0},{28,4},{1,9},{5... | collective-permute-start | bytes 1032200 | tf_op jit(solution)/shard_map/ppermute | solution.py:279
  86.0 25.2 %collective-permute-start.22 = (bf16[224,768]{1,0:T(8,128)(2,1)}, bf16[224,768]{1,0:T(8,128)(2,1)}, u32[]{:S(2)}, u32[]{:S(2)}) collective-permute-start(bf16[224,768]{1,0:T(8,128)(2,1)} %get-tuple-element.89), channel_id=1, source_target_pairs={{0,8},{4,12},{8,16},{12,20},{16,24},{20,28},{24,0},{28,4},{1,9},{5... | collective-permute-start | bytes 1032200 | tf_op jit(solution)/shard_map/ppermute | solution.py:279
  89.5 29.2 %collective-permute-start.19 = (bf16[688,256]{1,0:T(8,128)(2,1)}, bf16[688,256]{1,0:T(8,128)(2,1)}, u32[]{:S(2)}, u32[]{:S(2)}) collective-permute-start(bf16[688,256]{1,0:T(8,128)(2,1)} %accumulate.9), channel_id=1, source_target_pairs={{0,8},{4,12},{8,16},{12,20},{16,24},{20,28},{24,0},{28,4},{1,9},{5... | collective-permute-start | bytes 1056776 | tf_op jit(solution)/shard_map/ppermute | solution.py:279
  113.1 13.1 %collective-permute-start.24 = (bf16[240,768]{1,0:T(8,128)(2,1)}, bf16[240,768]{1,0:T(8,128)(2,1)}, u32[]{:S(2)}, u32[]{:S(2)}) collective-permute-start(bf16[240,768]{1,0:T(8,128)(2,1)} %accumulate.10), channel_id=1, source_target_pairs={{0,8},{4,12},{8,16},{12,20},{16,24},{20,28},{24,0},{28,4},{1,9},{5... | collective-permute-start | bytes 1105928 | tf_op jit(solution)/shard_map/ppermute | solution.py:279
  121.8 9.1 %collective-permute-start.23 = (bf16[688,256]{1,0:T(8,128)(2,1)}, bf16[688,256]{1,0:T(8,128)(2,1)}, u32[]{:S(2)}, u32[]{:S(2)}) collective-permute-start(bf16[688,256]{1,0:T(8,128)(2,1)} %get-tuple-element.99.refs_0_), channel_id=1, source_target_pairs={{0,1},{1,0},{2,3},{3,2},{4,5},{5,4},{6,7},{7,6},{8,9},{9,8},{10,11... | collective-permute-start | bytes 1056776 | tf_op jit(solution)/shard_map/ppermute | solution.py:273
  122.4 12.3 %collective-permute-start.29 = (bf16[224,768]{1,0:T(8,128)(2,1)}, bf16[224,768]{1,0:T(8,128)(2,1)}, u32[]{:S(2)}, u32[]{:S(2)}) collective-permute-start(bf16[224,768]{1,0:T(8,128)(2,1)} %accumulate.11), channel_id=1, source_target_pairs={{0,8},{4,12},{8,16},{12,20},{16,24},{20,28},{24,0},{28,4},{1,9},{5... | collective-permute-start | bytes 1032200 | tf_op jit(solution)/shard_map/ppermute | solution.py:279
  128.1 14.4 %collective-permute-start.28 = (bf16[240,768]{1,0:T(8,128)(2,1)}, bf16[240,768]{1,0:T(8,128)(2,1)}, u32[]{:S(2)}, u32[]{:S(2)}) collective-permute-start(bf16[240,768]{1,0:T(8,128)(2,1)} %accumulate.12), channel_id=1, source_target_pairs={{0,8},{4,12},{8,16},{12,20},{16,24},{20,28},{24,0},{28,4},{1,9},{5... | collective-permute-start | bytes 1105928 | tf_op jit(solution)/shard_map/ppermute | solution.py:279
  130.9 20.3 %collective-permute-start.25 = (bf16[688,256]{1,0:T(8,128)(2,1)}, bf16[688,256]{1,0:T(8,128)(2,1)}, u32[]{:S(2)}, u32[]{:S(2)}) collective-permute-start(bf16[688,256]{1,0:T(8,128)(2,1)} %get-tuple-element.99.refs_0_), channel_id=1, source_target_pairs={{0,2},{1,3},{2,0},{3,1},{4,6},{5,7},{6,4},{7,5},{8,10},{9,11},{10,... | collective-permute-start | bytes 1056776 | tf_op jit(solution)/shard_map/ppermute | solution.py:273
  131.3 18.6 %collective-permute-start.27 = (bf16[224,768]{1,0:T(8,128)(2,1)}, bf16[224,768]{1,0:T(8,128)(2,1)}, u32[]{:S(2)}, u32[]{:S(2)}) collective-permute-start(bf16[224,768]{1,0:T(8,128)(2,1)} %accumulate.13), channel_id=1, source_target_pairs={{0,8},{4,12},{8,16},{12,20},{16,24},{20,28},{24,0},{28,4},{1,9},{5... | collective-permute-start | bytes 1032200 | tf_op jit(solution)/shard_map/ppermute | solution.py:279
  132.2 19.5 %collective-permute-start.26 = (bf16[688,256]{1,0:T(8,128)(2,1)}, bf16[688,256]{1,0:T(8,128)(2,1)}, u32[]{:S(2)}, u32[]{:S(2)}) collective-permute-start(bf16[688,256]{1,0:T(8,128)(2,1)} %collective-permute-done.23.refs_1_), channel_id=1, source_target_pairs={{0,2},{1,3},{2,0},{3,1},{4,6},{5,7},{6,4},{7,5},{8,10},{9,11},{10,... | collective-permute-start | bytes 1056776 | tf_op jit(solution)/shard_map/ppermute | solution.py:273
  136.6 21.2 %collective-permute-start.31 = (bf16[224,768]{1,0:T(8,128)(2,1)}, bf16[224,768]{1,0:T(8,128)(2,1)}, u32[]{:S(2)}, u32[]{:S(2)}) collective-permute-start(bf16[224,768]{1,0:T(8,128)(2,1)} %accumulate.14), channel_id=1, source_target_pairs={{0,8},{4,12},{8,16},{12,20},{16,24},{20,28},{24,0},{28,4},{1,9},{5... | collective-permute-start | bytes 1032200 | tf_op jit(solution)/shard_map/ppermute | solution.py:279
  145.7 25.5 %collective-permute-start.34 = (bf16[240,768]{1,0:T(8,128)(2,1)}, bf16[240,768]{1,0:T(8,128)(2,1)}, u32[]{:S(2)}, u32[]{:S(2)}) collective-permute-start(bf16[240,768]{1,0:T(8,128)(2,1)} %get-tuple-element.118.refs_4_), channel_id=1, source_target_pairs={{0,3},{1,2},{2,1},{3,0},{4,7},{5,6},{6,5},{7,4},{8,11},{9,10},{10,... | collective-permute-start | bytes 1105928 | tf_op jit(solution)/shard_map/ppermute | solution.py:273
  149.9 22.1 %collective-permute-start.33 = (bf16[240,768]{1,0:T(8,128)(2,1)}, bf16[240,768]{1,0:T(8,128)(2,1)}, u32[]{:S(2)}, u32[]{:S(2)}) collective-permute-start(bf16[240,768]{1,0:T(8,128)(2,1)} %get-tuple-element.118.refs_4_), channel_id=1, source_target_pairs={{0,2},{1,3},{2,0},{3,1},{4,6},{5,7},{6,4},{7,5},{8,10},{9,11},{10,... | collective-permute-start | bytes 1105928 | tf_op jit(solution)/shard_map/ppermute | solution.py:273
  151.2 20.8 %collective-permute-start.32 = (bf16[240,768]{1,0:T(8,128)(2,1)}, bf16[240,768]{1,0:T(8,128)(2,1)}, u32[]{:S(2)}, u32[]{:S(2)}) collective-permute-start(bf16[240,768]{1,0:T(8,128)(2,1)} %get-tuple-element.118.refs_4_), channel_id=1, source_target_pairs={{0,1},{1,0},{2,3},{3,2},{4,5},{5,4},{6,7},{7,6},{8,9},{9,8},{10,11... | collective-permute-start | bytes 1105928 | tf_op jit(solution)/shard_map/ppermute | solution.py:273
  153.6 13.5 %collective-permute-start.30 = (bf16[224,768]{1,0:T(8,128)(2,1)}, bf16[224,768]{1,0:T(8,128)(2,1)}, u32[]{:S(2)}, u32[]{:S(2)}) collective-permute-start(bf16[224,768]{1,0:T(8,128)(2,1)} %accumulate.15), channel_id=1, source_target_pairs={{0,8},{4,12},{8,16},{12,20},{16,24},{20,28},{24,0},{28,4},{1,9},{5... | collective-permute-start | bytes 1032200 | tf_op jit(solution)/shard_map/ppermute | solution.py:279
  160.8 13.9 %collective-permute-start.40 = (bf16[224,768]{1,0:T(8,128)(2,1)}, bf16[224,768]{1,0:T(8,128)(2,1)}, u32[]{:S(2)}, u32[]{:S(2)}) collective-permute-start(bf16[224,768]{1,0:T(8,128)(2,1)} %get-tuple-element.117.refs_4_), channel_id=1, source_target_pairs={{0,3},{1,2},{2,1},{3,0},{4,7},{5,6},{6,5},{7,4},{8,11},{9,10},{10,... | collective-permute-start | bytes 1032200 | tf_op jit(solution)/shard_map/ppermute | solution.py:273
  167.1 18.7 %collective-permute-start.39 = (bf16[224,768]{1,0:T(8,128)(2,1)}, bf16[224,768]{1,0:T(8,128)(2,1)}, u32[]{:S(2)}, u32[]{:S(2)}) collective-permute-start(bf16[224,768]{1,0:T(8,128)(2,1)} %get-tuple-element.117.refs_4_), channel_id=1, source_target_pairs={{0,2},{1,3},{2,0},{3,1},{4,6},{5,7},{6,4},{7,5},{8,10},{9,11},{10,... | collective-permute-start | bytes 1032200 | tf_op jit(solution)/shard_map/ppermute | solution.py:273
  171.2 14.6 %collective-permute-start.38 = (bf16[224,768]{1,0:T(8,128)(2,1)}, bf16[224,768]{1,0:T(8,128)(2,1)}, u32[]{:S(2)}, u32[]{:S(2)}) collective-permute-start(bf16[224,768]{1,0:T(8,128)(2,1)} %get-tuple-element.117.refs_4_), channel_id=1, source_target_pairs={{0,1},{1,0},{2,3},{3,2},{4,5},{5,4},{6,7},{7,6},{8,9},{9,8},{10,11... | collective-permute-start | bytes 1032200 | tf_op jit(solution)/shard_map/ppermute | solution.py:273
  172.0 23.1 %collective-permute-start.37 = (bf16[224,768]{1,0:T(8,128)(2,1)}, bf16[224,768]{1,0:T(8,128)(2,1)}, u32[]{:S(2)}, u32[]{:S(2)}) collective-permute-start(bf16[224,768]{1,0:T(8,128)(2,1)} %get-tuple-element.116.refs_4_), channel_id=1, source_target_pairs={{0,3},{1,2},{2,1},{3,0},{4,7},{5,6},{6,5},{7,4},{8,11},{9,10},{10,... | collective-permute-start | bytes 1032200 | tf_op jit(solution)/shard_map/ppermute | solution.py:273
  173.6 21.5 %collective-permute-start.36 = (bf16[224,768]{1,0:T(8,128)(2,1)}, bf16[224,768]{1,0:T(8,128)(2,1)}, u32[]{:S(2)}, u32[]{:S(2)}) collective-permute-start(bf16[224,768]{1,0:T(8,128)(2,1)} %get-tuple-element.116.refs_4_), channel_id=1, source_target_pairs={{0,2},{1,3},{2,0},{3,1},{4,6},{5,7},{6,4},{7,5},{8,10},{9,11},{10,... | collective-permute-start | bytes 1032200 | tf_op jit(solution)/shard_map/ppermute | solution.py:273
  174.7 20.4 %collective-permute-start.35 = (bf16[224,768]{1,0:T(8,128)(2,1)}, bf16[224,768]{1,0:T(8,128)(2,1)}, u32[]{:S(2)}, u32[]{:S(2)}) collective-permute-start(bf16[224,768]{1,0:T(8,128)(2,1)} %get-tuple-element.116.refs_4_), channel_id=1, source_target_pairs={{0,1},{1,0},{2,3},{3,2},{4,5},{5,4},{6,7},{7,6},{8,9},{9,8},{10,11... | collective-permute-start | bytes 1032200 | tf_op jit(solution)/shard_map/ppermute | solution.py:273

commit v11 on v9

--- a/solution.py
+++ b/solution.py
@@ -51,23 +51,21 @@
     )(core, grads)
 
 
-def plus(ones, twos, runs=1):
+def plus(ones, twos):
     rows, width = ones[0].shape
-    count, size = len(ones), width // runs
+    count = len(ones)
     block = pl.BlockSpec((rows // 2, width), lambda i: (i, 0))
 
     def kernel(*refs):
-        for index in range(count):
-            total = (refs[index][...].astype(F32) + refs[count + index][...].astype(F32)).astype(BF16)
-            for run in range(runs):
-                refs[(2 + run) * count + index][...] = total[:, run * size : (run + 1) * size]
+        for one_ref, two_ref, out_ref in zip(refs, refs[count:], refs[2 * count :]):
+            out_ref[...] = (one_ref[...].astype(F32) + two_ref[...].astype(F32)).astype(BF16)
 
     return pl.pallas_call(
         kernel,
         grid=(2,),
-        out_shape=[jax.ShapeDtypeStruct((rows, size), BF16)] * (count * runs),
+        out_shape=[jax.ShapeDtypeStruct((rows, width), BF16)] * count,
         in_specs=[block] * (2 * count),
-        out_specs=[pl.BlockSpec((rows // 2, size), lambda i: (i, 0))] * (count * runs),
+        out_specs=[block] * count,
         compiler_params=RING_PARAMS,
         cost_estimate=COST,
         name="plus",
@@ -76,8 +74,7 @@
 
 def gradient(stacks, pieces, order, cuts=None):
     _, owned, tokens = stacks[0].shape
-    rows, run = pieces[0].shape
-    width = run * len(pieces) // 4
+    rows, width = pieces[0].shape
     count = order.shape[0]
 
     def kernel(order_ref, *refs):
@@ -99,9 +96,7 @@
                 for side in range(2):
                     fetch(block, side).start()
             for index, piece_ref in enumerate(piece_refs):
-                side, place = divmod(index, len(pieces) // 2)
-                row, column = side * tokens + place % 2 * rows, place // 2 * run
-                whole_ref[row : row + rows, column : column + run] = piece_ref[...]
+                whole_ref[index * rows : (index + 1) * rows, :] = piece_ref[...]
 
         for side in range(2):
             fetch(step, side).wait()
@@ -124,7 +119,7 @@
         grid_spec=pltpu.PrefetchScalarGridSpec(
             num_scalar_prefetch=1,
             grid=(count,),
-            in_specs=[pl.BlockSpec((rows, run), lambda i, order_ref: (0, 0))] * len(pieces)
+            in_specs=[pl.BlockSpec((rows, width), lambda i, order_ref: (0, 0))] * len(pieces)
             + [pl.BlockSpec(memory_space=pl.ANY)] * 2,
             out_specs=out_specs,
             scratch_shapes=[
@@ -263,7 +258,7 @@
     dp, fsdp = lax.axis_index("dp"), lax.axis_index("fsdp")
     chips = dp_count // 2
     chip, core = dp // 2, dp % 2
-    width = rank // 4
+    width = rank * 3 // 8
 
     offsets = [1 << bit for bit in range(fsdp_count.bit_length() - 1)]
     order = jnp.stack([fsdp ^ offset for offset in range(fsdp_count)]).astype(jnp.int32)
@@ -285,13 +280,6 @@
     def add(halves, arrived):
         return [total_of(half, term) for half, term in zip(halves, arrived)]
 
-    def add_pairs(pieces, arrived):
-        return [
-            total
-            for index in range(0, len(pieces), 2)
-            for total in plus(pieces[index : index + 2], arrived[index : index + 2])
-        ]
-
     def projected(features, columns):
         partial = jnp.dot(features, basis[:, columns], preferred_element_type=F32).astype(BF16)
         return [partial[: tokens // 2], partial[tokens // 2 :]]
@@ -300,7 +288,11 @@
     others_grads = sibling(grads)
     sums_0 = projected(features, slice(0, width))
     coming_0 = exchange(sums_0, 0)
-    sums_1 = projected(after(features, *sums_0), slice(width, rank))
+    later = after(features, *sums_0)
+    sums_1 = [
+        jnp.dot(half, basis[:, width:], preferred_element_type=F32).astype(BF16)
+        for half in (later[: tokens // 2], later[tokens // 2 :])
+    ]
     parity = jnp.reshape(core, (1,)).astype(jnp.int32)
     mine = turn(parity, after(grads, *sums_1), owned)
     sums_0 = add(sums_0, [after(term, mine) for term in coming_0])
@@ -316,29 +308,29 @@
     whole = slice(0, owned)
     leaving = gradient(stacks, both_0, ring_order[:1], [whole])
     arrived_0 = onward(leaving[0])
-    sums_1 = plus(sums_1, [after(term, *leaving) for term in coming_1], 2)
+    sums_1 = plus(sums_1, [after(term, *leaving) for term in coming_1])
     coming_1 = exchange(sums_1, 1)
     others_0 = gradient([after(mine, *sums_1), theirs], both_0, ring_order[1:])
     token = others_0
     for hop in range(1, hops - 1):
         token = accumulate(after(arrived_0, token), others_0, hop - 1, whole)
         arrived_0 = onward(token)
-    sums_1 = add_pairs(sums_1, [after(term, token) for term in coming_1])
+    sums_1 = plus(sums_1, [after(term, token) for term in coming_1])
     for step in range(2, len(offsets)):
-        sums_1 = add_pairs(sums_1, exchange(sums_1, step))
-    both_1 = sums_1 + [sibling(half) for half in sums_1]
+        sums_1 = plus(sums_1, exchange(sums_1, step))
+    both_1 = list(sums_1) + [sibling(half) for half in sums_1]
 
     ends = [0, owned]
     if owned % 16 == 0:
-        ends = [-(-owned * index // 48) * 16 for index in range(4)]
+        ends = [-(-owned * index // 32) * 16 for index in range(3)]
     parts = [slice(*pair) for pair in zip(ends, ends[1:])]
     count = len(parts)
 
     leaving = gradient(stacks, both_1, ring_order[:1], parts)
     arrived = [onward(value) for value in leaving]
-    token = accumulate(after(arrived_0, *leaving), others_0, hops - 2, whole)
+    others = gradient([after(mine, *leaving), theirs], both_1, ring_order[1:])
+    token = accumulate(after(arrived_0, others), others_0, hops - 2, whole)
     arrived_0 = onward(token)
-    others = gradient([after(mine, token), theirs], both_1, ring_order[1:])
 
     held = ()
 
@@ -351,7 +343,6 @@
         return direction
 
     starts = []
-    token = others
     stages = list(offsets)
 
     def spread(token):
@@ -362,9 +353,11 @@
     events = sorted((2 * hop + 1.5 * part, part, hop) for part in range(count) for hop in range(1, chips))
     for number, (_, part, hop) in enumerate(events):
         rows = parts[part]
-        if number == 1:
+        if number == 0:
+            token = [token, *arrived]
+        if number == 2:
             starts.append(step_of(after(arrived_0, token), others_0, whole, 0))
-        if number in (1, 3, 5):
+        if number in (2, 4, 5):
             token = [token, *starts]
             if stages:
                 spread(token)

time: 204 us -> 224 us (1.098)
  waiting for transfers between devices: 36.1 us -> 77.1 us
  starting transfers between devices: 39.8 us -> 25.9 us
  Pallas kernels: 111 us -> 102 us
  matrix products: 10.3 us -> 12.8 us
    ppermute x22 -> x17, waiting for transfers between devices: 7.59 us -> 35.6 us  [across(): lax.ppermute(value, 'fsdp', [(index, index ^ offset) for index in range(f...]
    ppermute x12 -> x9, waiting for transfers between devices: 27 us -> 37.4 us  [onward(): lax.ppermute(value, 'dp', [(index, (index + 2) % dp_count) for index in r...]
    ppermute x22 -> x17, starting transfers between devices: 27.9 us -> 19.8 us  [across(): lax.ppermute(value, 'fsdp', [(index, index ^ offset) for index in range(f...]
    dot_general x0 -> x2, matrix products: none -> 7.8 us  [local(): jnp.dot(half, basis[:, width:], preferred_element_type=F32).astype(BF16)]
    ppermute x12 -> x9, starting transfers between devices: 10.3 us -> 4.51 us  [onward(): lax.ppermute(value, 'dp', [(index, (index + 2) % dp_count) for index in r...]
    dot_general x2 -> x1, matrix products: 10.3 us -> 4.99 us  [projected(): jnp.dot(features, basis[:, columns], preferred_element_type=F32)]
    pallas_call x3 -> x2, Pallas kernels: 28.2 us -> 23.4 us  [expand(): pl.pallas_call(kernel, out_shape=jax.ShapeDtypeStruct((count, owned, feat...]
    pallas_call x8 -> x6, Pallas kernels: 15.4 us -> 12.4 us  [accumulate(): pl.pallas_call(kernel, grid=(1,), out_shape=jax.ShapeDtypeStruct(arrived....]
  transfers between devices with their start and end apart: 41 -> 31, of which waited for: 14 -> 17; matrix products, arithmetic and copies ran while one was open for 7% -> 7% of each run, Pallas kernels for 49% -> 38%
where the time goes in v11:
time: 224 us; the launch traced here: 223 us
  Pallas kernels  102 us (46%)
  waiting for transfers between devices  77.1 us (34%)
  starting transfers between devices  25.9 us (12%)
  matrix products  12.8 us (6%)
  local copies, waits for them, and re-layouts  2.33 us (1%)
    ppermute x9, waiting for transfers between devices, onward(): lax.ppermute(value, 'dp', [(index, (index + 2) % dp_count) for index in r...  37.4 us
    ppermute x17, waiting for transfers between devices, across(): lax.ppermute(value, 'fsdp', [(index, index ^ offset) for index in range(f...  35.6 us
    pallas_call x4, Pallas kernels, gradient(): pl.pallas_call(kernel, out_shape=out_shape, grid_spec=pltpu.PrefetchScala...  35.3 us
    pallas_call x2, Pallas kernels, expand(): pl.pallas_call(kernel, out_shape=jax.ShapeDtypeStruct((count, owned, feat...  23.4 us
    ppermute x17, starting transfers between devices, across(): lax.ppermute(value, 'fsdp', [(index, index ^ offset) for index in range(f...  19.8 us
    pallas_call x2, Pallas kernels, turn(): pl.pallas_call(kernel, out_shape=jax.ShapeDtypeStruct((chips, owned, toke...  15.1 us
    pallas_call x6, Pallas kernels, accumulate(): pl.pallas_call(kernel, grid=(1,), out_shape=jax.ShapeDtypeStruct(arrived....  12.4 us
    pallas_call x3, Pallas kernels, adam(): pl.pallas_call(kernel, grid=(1,), out_shape=[jax.ShapeDtypeStruct((owned,...  10.8 us
  transfers between devices with their start and end apart: 31, of which 17 were waited for; matrix products, arithmetic and copies ran while one was open for 7% of the time, Pallas kernels for 38%

profile of v11, /device:TPU:0, one launch (start us, length us, event | category | flops | bytes accessed | tf_op | source)
XLA Modules:
  0.0 222.6 jit_solution(10231203715680869507)
XLA Ops:
  0.6 0.5 collective-permute-start.2
  1.1 5.0 %fusion.8 = bf16[1024,384]{1,0:T(8,128)(2,1)S(1)} fusion(bf16[2048,1024]{1,0:T(8,128)(2,1)} %bitcast.23, bf16[1,1024,2048]{2,1,0:T(8,128)(2,1)} %param.5), kind=kOutput, calls=%fused_computation.8 | convolution fusion | flops 1611005952 | bytes 6553600 | tf_op jit(solution)/shard_map/dot_general | solution.py:284
  6.2 2.6 %collective-permute-start.3 = (bf16[512,384]{1,0:T(8,128)(2,1)S(1)}, bf16[512,384]{1,0:T(8,128)(2,1)S(1)}, u32[]{:S(2)}, u32[]{:S(2)}) collective-permute-start(bf16[512,384]{1,0:T(8,128)(2,1)S(1)} %get-tuple-element.93), channel_id=1, source_target_pairs={{0,2},{1,3},{2,0},{3,1},{4,6},{5,7},{6,4},{7,5},{8,10},{9,11},{10,... | collective-permute-start | bytes 1179656 | tf_op jit(solution)/shard_map/ppermute | solution.py:269
  8.8 1.5 collective-permute-start
  10.3 5.1 %fusion.16.refs_1_ = bf16[512,640]{1,0:T(8,128)(2,1)} fusion(bf16[2048,1024]{1,0:T(8,128)(2,1)} %bitcast.24, bf16[1024,2048]{1,0:T(8,128)(2,1)} %bitcast.34), kind=kOutput, calls=%fused_computation.10 | convolution fusion | flops 1342504960 | bytes 5373952 | tf_op jit(solution)/shard_map/dot_general | solution.py:293
  15.5 2.7 %fusion.11.refs_0_ = bf16[512,640]{1,0:T(8,128)(2,1)} fusion(bf16[2048,1024]{1,0:T(8,128)(2,1)S(1)} %bitcast.27, bf16[1024,2048]{1,0:T(8,128)(2,1)S(1)} %bitcast.35), kind=kOutput, calls=%fused_computation.9 | convolution fusion | flops 1342504960 | bytes 5373952 | tf_op jit(solution)/shard_map/dot_general | solution.py:293
  18.1 7.5 %turn.2.refs_4_ = bf16[4,688,1024]{2,1,0:T(8,128)(2,1)} custom-call(s32[1]{0:T(128)} %bitcast.6.core_ref, bf16[1024,5504]{1,0:T(8,128)(2,1)} %bitcast.31), custom_call_target="tpu_custom_call" | custom-call | flops 1024 | bytes 1048576 | tf_op jit(solution)/shard_map/turn/pallas_call | solution.py:39
  25.8 0.6 collective-permute-start.4
  26.5 1.9 collective-permute-start.7
  28.5 1.5 collective-permute-start.8
  30.0 7.6 %turn.3.refs_5_ = bf16[4,688,1024]{2,1,0:T(8,128)(2,1)} custom-call(s32[1]{0:T(128)} %bitcast.6.core_ref, bf16[1024,5504]{1,0:T(8,128)(2,1)} %collective-permute-done.2.grads_ref), custom_call_target="tpu_custom_call" | custom-call | flops 1024 | bytes 1048576 | tf_op jit(solution)/shard_map/turn/pallas_call | solution.py:39
  37.5 0.4 collective-permute-done.4
  38.0 0.5 collective-permute-done.1
  38.7 0.4 collective-permute-start.6
  39.2 0.5 and_select_fusion
  39.7 0.7 collective-permute-done.5.refs_2_
  40.4 0.6 collective-permute-done.6.refs_3_
  41.1 0.7 copy-done.4
  41.9 6.2 %gradient.4 = bf16[688,384]{1,0:T(8,128)(2,1)} custom-call(s32[1]{0:T(128)} %bitcast.32, bf16[512,384]{1,0:T(8,128)(2,1)} %copy-done.2, bf16[512,384]{1,0:T(8,128)(2,1)} %copy-done.1, bf16[512,384]{1,0:T(8,128)(2,1)} %copy-done.3, bf16[512,384]{1,0:T(8,128)(2,1)} %copy-done.4, bf16[4,688,1024]{2,1,0:T(8,128)(2,1)} %turn.2.refs_4_, ...), custom_call_target="tpu_custom_call" | custom-call | flops 1024 | bytes 1048576 | tf_op jit(solution)/shard_map/gradient/pallas_call | solution.py:116
  48.1 3.2 %collective-permute-done.8.refs_3_ = bf16[512,640]{1,0:T(8,128)(2,1)} collective-permute-done((bf16[512,640]{1,0:T(8,128)(2,1)}, bf16[512,640]{1,0:T(8,128)(2,1)}, u32[]{:S(2)}, u32[]{:S(2)}) %collective-permute-start.8) | collective-permute-done | bytes 655392 | tf_op jit(solution)/shard_map/ppermute | solution.py:269
  51.3 2.6 %plus.2 = (bf16[512,640]{1,0:T(8,128)(2,1)}, bf16[512,640]{1,0:T(8,128)(2,1)}) custom-call(bf16[512,640]{1,0:T(8,128)(2,1)} %fusion.11.refs_0_, bf16[512,640]{1,0:T(8,128)(2,1)} %fusion.16.refs_1_, bf16[512,640]{1,0:T(8,128)(2,1)} %collective-permute-done.7.refs_2_, bf16[512,640]{1,0:T(8,128)(2,1)} %collective-permute-done.8.refs_3_), custom_call_target="tpu_custom_call" | custom-call | flops 1024 | bytes 1048576 | tf_op jit(solution)/shard_map/plus/pallas_call | solution.py:63
  54.2 1.7 collective-permute-start.12
  55.9 1.6 collective-permute-start.9
  57.5 1.2 slice.27.order_ref
  58.7 9.6 %gradient.5.own_ref.stack_ref = bf16[3,688,384]{2,1,0:T(8,128)(2,1)} custom-call(s32[3]{0:T(128)} %slice.27.order_ref, bf16[512,384]{1,0:T(8,128)(2,1)} %copy-done.2, bf16[512,384]{1,0:T(8,128)(2,1)} %copy-done.1, bf16[512,384]{1,0:T(8,128)(2,1)} %copy-done.3, bf16[512,384]{1,0:T(8,128)(2,1)} %copy-done.4, bf16[4,688,1024]{2,1,0:T(8,128)(2,1)} %turn.2.refs_4_, ...), custom_call_target="tpu_custom_call" | custom-call | flops 1024 | bytes 1048576 | tf_op jit(solution)/shard_map/gradient/pallas_call | solution.py:116
  68.3 1.9 collective-permute-done.9.arrived_ref
  70.1 2.1 accumulate.6
  72.3 2.6 %plus.3 = (bf16[512,640]{1,0:T(8,128)(2,1)}, bf16[512,640]{1,0:T(8,128)(2,1)}) custom-call(bf16[512,640]{1,0:T(8,128)(2,1)} %get-tuple-element.58.refs_0_, bf16[512,640]{1,0:T(8,128)(2,1)} %get-tuple-element.59.refs_1_, bf16[512,640]{1,0:T(8,128)(2,1)} %collective-permute-done.11.refs_2_, bf16[512,640]{1,0:T(8,128)(2,1)} %collective-permute-done.12.refs_3_), custom_call_target="tpu_custom_call" | custom-call | flops 1024 | bytes 1048576 | tf_op jit(solution)/shard_map/plus/pallas_call | solution.py:63
  74.9 0.5 collective-permute-start.14
  75.4 1.9 collective-permute-done.13.refs_2_
  77.3 0.9 collective-permute-done.14.refs_3_
  78.3 7.3 %gradient.6 = (bf16[352,640]{1,0:T(8,128)(2,1)}, bf16[336,640]{1,0:T(8,128)(2,1)}) custom-call(s32[1]{0:T(128)} %bitcast.33, bf16[512,640]{1,0:T(8,128)(2,1)} %get-tuple-element.64.refs_0_, bf16[512,640]{1,0:T(8,128)(2,1)} %get-tuple-element.65.refs_1_, bf16[512,640]{1,0:T(8,128)(2,1)} %collective-permute-done.13.refs_2_, ...), custom_call_target="tpu_custom_call" | custom-call | flops 1024 | bytes 1048576 | tf_op jit(solution)/shard_map/gradient/pallas_call | solution.py:116
  85.6 1.3 collective-permute-start.16
  86.9 12.2 %gradient.7.own_ref.stack_ref = bf16[3,688,640]{2,1,0:T(8,128)(2,1)} custom-call(s32[3]{0:T(128)} %slice.27.order_ref, bf16[512,640]{1,0:T(8,128)(2,1)} %get-tuple-element.64.refs_0_, bf16[512,640]{1,0:T(8,128)(2,1)} %get-tuple-element.65.refs_1_, bf16[512,640]{1,0:T(8,128)(2,1)} %collective-permute-done.13.refs_2_, ...), custom_call_target="tpu_custom_call" | custom-call | flops 1024 | bytes 1048576 | tf_op jit(solution)/shard_map/gradient/pallas_call | solution.py:116
  99.2 2.1 accumulate.7
  101.3 1.6 collective-permute-start.15
  102.8 8.4 %collective-permute-done.16.arrived_ref = bf16[336,640]{1,0:T(8,128)(2,1)} collective-permute-done((bf16[336,640]{1,0:T(8,128)(2,1)}, bf16[336,640]{1,0:T(8,128)(2,1)}, u32[]{:S(2)}, u32[]{:S(2)}) %collective-permute-start.16) | collective-permute-done | bytes 430112 | tf_op jit(solution)/shard_map/ppermute | solution.py:275
  111.2 2.0 accumulate.8
  113.3 2.0 accumulate.9
  115.3 7.3 %collective-permute-done.15.arrived_ref = bf16[688,384]{1,0:T(8,128)(2,1)} collective-permute-done((bf16[688,384]{1,0:T(8,128)(2,1)}, bf16[688,384]{1,0:T(8,128)(2,1)}, u32[]{:S(2)}, u32[]{:S(2)}) %collective-permute-start.15) | collective-permute-done | bytes 528416 | tf_op jit(solution)/shard_map/ppermute | solution.py:275
  122.6 3.9 %adam.3 = (f32[688,1024]{1,0:T(8,128)}, f32[688,1024]{1,0:T(8,128)}, bf16[688,384]{1,0:T(8,128)(2,1)}) custom-call(bf16[688,384]{1,0:T(8,128)(2,1)} %collective-permute-done.15.arrived_ref, bf16[3,688,384]{2,1,0:T(8,128)(2,1)} %gradient.5.own_ref.stack_ref, f32[688,1024]{1,0:T(8,128)} %bitcast.17, f32[688,1024]{1,0:T(8,128)} %bitcast.20), custom_call_target="tpu_custom_call" | custom-call | flops 1024 | bytes 1048576 | tf_op jit(solution)/shard_map/adam/pallas_call | solution.py:176
  126.5 0.6 collective-permute-start.18
  127.1 5.1 %collective-permute-done.20.arrived_ref = bf16[352,640]{1,0:T(8,128)(2,1)} collective-permute-done((bf16[352,640]{1,0:T(8,128)(2,1)}, bf16[352,640]{1,0:T(8,128)(2,1)}, u32[]{:S(2)}, u32[]{:S(2)}) %collective-permute-start.20) | collective-permute-done | bytes 450592 | tf_op jit(solution)/shard_map/ppermute | solution.py:275
  132.2 2.0 accumulate.10
  134.2 7.8 %collective-permute-done.19.arrived_ref = bf16[336,640]{1,0:T(8,128)(2,1)} collective-permute-done((bf16[336,640]{1,0:T(8,128)(2,1)}, bf16[336,640]{1,0:T(8,128)(2,1)}, u32[]{:S(2)}, u32[]{:S(2)}) %collective-permute-start.19) | collective-permute-done | bytes 430112 | tf_op jit(solution)/shard_map/ppermute | solution.py:275
  142.1 2.0 accumulate.11
  144.1 1.5 collective-permute-start.21
  145.6 0.5 collective-permute-start.22
  146.1 5.6 %collective-permute-done.24.arrived_ref = bf16[352,640]{1,0:T(8,128)(2,1)} collective-permute-done((bf16[352,640]{1,0:T(8,128)(2,1)}, bf16[352,640]{1,0:T(8,128)(2,1)}, u32[]{:S(2)}, u32[]{:S(2)}) %collective-permute-start.24) | collective-permute-done | bytes 450592 | tf_op jit(solution)/shard_map/ppermute | solution.py:275
  151.7 3.5 %adam.4 = (f32[688,1024]{1,0:T(8,128)}, f32[688,1024]{1,0:T(8,128)}, bf16[352,640]{1,0:T(8,128)(2,1)}) custom-call(bf16[352,640]{1,0:T(8,128)(2,1)} %collective-permute-done.24.arrived_ref, bf16[3,688,640]{2,1,0:T(8,128)(2,1)} %gradient.7.own_ref.stack_ref, f32[688,1024]{1,0:T(8,128)} %bitcast.18, ...), custom_call_target="tpu_custom_call", output_to_operand_aliasing={{0}: (4, {}), {1}: (5, {})} | custom-call | flops 1024 | bytes 1048576 | tf_op jit(solution)/shard_map/adam/pallas_call | solution.py:176
  155.3 2.4 %collective-permute-start.30 = (bf16[352,640]{1,0:T(8,128)(2,1)}, bf16[352,640]{1,0:T(8,128)(2,1)}, u32[]{:S(2)}, u32[]{:S(2)}) collective-permute-start(bf16[352,640]{1,0:T(8,128)(2,1)} %get-tuple-element.88.refs_4_), channel_id=1, source_target_pairs={{0,3},{1,2},{2,1},{3,0},{4,7},{5,6},{6,5},{7,4},{8,11},{9,10},{10,... | collective-permute-start | bytes 1351688 | tf_op jit(solution)/shard_map/ppermute | solution.py:269
  157.6 0.5 collective-permute-start.29
  158.1 1.3 collective-permute-done.23.arrived_ref
  159.4 0.6 collective-permute-start.28
  160.1 8.2 %collective-permute-done.21.refs_2_ = bf16[688,384]{1,0:T(8,128)(2,1)} collective-permute-done((bf16[688,384]{1,0:T(8,128)(2,1)}, bf16[688,384]{1,0:T(8,128)(2,1)}, u32[]{:S(2)}, u32[]{:S(2)}) %collective-permute-start.21) | collective-permute-done | bytes 528416 | tf_op jit(solution)/shard_map/ppermute | solution.py:269
  168.3 16.7 %collective-permute-done.22.refs_3_ = bf16[688,384]{1,0:T(8,128)(2,1)} collective-permute-done((bf16[688,384]{1,0:T(8,128)(2,1)}, bf16[688,384]{1,0:T(8,128)(2,1)}, u32[]{:S(2)}, u32[]{:S(2)}) %collective-permute-start.22) | collective-permute-done | bytes 528416 | tf_op jit(solution)/shard_map/ppermute | solution.py:269
  184.9 3.4 %adam.5 = (f32[688,1024]{1,0:T(8,128)}, f32[688,1024]{1,0:T(8,128)}, bf16[336,640]{1,0:T(8,128)(2,1)}) custom-call(bf16[336,640]{1,0:T(8,128)(2,1)} %collective-permute-done.23.arrived_ref, bf16[3,688,640]{2,1,0:T(8,128)(2,1)} %gradient.7.own_ref.stack_ref, f32[688,1024]{1,0:T(8,128)} %bitcast.19, ...), custom_call_target="tpu_custom_call", output_to_operand_aliasing={{0}: (4, {}), {1}: (5, {})} | custom-call | flops 1024 | bytes 1048576 | tf_op jit(solution)/shard_map/adam/pallas_call | solution.py:176
  188.3 2.4 %collective-permute-start.27 = (bf16[336,640]{1,0:T(8,128)(2,1)}, bf16[336,640]{1,0:T(8,128)(2,1)}, u32[]{:S(2)}, u32[]{:S(2)}) collective-permute-start(bf16[336,640]{1,0:T(8,128)(2,1)} %get-tuple-element.87.refs_4_), channel_id=1, source_target_pairs={{0,3},{1,2},{2,1},{3,0},{4,7},{5,6},{6,5},{7,4},{8,11},{9,10},{10,... | collective-permute-start | bytes 1290248 | tf_op jit(solution)/shard_map/ppermute | solution.py:269
  190.7 0.5 collective-permute-start.26
  191.2 0.6 collective-permute-start.25
  191.8 0.7 pad_add_fusion.targets_ref
  192.5 6.7 %collective-permute-done.29.refs_6_ = bf16[352,640]{1,0:T(8,128)(2,1)} collective-permute-done((bf16[352,640]{1,0:T(8,128)(2,1)}, bf16[352,640]{1,0:T(8,128)(2,1)}, u32[]{:S(2)}, u32[]{:S(2)}) %collective-permute-start.29) | collective-permute-done | bytes 450592 | tf_op jit(solution)/shard_map/ppermute | solution.py:269
  199.2 11.8 %expand.2.refs_8_ = f32[4,688,2048]{2,1,0:T(8,128)} custom-call(s32[4]{0:T(128)} %pad_add_fusion.targets_ref, bf16[2048,1024]{1,0:T(8,128)(2,1)} %bitcast.25, bf16[688,384]{1,0:T(8,128)(2,1)} %get-tuple-element.77.refs_0_, bf16[688,384]{1,0:T(8,128)(2,1)} %collective-permute-done.18.refs_1_, bf16[688,384]{1,0:T(8,128)(2,1)} %collective-permute-done.21.refs_2_, ...), custom_call_target="tpu_custom_call" | custom-call | flops 1024 | bytes 1048576 | tf_op jit(solution)/shard_map/expand/pallas_call | solution.py:217
  211.1 11.6 %expand.3 = f32[4,688,2048]{2,1,0:T(8,128)} custom-call(s32[4]{0:T(128)} %pad_add_fusion.targets_ref, bf16[2048,1024]{1,0:T(8,128)(2,1)} %bitcast.26, bf16[688,384]{1,0:T(8,128)(2,1)} %get-tuple-element.77.refs_0_, bf16[688,384]{1,0:T(8,128)(2,1)} %collective-permute-done.18.refs_1_, ...), custom_call_target="tpu_custom_call", output_to_operand_aliasing={{}: (10, {})} | custom-call | flops 1024 | bytes 1048576 | tf_op jit(solution)/shard_map/expand/pallas_call | solution.py:217
  (39 shorter events, 1.4 us)
Async XLA Ops:
  0.6 29.3 %collective-permute-start.2 = (bf16[1024,5504]{1,0:T(8,128)(2,1)}, bf16[1024,5504]{1,0:T(8,128)(2,1)}, u32[]{:S(2)}, u32[]{:S(2)}) collective-permute-start(bf16[1024,5504]{1,0:T(8,128)(2,1)} %bitcast.30), channel_id=1, source_target_pairs={{0,4},{4,0},{8,12},{12,8},{16,20},{20,16},{24,28},{28,24},{1,5},{5... | collective-permute-start | bytes 33816584 | tf_op jit(solution)/shard_map/ppermute | solution.py:272
  6.2 19.4 %collective-permute-start.3 = (bf16[512,384]{1,0:T(8,128)(2,1)S(1)}, bf16[512,384]{1,0:T(8,128)(2,1)S(1)}, u32[]{:S(2)}, u32[]{:S(2)}) collective-permute-start(bf16[512,384]{1,0:T(8,128)(2,1)S(1)} %get-tuple-element.93), channel_id=1, source_target_pairs={{0,2},{1,3},{2,0},{3,1},{4,6},{5,7},{6,4},{7,5},{8,10},{9,11},{10,... | collective-permute-start | bytes 1179656 | tf_op jit(solution)/shard_map/ppermute | solution.py:269
  8.8 16.8 %collective-permute-start = (bf16[512,384]{1,0:T(8,128)(2,1)S(1)}, bf16[512,384]{1,0:T(8,128)(2,1)S(1)}, u32[]{:S(2)}, u32[]{:S(2)}) collective-permute-start(bf16[512,384]{1,0:T(8,128)(2,1)S(1)} %get-tuple-element.94), channel_id=1, source_target_pairs={{0,1},{1,0},{2,3},{3,2},{4,5},{5,4},{6,7},{7,6},{8,9},{9,8},{10,11... | collective-permute-start | bytes 1179656 | tf_op jit(solution)/shard_map/ppermute | solution.py:269
  10.3 5.1 %copy-start = (bf16[1,2048,1024]{2,1,0:T(8,128)(2,1)S(1)}, bf16[1,2048,1024]{2,1,0:T(8,128)(2,1)}, u32[]{:S(2)}) copy-start(bf16[1,2048,1024]{2,1,0:T(8,128)(2,1)} %param.7) | copy-start | bytes 12582916
  10.3 5.1 %copy-start.5 = (bf16[1,1024,2048]{2,1,0:T(8,128)(2,1)S(1)}, bf16[1,1024,2048]{2,1,0:T(8,128)(2,1)}, u32[]{:S(2)}) copy-start(bf16[1,1024,2048]{2,1,0:T(8,128)(2,1)} %param.5) | copy-start | bytes 12582916
  25.8 12.1 %collective-permute-start.4 = (bf16[512,384]{1,0:T(8,128)(2,1)S(1)}, bf16[512,384]{1,0:T(8,128)(2,1)S(1)}, u32[]{:S(2)}, u32[]{:S(2)}) collective-permute-start(bf16[512,384]{1,0:T(8,128)(2,1)S(1)} %get-tuple-element.91), channel_id=1, source_target_pairs={{0,1},{1,0},{2,3},{3,2},{4,5},{5,4},{6,7},{7,6},{8,9},{9,8},{10,11... | collective-permute-start | bytes 1179656 | tf_op jit(solution)/shard_map/ppermute | solution.py:269
  26.4 12.0 %collective-permute-start.1 = (bf16[512,384]{1,0:T(8,128)(2,1)S(1)}, bf16[512,384]{1,0:T(8,128)(2,1)S(1)}, u32[]{:S(2)}, u32[]{:S(2)}) collective-permute-start(bf16[512,384]{1,0:T(8,128)(2,1)S(1)} %get-tuple-element.92), channel_id=1, source_target_pairs={{0,2},{1,3},{2,0},{3,1},{4,6},{5,7},{6,4},{7,5},{8,10},{9,11},{10,... | collective-permute-start | bytes 1179656 | tf_op jit(solution)/shard_map/ppermute | solution.py:269
  26.5 24.7 %collective-permute-start.7 = (bf16[512,640]{1,0:T(8,128)(2,1)}, bf16[512,640]{1,0:T(8,128)(2,1)}, u32[]{:S(2)}, u32[]{:S(2)}) collective-permute-start(bf16[512,640]{1,0:T(8,128)(2,1)} %fusion.11.refs_0_), channel_id=1, source_target_pairs={{0,1},{1,0},{2,3},{3,2},{4,5},{5,4},{6,7},{7,6},{8,9},{9,8},{10,11... | collective-permute-start | bytes 1966088 | tf_op jit(solution)/shard_map/ppermute | solution.py:269
  28.5 22.8 %collective-permute-start.8 = (bf16[512,640]{1,0:T(8,128)(2,1)}, bf16[512,640]{1,0:T(8,128)(2,1)}, u32[]{:S(2)}, u32[]{:S(2)}) collective-permute-start(bf16[512,640]{1,0:T(8,128)(2,1)} %fusion.16.refs_1_), channel_id=1, source_target_pairs={{0,2},{1,3},{2,0},{3,1},{4,6},{5,7},{6,4},{7,5},{8,10},{9,11},{10,... | collective-permute-start | bytes 1966088 | tf_op jit(solution)/shard_map/ppermute | solution.py:269
  38.0 0.8 copy-start.1
  38.6 2.4 %copy-start.2 = (bf16[512,384]{1,0:T(8,128)(2,1)}, bf16[512,384]{1,0:T(8,128)(2,1)S(1)}, u32[]{:S(2)}) copy-start(bf16[512,384]{1,0:T(8,128)(2,1)S(1)} %add_convert_fusion.1.refs_0_) | copy-start | bytes 1179652
  38.6 1.8 collective-permute-start.5
  38.7 2.2 collective-permute-start.6
  40.4 0.8 copy-start.3
  41.1 0.7 copy-start.4
  53.9 18.4 %collective-permute-start.11 = (bf16[512,640]{1,0:T(8,128)(2,1)}, bf16[512,640]{1,0:T(8,128)(2,1)}, u32[]{:S(2)}, u32[]{:S(2)}) collective-permute-start(bf16[512,640]{1,0:T(8,128)(2,1)} %get-tuple-element.58.refs_0_), channel_id=1, source_target_pairs={{0,2},{1,3},{2,0},{3,1},{4,6},{5,7},{6,4},{7,5},{8,10},{9,11},{10,... | collective-permute-start | bytes 1966088 | tf_op jit(solution)/shard_map/ppermute | solution.py:269
  54.2 18.1 %collective-permute-start.12 = (bf16[512,640]{1,0:T(8,128)(2,1)}, bf16[512,640]{1,0:T(8,128)(2,1)}, u32[]{:S(2)}, u32[]{:S(2)}) collective-permute-start(bf16[512,640]{1,0:T(8,128)(2,1)} %get-tuple-element.59.refs_1_), channel_id=1, source_target_pairs={{0,1},{1,0},{2,3},{3,2},{4,5},{5,4},{6,7},{7,6},{8,9},{9,8},{10,11... | collective-permute-start | bytes 1966088 | tf_op jit(solution)/shard_map/ppermute | solution.py:269
  55.9 14.3 %collective-permute-start.9 = (bf16[688,384]{1,0:T(8,128)(2,1)}, bf16[688,384]{1,0:T(8,128)(2,1)}, u32[]{:S(2)}, u32[]{:S(2)}) collective-permute-start(bf16[688,384]{1,0:T(8,128)(2,1)} %gradient.4), channel_id=1, source_target_pairs={{0,8},{4,12},{8,16},{12,20},{16,24},{20,28},{24,0},{28,4},{1,9},{5... | collective-permute-start | bytes 1585160 | tf_op jit(solution)/shard_map/ppermute | solution.py:275
  74.9 2.4 %collective-permute-start.13 = (bf16[512,640]{1,0:T(8,128)(2,1)}, bf16[512,640]{1,0:T(8,128)(2,1)}, u32[]{:S(2)}, u32[]{:S(2)}) collective-permute-start(bf16[512,640]{1,0:T(8,128)(2,1)} %get-tuple-element.64.refs_0_), channel_id=1, source_target_pairs={{0,4},{4,0},{8,12},{12,8},{16,20},{20,16},{24,28},{28,24},{1,5},{5... | collective-permute-start | bytes 1966088 | tf_op jit(solution)/shard_map/ppermute | solution.py:272
  74.9 3.4 %collective-permute-start.14 = (bf16[512,640]{1,0:T(8,128)(2,1)}, bf16[512,640]{1,0:T(8,128)(2,1)}, u32[]{:S(2)}, u32[]{:S(2)}) collective-permute-start(bf16[512,640]{1,0:T(8,128)(2,1)} %get-tuple-element.65.refs_1_), channel_id=1, source_target_pairs={{0,4},{4,0},{8,12},{12,8},{16,20},{20,16},{24,28},{28,24},{1,5},{5... | collective-permute-start | bytes 1966088 | tf_op jit(solution)/shard_map/ppermute | solution.py:272
  75.4 23.8 %collective-permute-start.10 = (bf16[688,384]{1,0:T(8,128)(2,1)}, bf16[688,384]{1,0:T(8,128)(2,1)}, u32[]{:S(2)}, u32[]{:S(2)}) collective-permute-start(bf16[688,384]{1,0:T(8,128)(2,1)} %accumulate.6), channel_id=1, source_target_pairs={{0,8},{4,12},{8,16},{12,20},{16,24},{20,28},{24,0},{28,4},{1,9},{5... | collective-permute-start | bytes 1585160 | tf_op jit(solution)/shard_map/ppermute | solution.py:275
  85.6 25.7 %collective-permute-start.17 = (bf16[352,640]{1,0:T(8,128)(2,1)}, bf16[352,640]{1,0:T(8,128)(2,1)}, u32[]{:S(2)}, u32[]{:S(2)}) collective-permute-start(bf16[352,640]{1,0:T(8,128)(2,1)} %get-tuple-element.66), channel_id=1, source_target_pairs={{0,8},{4,12},{8,16},{12,20},{16,24},{20,28},{24,0},{28,4},{1,9},{5... | collective-permute-start | bytes 1351688 | tf_op jit(solution)/shard_map/ppermute | solution.py:275
  85.6 25.6 %collective-permute-start.16 = (bf16[336,640]{1,0:T(8,128)(2,1)}, bf16[336,640]{1,0:T(8,128)(2,1)}, u32[]{:S(2)}, u32[]{:S(2)}) collective-permute-start(bf16[336,640]{1,0:T(8,128)(2,1)} %get-tuple-element.67), channel_id=1, source_target_pairs={{0,8},{4,12},{8,16},{12,20},{16,24},{20,28},{24,0},{28,4},{1,9},{5... | collective-permute-start | bytes 1290248 | tf_op jit(solution)/shard_map/ppermute | solution.py:275
  101.3 21.3 %collective-permute-start.15 = (bf16[688,384]{1,0:T(8,128)(2,1)}, bf16[688,384]{1,0:T(8,128)(2,1)}, u32[]{:S(2)}, u32[]{:S(2)}) collective-permute-start(bf16[688,384]{1,0:T(8,128)(2,1)} %accumulate.7), channel_id=1, source_target_pairs={{0,8},{4,12},{8,16},{12,20},{16,24},{20,28},{24,0},{28,4},{1,9},{5... | collective-permute-start | bytes 1585160 | tf_op jit(solution)/shard_map/ppermute | solution.py:275
  113.3 18.9 %collective-permute-start.20 = (bf16[352,640]{1,0:T(8,128)(2,1)}, bf16[352,640]{1,0:T(8,128)(2,1)}, u32[]{:S(2)}, u32[]{:S(2)}) collective-permute-start(bf16[352,640]{1,0:T(8,128)(2,1)} %accumulate.8), channel_id=1, source_target_pairs={{0,8},{4,12},{8,16},{12,20},{16,24},{20,28},{24,0},{28,4},{1,9},{5... | collective-permute-start | bytes 1351688 | tf_op jit(solution)/shard_map/ppermute | solution.py:275
  126.5 17.6 %collective-permute-start.18 = (bf16[688,384]{1,0:T(8,128)(2,1)}, bf16[688,384]{1,0:T(8,128)(2,1)}, u32[]{:S(2)}, u32[]{:S(2)}) collective-permute-start(bf16[688,384]{1,0:T(8,128)(2,1)} %get-tuple-element.77.refs_0_), channel_id=1, source_target_pairs={{0,1},{1,0},{2,3},{3,2},{4,5},{5,4},{6,7},{7,6},{8,9},{9,8},{10,11... | collective-permute-start | bytes 1585160 | tf_op jit(solution)/shard_map/ppermute | solution.py:269
  127.1 15.0 %collective-permute-start.19 = (bf16[336,640]{1,0:T(8,128)(2,1)}, bf16[336,640]{1,0:T(8,128)(2,1)}, u32[]{:S(2)}, u32[]{:S(2)}) collective-permute-start(bf16[336,640]{1,0:T(8,128)(2,1)} %accumulate.9), channel_id=1, source_target_pairs={{0,8},{4,12},{8,16},{12,20},{16,24},{20,28},{24,0},{28,4},{1,9},{5... | collective-permute-start | bytes 1290248 | tf_op jit(solution)/shard_map/ppermute | solution.py:275
  134.2 17.5 %collective-permute-start.24 = (bf16[352,640]{1,0:T(8,128)(2,1)}, bf16[352,640]{1,0:T(8,128)(2,1)}, u32[]{:S(2)}, u32[]{:S(2)}) collective-permute-start(bf16[352,640]{1,0:T(8,128)(2,1)} %accumulate.10), channel_id=1, source_target_pairs={{0,8},{4,12},{8,16},{12,20},{16,24},{20,28},{24,0},{28,4},{1,9},{5... | collective-permute-start | bytes 1351688 | tf_op jit(solution)/shard_map/ppermute | solution.py:275
  144.1 24.2 %collective-permute-start.21 = (bf16[688,384]{1,0:T(8,128)(2,1)}, bf16[688,384]{1,0:T(8,128)(2,1)}, u32[]{:S(2)}, u32[]{:S(2)}) collective-permute-start(bf16[688,384]{1,0:T(8,128)(2,1)} %get-tuple-element.77.refs_0_), channel_id=1, source_target_pairs={{0,2},{1,3},{2,0},{3,1},{4,6},{5,7},{6,4},{7,5},{8,10},{9,11},{10,... | collective-permute-start | bytes 1585160 | tf_op jit(solution)/shard_map/ppermute | solution.py:269
  145.6 39.4 %collective-permute-start.22 = (bf16[688,384]{1,0:T(8,128)(2,1)}, bf16[688,384]{1,0:T(8,128)(2,1)}, u32[]{:S(2)}, u32[]{:S(2)}) collective-permute-start(bf16[688,384]{1,0:T(8,128)(2,1)} %collective-permute-done.18.refs_1_), channel_id=1, source_target_pairs={{0,2},{1,3},{2,0},{3,1},{4,6},{5,7},{6,4},{7,5},{8,10},{9,11},{10,... | collective-permute-start | bytes 1585160 | tf_op jit(solution)/shard_map/ppermute | solution.py:269
  146.1 13.3 %collective-permute-start.23 = (bf16[336,640]{1,0:T(8,128)(2,1)}, bf16[336,640]{1,0:T(8,128)(2,1)}, u32[]{:S(2)}, u32[]{:S(2)}) collective-permute-start(bf16[336,640]{1,0:T(8,128)(2,1)} %accumulate.11), channel_id=1, source_target_pairs={{0,8},{4,12},{8,16},{12,20},{16,24},{20,28},{24,0},{28,4},{1,9},{5... | collective-permute-start | bytes 1290248 | tf_op jit(solution)/shard_map/ppermute | solution.py:275
  155.3 35.9 %collective-permute-start.30 = (bf16[352,640]{1,0:T(8,128)(2,1)}, bf16[352,640]{1,0:T(8,128)(2,1)}, u32[]{:S(2)}, u32[]{:S(2)}) collective-permute-start(bf16[352,640]{1,0:T(8,128)(2,1)} %get-tuple-element.88.refs_4_), channel_id=1, source_target_pairs={{0,3},{1,2},{2,1},{3,0},{4,7},{5,6},{6,5},{7,4},{8,11},{9,10},{10,... | collective-permute-start | bytes 1351688 | tf_op jit(solution)/shard_map/ppermute | solution.py:269
  157.6 41.6 %collective-permute-start.29 = (bf16[352,640]{1,0:T(8,128)(2,1)}, bf16[352,640]{1,0:T(8,128)(2,1)}, u32[]{:S(2)}, u32[]{:S(2)}) collective-permute-start(bf16[352,640]{1,0:T(8,128)(2,1)} %get-tuple-element.88.refs_4_), channel_id=1, source_target_pairs={{0,2},{1,3},{2,0},{3,1},{4,6},{5,7},{6,4},{7,5},{8,10},{9,11},{10,... | collective-permute-start | bytes 1351688 | tf_op jit(solution)/shard_map/ppermute | solution.py:269
  159.4 39.8 %collective-permute-start.28 = (bf16[352,640]{1,0:T(8,128)(2,1)}, bf16[352,640]{1,0:T(8,128)(2,1)}, u32[]{:S(2)}, u32[]{:S(2)}) collective-permute-start(bf16[352,640]{1,0:T(8,128)(2,1)} %get-tuple-element.88.refs_4_), channel_id=1, source_target_pairs={{0,1},{1,0},{2,3},{3,2},{4,5},{5,4},{6,7},{7,6},{8,9},{9,8},{10,11... | collective-permute-start | bytes 1351688 | tf_op jit(solution)/shard_map/ppermute | solution.py:269
  188.3 22.7 %collective-permute-start.27 = (bf16[336,640]{1,0:T(8,128)(2,1)}, bf16[336,640]{1,0:T(8,128)(2,1)}, u32[]{:S(2)}, u32[]{:S(2)}) collective-permute-start(bf16[336,640]{1,0:T(8,128)(2,1)} %get-tuple-element.87.refs_4_), channel_id=1, source_target_pairs={{0,3},{1,2},{2,1},{3,0},{4,7},{5,6},{6,5},{7,4},{8,11},{9,10},{10,... | collective-permute-start | bytes 1290248 | tf_op jit(solution)/shard_map/ppermute | solution.py:269
  190.7 20.4 %collective-permute-start.26 = (bf16[336,640]{1,0:T(8,128)(2,1)}, bf16[336,640]{1,0:T(8,128)(2,1)}, u32[]{:S(2)}, u32[]{:S(2)}) collective-permute-start(bf16[336,640]{1,0:T(8,128)(2,1)} %get-tuple-element.87.refs_4_), channel_id=1, source_target_pairs={{0,2},{1,3},{2,0},{3,1},{4,6},{5,7},{6,4},{7,5},{8,10},{9,11},{10,... | collective-permute-start | bytes 1290248 | tf_op jit(solution)/shard_map/ppermute | solution.py:269
  191.2 19.9 %collective-permute-start.25 = (bf16[336,640]{1,0:T(8,128)(2,1)}, bf16[336,640]{1,0:T(8,128)(2,1)}, u32[]{:S(2)}, u32[]{:S(2)}) collective-permute-start(bf16[336,640]{1,0:T(8,128)(2,1)} %get-tuple-element.87.refs_4_), channel_id=1, source_target_pairs={{0,1},{1,0},{2,3},{3,2},{4,5},{5,4},{6,7},{7,6},{8,9},{9,8},{10,11... | collective-permute-start | bytes 1290248 | tf_op jit(solution)/shard_map/ppermute | solution.py:269
